TPU v7x, 256 devices: a whole 4x4x8 slice. The times are simulated.
256 devices in a mesh: slab: 16 (over x, y), col: 8 (over z), energy: 2 (over core).
Axes of the slice: x: 4, y: 4, z: 8, core: 2. Of those that a mesh axis runs over, the one named last changes fastest.
Arguments:
- diag_inverse: float32 [64, 2, 2048, 2048], P(('energy', 'slab'), None, None, 'col'), parts along dimension 0, may hold values from -2 to 2
- couplings: float32 [64, 2, 256, 256], P(('energy', 'slab')), parts along dimension 0, may hold values from -1 to 1
- sources: float32 [4, 2, 2048, 64], P('energy', None, 'col'), parts along dimension 0, may hold values from -6 to 6
- inject: int32 [2, 64], replicated, may hold values from 0 to 31, as said below
- leads: float32 [4, 2, 256, 64], P('energy'), parts along dimension 0, may hold values from -6 to 6
Outputs:
- left_states: float32 [64, 2, 2048, 64], P(('energy', 'slab'), None, 'col'), parts along dimension 0
- right_states: float32 [64, 2, 2048, 64], P(('energy', 'slab'), None, 'col'), parts along dimension 0
There are 2 independent parts, one for each index of `energy`. A program takes and returns all parts, laid end to end along the dimension named above; an argument that names none is the same for every part. Nothing has to cross between parts.
Inputs may be any that keep to these rules, and one draw needn't show every extreme that they name: `inject`: slab index of each injected column; in each sweep column 0 goes into slab 0 and column 1 into the last slab.
All inputs are finite; a program needn't handle non-finite values.
Results may differ from a plain program's by a relative error of at most 0.0003.
Values sent between devices are 32-bit elements; how exact they have to be, the bound alone decides.
No kernel may reach another device: no remote copies, remote signals or barrier semaphores. Data moves between devices by JAX's collectives and lax.ppermute only.
A program may use at most 192 MiB of HBM per device.

v0:
```python
import jax
import jax.numpy as jnp
from jax import lax
from jax.sharding import PartitionSpec as P


def shifted(value, axis, steps):
    count = lax.axis_size(axis)
    leading, last = (max(0, -steps), min(count, count - steps))
    return lax.ppermute(value, axis, [(source, source + steps) for source in range(leading, last)])


def real_dot(left, right):
    return jnp.dot(left, right, precision=lax.Precision.HIGHEST, preferred_element_type=jnp.float32)


def apply_complex(matrix, vector):
    real_part = real_dot(matrix[0], vector[:, 0]) - real_dot(matrix[1], vector[:, 1])
    imag_part = real_dot(matrix[0], vector[:, 1]) + real_dot(matrix[1], vector[:, 0])
    return jnp.stack([real_part, imag_part], axis=1)


def as_matrix(rows_first):
    return jnp.transpose(rows_first, (1, 0, 2))


def place_rows(values, slot, stride):
    rim_count = values.shape[0]
    spread = jnp.zeros((rim_count, stride) + values.shape[1:], jnp.float32)
    return spread.at[:, slot].set(values).reshape((rim_count * stride,) + values.shape[1:])


def adjoint_of(coupling):
    return jnp.stack([coupling[0].T, -coupling[1].T], axis=0)


def on_device(diag_inverse, couplings, sources, inject, leads):
    slab_count = diag_inverse.shape[0]
    orbitals = diag_inverse.shape[2]
    part_cols = diag_inverse.shape[3]
    iface_width = couplings.shape[2]
    mode_count = sources.shape[3]
    stride = orbitals // iface_width
    rim_count = part_cols // stride
    slab_total = lax.axis_size("slab")
    col_index = lax.axis_index("col")
    slab_index = lax.axis_index("slab")
    first_slab = slab_index * slab_count
    row_start = col_index * rim_count
    global_rows = row_start + jnp.arange(rim_count, dtype=jnp.int32)
    unit_rows = (jnp.arange(iface_width, dtype=jnp.int32)[None, :] == global_rows[:, None]).astype(
        jnp.float32
    )
    unit_rows = jnp.stack([unit_rows, jnp.zeros_like(unit_rows)], axis=1)
    own_sources = jnp.transpose(sources, (0, 2, 1, 3))
    width_zeros = jnp.zeros((part_cols, 2, iface_width), jnp.float32)
    mode_zeros = jnp.zeros((rim_count, 2, mode_count), jnp.float32)

    def source_block(table, sweep, slab_local):
        chosen = inject[sweep] == first_slab + slab_local
        return jnp.where(chosen[None, None, :], table[sweep], jnp.float32(0.0))

    results = []
    gathered = None
    for step_index in range(slab_count):
        left_slab = step_index
        right_slab = slab_count - 1 - step_index
        left_base = jnp.concatenate([source_block(own_sources, 0, left_slab), width_zeros], axis=2)
        right_base = jnp.concatenate(
            [source_block(own_sources, 1, right_slab), width_zeros], axis=2
        )
        if step_index == 0:
            own_rows = jnp.transpose(
                lax.dynamic_slice_in_dim(couplings[0], row_start, rim_count, 1), (1, 0, 2)
            )
            left_rim = jnp.concatenate([mode_zeros, own_rows], axis=2)
            right_rim = jnp.concatenate([mode_zeros, unit_rows], axis=2)
        else:
            left_rows = lax.dynamic_slice_in_dim(couplings[left_slab], row_start, rim_count, 1)
            left_rim = apply_complex(left_rows, gathered[:, 0])
            columns = lax.dynamic_slice_in_dim(couplings[right_slab + 1], row_start, rim_count, 2)
            right_rim = apply_complex(
                jnp.stack([columns[0].T, -columns[1].T], axis=0), gathered[:, 1]
            )
        left_input = left_base + place_rows(left_rim, 0, stride)
        right_input = right_base + place_rows(right_rim, 1, stride)
        state = jnp.stack([left_input, right_input], axis=1)

        def slab_term(start, count, state=state, left_slab=left_slab, right_slab=right_slab):
            left_block = diag_inverse[left_slab]
            right_block = diag_inverse[right_slab]
            return jnp.stack(
                [apply_complex(left_block, state[:, 0]), apply_complex(right_block, state[:, 1])],
                axis=1,
            )

        product = lax.psum_scatter(
            slab_term(jnp.int32(0), part_cols * lax.axis_size("col")),
            "col",
            scatter_dimension=0,
            tiled=True,
        )
        results.append(product)
        split_rows = product.reshape((rim_count, stride) + product.shape[1:])
        rim_values = jnp.stack([split_rows[:, 1, 0], split_rows[:, 0, 1]], axis=1)
        gathered = lax.all_gather(rim_values, "col", axis=0, tiled=True)
    left_map = (gathered[:, 0, :, mode_count:], gathered[:, 0, :, :mode_count])
    adjoint_full = adjoint_of(couplings[0])
    right_leaving = apply_complex(adjoint_full, gathered[:, 1])
    right_map = (right_leaving[:, :, mode_count:], right_leaving[:, :, :mode_count])
    left_lead = jnp.transpose(leads[0], (1, 0, 2))
    right_lead = jnp.transpose(leads[1], (1, 0, 2))

    def advance(tick, carry):
        left_now, right_now = carry
        right_active = slab_total - 1 - tick
        left_sent = lax.cond(
            slab_index == tick,
            lambda: apply_complex(as_matrix(left_map[0]), left_now) + left_map[1],
            lambda: jnp.zeros_like(left_now),
        )
        right_sent = lax.cond(
            slab_index == right_active,
            lambda: apply_complex(as_matrix(right_map[0]), right_now) + right_map[1],
            lambda: jnp.zeros_like(right_now),
        )
        left_recv = shifted(left_sent, "slab", 1)
        right_recv = shifted(right_sent, "slab", -1)
        left_now = jnp.where(slab_index == tick + 1, left_recv, left_now)
        right_now = jnp.where(slab_index == right_active - 1, right_recv, right_now)
        return (left_now, right_now)

    left_inflow, right_inflow = lax.fori_loop(0, slab_total - 1, advance, (left_lead, right_lead))
    left_list = []
    right_list = []
    for slab_local in range(slab_count):
        left_part = results[slab_local][:, 0]
        left_final = left_part[:, :, :mode_count] + apply_complex(
            as_matrix(left_part[:, :, mode_count:]), left_inflow
        )
        right_part = results[slab_count - 1 - slab_local][:, 1]
        right_final = right_part[:, :, :mode_count] + apply_complex(
            as_matrix(right_part[:, :, mode_count:]), right_inflow
        )
        left_list.append(jnp.transpose(left_final, (1, 0, 2)))
        right_list.append(jnp.transpose(right_final, (1, 0, 2)))
    return (jnp.stack(left_list, axis=0), jnp.stack(right_list, axis=0))


def solution(mesh):
    placed = (
        P(("energy", "slab"), None, None, "col"),
        P(("energy", "slab"), None, None, None),
        P("energy", None, "col", None),
        P(),
        P("energy", None, None, None),
    )
    return jax.shard_map(
        on_device,
        mesh=mesh,
        in_specs=placed,
        out_specs=(
            P(("energy", "slab"), None, "col", None),
            P(("energy", "slab"), None, "col", None),
        ),
        check_vma=False,
    )
```

profile of v0, /device:TPU:8, one launch (start us, length us, event | category | flops | bytes accessed | tf_op | source)
XLA Modules:
  0.0 680.5 jit_solution(16750083305788448023)
XLA Ops:
  10.1 7.0 %fusion.52 = f32[320,2048]{1,0:T(8,128)S(1)} fusion(f32[2,2,2048,256]{3,2,1,0:T(8,128)} %param.19, f32[256,2,320]{2,0,1:T(8,128)S(1)} %fusion.88), kind=kOutput, calls=%fused_computation.74 | convolution fusion | flops 2013265920 | bytes 5111808 | tf_op jit(solution)/shard_map/dot_general | solution.py:14
  17.1 6.9 %fusion.54 = f32[320,2048]{1,0:T(8,128)S(1)} fusion(f32[2,2,2048,256]{3,2,1,0:T(8,128)} %param.19, f32[256,2,320]{2,0,1:T(8,128)S(1)} %fusion.88), kind=kOutput, calls=%fused_computation.76 | convolution fusion | flops 2013265920 | bytes 5111808 | tf_op jit(solution)/shard_map/dot_general | solution.py:14
  24.8 5.4 fusion.42
  35.5 5.7 fusion.30
  51.7 5.4 fusion.28
  62.8 117.7 %reduce-scatter.3.cloned.1.call-done = f32[256,2,2,320]{0,3,2,1:T(8,128)} async-done(((f32[2048,2,2,320]{0,3,2,1:T(8,128)}), f32[256,2,2,320]{0,3,2,1:T(8,128)}) %reduce-scatter.3.cloned.1.call-update) | async-done | bytes 1310736 | tf_op jit(solution)/shard_map/reduce_scatter | solution.py:97
  183.2 38.8 %all-gather.3.cloned.1.call-done = f32[256,2,2,320]{3,0,2,1:T(8,128)} async-done(((f32[32,2,2,320]{3,0,2,1:T(8,128)}), f32[256,2,2,320]{3,0,2,1:T(8,128)}) %all-gather.3.cloned.1.call-update) | async-done | bytes 1310736 | tf_op jit(solution)/shard_map/all_gather | solution.py:106
  227.3 7.3 %fusion.38 = f32[320,2048]{1,0:T(8,128)S(1)} fusion(f32[2,2,2048,256]{3,2,1,0:T(8,128)} %param.19, f32[256,2,320]{2,0,1:T(8,128)S(1)} %get-tuple-element.429), kind=kOutput, calls=%fused_computation.60 | convolution fusion | flops 2013265920 | bytes 5111808 | tf_op jit(solution)/shard_map/dot_general | solution.py:14
  234.6 5.7 fusion.36
  261.5 5.5 fusion.25
  277.9 113.4 %reduce-scatter.5.cloned.1.call-done = f32[256,2,2,320]{0,3,2,1:T(8,128)} async-done(((f32[2048,2,2,320]{0,3,2,1:T(8,128)}), f32[256,2,2,320]{0,3,2,1:T(8,128)}) %reduce-scatter.5.cloned.1.call-update) | async-done | bytes 1310736 | tf_op jit(solution)/shard_map/reduce_scatter | solution.py:97
  397.3 35.5 %all-gather.5.cloned.1.call-done = f32[256,2,2,320]{3,0,2,1:T(8,128)} async-done(((f32[32,2,2,320]{3,0,2,1:T(8,128)}), f32[256,2,2,320]{3,0,2,1:T(8,128)}) %all-gather.5.cloned.1.call-update) | async-done | bytes 1310736 | tf_op jit(solution)/shard_map/all_gather | solution.py:106
  440.4 221.7 %while.23 = (s32[]{:T(128)}, f32[256,2,64]{0,2,1:T(8,128)S(1)}, f32[256,2,64]{0,2,1:T(8,128)S(1)}, s32[]{:T(128)}, f32[256,2,256]{2,1,0:T(2,128)S(1)}, /*index=5...) while((s32[]{:T(128)}, f32[256,2,64]{0,2,1:T(8,128)S(1)}, ...), condition=%wide.region_7.0_spmd, body=%wide.region_2.7_spmd.sunk | while | flops 402915328 | bytes 10224005 | solution.py:133
  466.4 6.3 collective-permute-start
  513.4 7.8 %collective-permute-done.1 = f32[256,2,64]{0,2,1:T(8,128)S(1)} collective-permute-done((f32[256,2,64]{0,2,1:T(8,128)}, f32[256,2,64]{0,2,1:T(8,128)S(1)}, u32[]{:S(2)}, u32[]{:S(2)}) %collective-permute-start.1) | collective-permute-done | bytes 131104 | tf_op jit(solution)/shard_map/while/body/eval_jaxpr/ppermute | solution.py:10
  567.3 6.5 collective-permute-done.1
  574.5 5.7 collective-permute-start
  583.1 7.1 %collective-permute-done.1 = f32[256,2,64]{0,2,1:T(8,128)S(1)} collective-permute-done((f32[256,2,64]{0,2,1:T(8,128)}, f32[256,2,64]{0,2,1:T(8,128)S(1)}, u32[]{:S(2)}, u32[]{:S(2)}) %collective-permute-start.1) | collective-permute-done | bytes 131104 | tf_op jit(solution)/shard_map/while/body/eval_jaxpr/ppermute | solution.py:10
  591.0 6.0 collective-permute-start
  599.8 9.0 %collective-permute-done.1 = f32[256,2,64]{0,2,1:T(8,128)S(1)} collective-permute-done((f32[256,2,64]{0,2,1:T(8,128)}, f32[256,2,64]{0,2,1:T(8,128)S(1)}, u32[]{:S(2)}, u32[]{:S(2)}) %collective-permute-start.1) | collective-permute-done | bytes 131104 | tf_op jit(solution)/shard_map/while/body/eval_jaxpr/ppermute | solution.py:10
  609.5 6.3 collective-permute-start
  618.6 8.6 %collective-permute-done.1 = f32[256,2,64]{0,2,1:T(8,128)S(1)} collective-permute-done((f32[256,2,64]{0,2,1:T(8,128)}, f32[256,2,64]{0,2,1:T(8,128)S(1)}, u32[]{:S(2)}, u32[]{:S(2)}) %collective-permute-start.1) | collective-permute-done | bytes 131104 | tf_op jit(solution)/shard_map/while/body/eval_jaxpr/ppermute | solution.py:10
  628.0 7.7 %collective-permute-start = (f32[256,2,64]{0,2,1:T(8,128)}, f32[256,2,64]{0,2,1:T(8,128)S(1)}, u32[]{:S(2)}, u32[]{:S(2)}) collective-permute-start(f32[256,2,64]{0,2,1:T(8,128)} %copy-done.4), channel_id=1, source_target_pairs={{0,16},{16,32},{32,48},{48,64},{64,80},{80,96},{96,112},{112,128},... | collective-permute-start | bytes 393224 | tf_op jit(solution)/shard_map/while/body/eval_jaxpr/ppermute | solution.py:10
  638.5 8.8 %collective-permute-done.1 = f32[256,2,64]{0,2,1:T(8,128)S(1)} collective-permute-done((f32[256,2,64]{0,2,1:T(8,128)}, f32[256,2,64]{0,2,1:T(8,128)S(1)}, u32[]{:S(2)}, u32[]{:S(2)}) %collective-permute-start.1) | collective-permute-done | bytes 131104 | tf_op jit(solution)/shard_map/while/body/eval_jaxpr/ppermute | solution.py:10
  (342 shorter events, 235.0 us)
Async XLA Ops:
  7.2 173.3 %reduce-scatter.3.cloned.1.call-start = ((), (), s32[]{:S(2)}) async-start(), calls=%async_computation.2 | async-start | bytes 11796480 | tf_op jit(solution)/shard_map/reduce_scatter | solution.py:97
  62.7 159.3 %all-gather.3.cloned.1.call-start = ((), (), s32[]{:S(2)}) async-start(), calls=%async_computation.3 | async-start | bytes 1769472 | tf_op jit(solution)/shard_map/all_gather | solution.py:106
  183.1 208.2 %reduce-scatter.5.cloned.1.call-start = ((), (), s32[]{:S(2)}) async-start(), calls=%async_computation.4 | async-start | bytes 11796480 | tf_op jit(solution)/shard_map/reduce_scatter | solution.py:97
  277.9 155.0 %all-gather.5.cloned.1.call-start = ((), (), s32[]{:S(2)}) async-start(), calls=%async_computation.5 | async-start | bytes 1769472 | tf_op jit(solution)/shard_map/all_gather | solution.py:106
  441.4 7.3 %collective-permute-start = (f32[256,2,64]{0,2,1:T(8,128)}, f32[256,2,64]{0,2,1:T(8,128)S(1)}, u32[]{:S(2)}, u32[]{:S(2)}) collective-permute-start(f32[256,2,64]{0,2,1:T(8,128)} %copy-done.4), channel_id=1, source_target_pairs={{0,16},{16,32},{32,48},{48,64},{64,80},{80,96},{96,112},{112,128},... | collective-permute-start | bytes 393224 | tf_op jit(solution)/shard_map/while/body/eval_jaxpr/ppermute | solution.py:10
  458.2 7.4 %collective-permute-start.1 = (f32[256,2,64]{0,2,1:T(8,128)}, f32[256,2,64]{0,2,1:T(8,128)S(1)}, u32[]{:S(2)}, u32[]{:S(2)}) collective-permute-start(f32[256,2,64]{0,2,1:T(8,128)} %copy-done.5), channel_id=1, source_target_pairs={{16,0},{32,16},{48,32},{64,48},{80,64},{96,80},{112,96},{128,112},... | collective-permute-start | bytes 393224 | tf_op jit(solution)/shard_map/while/body/eval_jaxpr/ppermute | solution.py:10
  466.4 9.1 %collective-permute-start = (f32[256,2,64]{0,2,1:T(8,128)}, f32[256,2,64]{0,2,1:T(8,128)S(1)}, u32[]{:S(2)}, u32[]{:S(2)}) collective-permute-start(f32[256,2,64]{0,2,1:T(8,128)} %copy-done.4), channel_id=1, source_target_pairs={{0,16},{16,32},{32,48},{48,64},{64,80},{80,96},{96,112},{112,128},... | collective-permute-start | bytes 393224 | tf_op jit(solution)/shard_map/while/body/eval_jaxpr/ppermute | solution.py:10
  483.8 9.3 %collective-permute-start.1 = (f32[256,2,64]{0,2,1:T(8,128)}, f32[256,2,64]{0,2,1:T(8,128)S(1)}, u32[]{:S(2)}, u32[]{:S(2)}) collective-permute-start(f32[256,2,64]{0,2,1:T(8,128)} %copy-done.5), channel_id=1, source_target_pairs={{16,0},{32,16},{48,32},{64,48},{80,64},{96,80},{112,96},{128,112},... | collective-permute-start | bytes 393224 | tf_op jit(solution)/shard_map/while/body/eval_jaxpr/ppermute | solution.py:10
  498.4 7.2 %collective-permute-start.1 = (f32[256,2,64]{0,2,1:T(8,128)}, f32[256,2,64]{0,2,1:T(8,128)S(1)}, u32[]{:S(2)}, u32[]{:S(2)}) collective-permute-start(f32[256,2,64]{0,2,1:T(8,128)} %copy-done.5), channel_id=1, source_target_pairs={{16,0},{32,16},{48,32},{64,48},{80,64},{96,80},{112,96},{128,112},... | collective-permute-start | bytes 393224 | tf_op jit(solution)/shard_map/while/body/eval_jaxpr/ppermute | solution.py:10
  511.0 10.2 %collective-permute-start.1 = (f32[256,2,64]{0,2,1:T(8,128)}, f32[256,2,64]{0,2,1:T(8,128)S(1)}, u32[]{:S(2)}, u32[]{:S(2)}) collective-permute-start(f32[256,2,64]{0,2,1:T(8,128)} %copy-done.5), channel_id=1, source_target_pairs={{16,0},{32,16},{48,32},{64,48},{80,64},{96,80},{112,96},{128,112},... | collective-permute-start | bytes 393224 | tf_op jit(solution)/shard_map/while/body/eval_jaxpr/ppermute | solution.py:10
  521.9 7.7 %collective-permute-start = (f32[256,2,64]{0,2,1:T(8,128)}, f32[256,2,64]{0,2,1:T(8,128)S(1)}, u32[]{:S(2)}, u32[]{:S(2)}) collective-permute-start(f32[256,2,64]{0,2,1:T(8,128)} %copy-done.4), channel_id=1, source_target_pairs={{0,16},{16,32},{32,48},{48,64},{64,80},{80,96},{96,112},{112,128},... | collective-permute-start | bytes 393224 | tf_op jit(solution)/shard_map/while/body/eval_jaxpr/ppermute | solution.py:10
  526.8 7.6 %collective-permute-start.1 = (f32[256,2,64]{0,2,1:T(8,128)}, f32[256,2,64]{0,2,1:T(8,128)S(1)}, u32[]{:S(2)}, u32[]{:S(2)}) collective-permute-start(f32[256,2,64]{0,2,1:T(8,128)} %copy-done.5), channel_id=1, source_target_pairs={{16,0},{32,16},{48,32},{64,48},{80,64},{96,80},{112,96},{128,112},... | collective-permute-start | bytes 393224 | tf_op jit(solution)/shard_map/while/body/eval_jaxpr/ppermute | solution.py:10
  539.4 7.4 %collective-permute-start.1 = (f32[256,2,64]{0,2,1:T(8,128)}, f32[256,2,64]{0,2,1:T(8,128)S(1)}, u32[]{:S(2)}, u32[]{:S(2)}) collective-permute-start(f32[256,2,64]{0,2,1:T(8,128)} %copy-done.5), channel_id=1, source_target_pairs={{16,0},{32,16},{48,32},{64,48},{80,64},{96,80},{112,96},{128,112},... | collective-permute-start | bytes 393224 | tf_op jit(solution)/shard_map/while/body/eval_jaxpr/ppermute | solution.py:10
  552.3 7.2 %collective-permute-start.1 = (f32[256,2,64]{0,2,1:T(8,128)}, f32[256,2,64]{0,2,1:T(8,128)S(1)}, u32[]{:S(2)}, u32[]{:S(2)}) collective-permute-start(f32[256,2,64]{0,2,1:T(8,128)} %copy-done.5), channel_id=1, source_target_pairs={{16,0},{32,16},{48,32},{64,48},{80,64},{96,80},{112,96},{128,112},... | collective-permute-start | bytes 393224 | tf_op jit(solution)/shard_map/while/body/eval_jaxpr/ppermute | solution.py:10
  564.8 9.0 %collective-permute-start.1 = (f32[256,2,64]{0,2,1:T(8,128)}, f32[256,2,64]{0,2,1:T(8,128)S(1)}, u32[]{:S(2)}, u32[]{:S(2)}) collective-permute-start(f32[256,2,64]{0,2,1:T(8,128)} %copy-done.5), channel_id=1, source_target_pairs={{16,0},{32,16},{48,32},{64,48},{80,64},{96,80},{112,96},{128,112},... | collective-permute-start | bytes 393224 | tf_op jit(solution)/shard_map/while/body/eval_jaxpr/ppermute | solution.py:10
  574.5 8.6 %collective-permute-start = (f32[256,2,64]{0,2,1:T(8,128)}, f32[256,2,64]{0,2,1:T(8,128)S(1)}, u32[]{:S(2)}, u32[]{:S(2)}) collective-permute-start(f32[256,2,64]{0,2,1:T(8,128)} %copy-done.4), channel_id=1, source_target_pairs={{0,16},{16,32},{32,48},{48,64},{64,80},{80,96},{96,112},{112,128},... | collective-permute-start | bytes 393224 | tf_op jit(solution)/shard_map/while/body/eval_jaxpr/ppermute | solution.py:10
  581.0 9.2 %collective-permute-start.1 = (f32[256,2,64]{0,2,1:T(8,128)}, f32[256,2,64]{0,2,1:T(8,128)S(1)}, u32[]{:S(2)}, u32[]{:S(2)}) collective-permute-start(f32[256,2,64]{0,2,1:T(8,128)} %copy-done.5), channel_id=1, source_target_pairs={{16,0},{32,16},{48,32},{64,48},{80,64},{96,80},{112,96},{128,112},... | collective-permute-start | bytes 393224 | tf_op jit(solution)/shard_map/while/body/eval_jaxpr/ppermute | solution.py:10
  591.0 8.8 %collective-permute-start = (f32[256,2,64]{0,2,1:T(8,128)}, f32[256,2,64]{0,2,1:T(8,128)S(1)}, u32[]{:S(2)}, u32[]{:S(2)}) collective-permute-start(f32[256,2,64]{0,2,1:T(8,128)} %copy-done.4), channel_id=1, source_target_pairs={{0,16},{16,32},{32,48},{48,64},{64,80},{80,96},{96,112},{112,128},... | collective-permute-start | bytes 393224 | tf_op jit(solution)/shard_map/while/body/eval_jaxpr/ppermute | solution.py:10
  597.6 11.1 %collective-permute-start.1 = (f32[256,2,64]{0,2,1:T(8,128)}, f32[256,2,64]{0,2,1:T(8,128)S(1)}, u32[]{:S(2)}, u32[]{:S(2)}) collective-permute-start(f32[256,2,64]{0,2,1:T(8,128)} %copy-done.5), channel_id=1, source_target_pairs={{16,0},{32,16},{48,32},{64,48},{80,64},{96,80},{112,96},{128,112},... | collective-permute-start | bytes 393224 | tf_op jit(solution)/shard_map/while/body/eval_jaxpr/ppermute | solution.py:10
  609.5 9.1 %collective-permute-start = (f32[256,2,64]{0,2,1:T(8,128)}, f32[256,2,64]{0,2,1:T(8,128)S(1)}, u32[]{:S(2)}, u32[]{:S(2)}) collective-permute-start(f32[256,2,64]{0,2,1:T(8,128)} %copy-done.4), channel_id=1, source_target_pairs={{0,16},{16,32},{32,48},{48,64},{64,80},{80,96},{96,112},{112,128},... | collective-permute-start | bytes 393224 | tf_op jit(solution)/shard_map/while/body/eval_jaxpr/ppermute | solution.py:10
  616.5 10.7 %collective-permute-start.1 = (f32[256,2,64]{0,2,1:T(8,128)}, f32[256,2,64]{0,2,1:T(8,128)S(1)}, u32[]{:S(2)}, u32[]{:S(2)}) collective-permute-start(f32[256,2,64]{0,2,1:T(8,128)} %copy-done.5), channel_id=1, source_target_pairs={{16,0},{32,16},{48,32},{64,48},{80,64},{96,80},{112,96},{128,112},... | collective-permute-start | bytes 393224 | tf_op jit(solution)/shard_map/while/body/eval_jaxpr/ppermute | solution.py:10
  628.0 10.5 %collective-permute-start = (f32[256,2,64]{0,2,1:T(8,128)}, f32[256,2,64]{0,2,1:T(8,128)S(1)}, u32[]{:S(2)}, u32[]{:S(2)}) collective-permute-start(f32[256,2,64]{0,2,1:T(8,128)} %copy-done.4), channel_id=1, source_target_pairs={{0,16},{16,32},{32,48},{48,64},{64,80},{80,96},{96,112},{112,128},... | collective-permute-start | bytes 393224 | tf_op jit(solution)/shard_map/while/body/eval_jaxpr/ppermute | solution.py:10
  636.4 10.9 %collective-permute-start.1 = (f32[256,2,64]{0,2,1:T(8,128)}, f32[256,2,64]{0,2,1:T(8,128)S(1)}, u32[]{:S(2)}, u32[]{:S(2)}) collective-permute-start(f32[256,2,64]{0,2,1:T(8,128)} %copy-done.5), channel_id=1, source_target_pairs={{16,0},{32,16},{48,32},{64,48},{80,64},{96,80},{112,96},{128,112},... | collective-permute-start | bytes 393224 | tf_op jit(solution)/shard_map/while/body/eval_jaxpr/ppermute | solution.py:10
  648.0 8.9 %collective-permute-start = (f32[256,2,64]{0,2,1:T(8,128)}, f32[256,2,64]{0,2,1:T(8,128)S(1)}, u32[]{:S(2)}, u32[]{:S(2)}) collective-permute-start(f32[256,2,64]{0,2,1:T(8,128)} %copy-done.4), channel_id=1, source_target_pairs={{0,16},{16,32},{32,48},{48,64},{64,80},{80,96},{96,112},{112,128},... | collective-permute-start | bytes 393224 | tf_op jit(solution)/shard_map/while/body/eval_jaxpr/ppermute | solution.py:10
  (54 other events, 424.1 us)
Sparse Core Ops, SparseCore 0:
  62.8 117.5 reduce-scatter.2
  183.2 38.6 all-gather.2
  278.0 113.3 reduce-scatter.4
  394.2 38.6 all-gather.4
where the time goes:
time: 690 us; the launch traced here: 681 us
  waiting for transfers between devices  399 us (58%)
  matrix products  107 us (16%)
  starting transfers between devices  100 us (14%)
  local copies, waits for them, and re-layouts  37.2 us (5%)
  other arithmetic  19.6 us (3%)
  between operations  14.9 us (2%)
    reduce_scatter x2, waiting for transfers between devices, on_device(): lax.psum_scatter(slab_term(jnp.int32(0), part_cols * lax.axis_size('col')...  231 us
    dot_general x52, matrix products, real_dot(): jnp.dot(left, right, precision=lax.Precision.HIGHEST, preferred_element_t...  107 us
    ppermute x30, starting transfers between devices, shifted(): lax.ppermute(value, axis, [(source, source + steps) for source in range(l...  100 us
    ppermute x30, waiting for transfers between devices, shifted(): lax.ppermute(value, axis, [(source, source + steps) for source in range(l...  93.9 us
    all_gather x2, waiting for transfers between devices, on_device(): gathered = lax.all_gather(rim_values, 'col', axis=0, tiled=True)  74.3 us
    while x60, local copies, waits for them, and re-layouts  19.5 us
  transfers between devices with their start and end apart: 34, of which 33 were waited for; matrix products, arithmetic and copies ran while one was open for 1% of the time, Pallas kernels for 0%

commit v1 on v0

v1 whole, which is shorter than its diff:
```python
import jax
import jax.numpy as jnp
from jax import lax
from jax.experimental import pallas as pl
from jax.experimental.pallas import tpu as pltpu
from jax.sharding import PartitionSpec as P

F32 = jnp.float32
BF16 = jnp.bfloat16
LIMIT = 48 * 1024 * 1024


def split(value):
    high = value.astype(BF16)
    return high, (value - high.astype(F32)).astype(BF16)


def mm(left, right):
    return lax.dot_general(left, right, (((1,), (0,)), ((), ())), preferred_element_type=F32)


def mm_t(left, right):
    return lax.dot_general(left, right, (((1,), (1,)), ((), ())), preferred_element_type=F32)


def mm3(left, right):
    return mm(left[0], right[0]) + (mm(left[0], right[1]) + mm(left[1], right[0]))


def mm3_t(left, right):
    return mm_t(left[0], right[0]) + (mm_t(left[0], right[1]) + mm_t(left[1], right[0]))


def complex_rows(left, right):
    half = left.shape[0] // 2
    parts = split(left)
    by_real = mm3(parts, split(right[0]))
    by_imag = mm3(parts, split(right[1]))
    return jnp.concatenate(
        [by_real[:half] - by_imag[half:], by_imag[:half] + by_real[half:]], axis=0
    )


def interface_kernel(
    first_ref, inject_ref, src_ref, g0_ref, g1_ref, out_ref, high_ref, low_ref, acc_ref
):
    step = pl.program_id(0)
    slab = step // 2
    plane = step % 2
    width = src_ref.shape[2]
    modes = src_ref.shape[3]

    @pl.when(step == 0)
    def _():
        rows = lax.broadcasted_iota(jnp.int32, (width // 8, width), 0)
        cols = lax.broadcasted_iota(jnp.int32, (width // 8, width), 1)
        for local in range(2):
            pieces = []
            for sweep in range(2):
                pieces.append((cols == rows * 8 + sweep).astype(F32))
                chosen = inject_ref[sweep : sweep + 1, :] == first_ref[0] + local
                for part in range(2):
                    pieces.append(jnp.where(chosen, src_ref[sweep, part], 0.0).T)
            high, low = split(jnp.concatenate(pieces, axis=0))
            high_ref[local] = high
            low_ref[local] = low
        acc_ref[...] = jnp.zeros_like(acc_ref)

    half = high_ref.shape[1] // 2
    lead = width // 8
    count = g0_ref.shape[2] // 8
    for sweep in range(2):
        rows = jnp.concatenate(
            [ref[0, 0, pl.ds(1 - sweep, count, stride=8), :] for ref in (g0_ref, g1_ref)], axis=1
        )
        picked = pl.ds(sweep * half, half)
        term = mm3_t((high_ref[slab, picked, :], low_ref[slab, picked, :]), split(rows))
        order = slab if sweep == 0 else 1 - slab
        place = pl.ds(pl.multiple_of((order * 2 + plane) * lead, lead), lead)
        for member in range(4):
            out_ref[sweep * 4 + member, place, :] = term[:lead]
        real, imag = term[lead : lead + modes], term[lead + modes :]

        @pl.when(plane == 0)
        def _():
            acc_ref[sweep, :modes] += real
            acc_ref[sweep, modes:] += imag

        @pl.when(plane == 1)
        def _():
            acc_ref[sweep, :modes] -= imag
            acc_ref[sweep, modes:] += real

    @pl.when(step == 3)
    def _():
        for dest in range(8):
            sweep, member = divmod(dest, 4)
            for part in range(2):
                start = part * modes + member * 16
                out_ref[dest, 4 * lead + part * 16 : 4 * lead + (part + 1) * 16, :] = acc_ref[
                    sweep, start : start + 16, :
                ]


def spread_kernel(high_ref, low_ref, g_ref, out_ref):
    half = high_ref.shape[1] // 2
    lead = g_ref.shape[3] // 8
    modes = (half - lead) // 2
    total = [0.0] * 4
    for slab in range(2):
        parts = (high_ref[slab], low_ref[slab])
        real = mm3_t(parts, split(g_ref[slab, 0]))
        imag = mm3_t(parts, split(g_ref[slab, 1]))
        for sweep in range(2):
            base = sweep * half
            place = slab * 4 * lead + sweep * 2 * lead
            out_ref[0, place : place + lead, :] = real[base : base + lead]
            out_ref[0, place + lead : place + 2 * lead, :] = imag[base : base + lead]
            one, two, three = base + lead, base + lead + modes, base + half
            total[2 * sweep] += real[one:two] - imag[two:three]
            total[2 * sweep + 1] += real[two:three] + imag[one:two]
    for item in range(4):
        place = 8 * lead + item * modes
        out_ref[0, place : place + modes, :] = total[item]


def stacked(ref, start, count):
    return jnp.concatenate([ref[block, start : start + count, :] for block in range(8)], axis=0)


def pair_map_kernel(team_ref, recv_ref, c_ref, mask_ref, out_ref, x_ref, qa_ref):
    left = team_ref[0] == 0
    size = c_ref.shape[3]
    lead = size // 8
    coupled = []
    for slab in range(2):
        real = jnp.where(left, c_ref[slab, 0].T, c_ref[slab, 0])
        imag = jnp.where(left, c_ref[slab, 1].T, -c_ref[slab, 1])
        x_ref[slab, :size] = real
        x_ref[slab, size:] = imag
        coupled.append((real, imag))
    blocks = [
        (stacked(recv_ref, 2 * item * lead, lead), stacked(recv_ref, (2 * item + 1) * lead, lead))
        for item in range(2)
    ]
    flow = recv_ref[0, 4 * lead :, :]
    for block in range(1, 8):
        flow = flow + recv_ref[block, 4 * lead :, :]
    flow_a = jnp.where(mask_ref[0] != 0, flow, 0.0)
    flow_b = jnp.where(mask_ref[1] != 0, flow, 0.0)
    qa_ref[...] = flow_a

    def pick(one, two):
        return (jnp.where(left, one[0], two[0]), jnp.where(left, one[1], two[1]))

    def times(one, two):
        both = complex_rows(jnp.concatenate(one, axis=0), two)
        return both, (both[:size], both[size:])

    first, _ = times(pick(coupled[0], blocks[0]), pick(blocks[0], coupled[1]))
    _, second = times(pick(coupled[1], blocks[1]), pick(blocks[1], coupled[0]))
    out_ref[: 2 * size, :] = complex_rows(first, second)
    flow_a = jnp.where(left, flow_a, complex_rows(flow_a, coupled[1]))
    flow_b = jnp.where(left, flow_b, complex_rows(flow_b, coupled[0]))
    out_ref[2 * size :, :] = complex_rows(flow_a, second) + flow_b


def chain_kernel(order_ref, lead_ref, map_ref, recv_ref, x_ref, qa_ref, out_ref, state_ref):
    step = pl.program_id(0)
    size = x_ref.shape[2]
    lead = size // 8

    @pl.when(step == 0)
    def _():
        state_ref[...] = lead_ref[...]

    @pl.when(step < order_ref[16])
    def _():
        flow = complex_rows(state_ref[...], (map_ref[0, :size], map_ref[0, size : 2 * size]))
        state_ref[...] = flow + map_ref[0, 2 * size :]

    @pl.when(step == 14)
    def _():
        left = order_ref[17] == 0
        state = state_ref[...]
        turned = complex_rows(state, (x_ref[0, :size], x_ref[0, size:]))
        inner_a = jnp.where(left, turned, state)
        block = (stacked(recv_ref, 0, lead), stacked(recv_ref, lead, lead))
        middle = complex_rows(inner_a, block) + qa_ref[...]
        inner_b = complex_rows(middle, (x_ref[1, :size], x_ref[1, size:]))
        for dest in range(8):
            out_ref[dest, :32, :] = inner_a
            out_ref[dest, 32:, :] = inner_b


def arrange_kernel(first_ref, inject_ref, recv_ref, high_ref, low_ref, base_ref):
    lead = recv_ref.shape[2] // 8
    modes = inject_ref.shape[1]
    for slab in range(2):
        for kind in range(4):
            value = stacked(recv_ref, (slab * 4 + kind) * lead, lead)
            high, low = split(value)
            sweep, part = divmod(kind, 2)
            high_ref[slab, sweep, part] = high
            low_ref[slab, sweep, part] = low
    total = recv_ref[0, 8 * lead :, :]
    for block in range(1, 8):
        total = total + recv_ref[block, 8 * lead :, :]
    for sweep in range(2):
        for part in range(2):
            start = (2 * sweep + part) * modes
            turned = total[start : start + modes].T
            for slab in range(2):
                chosen = inject_ref[sweep : sweep + 1, :] == first_ref[0] + slab
                base_ref[sweep, slab, part] = jnp.where(chosen, turned, 0.0)


def state_kernel(inner_ref, high_ref, low_ref, base_ref, left_ref, right_ref):
    for sweep, out_ref in enumerate((left_ref, right_ref)):
        for slab in range(2):
            item = slab if sweep == 0 else 1 - slab
            pieces = []
            for part in range(2):
                start = item * 32 + part * 16
                for member in range(4):
                    pieces.append(inner_ref[sweep * 4 + member, start : start + 16, :])
            parts = split(jnp.concatenate(pieces, axis=0))
            half = parts[0].shape[0] // 2
            by = []
            for part in range(2):
                by.append(mm3(parts, (high_ref[slab, sweep, part], low_ref[slab, sweep, part])))
            out_ref[slab, 0] = base_ref[sweep, slab, 0] + (by[0][:half] - by[1][half:]).T
            out_ref[slab, 1] = base_ref[sweep, slab, 1] + (by[1][:half] + by[0][half:]).T


def params(**extra):
    return pltpu.CompilerParams(vmem_limit_bytes=LIMIT, **extra)


def whole(shape):
    zeros = (0,) * len(shape)
    return pl.BlockSpec(shape, lambda *_: zeros)


SMEM = pl.BlockSpec(memory_space=pltpu.SMEM)
VMEM = pl.BlockSpec(memory_space=pltpu.VMEM)


def exchange(value):
    return lax.all_to_all(value, "col", split_axis=0, concat_axis=0, tiled=True)


def on_device(diag_inverse, couplings, sources, inject, leads):
    orbitals = diag_inverse.shape[2]
    width = diag_inverse.shape[3]
    size = couplings.shape[2]
    modes = sources.shape[3]
    lead = size // 8
    slabs = lax.axis_size("slab")
    slab_index = lax.axis_index("slab")
    col_index = lax.axis_index("col")
    team = col_index // 4
    member = col_index % 4
    first = jnp.reshape(slab_index * 2, (1,)).astype(jnp.int32)
    team_flag = jnp.reshape(team, (1,)).astype(jnp.int32)
    stack = 2 * (lead + 2 * modes)
    block_rows = 4 * lead + 32

    sent, high, low = pl.pallas_call(
        interface_kernel,
        grid=(4,),
        in_specs=[
            SMEM,
            whole(inject.shape),
            whole(sources.shape),
            pl.BlockSpec((1, 1, orbitals, width // 2), lambda step: (step // 2, step % 2, 0, 0)),
            pl.BlockSpec((1, 1, orbitals, width // 2), lambda step: (step // 2, step % 2, 0, 1)),
        ],
        out_specs=[
            whole((8, block_rows, size)),
            whole((2, stack, width)),
            whole((2, stack, width)),
        ],
        out_shape=[
            jax.ShapeDtypeStruct((8, block_rows, size), F32),
            jax.ShapeDtypeStruct((2, stack, width), BF16),
            jax.ShapeDtypeStruct((2, stack, width), BF16),
        ],
        scratch_shapes=[pltpu.VMEM((2, 2 * modes, size), F32)],
        compiler_params=params(),
        name="interface_terms",
    )(first, inject, sources, diag_inverse, diag_inverse)
    received = exchange(sent)

    own_inject = lax.dynamic_slice(inject, (team, member * 16), (1, 16))[0]
    own_inject = jnp.concatenate([own_inject, own_inject])
    slab_a = first[0] + team
    slab_b = first[0] + 1 - team
    marks = jnp.stack([own_inject == slab_a, own_inject == slab_b]).astype(F32)
    marks = jnp.broadcast_to(marks[:, :, None], (2, 32, size))
    packed, turned, flow_a = pl.pallas_call(
        pair_map_kernel,
        in_specs=[SMEM, VMEM, VMEM, VMEM],
        out_specs=[VMEM, VMEM, VMEM],
        out_shape=[
            jax.ShapeDtypeStruct((2 * size + 32, size), F32),
            jax.ShapeDtypeStruct((2, 2 * size, size), F32),
            jax.ShapeDtypeStruct((32, size), F32),
        ],
        compiler_params=params(),
        name="pair_map",
    )(team_flag, received, couplings, marks)
    high, low, packed = lax.optimization_barrier((high, low, packed))
    maps = lax.all_gather(packed, "slab", axis=0)

    spread = pl.pallas_call(
        spread_kernel,
        grid=(8,),
        in_specs=[
            whole((2, stack, width)),
            whole((2, stack, width)),
            pl.BlockSpec((2, 2, orbitals // 8, width), lambda step: (0, 0, step, 0)),
        ],
        out_specs=pl.BlockSpec((1, 8 * lead + 4 * modes, orbitals // 8), lambda step: (step, 0, 0)),
        out_shape=jax.ShapeDtypeStruct((8, 8 * lead + 4 * modes, orbitals // 8), F32),
        compiler_params=params(),
        name="spread_terms",
    )(high, low, diag_inverse)
    rows = exchange(spread)
    part_rows = orbitals // 8
    row_high, row_low, base = pl.pallas_call(
        arrange_kernel,
        in_specs=[SMEM, VMEM, VMEM],
        out_specs=[VMEM, VMEM, VMEM],
        out_shape=[
            jax.ShapeDtypeStruct((2, 2, 2, size, part_rows), BF16),
            jax.ShapeDtypeStruct((2, 2, 2, size, part_rows), BF16),
            jax.ShapeDtypeStruct((2, 2, 2, part_rows, modes), F32),
        ],
        compiler_params=params(),
        name="arrange_rows",
    )(first, inject, rows)

    own_lead = lax.dynamic_slice(
        leads, (team, 0, 0, member * 16), (1, 2, size, 16)
    )[0]
    own_lead = jnp.transpose(own_lead, (0, 2, 1)).reshape(32, size)
    position = jnp.where(team == 0, slab_index, slabs - 1 - slab_index)
    steps = jnp.minimum(jnp.arange(16, dtype=jnp.int32), jnp.maximum(position - 1, 0))
    steps = jnp.where(team == 0, steps, slabs - 1 - steps)
    order = jnp.concatenate([steps, jnp.stack([position, team])]).astype(jnp.int32)
    inner = pl.pallas_call(
        chain_kernel,
        grid_spec=pltpu.PrefetchScalarGridSpec(
            num_scalar_prefetch=1,
            grid=(15,),
            in_specs=[
                whole((32, size)),
                pl.BlockSpec((1, 2 * size + 32, size), lambda step, order: (order[step], 0, 0)),
                whole((8, block_rows, size)),
                whole((2, 2 * size, size)),
                whole((32, size)),
            ],
            out_specs=whole((8, 64, size)),
            scratch_shapes=[pltpu.VMEM((32, size), F32)],
        ),
        out_shape=jax.ShapeDtypeStruct((8, 64, size), F32),
        compiler_params=params(),
        name="chain",
    )(order, own_lead, maps, received, turned, flow_a)
    inner = exchange(inner)

    shape = (2, 2, part_rows, modes)
    return pl.pallas_call(
        state_kernel,
        in_specs=[VMEM, VMEM, VMEM, VMEM],
        out_specs=[VMEM, VMEM],
        out_shape=[jax.ShapeDtypeStruct(shape, F32), jax.ShapeDtypeStruct(shape, F32)],
        compiler_params=params(),
        name="states",
    )(inner, row_high, row_low, base)


def solution(mesh):
    placed = (
        P(("energy", "slab"), None, None, "col"),
        P(("energy", "slab"), None, None, None),
        P("energy", None, "col", None),
        P(),
        P("energy", None, None, None),
    )

    def run(*args):
        left, right = on_device(*args)
        return left, right

    return jax.shard_map(
        run,
        mesh=mesh,
        in_specs=placed,
        out_specs=(
            P(("energy", "slab"), None, "col", None),
            P(("energy", "slab"), None, "col", None),
        ),
        check_vma=False,
    )
```

time: 690 us -> 208 us (0.30); the launches traced: 681 us -> 207 us
  waiting for transfers between devices: 399 us -> 139 us
  matrix products: 107 us -> 0 us
  starting transfers between devices: 100 us -> 16.6 us
  local copies, waits for them, and re-layouts: 37.2 us -> 11 us
  Pallas kernels: 0 us -> 26.1 us
  other arithmetic: 19.6 us -> 0.18 us
    reduce_scatter x2 -> x0, waiting for transfers between devices: 231 us -> none  [on_device(): lax.psum_scatter(slab_term(jnp.int32(0), part_cols * lax.axis_size('col')...]
    dot_general x52 -> x0, matrix products: 107 us -> none  [real_dot(): jnp.dot(left, right, precision=lax.Precision.HIGHEST, preferred_element_t...]
    ppermute x30 -> x0, starting transfers between devices: 100 us -> none  [shifted(): lax.ppermute(value, axis, [(source, source + steps) for source in range(l...]
    ppermute x30 -> x0, waiting for transfers between devices: 93.9 us -> none  [shifted(): lax.ppermute(value, axis, [(source, source + steps) for source in range(l...]
    all_to_all x0 -> x3, waiting for transfers between devices: none -> 79.8 us  [exchange(): return lax.all_to_all(value, 'col', split_axis=0, concat_axis=0, tiled=True)]
    pallas_call x0 -> x6, Pallas kernels: none -> 26.1 us  [the longest x1 8.76 us: on_device(): pl.pallas_call(spread_kernel, grid=(8,), in_specs=[whole((2, stack, width...]
    while x63 -> x0, local copies, waits for them, and re-layouts: 20.2 us -> none
    another operation x18 -> x0, other arithmetic: 17.7 us -> none  [the longest x6 11.1 us: slab_term(): jnp.stack([apply_complex(left_block, state[:, 0]), apply_complex(right_bl...]
  transfers between devices with their start and end apart: 34 -> 4, of which waited for: 33 -> 4; matrix products, arithmetic and copies ran while one was open for 1% -> 0% of each run, Pallas kernels for 0% -> 8%
where the time goes in v1:
time: 208 us; the launch traced here: 207 us
  waiting for transfers between devices  139 us (67%)
  Pallas kernels  26.1 us (13%)
  starting transfers between devices  16.6 us (8%)
  between operations  14.2 us (7%)
  local copies, waits for them, and re-layouts  11 us (5%)
    all_to_all x3, waiting for transfers between devices, exchange(): return lax.all_to_all(value, 'col', split_axis=0, concat_axis=0, tiled=True)  79.8 us
    all_gather x1, waiting for transfers between devices, on_device(): maps = lax.all_gather(packed, 'slab', axis=0)  59.1 us
    all_to_all x3, starting transfers between devices, exchange(): return lax.all_to_all(value, 'col', split_axis=0, concat_axis=0, tiled=True)  16.5 us
    pallas_call x1, Pallas kernels, on_device(): pl.pallas_call(spread_kernel, grid=(8,), in_specs=[whole((2, stack, width...  8.76 us
    unnamed x17, local copies, waits for them, and re-layouts  8.02 us
    pallas_call x1, Pallas kernels, on_device(): pl.pallas_call(interface_kernel, grid=(4,), in_specs=[SMEM, whole(inject....  7 us
  transfers between devices with their start and end apart: 4, of which 4 were waited for; matrix products, arithmetic and copies ran while one was open for 0% of the time, Pallas kernels for 8%

profile of v1, /device:TPU:8, one launch (start us, length us, event | category | flops | bytes accessed | tf_op | source)
XLA Modules:
  0.0 206.9 jit_solution(11026094264328809794)
XLA Ops:
  7.2 1.2 copy.7.src_ref
  8.4 0.7 copy-done.6
  9.1 7.0 %interface_terms.1 = (f32[8,160,256]{2,1,0:T(8,128)}, bf16[2,320,256]{2,1,0:T(8,128)(2,1)S(1)}, bf16[2,320,256]{2,1,0:T(8,128)(2,1)S(1)}) custom-call(s32[1]{0:T(128)} %bitcast.5.first_ref, s32[2,64]{1,0:T(2,128)S(1)} %copy-done.6, f32[2,2,256,64]{3,2,1,0:T(8,128)S(1)} %copy.7.src_ref, f32[2,2,2048,256]{3,2,1,0:T(8,128)} %g_ref.1, f32[2,2,2048,256]{3,2,1,0:T(8,128)} %g_ref.1), custom_call_target="tpu_custom_call" | custom-call | tf_op jit(solution)/shard_map/interface_terms/pallas_call | solution.py:269
  16.1 8.5 %all-to-all-start = ((f32[8,160,256]{2,1,0:T(8,128)}), f32[8,160,256]{2,1,0:T(8,128)S(1)}, u32[]{:S(2)}, u32[]{:S(2)}) async-start(f32[8,160,256]{2,1,0:T(8,128)} %get-tuple-element.16), calls=%async_computation | async-start | bytes 2621440 | tf_op jit(solution)/shard_map/all_to_all | solution.py:250
  24.7 0.1 broadcast_compare_fusion.1
  24.8 34.2 %all-to-all-done.recv_ref = f32[8,160,256]{2,1,0:T(8,128)S(1)} async-done(((f32[8,160,256]{2,1,0:T(8,128)}), f32[8,160,256]{2,1,0:T(8,128)S(1)}, u32[]{:S(2)}, u32[]{:S(2)}) %all-to-all-start) | async-done | bytes 1310752 | tf_op jit(solution)/shard_map/all_to_all | solution.py:250
  59.0 1.2 copy-done.4
  60.3 2.8 %pair_map.1 = (f32[544,256]{1,0:T(8,128)}, f32[2,512,256]{2,1,0:T(8,128)S(1)}, f32[32,256]{1,0:T(8,128)S(1)}) custom-call(s32[1]{0:T(128)} %bitcast.1.team_ref, f32[8,160,256]{2,1,0:T(8,128)S(1)} %all-to-all-done.recv_ref, f32[2,2,256,256]{3,2,1,0:T(8,128)S(1)} %copy-done.4, f32[2,32,256]{2,1,0:T(8,128)S(1)} %broadcast_in_dim.2.mask_ref), custom_call_target="tpu_custom_call" | custom-call | tf_op jit(solution)/shard_map/pair_map/pallas_call | solution.py:301
  63.1 8.8 %spread_terms.1 = f32[8,512,256]{2,1,0:T(8,128)S(1)} custom-call(bf16[2,320,256]{2,1,0:T(8,128)(2,1)S(1)} %get-tuple-element.21.high_ref, bf16[2,320,256]{2,1,0:T(8,128)(2,1)S(1)} %get-tuple-element.22.low_ref, f32[2,2,2048,256]{3,2,1,0:T(8,128)} %g_ref.1), custom_call_target="tpu_custom_call" | custom-call | tf_op jit(solution)/shard_map/spread_terms/pallas_call | solution.py:316
  71.9 1.9 copy-done.1
  73.8 4.6 %all-to-all-start.2 = ((f32[8,512,256]{2,1,0:T(8,128)}), f32[8,512,256]{2,1,0:T(8,128)}, u32[]{:S(2)}, u32[]{:S(2)}) async-start(f32[8,512,256]{2,1,0:T(8,128)} %copy-done.1), calls=%async_computation.2 | async-start | bytes 8388608 | tf_op jit(solution)/shard_map/all_to_all | solution.py:250
  78.4 0.1 pad_add_fusion.order_ref
  78.5 59.1 %all-gather.3.cloned.1.call-done = f32[8704,256]{1,0:T(8,128)} async-done(((f32[544,256]{1,0:T(8,128)}), f32[8704,256]{1,0:T(8,128)}) %all-gather.3.cloned.1.call-update) | async-done | bytes 8912912 | tf_op jit(solution)/shard_map/all_gather | solution.py:314
  137.6 3.9 %chain.1 = f32[8,64,256]{2,1,0:T(8,128)} custom-call(s32[18]{0:T(128)S(1)} %pad_add_fusion.order_ref, f32[32,256]{1,0:T(8,128)S(1)} %bitcast.9, f32[16,544,256]{2,1,0:T(8,128)} %bitcast.10, f32[8,160,256]{2,1,0:T(8,128)S(1)} %all-to-all-done.recv_ref, f32[2,512,256]{2,1,0:T(8,128)S(1)} %get-tuple-element.19.x_ref, f32[32,256]{1,0:T(8,128)S(1)} %get-tuple-element.20.qa_ref), custom_call_target="tpu_custom_call" | custom-call | tf_op jit(solution)/shard_map/chain/pallas_call | solution.py:352
  141.5 33.6 %all-to-all-done.2.recv_ref = f32[8,512,256]{2,1,0:T(8,128)} async-done(((f32[8,512,256]{2,1,0:T(8,128)}), f32[8,512,256]{2,1,0:T(8,128)}, u32[]{:S(2)}, u32[]{:S(2)}) %all-to-all-start.2) | async-done | bytes 4194336 | tf_op jit(solution)/shard_map/all_to_all | solution.py:250
  175.1 3.5 %all-to-all-start.1 = ((f32[8,64,256]{2,1,0:T(8,128)}), f32[8,64,256]{2,1,0:T(8,128)S(1)}, u32[]{:S(2)}, u32[]{:S(2)}) async-start(f32[8,64,256]{2,1,0:T(8,128)} %chain.1), calls=%async_computation.1 | async-start | bytes 1048576 | tf_op jit(solution)/shard_map/all_to_all | solution.py:250
  178.6 2.9 %arrange_rows.1 = (bf16[2,2,2,256,256]{4,3,2,1,0:T(8,128)(2,1)S(1)}, bf16[2,2,2,256,256]{4,3,2,1,0:T(8,128)(2,1)S(1)}, f32[2,2,2,256,64]{4,3,2,1,0:T(8,128)S(1)}) custom-call(s32[1]{0:T(128)} %bitcast.5.first_ref, s32[2,64]{1,0:T(2,128)S(1)} %copy-done.7, f32[8,512,256]{2,1,0:T(8,128)} %all-to-all-done.2.recv_ref), custom_call_target="tpu_custom_call" | custom-call | tf_op jit(solution)/shard_map/arrange_rows/pallas_call | solution.py:331
  181.5 1.0 copy-done.2
  182.5 12.0 %all-to-all-done.1.inner_ref = f32[8,64,256]{2,1,0:T(8,128)S(1)} async-done(((f32[8,64,256]{2,1,0:T(8,128)}), f32[8,64,256]{2,1,0:T(8,128)S(1)}, u32[]{:S(2)}, u32[]{:S(2)}) %all-to-all-start.1) | async-done | bytes 524320 | tf_op jit(solution)/shard_map/all_to_all | solution.py:250
  194.5 1.2 copy-done.3
  195.7 0.8 states.1
  196.5 0.8 copy-done.5
  197.3 1.9 copy.8
  199.2 0.9 copy.9
  (17 shorter events, 0.2 us)
Async XLA Ops:
  7.2 71.3 %copy-start = (f32[2,2,256,64]{2,3,1,0:T(8,128)S(1)}, f32[2,2,256,64]{2,3,1,0:T(8,128)}, u32[]{:S(2)}) copy-start(f32[2,2,256,64]{2,3,1,0:T(8,128)} %param.9) | copy-start | bytes 786436
  8.4 0.7 copy-start.6
  9.1 15.6 %copy-start.7 = (s32[2,64]{1,0:T(2,128)S(1)}, s32[2,64]{1,0:T(2,128)}, u32[]{:S(2)}) copy-start(s32[2,64]{1,0:T(2,128)} %inject_ref.3) | copy-start | bytes 1540
  16.1 42.9 %all-to-all-start = ((f32[8,160,256]{2,1,0:T(8,128)}), f32[8,160,256]{2,1,0:T(8,128)S(1)}, u32[]{:S(2)}, u32[]{:S(2)}) async-start(f32[8,160,256]{2,1,0:T(8,128)} %get-tuple-element.16), calls=%async_computation | async-start | bytes 2621440 | tf_op jit(solution)/shard_map/all_to_all | solution.py:250
  24.5 113.1 %all-gather.3.cloned.1.call-start = ((), (), s32[]{:S(2)}) async-start(), calls=%async_computation.3 | async-start | bytes 9469952 | tf_op jit(solution)/shard_map/all_gather | solution.py:314
  59.0 1.2 copy-start.4
  71.9 1.9 copy-start.1
  73.8 101.3 %all-to-all-start.2 = ((f32[8,512,256]{2,1,0:T(8,128)}), f32[8,512,256]{2,1,0:T(8,128)}, u32[]{:S(2)}, u32[]{:S(2)}) async-start(f32[8,512,256]{2,1,0:T(8,128)} %copy-done.1), calls=%async_computation.2 | async-start | bytes 8388608 | tf_op jit(solution)/shard_map/all_to_all | solution.py:250
  175.1 19.4 %all-to-all-start.1 = ((f32[8,64,256]{2,1,0:T(8,128)}), f32[8,64,256]{2,1,0:T(8,128)S(1)}, u32[]{:S(2)}, u32[]{:S(2)}) async-start(f32[8,64,256]{2,1,0:T(8,128)} %chain.1), calls=%async_computation.1 | async-start | bytes 1048576 | tf_op jit(solution)/shard_map/all_to_all | solution.py:250
  181.5 1.0 copy-start.2
  194.5 1.2 copy-start.3
  196.5 0.8 copy-start.5
Sparse Core Ops, SparseCore 0:
  63.2 74.3 all-gather.2

commit v2 on v1

v2 whole, which is shorter than its diff:
```python
import jax
import jax.numpy as jnp
from jax import lax
from jax.experimental import pallas as pl
from jax.experimental.pallas import tpu as pltpu
from jax.sharding import PartitionSpec as P

F32 = jnp.float32
BF16 = jnp.bfloat16
LIMIT = 48 * 1024 * 1024


def split(value):
    high = value.astype(BF16)
    return high, (value - high.astype(F32)).astype(BF16)


def mm(left, right, transposed=False):
    dims = (((1,), (1 if transposed else 0,)), ((), ()))
    return lax.dot_general(left, right, dims, preferred_element_type=F32)


def mm3(left, right, transposed=False):
    rows = left[0].shape[0]
    wide = mm(jnp.concatenate(left, axis=0), right[0], transposed)
    return wide[:rows] + (wide[rows:] + mm(left[0], right[1], transposed))


def complex_rows(left, right):
    half = left.shape[0] // 2
    parts = split(left)
    by_real = mm3(parts, split(right[0]))
    by_imag = mm3(parts, split(right[1]))
    return jnp.concatenate(
        [by_real[:half] - by_imag[half:], by_imag[:half] + by_real[half:]], axis=0
    )


def interface_kernel(
    first_ref, inject_ref, src_ref, g0_ref, g1_ref, out_ref, high_ref, low_ref, acc_ref
):
    step = pl.program_id(0)
    slab = step // 2
    plane = step % 2
    modes = src_ref.shape[2]
    width = src_ref.shape[3]

    @pl.when(step == 0)
    def _():
        rows = lax.broadcasted_iota(jnp.int32, (width // 8, width), 0)
        cols = lax.broadcasted_iota(jnp.int32, (width // 8, width), 1)
        targets = [
            jnp.broadcast_to(inject_ref[sweep : sweep + 1, :].astype(F32), (width, modes)).T
            for sweep in range(2)
        ]
        for local in range(2):
            pieces = []
            for sweep in range(2):
                pieces.append((cols == rows * 8 + sweep).astype(F32))
                chosen = targets[sweep] == (first_ref[0] + local).astype(F32)
                for part in range(2):
                    pieces.append(jnp.where(chosen, src_ref[sweep, part], 0.0))
            high, low = split(jnp.concatenate(pieces, axis=0))
            high_ref[local] = high
            low_ref[local] = low
        acc_ref[...] = jnp.zeros_like(acc_ref)

    half = high_ref.shape[1] // 2
    lead = width // 8
    count = g0_ref.shape[2] // 8
    for sweep in range(2):
        rows = jnp.concatenate(
            [ref[0, 0, pl.ds(1 - sweep, count, stride=8), :] for ref in (g0_ref, g1_ref)], axis=1
        )
        picked = pl.ds(sweep * half, half)
        term = mm3((high_ref[slab, picked, :], low_ref[slab, picked, :]), split(rows), True)
        order = slab if sweep == 0 else 1 - slab
        place = pl.ds(pl.multiple_of((order * 2 + plane) * lead, lead), lead)
        for member in range(4):
            out_ref[sweep * 4 + member, place, :] = term[:lead]
        real, imag = term[lead : lead + modes], term[lead + modes :]

        @pl.when(plane == 0)
        def _():
            acc_ref[sweep, :modes] += real
            acc_ref[sweep, modes:] += imag

        @pl.when(plane == 1)
        def _():
            acc_ref[sweep, :modes] -= imag
            acc_ref[sweep, modes:] += real

    @pl.when(step == 3)
    def _():
        for dest in range(8):
            sweep, member = divmod(dest, 4)
            for part in range(2):
                start = part * modes + member * 16
                out_ref[dest, 4 * lead + part * 16 : 4 * lead + (part + 1) * 16, :] = acc_ref[
                    sweep, start : start + 16, :
                ]


def spread_kernel(high_ref, low_ref, g_ref, out_ref, flow_ref):
    half = high_ref.shape[1] // 2
    lead = g_ref.shape[3] // 8
    modes = (half - lead) // 2
    total = [0.0] * 4
    for slab in range(2):
        parts = (high_ref[slab], low_ref[slab])
        real = mm3(parts, split(g_ref[slab, 0]), True)
        imag = mm3(parts, split(g_ref[slab, 1]), True)
        for sweep in range(2):
            base = sweep * half
            place = slab * 4 * lead + sweep * 2 * lead
            out_ref[0, place : place + lead, :] = real[base : base + lead]
            out_ref[0, place + lead : place + 2 * lead, :] = imag[base : base + lead]
            one, two, three = base + lead, base + lead + modes, base + half
            total[2 * sweep] += real[one:two] - imag[two:three]
            total[2 * sweep + 1] += real[two:three] + imag[one:two]
    for item in range(4):
        flow_ref[0, item * modes : (item + 1) * modes, :] = total[item]


def coupling_kernel(team_ref, c_ref, x_ref):
    left = team_ref[0] == 0
    size = c_ref.shape[3]
    for slab in range(2):
        x_ref[slab, :size] = jnp.where(left, c_ref[slab, 0].T, c_ref[slab, 0])
        x_ref[slab, size:] = jnp.where(left, c_ref[slab, 1].T, -c_ref[slab, 1])


def stacked(ref, start, count):
    return jnp.concatenate([ref[block, start : start + count, :] for block in range(8)], axis=0)


def pair_map_kernel(team_ref, recv_ref, x_ref, mask_ref, out_ref, qa_ref):
    left = team_ref[0] == 0
    size = x_ref.shape[2]
    lead = size // 8
    coupled = [(x_ref[slab, :size], x_ref[slab, size:]) for slab in range(2)]
    blocks = [
        (stacked(recv_ref, 2 * item * lead, lead), stacked(recv_ref, (2 * item + 1) * lead, lead))
        for item in range(2)
    ]
    flow = recv_ref[0, 4 * lead :, :]
    for block in range(1, 8):
        flow = flow + recv_ref[block, 4 * lead :, :]
    flow_a = jnp.where(mask_ref[0] != 0, flow, 0.0)
    flow_b = jnp.where(mask_ref[1] != 0, flow, 0.0)
    qa_ref[...] = flow_a

    def pick(one, two):
        return (jnp.where(left, one[0], two[0]), jnp.where(left, one[1], two[1]))

    def times(one, two):
        both = complex_rows(jnp.concatenate(one, axis=0), two)
        return both, (both[:size], both[size:])

    first, _ = times(pick(coupled[0], blocks[0]), pick(blocks[0], coupled[1]))
    _, second = times(pick(coupled[1], blocks[1]), pick(blocks[1], coupled[0]))
    out_ref[: 2 * size, :] = complex_rows(first, second)
    flow_a = jnp.where(left, flow_a, complex_rows(flow_a, coupled[1]))
    flow_b = jnp.where(left, flow_b, complex_rows(flow_b, coupled[0]))
    out_ref[2 * size :, :] = complex_rows(flow_a, second) + flow_b


def advance(state, maps_ref, index):
    size = maps_ref.shape[2]
    flow = complex_rows(state, (maps_ref[index, :size], maps_ref[index, size : 2 * size]))
    return flow + maps_ref[index, 2 * size :]


def row_kernel(info_ref, lead_ref, flow_ref, maps_ref, out_ref):
    state = jnp.where(info_ref[1] == 0, lead_ref[...], flow_ref[...])
    for item in range(4):
        state = advance(state, maps_ref, jnp.where(info_ref[0] == 0, item, 3 - item))
    out_ref[...] = state


def inflow_kernel(info_ref, lead_ref, flow_ref, maps_ref, recv_ref, x_ref, qa_ref, out_ref):
    size = x_ref.shape[2]
    lead = size // 8
    left = info_ref[0] == 0
    state = jnp.where(info_ref[1] == 0, lead_ref[...], flow_ref[...])
    for item in range(3):
        later = advance(state, maps_ref, jnp.where(left, item, 3 - item))
        state = jnp.where(item < info_ref[2], later, state)
    turned = complex_rows(state, (x_ref[0, :size], x_ref[0, size:]))
    inner_a = jnp.where(left, turned, state)
    block = (stacked(recv_ref, 0, lead), stacked(recv_ref, lead, lead))
    middle = complex_rows(inner_a, block) + qa_ref[...]
    inner_b = complex_rows(middle, (x_ref[1, :size], x_ref[1, size:]))
    for dest in range(8):
        out_ref[dest, :32, :] = inner_a
        out_ref[dest, 32:, :] = inner_b


def arrange_kernel(recv_ref, high_ref, low_ref):
    lead = recv_ref.shape[2] // 8
    for slab in range(2):
        for kind in range(4):
            value = stacked(recv_ref, (slab * 4 + kind) * lead, lead)
            high, low = split(value)
            sweep, part = divmod(kind, 2)
            high_ref[slab, sweep, part] = high
            low_ref[slab, sweep, part] = low


def state_kernel(
    first_ref, inject_ref, inner_ref, high_ref, low_ref, base_ref, left_ref, right_ref
):
    modes = inject_ref.shape[1]
    width = base_ref.shape[1]
    for sweep, out_ref in enumerate((left_ref, right_ref)):
        target = jnp.broadcast_to(
            inject_ref[sweep : sweep + 1, :].astype(F32), (width, modes)
        ).T
        for slab in range(2):
            item = slab if sweep == 0 else 1 - slab
            pieces = []
            for part in range(2):
                start = item * 32 + part * 16
                for member in range(4):
                    pieces.append(inner_ref[sweep * 4 + member, start : start + 16, :])
            parts = split(jnp.concatenate(pieces, axis=0))
            by = []
            for part in range(2):
                by.append(mm3(parts, (high_ref[slab, sweep, part], low_ref[slab, sweep, part])))
            chosen = target == (first_ref[0] + slab).astype(F32)
            for part in range(2):
                start = (2 * sweep + part) * modes
                base = jnp.where(chosen, base_ref[start : start + modes, :], 0.0)
                if part == 0:
                    out_ref[slab, part] = base + (by[0][:modes] - by[1][modes:])
                else:
                    out_ref[slab, part] = base + (by[1][:modes] + by[0][modes:])


def params(**extra):
    return pltpu.CompilerParams(vmem_limit_bytes=LIMIT, **extra)


def whole(shape):
    zeros = (0,) * len(shape)
    return pl.BlockSpec(shape, lambda *_: zeros)


SMEM = pl.BlockSpec(memory_space=pltpu.SMEM)
VMEM = pl.BlockSpec(memory_space=pltpu.VMEM)


def exchange(value):
    return lax.all_to_all(value, "col", split_axis=0, concat_axis=0, tiled=True)


def on_device(diag_inverse, couplings, sources, inject, leads):
    orbitals = diag_inverse.shape[2]
    width = diag_inverse.shape[3]
    size = couplings.shape[2]
    modes = sources.shape[3]
    lead = size // 8
    part_rows = orbitals // 8
    slabs = lax.axis_size("slab")
    slab_index = lax.axis_index("slab")
    col_index = lax.axis_index("col")
    team = col_index // 4
    member = col_index % 4
    first = jnp.reshape(slab_index * 2, (1,)).astype(jnp.int32)
    position = jnp.where(team == 0, slab_index, slabs - 1 - slab_index)
    info = jnp.stack([team, position // 4, position % 4]).astype(jnp.int32)
    stack = 2 * (lead + 2 * modes)
    block_rows = 4 * lead + 32
    sources = jnp.transpose(sources, (0, 1, 3, 2))
    leads = jnp.transpose(leads, (0, 1, 3, 2))

    sent, high, low = pl.pallas_call(
        interface_kernel,
        grid=(4,),
        in_specs=[
            SMEM,
            whole(inject.shape),
            whole(sources.shape),
            pl.BlockSpec((1, 1, orbitals, width // 2), lambda step: (step // 2, step % 2, 0, 0)),
            pl.BlockSpec((1, 1, orbitals, width // 2), lambda step: (step // 2, step % 2, 0, 1)),
        ],
        out_specs=[
            whole((8, block_rows, size)),
            whole((2, stack, width)),
            whole((2, stack, width)),
        ],
        out_shape=[
            jax.ShapeDtypeStruct((8, block_rows, size), F32),
            jax.ShapeDtypeStruct((2, stack, width), BF16),
            jax.ShapeDtypeStruct((2, stack, width), BF16),
        ],
        scratch_shapes=[pltpu.VMEM((2, 2 * modes, size), F32)],
        compiler_params=params(),
        name="interface_terms",
    )(first, inject, sources, diag_inverse, diag_inverse)
    received = exchange(sent)

    spread, flows = pl.pallas_call(
        spread_kernel,
        grid=(8,),
        in_specs=[
            whole((2, stack, width)),
            whole((2, stack, width)),
            pl.BlockSpec((2, 2, part_rows, width), lambda step: (0, 0, step, 0)),
        ],
        out_specs=[
            pl.BlockSpec((1, 8 * lead, part_rows), lambda step: (step, 0, 0)),
            pl.BlockSpec((1, 4 * modes, part_rows), lambda step: (step, 0, 0)),
        ],
        out_shape=[
            jax.ShapeDtypeStruct((8, 8 * lead, part_rows), F32),
            jax.ShapeDtypeStruct((8, 4 * modes, part_rows), F32),
        ],
        compiler_params=params(),
        name="spread_terms",
    )(high, low, diag_inverse)
    turned = pl.pallas_call(
        coupling_kernel,
        in_specs=[SMEM, VMEM],
        out_specs=VMEM,
        out_shape=jax.ShapeDtypeStruct((2, 2 * size, size), F32),
        compiler_params=params(),
        name="coupling_rows",
    )(info, couplings)
    own_inject = lax.dynamic_slice(inject, (team, member * 16), (1, 16))[0]
    own_inject = jnp.concatenate([own_inject, own_inject])
    marks = jnp.stack([own_inject == first[0] + team, own_inject == first[0] + 1 - team])
    marks = jnp.broadcast_to(marks.astype(F32)[:, :, None], (2, 32, size))
    own_lead = lax.dynamic_slice(leads, (team, 0, member * 16, 0), (1, 2, 16, size))
    own_lead = own_lead.reshape(32, size)
    received, spread, turned, marks, own_lead = lax.optimization_barrier(
        (received, spread, turned, marks, own_lead)
    )

    packed, flow_a = pl.pallas_call(
        pair_map_kernel,
        in_specs=[SMEM, VMEM, VMEM, VMEM],
        out_specs=[VMEM, VMEM],
        out_shape=[
            jax.ShapeDtypeStruct((2 * size + 32, size), F32),
            jax.ShapeDtypeStruct((32, size), F32),
        ],
        compiler_params=params(),
        name="pair_map",
    )(info, received, turned, marks)
    rows = exchange(spread)
    groups = [[4 * row + item for item in range(4)] for row in range(slabs // 4)]
    maps = lax.all_gather(packed, "slab", axis=0, axis_index_groups=groups)
    maps, flows = lax.optimization_barrier((maps, flows))
    base = lax.psum_scatter(flows, "col", scatter_dimension=0, tiled=False)

    cols = lax.axis_size("col")
    pairs = []
    for slab in range(slabs):
        for col in range(cols):
            target = (slab + (4 if col < 4 else -4)) % slabs
            pairs.append((slab * cols + col, target * cols + col))
    flow = own_lead
    for _ in range(slabs // 4 - 1):
        flow = pl.pallas_call(
            row_kernel,
            in_specs=[SMEM, VMEM, VMEM, VMEM],
            out_specs=VMEM,
            out_shape=jax.ShapeDtypeStruct((32, size), F32),
            compiler_params=params(),
            name="row_step",
        )(info, own_lead, flow, maps)
        flow = lax.ppermute(flow, ("slab", "col"), pairs)
    inner = pl.pallas_call(
        inflow_kernel,
        in_specs=[SMEM] + [VMEM] * 6,
        out_specs=VMEM,
        out_shape=jax.ShapeDtypeStruct((8, 64, size), F32),
        compiler_params=params(),
        name="inflow",
    )(info, own_lead, flow, maps, received, turned, flow_a)
    rows, inner = lax.optimization_barrier((rows, inner))
    inner = exchange(inner)
    row_high, row_low = pl.pallas_call(
        arrange_kernel,
        in_specs=[VMEM],
        out_specs=[VMEM, VMEM],
        out_shape=[
            jax.ShapeDtypeStruct((2, 2, 2, size, part_rows), BF16),
            jax.ShapeDtypeStruct((2, 2, 2, size, part_rows), BF16),
        ],
        compiler_params=params(),
        name="arrange_rows",
    )(rows)

    shape = (2, 2, modes, part_rows)
    left, right = pl.pallas_call(
        state_kernel,
        in_specs=[SMEM, VMEM, VMEM, VMEM, VMEM, VMEM],
        out_specs=[VMEM, VMEM],
        out_shape=[jax.ShapeDtypeStruct(shape, F32), jax.ShapeDtypeStruct(shape, F32)],
        compiler_params=params(),
        name="states",
    )(first, inject, inner, row_high, row_low, base)
    return jnp.transpose(left, (0, 1, 3, 2)), jnp.transpose(right, (0, 1, 3, 2))


def solution(mesh):
    placed = (
        P(("energy", "slab"), None, None, "col"),
        P(("energy", "slab"), None, None, None),
        P("energy", None, "col", None),
        P(),
        P("energy", None, None, None),
    )

    return jax.shard_map(
        on_device,
        mesh=mesh,
        in_specs=placed,
        out_specs=(
            P(("energy", "slab"), None, "col", None),
            P(("energy", "slab"), None, "col", None),
        ),
        check_vma=False,
    )
```

time: 208 us -> 160 us (0.77)
  waiting for transfers between devices: 139 us -> 85.3 us
  starting transfers between devices: 16.6 us -> 21.3 us
  Pallas kernels: 26.1 us -> 30.2 us
  local copies, waits for them, and re-layouts: 11 us -> 8.38 us
    all_to_all x3, waiting for transfers between devices: 79.8 us -> 43 us  [exchange(): return lax.all_to_all(value, 'col', split_axis=0, concat_axis=0, tiled=True)]
    all_gather x1, waiting for transfers between devices: 59.1 us -> 25.5 us  [on_device(): maps = lax.all_gather(packed, 'slab', axis=0, axis_index_groups=groups)]
    ppermute x0 -> x3, waiting for transfers between devices: none -> 13.6 us  [on_device(): flow = lax.ppermute(flow, ('slab', 'col'), pairs)]
    pallas_call x3 -> x7, Pallas kernels: 7.53 us -> 11.2 us  [the longest x3 4.37 us: on_device(): pl.pallas_call(row_kernel, in_specs=[SMEM, VMEM, VMEM, VMEM], out_specs=V...]
    reduce_scatter x0 -> x1, waiting for transfers between devices: none -> 3.11 us  [on_device(): base = lax.psum_scatter(flows, 'col', scatter_dimension=0, tiled=False)]
    pallas_call x2 -> x0, local copies, waits for them, and re-layouts: 2.81 us -> none  [on_device(): pl.pallas_call(state_kernel, in_specs=[VMEM, VMEM, VMEM, VMEM], out_specs...]
    all_to_all x3, starting transfers between devices: 16.5 us -> 19.2 us  [exchange(): return lax.all_to_all(value, 'col', split_axis=0, concat_axis=0, tiled=True)]
    unnamed x17 -> x20, local copies, waits for them, and re-layouts: 8.02 us -> 8.22 us
  transfers between devices with their start and end apart: 4 -> 8, of which waited for: 4 -> 8; matrix products, arithmetic and copies ran while one was open for 0% -> 0% of each run, Pallas kernels for 8% -> 12%
where the time goes in v2:
time: 160 us
  waiting for transfers between devices  85.3 us (53%)
  Pallas kernels  30.2 us (19%)
  starting transfers between devices  21.3 us (13%)
  between operations  14.2 us (9%)
  local copies, waits for them, and re-layouts  8.38 us (5%)
    all_to_all x3, waiting for transfers between devices, exchange(): return lax.all_to_all(value, 'col', split_axis=0, concat_axis=0, tiled=True)  43 us
    all_gather x1, waiting for transfers between devices, on_device(): maps = lax.all_gather(packed, 'slab', axis=0, axis_index_groups=groups)  25.5 us
    all_to_all x3, starting transfers between devices, exchange(): return lax.all_to_all(value, 'col', split_axis=0, concat_axis=0, tiled=True)  19.2 us
    ppermute x3, waiting for transfers between devices, on_device(): flow = lax.ppermute(flow, ('slab', 'col'), pairs)  13.6 us
    pallas_call x1, Pallas kernels, on_device(): pl.pallas_call(spread_kernel, grid=(8,), in_specs=[whole((2, stack, width...  8.81 us
    unnamed x20, local copies, waits for them, and re-layouts  8.22 us
    pallas_call x1, Pallas kernels, on_device(): pl.pallas_call(interface_kernel, grid=(4,), in_specs=[SMEM, whole(inject....  6.58 us
    pallas_call x3, Pallas kernels, on_device(): pl.pallas_call(row_kernel, in_specs=[SMEM, VMEM, VMEM, VMEM], out_specs=V...  4.37 us
  transfers between devices with their start and end apart: 8, of which 8 were waited for; matrix products, arithmetic and copies ran while one was open for 0% of the time, Pallas kernels for 12%

profile of v2, /device:TPU:8, one launch (start us, length us, event | category | flops | bytes accessed | tf_op | source)
XLA Modules:
  0.0 159.6 jit_solution(8558827791974211622)
XLA Ops:
  8.9 6.6 %interface_terms.1 = (f32[8,160,256]{2,1,0:T(8,128)}, bf16[2,320,256]{2,1,0:T(8,128)(2,1)S(1)}, bf16[2,320,256]{2,1,0:T(8,128)(2,1)S(1)}) custom-call(s32[1]{0:T(128)} %bitcast.first_ref, s32[2,64]{1,0:T(2,128)S(1)} %copy-done.8, f32[2,2,64,256]{3,2,1,0:T(8,128)S(1)} %bitcast.21, f32[2,2,2048,256]{3,2,1,0:T(8,128)} %g_ref.1, f32[2,2,2048,256]{3,2,1,0:T(8,128)} %g_ref.1), custom_call_target="tpu_custom_call" | custom-call | tf_op jit(solution)/shard_map/interface_terms/pallas_call | solution.py:277
  15.4 8.6 %all-to-all-start = ((f32[8,160,256]{2,1,0:T(8,128)}), f32[8,160,256]{2,1,0:T(8,128)S(1)}, u32[]{:S(2)}, u32[]{:S(2)}) async-start(f32[8,160,256]{2,1,0:T(8,128)} %get-tuple-element.22), calls=%async_computation | async-start | bytes 2621440 | tf_op jit(solution)/shard_map/all_to_all | solution.py:254
  24.3 1.2 copy-done.5
  26.4 8.8 %spread_terms.1 = (f32[8,256,256]{2,1,0:T(8,128)S(1)}, f32[8,256,256]{2,1,0:T(8,128)S(1)}) custom-call(bf16[2,320,256]{2,1,0:T(8,128)(2,1)S(1)} %get-tuple-element.23.high_ref, bf16[2,320,256]{2,1,0:T(8,128)(2,1)S(1)} %get-tuple-element.24.low_ref, f32[2,2,2048,256]{3,2,1,0:T(8,128)} %g_ref.1), custom_call_target="tpu_custom_call" | custom-call | tf_op jit(solution)/shard_map/spread_terms/pallas_call | solution.py:303
  35.2 1.3 copy-done.3
  36.6 1.4 copy-done.4
  38.1 20.4 %all-to-all-done.recv_ref = f32[8,160,256]{2,1,0:T(8,128)S(1)} async-done(((f32[8,160,256]{2,1,0:T(8,128)}), f32[8,160,256]{2,1,0:T(8,128)S(1)}, u32[]{:S(2)}, u32[]{:S(2)}) %all-to-all-start) | async-done | bytes 1310752 | tf_op jit(solution)/shard_map/all_to_all | solution.py:254
  58.5 3.6 %pair_map.1 = (f32[544,256]{1,0:T(8,128)}, f32[32,256]{1,0:T(8,128)S(1)}) custom-call(s32[3]{0:T(128)S(1)} %pad_add_fusion.team_ref.info_ref, f32[8,160,256]{2,1,0:T(8,128)S(1)} %all-to-all-done.recv_ref, f32[2,512,256]{2,1,0:T(8,128)S(1)} %coupling_rows.1.x_ref, f32[2,32,256]{2,1,0:T(8,128)S(1)} %broadcast_in_dim.2.mask_ref), custom_call_target="tpu_custom_call" | custom-call | tf_op jit(solution)/shard_map/pair_map/pallas_call | solution.py:340
  62.1 4.4 %all-to-all-start.1 = ((f32[8,256,256]{2,1,0:T(8,128)}), f32[8,256,256]{2,1,0:T(8,128)}, u32[]{:S(2)}, u32[]{:S(2)}) async-start(f32[8,256,256]{2,1,0:T(8,128)} %copy-done.4), calls=%async_computation.1 | async-start | bytes 4194304 | tf_op jit(solution)/shard_map/all_to_all | solution.py:254
  66.6 25.5 %all-gather.3.cloned.1.call-done = f32[2176,256]{1,0:T(8,128)} async-done(((f32[544,256]{1,0:T(8,128)}), f32[2176,256]{1,0:T(8,128)}) %all-gather.3.cloned.1.call-update) | async-done | bytes 2228240 | tf_op jit(solution)/shard_map/all_gather | solution.py:353
  92.1 1.6 %copy-done.1 = f32[2176,256]{1,0:T(8,128)S(1)} copy-done((f32[2176,256]{1,0:T(8,128)S(1)}, f32[2176,256]{1,0:T(8,128)}, u32[]{:S(2)}) %copy-start.1) | copy-done | bytes 2228248
  93.8 1.5 row_step.3
  95.3 1.5 collective-permute-start
  96.8 3.7 %collective-permute-done.flow_ref = f32[32,256]{1,0:T(8,128)S(1)} collective-permute-done((f32[32,256]{1,0:T(8,128)S(1)}, f32[32,256]{1,0:T(8,128)S(1)}, u32[]{:S(2)}, u32[]{:S(2)}) %collective-permute-start) | collective-permute-done | bytes 32800 | tf_op jit(solution)/shard_map/ppermute | solution.py:373
  100.5 1.5 row_step.4
  102.3 4.9 %collective-permute-done.1.flow_ref = f32[32,256]{1,0:T(8,128)S(1)} collective-permute-done((f32[32,256]{1,0:T(8,128)S(1)}, f32[32,256]{1,0:T(8,128)S(1)}, u32[]{:S(2)}, u32[]{:S(2)}) %collective-permute-start.1) | collective-permute-done | bytes 32800 | tf_op jit(solution)/shard_map/ppermute | solution.py:373
  107.2 1.5 row_step.5
  108.7 5.1 %collective-permute-done.2.flow_ref = f32[32,256]{1,0:T(8,128)S(1)} collective-permute-done((f32[32,256]{1,0:T(8,128)S(1)}, f32[32,256]{1,0:T(8,128)S(1)}, u32[]{:S(2)}, u32[]{:S(2)}) %collective-permute-start.2) | collective-permute-done | bytes 32800 | tf_op jit(solution)/shard_map/ppermute | solution.py:373
  113.9 2.8 %inflow.1 = f32[8,64,256]{2,1,0:T(8,128)} custom-call(s32[3]{0:T(128)S(1)} %pad_add_fusion.team_ref.info_ref, f32[32,256]{1,0:T(8,128)S(1)} %bitcast.20, f32[32,256]{1,0:T(8,128)S(1)} %collective-permute-done.2.flow_ref, f32[4,544,256]{2,1,0:T(8,128)S(1)} %bitcast.15, f32[8,160,256]{2,1,0:T(8,128)S(1)} %all-to-all-done.recv_ref, ...), custom_call_target="tpu_custom_call" | custom-call | tf_op jit(solution)/shard_map/inflow/pallas_call | solution.py:374
  117.7 6.3 %all-to-all-start.2 = ((f32[8,64,256]{2,1,0:T(8,128)}), f32[8,64,256]{2,1,0:T(8,128)S(1)}, u32[]{:S(2)}, u32[]{:S(2)}) async-start(f32[8,64,256]{2,1,0:T(8,128)} %inflow.1), calls=%async_computation.2 | async-start | bytes 1048576 | tf_op jit(solution)/shard_map/all_to_all | solution.py:254
  123.9 1.9 %arrange_rows.1 = (bf16[2,2,2,256,256]{4,3,2,1,0:T(8,128)(2,1)S(1)}, bf16[2,2,2,256,256]{4,3,2,1,0:T(8,128)(2,1)S(1)}) custom-call(f32[8,256,256]{2,1,0:T(8,128)} %all-to-all-done.1.recv_ref), custom_call_target="tpu_custom_call" | custom-call | tf_op jit(solution)/shard_map/arrange_rows/pallas_call | solution.py:384
  125.9 21.6 %all-to-all-done.2.inner_ref = f32[8,64,256]{2,1,0:T(8,128)S(1)} async-done(((f32[8,64,256]{2,1,0:T(8,128)}), f32[8,64,256]{2,1,0:T(8,128)S(1)}, u32[]{:S(2)}, u32[]{:S(2)}) %all-to-all-start.2) | async-done | bytes 524320 | tf_op jit(solution)/shard_map/all_to_all | solution.py:254
  147.4 3.1 %reduce-scatter.2.cloned.1.call-done = f32[1,256,256]{2,1,0:T(8,128)} async-done(((f32[8,256,256]{2,1,0:T(8,128)}), f32[1,256,256]{2,1,0:T(8,128)}) %reduce-scatter.2.cloned.1.call-update) | async-done | bytes 262160 | tf_op jit(solution)/shard_map/reduce_scatter | solution.py:355
  151.5 1.3 states.1
  (30 shorter events, 5.5 us)
Async XLA Ops:
  7.2 30.9 %copy-start = (f32[2,2,256,64]{2,3,1,0:T(8,128)S(1)}, f32[2,2,256,64]{2,3,1,0:T(8,128)}, u32[]{:S(2)}) copy-start(f32[2,2,256,64]{2,3,1,0:T(8,128)} %param.9) | copy-start | bytes 786436
  7.2 1.0 copy-start.6
  8.2 0.7 copy-start.8
  15.4 8.7 %copy-start.9 = (s32[2,64]{1,0:T(2,128)S(1)}, s32[2,64]{1,0:T(2,128)}, u32[]{:S(2)}) copy-start(s32[2,64]{1,0:T(2,128)} %inject_ref.3) | copy-start | bytes 1540
  15.4 43.0 %all-to-all-start = ((f32[8,160,256]{2,1,0:T(8,128)}), f32[8,160,256]{2,1,0:T(8,128)S(1)}, u32[]{:S(2)}, u32[]{:S(2)}) async-start(f32[8,160,256]{2,1,0:T(8,128)} %get-tuple-element.22), calls=%async_computation | async-start | bytes 2621440 | tf_op jit(solution)/shard_map/all_to_all | solution.py:254
  24.0 68.1 %all-gather.3.cloned.1.call-start = ((), (), s32[]{:S(2)}) async-start(), calls=%async_computation.5 | async-start | bytes 2785280 | tf_op jit(solution)/shard_map/all_gather | solution.py:353
  24.3 1.2 copy-start.5
  35.2 1.3 copy-start.3
  36.6 1.4 copy-start.4
  62.1 55.5 %all-to-all-start.1 = ((f32[8,256,256]{2,1,0:T(8,128)}), f32[8,256,256]{2,1,0:T(8,128)}, u32[]{:S(2)}, u32[]{:S(2)}) async-start(f32[8,256,256]{2,1,0:T(8,128)} %copy-done.4), calls=%async_computation.1 | async-start | bytes 4194304 | tf_op jit(solution)/shard_map/all_to_all | solution.py:254
  66.5 84.1 %reduce-scatter.2.cloned.1.call-start = ((), (), s32[]{:S(2)}) async-start(), calls=%async_computation.4 | async-start | bytes 2359296 | tf_op jit(solution)/shard_map/reduce_scatter | solution.py:355
  92.1 1.6 %copy-start.1 = (f32[2176,256]{1,0:T(8,128)S(1)}, f32[2176,256]{1,0:T(8,128)}, u32[]{:S(2)}) copy-start(f32[2176,256]{1,0:T(8,128)} %all-gather.3.cloned.1.call-done) | copy-start | bytes 6684676
  95.2 18.6 %copy-start.2 = (f32[2176,256]{1,0:T(8,128)S(1)}, f32[2176,256]{1,0:T(8,128)}, u32[]{:S(2)}) copy-start(f32[2176,256]{1,0:T(8,128)} %all-gather.3.cloned.1.call-done) | copy-start | bytes 6684676
  95.3 5.2 %collective-permute-start = (f32[32,256]{1,0:T(8,128)S(1)}, f32[32,256]{1,0:T(8,128)S(1)}, u32[]{:S(2)}, u32[]{:S(2)}) collective-permute-start(f32[32,256]{1,0:T(8,128)S(1)} %row_step.3), channel_id=1, source_target_pairs={{0,64},{2,66},{4,68},{6,70},{8,200},{10,202},{12,204},{14,206},{16... | collective-permute-start | bytes 98312 | tf_op jit(solution)/shard_map/ppermute | solution.py:373
  101.9 5.2 %collective-permute-start.1 = (f32[32,256]{1,0:T(8,128)S(1)}, f32[32,256]{1,0:T(8,128)S(1)}, u32[]{:S(2)}, u32[]{:S(2)}) collective-permute-start(f32[32,256]{1,0:T(8,128)S(1)} %row_step.4), channel_id=1, source_target_pairs={{0,64},{2,66},{4,68},{6,70},{8,200},{10,202},{12,204},{14,206},{16... | collective-permute-start | bytes 98312 | tf_op jit(solution)/shard_map/ppermute | solution.py:373
  108.6 5.2 %collective-permute-start.2 = (f32[32,256]{1,0:T(8,128)S(1)}, f32[32,256]{1,0:T(8,128)S(1)}, u32[]{:S(2)}, u32[]{:S(2)}) collective-permute-start(f32[32,256]{1,0:T(8,128)S(1)} %row_step.5), channel_id=1, source_target_pairs={{0,64},{2,66},{4,68},{6,70},{8,200},{10,202},{12,204},{14,206},{16... | collective-permute-start | bytes 98312 | tf_op jit(solution)/shard_map/ppermute | solution.py:373
  117.7 29.8 %all-to-all-start.2 = ((f32[8,64,256]{2,1,0:T(8,128)}), f32[8,64,256]{2,1,0:T(8,128)S(1)}, u32[]{:S(2)}, u32[]{:S(2)}) async-start(f32[8,64,256]{2,1,0:T(8,128)} %inflow.1), calls=%async_computation.2 | async-start | bytes 1048576 | tf_op jit(solution)/shard_map/all_to_all | solution.py:254
  150.6 0.9 copy-start.7
Sparse Core Ops, SparseCore 0:
  62.3 29.8 all-gather.2
  94.7 55.8 reduce-scatter.1

commit v3 on v2

--- a/solution.py
+++ b/solution.py
@@ -165,26 +165,74 @@
     out_ref[2 * size :, :] = complex_rows(flow_a, second) + flow_b
 
 
-def advance(state, maps_ref, index):
-    size = maps_ref.shape[2]
-    flow = complex_rows(state, (maps_ref[index, :size], maps_ref[index, size : 2 * size]))
-    return flow + maps_ref[index, 2 * size :]
-
-
-def row_kernel(info_ref, lead_ref, flow_ref, maps_ref, out_ref):
-    state = jnp.where(info_ref[1] == 0, lead_ref[...], flow_ref[...])
+def advance(state, maps, flow):
+    size = maps[0].shape[1]
+    half = state.shape[0] // 2
+    parts = split(state)
+    by_real = mm3(parts, tuple(ref[:size, :] for ref in maps))
+    by_imag = mm3(parts, tuple(ref[size:, :] for ref in maps))
+    moved = jnp.concatenate(
+        [by_real[:half] - by_imag[half:], by_imag[:half] + by_real[half:]], axis=0
+    )
+    return moved + flow
+
+
+def item_of(info_ref, item):
+    return jnp.where(info_ref[0] == 0, item, 3 - item)
+
+
+def row_state(info_ref, state, high_ref, low_ref, flow_ref):
     for item in range(4):
-        state = advance(state, maps_ref, jnp.where(info_ref[0] == 0, item, 3 - item))
-    out_ref[...] = state
-
-
-def inflow_kernel(info_ref, lead_ref, flow_ref, maps_ref, recv_ref, x_ref, qa_ref, out_ref):
+        index = item_of(info_ref, item)
+        state = advance(state, (high_ref.at[index], low_ref.at[index]), flow_ref[index])
+    return state
+
+
+def gather_kernel(info_ref, lead_ref, own_ref, *refs):
+    pieces, (high_ref, low_ref, flow_ref, out_ref) = refs[:6], refs[6:]
+    size = own_ref.shape[1]
+    half = pieces[0].shape[0]
+    for shift in range(4):
+        place = lax.rem(info_ref[3] + shift, 4)
+        if shift == 0:
+            top, bottom = own_ref[:half, :], own_ref[half:, :]
+        else:
+            top, bottom = pieces[2 * shift - 2][...], pieces[2 * shift - 1][...]
+        rest = 2 * size - half
+        high, low = split(top)
+        high_ref[place, :half, :] = high
+        low_ref[place, :half, :] = low
+        high, low = split(bottom[:rest])
+        high_ref[place, half:, :] = high
+        low_ref[place, half:, :] = low
+        flow_ref[place] = bottom[rest:]
+    out_ref[...] = row_state(info_ref, lead_ref[...], high_ref, low_ref, flow_ref)
+
+
+def row_kernel(info_ref, lead_ref, state_ref, high_ref, low_ref, flow_ref, out_ref):
+    state = jnp.where(info_ref[1] == 0, lead_ref[...], state_ref[...])
+    out_ref[...] = row_state(info_ref, state, high_ref, low_ref, flow_ref)
+
+
+def inflow_kernel(
+    info_ref,
+    lead_ref,
+    state_ref,
+    high_ref,
+    low_ref,
+    flow_ref,
+    recv_ref,
+    x_ref,
+    qa_ref,
+    out_ref,
+):
     size = x_ref.shape[2]
     lead = size // 8
     left = info_ref[0] == 0
-    state = jnp.where(info_ref[1] == 0, lead_ref[...], flow_ref[...])
+    state = jnp.where(info_ref[1] == 0, lead_ref[...], state_ref[...])
     for item in range(3):
-        later = advance(state, maps_ref, jnp.where(left, item, 3 - item))
+        index = item_of(info_ref, item)
+        later = advance(state, (high_ref.at[index], low_ref.at[index]), flow_ref[index])
         state = jnp.where(item < info_ref[2], later, state)
     turned = complex_rows(state, (x_ref[0, :size], x_ref[0, size:]))
     inner_a = jnp.where(left, turned, state)
@@ -268,7 +316,7 @@
     member = col_index % 4
     first = jnp.reshape(slab_index * 2, (1,)).astype(jnp.int32)
     position = jnp.where(team == 0, slab_index, slabs - 1 - slab_index)
-    info = jnp.stack([team, position // 4, position % 4]).astype(jnp.int32)
+    info = jnp.stack([team, position // 4, position % 4, slab_index % 4]).astype(jnp.int32)
     stack = 2 * (lead + 2 * modes)
     block_rows = 4 * lead + 32
     sources = jnp.transpose(sources, (0, 1, 3, 2))
@@ -333,8 +381,8 @@
     marks = jnp.broadcast_to(marks.astype(F32)[:, :, None], (2, 32, size))
     own_lead = lax.dynamic_slice(leads, (team, 0, member * 16, 0), (1, 2, 16, size))
     own_lead = own_lead.reshape(32, size)
-    received, spread, turned, marks, own_lead = lax.optimization_barrier(
-        (received, spread, turned, marks, own_lead)
+    received, spread, flows, turned, marks, own_lead = lax.optimization_barrier(
+        (received, spread, flows, turned, marks, own_lead)
     )
 
     packed, flow_a = pl.pallas_call(
@@ -348,11 +396,34 @@
         compiler_params=params(),
         name="pair_map",
     )(info, received, turned, marks)
+    packed, spread = lax.optimization_barrier((packed, spread))
     rows = exchange(spread)
-    groups = [[4 * row + item for item in range(4)] for row in range(slabs // 4)]
-    maps = lax.all_gather(packed, "slab", axis=0, axis_index_groups=groups)
-    maps, flows = lax.optimization_barrier((maps, flows))
     base = lax.psum_scatter(flows, "col", scatter_dimension=0, tiled=False)
+
+    def turn(value, step):
+        return lax.ppermute(
+            value, "slab", [(slab, slab // 4 * 4 + (slab + step) % 4) for slab in range(slabs)]
+        )
+
+    top, bottom = packed[: size + 16], packed[size + 16 :]
+    before_top, after_bottom = turn(top, 1), turn(bottom, -1)
+    before_bottom, after_top = turn(bottom, 1), turn(top, -1)
+    across_top, across_bottom = turn(before_top, 1), turn(after_bottom, -1)
+    pieces = (after_top, after_bottom, across_top, across_bottom, before_top, before_bottom)
+    row_maps = [
+        jax.ShapeDtypeStruct((4, 2 * size, size), BF16),
+        jax.ShapeDtypeStruct((4, 2 * size, size), BF16),
+        jax.ShapeDtypeStruct((4, 32, size), F32),
+    ]
+    state_shape = jax.ShapeDtypeStruct((32, size), F32)
+    *maps, flow = pl.pallas_call(
+        gather_kernel,
+        in_specs=[SMEM] + [VMEM] * 8,
+        out_specs=[VMEM] * 4,
+        out_shape=row_maps + [state_shape],
+        compiler_params=params(),
+        name="gather_maps",
+    )(info, own_lead, packed, *pieces)
 
     cols = lax.axis_size("col")
     pairs = []
@@ -360,25 +431,25 @@
         for col in range(cols):
             target = (slab + (4 if col < 4 else -4)) % slabs
             pairs.append((slab * cols + col, target * cols + col))
-    flow = own_lead
-    for _ in range(slabs // 4 - 1):
+    flow = lax.ppermute(flow, ("slab", "col"), pairs)
+    for _ in range(slabs // 4 - 2):
         flow = pl.pallas_call(
             row_kernel,
-            in_specs=[SMEM, VMEM, VMEM, VMEM],
+            in_specs=[SMEM] + [VMEM] * 5,
             out_specs=VMEM,
-            out_shape=jax.ShapeDtypeStruct((32, size), F32),
+            out_shape=state_shape,
             compiler_params=params(),
             name="row_step",
-        )(info, own_lead, flow, maps)
+        )(info, own_lead, flow, *maps)
         flow = lax.ppermute(flow, ("slab", "col"), pairs)
     inner = pl.pallas_call(
         inflow_kernel,
-        in_specs=[SMEM] + [VMEM] * 6,
+        in_specs=[SMEM] + [VMEM] * 8,
         out_specs=VMEM,
         out_shape=jax.ShapeDtypeStruct((8, 64, size), F32),
         compiler_params=params(),
         name="inflow",
-    )(info, own_lead, flow, maps, received, turned, flow_a)
+    )(info, own_lead, flow, *maps, received, turned, flow_a)
     rows, inner = lax.optimization_barrier((rows, inner))
     inner = exchange(inner)
     row_high, row_low = pl.pallas_call(

time: 160 us -> 160 us (level)
  starting transfers between devices: 21.3 us -> 24.3 us
  waiting for transfers between devices: 85.3 us -> 83.5 us
  local copies, waits for them, and re-layouts: 8.38 us -> 6.7 us
    all_gather x1 -> x0, waiting for transfers between devices: 25.5 us -> none  [on_device(): maps = lax.all_gather(packed, 'slab', axis=0, axis_index_groups=groups)]
    ppermute x0 -> x6, waiting for transfers between devices: none -> 16.3 us  [turn(): lax.ppermute(value, 'slab', [(slab, slab // 4 * 4 + (slab + step) % 4) fo...]
    all_to_all x3, waiting for transfers between devices: 43 us -> 50.2 us  [exchange(): return lax.all_to_all(value, 'col', split_axis=0, concat_axis=0, tiled=True)]
    ppermute x0 -> x6, starting transfers between devices: none -> 5.74 us  [turn(): lax.ppermute(value, 'slab', [(slab, slab // 4 * 4 + (slab + step) % 4) fo...]
    all_to_all x3, starting transfers between devices: 19.2 us -> 16.5 us  [exchange(): return lax.all_to_all(value, 'col', split_axis=0, concat_axis=0, tiled=True)]
    unnamed x20 -> x16, local copies, waits for them, and re-layouts: 8.22 us -> 6.5 us
  transfers between devices with their start and end apart: 8 -> 13, of which waited for: 8 -> 12; matrix products, arithmetic and copies ran while one was open for 0% -> 0% of each run, Pallas kernels for 12% -> 12%
where the time goes in v3:
time: 160 us; the launch traced here: 159 us
  waiting for transfers between devices  83.5 us (52%)
  Pallas kernels  29.6 us (18%)
  starting transfers between devices  24.3 us (15%)
  between operations  14.2 us (9%)
  local copies, waits for them, and re-layouts  6.7 us (4%)
    all_to_all x3, waiting for transfers between devices, exchange(): return lax.all_to_all(value, 'col', split_axis=0, concat_axis=0, tiled=True)  50.2 us
    all_to_all x3, starting transfers between devices, exchange(): return lax.all_to_all(value, 'col', split_axis=0, concat_axis=0, tiled=True)  16.5 us
    ppermute x6, waiting for transfers between devices, turn(): lax.ppermute(value, 'slab', [(slab, slab // 4 * 4 + (slab + step) % 4) fo...  16.3 us
    ppermute x3, waiting for transfers between devices, on_device(): flow = lax.ppermute(flow, ('slab', 'col'), pairs)  13.6 us
    pallas_call x1, Pallas kernels, on_device(): pl.pallas_call(spread_kernel, grid=(8,), in_specs=[whole((2, stack, width...  8.8 us
    pallas_call x1, Pallas kernels, on_device(): pl.pallas_call(interface_kernel, grid=(4,), in_specs=[SMEM, whole(inject....  6.61 us
    unnamed x16, local copies, waits for them, and re-layouts  6.5 us
    ppermute x6, starting transfers between devices, turn(): lax.ppermute(value, 'slab', [(slab, slab // 4 * 4 + (slab + step) % 4) fo...  5.74 us
  transfers between devices with their start and end apart: 13, of which 12 were waited for; matrix products, arithmetic and copies ran while one was open for 0% of the time, Pallas kernels for 12%

profile of v3, /device:TPU:8, one launch (start us, length us, event | category | flops | bytes accessed | tf_op | source)
XLA Modules:
  0.0 158.5 jit_solution(15681366949452131910)
XLA Ops:
  8.9 6.6 %interface_terms.1 = (f32[8,160,256]{2,1,0:T(8,128)}, bf16[2,320,256]{2,1,0:T(8,128)(2,1)S(1)}, bf16[2,320,256]{2,1,0:T(8,128)(2,1)S(1)}) custom-call(s32[1]{0:T(128)} %bitcast.first_ref, s32[2,64]{1,0:T(2,128)S(1)} %copy-done.6, f32[2,2,64,256]{3,2,1,0:T(8,128)S(1)} %bitcast.16, f32[2,2,2048,256]{3,2,1,0:T(8,128)} %g_ref.1, f32[2,2,2048,256]{3,2,1,0:T(8,128)} %g_ref.1), custom_call_target="tpu_custom_call" | custom-call | tf_op jit(solution)/shard_map/interface_terms/pallas_call | solution.py:325
  15.5 8.6 %all-to-all-start = ((f32[8,160,256]{2,1,0:T(8,128)}), f32[8,160,256]{2,1,0:T(8,128)S(1)}, u32[]{:S(2)}, u32[]{:S(2)}) async-start(f32[8,160,256]{2,1,0:T(8,128)} %get-tuple-element.27), calls=%async_computation | async-start | bytes 2621440 | tf_op jit(solution)/shard_map/all_to_all | solution.py:302
  26.3 8.8 %spread_terms.1 = (f32[8,256,256]{2,1,0:T(8,128)S(1)}, f32[8,256,256]{2,1,0:T(8,128)S(1)}) custom-call(bf16[2,320,256]{2,1,0:T(8,128)(2,1)S(1)} %get-tuple-element.28.high_ref, bf16[2,320,256]{2,1,0:T(8,128)(2,1)S(1)} %get-tuple-element.29.low_ref, f32[2,2,2048,256]{3,2,1,0:T(8,128)} %g_ref.1), custom_call_target="tpu_custom_call" | custom-call | tf_op jit(solution)/shard_map/spread_terms/pallas_call | solution.py:351
  37.9 20.6 %all-to-all-done.recv_ref = f32[8,160,256]{2,1,0:T(8,128)S(1)} async-done(((f32[8,160,256]{2,1,0:T(8,128)}), f32[8,160,256]{2,1,0:T(8,128)S(1)}, u32[]{:S(2)}, u32[]{:S(2)}) %all-to-all-start) | async-done | bytes 1310752 | tf_op jit(solution)/shard_map/all_to_all | solution.py:302
  58.6 2.7 %pair_map.1 = (f32[544,256]{1,0:T(8,128)S(1)}, f32[32,256]{1,0:T(8,128)S(1)}) custom-call(s32[4]{0:T(128)S(1)} %pad_add_fusion.team_ref.info_ref, f32[8,160,256]{2,1,0:T(8,128)S(1)} %all-to-all-done.recv_ref, f32[2,512,256]{2,1,0:T(8,128)S(1)} %coupling_rows.1.x_ref, f32[2,32,256]{2,1,0:T(8,128)S(1)} %broadcast_in_dim.2.mask_ref), custom_call_target="tpu_custom_call" | custom-call | tf_op jit(solution)/shard_map/pair_map/pallas_call | solution.py:388
  61.3 4.4 %all-to-all-start.1 = ((f32[8,256,256]{2,1,0:T(8,128)}), f32[8,256,256]{2,1,0:T(8,128)}, u32[]{:S(2)}, u32[]{:S(2)}) async-start(f32[8,256,256]{2,1,0:T(8,128)} %copy-done.2), calls=%async_computation.1 | async-start | bytes 4194304 | tf_op jit(solution)/shard_map/all_to_all | solution.py:302
  67.0 1.6 collective-permute-start.2
  68.6 1.6 collective-permute-start.5
  70.6 5.5 %collective-permute-done.1.refs_1_ = f32[272,256]{1,0:T(8,128)S(1)} collective-permute-done((f32[272,256]{1,0:T(8,128)S(1)}, f32[272,256]{1,0:T(8,128)S(1)}, u32[]{:S(2)}, u32[]{:S(2)}) %collective-permute-start.1) | collective-permute-done | bytes 278560 | tf_op jit(solution)/shard_map/ppermute | solution.py:404
  78.1 5.3 %collective-permute-done.5.refs_5_ = f32[272,256]{1,0:T(8,128)S(1)} collective-permute-done((f32[272,256]{1,0:T(8,128)S(1)}, f32[272,256]{1,0:T(8,128)S(1)}, u32[]{:S(2)}, u32[]{:S(2)}) %collective-permute-start.5) | collective-permute-done | bytes 278560 | tf_op jit(solution)/shard_map/ppermute | solution.py:404
  83.5 3.6 %collective-permute-done.4.refs_3_ = f32[272,256]{1,0:T(8,128)S(1)} collective-permute-done((f32[272,256]{1,0:T(8,128)S(1)}, f32[272,256]{1,0:T(8,128)S(1)}, u32[]{:S(2)}, u32[]{:S(2)}) %collective-permute-start.4) | collective-permute-done | bytes 278560 | tf_op jit(solution)/shard_map/ppermute | solution.py:404
  88.5 1.7 %gather_maps.1 = (bf16[4,512,256]{2,1,0:T(8,128)(2,1)S(1)}, bf16[4,512,256]{2,1,0:T(8,128)(2,1)S(1)}, f32[4,32,256]{2,1,0:T(8,128)S(1)}, f32[32,256]{1,0:T(8,128)S(1)}) custom-call(s32[4]{0:T(128)S(1)} %pad_add_fusion.team_ref.info_ref, f32[32,256]{1,0:T(8,128)S(1)} %bitcast.12, f32[544,256]{1,0:T(8,128)S(1)} %get-tuple-element.39.own_ref, ...), custom_call_target="tpu_custom_call" | custom-call | tf_op jit(solution)/shard_map/gather_maps/pallas_call | solution.py:419
  90.2 1.6 %collective-permute-start.6 = (f32[32,256]{1,0:T(8,128)S(1)}, f32[32,256]{1,0:T(8,128)S(1)}, u32[]{:S(2)}, u32[]{:S(2)}) collective-permute-start(f32[32,256]{1,0:T(8,128)S(1)} %get-tuple-element.40), channel_id=1, source_target_pairs={{0,64},{2,66},{4,68},{6,70},{8,200},{10,202},{12,204},{14,206},{16... | collective-permute-start | bytes 98312 | tf_op jit(solution)/shard_map/ppermute | solution.py:434
  91.8 3.6 %collective-permute-done.6.state_ref = f32[32,256]{1,0:T(8,128)S(1)} collective-permute-done((f32[32,256]{1,0:T(8,128)S(1)}, f32[32,256]{1,0:T(8,128)S(1)}, u32[]{:S(2)}, u32[]{:S(2)}) %collective-permute-start.6) | collective-permute-done | bytes 32800 | tf_op jit(solution)/shard_map/ppermute | solution.py:434
  95.5 1.5 row_step.2
  97.3 4.8 %collective-permute-done.7.state_ref = f32[32,256]{1,0:T(8,128)S(1)} collective-permute-done((f32[32,256]{1,0:T(8,128)S(1)}, f32[32,256]{1,0:T(8,128)S(1)}, u32[]{:S(2)}, u32[]{:S(2)}) %collective-permute-start.7) | collective-permute-done | bytes 32800 | tf_op jit(solution)/shard_map/ppermute | solution.py:444
  102.1 1.5 row_step.3
  103.7 5.1 %collective-permute-done.8.state_ref = f32[32,256]{1,0:T(8,128)S(1)} collective-permute-done((f32[32,256]{1,0:T(8,128)S(1)}, f32[32,256]{1,0:T(8,128)S(1)}, u32[]{:S(2)}, u32[]{:S(2)}) %collective-permute-start.8) | collective-permute-done | bytes 32800 | tf_op jit(solution)/shard_map/ppermute | solution.py:444
  108.8 2.8 %inflow.1 = f32[8,64,256]{2,1,0:T(8,128)} custom-call(s32[4]{0:T(128)S(1)} %pad_add_fusion.team_ref.info_ref, f32[32,256]{1,0:T(8,128)S(1)} %bitcast.15, f32[32,256]{1,0:T(8,128)S(1)} %collective-permute-done.8.state_ref, bf16[4,512,256]{2,1,0:T(8,128)(2,1)S(1)} %get-tuple-element.41.high_ref, bf16[4,512,256]{2,1,0:T(8,128)(2,1)S(1)} %get-tuple-element.42.low_ref, ...), custom_call_target="tpu_custom_call" | custom-call | tf_op jit(solution)/shard_map/inflow/pallas_call | solution.py:445
  111.6 18.1 %all-to-all-done.1.recv_ref = f32[8,256,256]{2,1,0:T(8,128)} async-done(((f32[8,256,256]{2,1,0:T(8,128)}), f32[8,256,256]{2,1,0:T(8,128)}, u32[]{:S(2)}, u32[]{:S(2)}) %all-to-all-start.1) | async-done | bytes 2097184 | tf_op jit(solution)/shard_map/all_to_all | solution.py:302
  129.7 3.5 %all-to-all-start.2 = ((f32[8,64,256]{2,1,0:T(8,128)}), f32[8,64,256]{2,1,0:T(8,128)S(1)}, u32[]{:S(2)}, u32[]{:S(2)}) async-start(f32[8,64,256]{2,1,0:T(8,128)} %inflow.1), calls=%async_computation.2 | async-start | bytes 1048576 | tf_op jit(solution)/shard_map/all_to_all | solution.py:302
  133.2 1.9 %arrange_rows.1 = (bf16[2,2,2,256,256]{4,3,2,1,0:T(8,128)(2,1)S(1)}, bf16[2,2,2,256,256]{4,3,2,1,0:T(8,128)(2,1)S(1)}) custom-call(f32[8,256,256]{2,1,0:T(8,128)} %all-to-all-done.1.recv_ref), custom_call_target="tpu_custom_call" | custom-call | tf_op jit(solution)/shard_map/arrange_rows/pallas_call | solution.py:455
  135.2 2.8 %reduce-scatter.2.cloned.1.call-done = f32[1,256,256]{2,1,0:T(8,128)} async-done(((f32[8,256,256]{2,1,0:T(8,128)}), f32[1,256,256]{2,1,0:T(8,128)}) %reduce-scatter.2.cloned.1.call-update) | async-done | bytes 262160 | tf_op jit(solution)/shard_map/reduce_scatter | solution.py:401
  138.0 11.5 %all-to-all-done.2.inner_ref = f32[8,64,256]{2,1,0:T(8,128)S(1)} async-done(((f32[8,64,256]{2,1,0:T(8,128)}), f32[8,64,256]{2,1,0:T(8,128)S(1)}, u32[]{:S(2)}, u32[]{:S(2)}) %all-to-all-start.2) | async-done | bytes 524320 | tf_op jit(solution)/shard_map/all_to_all | solution.py:302
  (36 shorter events, 14.7 us)
Async XLA Ops:
  7.2 30.7 %copy-start = (f32[2,2,256,64]{2,3,1,0:T(8,128)S(1)}, f32[2,2,256,64]{2,3,1,0:T(8,128)}, u32[]{:S(2)}) copy-start(f32[2,2,256,64]{2,3,1,0:T(8,128)} %param.9) | copy-start | bytes 786436
  7.2 1.0 copy-start.4
  8.2 0.7 copy-start.6
  15.5 8.6 %copy-start.7 = (s32[2,64]{1,0:T(2,128)S(1)}, s32[2,64]{1,0:T(2,128)}, u32[]{:S(2)}) copy-start(s32[2,64]{1,0:T(2,128)} %inject_ref.3) | copy-start | bytes 1540
  15.5 43.0 %all-to-all-start = ((f32[8,160,256]{2,1,0:T(8,128)}), f32[8,160,256]{2,1,0:T(8,128)S(1)}, u32[]{:S(2)}, u32[]{:S(2)}) async-start(f32[8,160,256]{2,1,0:T(8,128)} %get-tuple-element.27), calls=%async_computation | async-start | bytes 2621440 | tf_op jit(solution)/shard_map/all_to_all | solution.py:302
  24.2 1.2 copy-start.3
  35.1 1.3 copy-start.1
  36.5 1.3 copy-start.2
  61.3 68.4 %all-to-all-start.1 = ((f32[8,256,256]{2,1,0:T(8,128)}), f32[8,256,256]{2,1,0:T(8,128)}, u32[]{:S(2)}, u32[]{:S(2)}) async-start(f32[8,256,256]{2,1,0:T(8,128)} %copy-done.2), calls=%async_computation.1 | async-start | bytes 4194304 | tf_op jit(solution)/shard_map/all_to_all | solution.py:302
  65.7 72.3 %reduce-scatter.2.cloned.1.call-start = ((), (), s32[]{:S(2)}) async-start(), calls=%async_computation.4 | async-start | bytes 2359296 | tf_op jit(solution)/shard_map/reduce_scatter | solution.py:401
  66.5 9.6 %collective-permute-start.1 = (f32[272,256]{1,0:T(8,128)S(1)}, f32[272,256]{1,0:T(8,128)S(1)}, u32[]{:S(2)}, u32[]{:S(2)}) collective-permute-start(f32[272,256]{1,0:T(8,128)S(1)} %get-tuple-element.52), channel_id=1, source_target_pairs={{0,48},{16,0},{32,16},{48,32},{64,112},{80,64},{96,80},{112,96},{1... | collective-permute-start | bytes 835592 | tf_op jit(solution)/shard_map/ppermute | solution.py:404
  67.0 10.5 %collective-permute-start.2 = (f32[272,256]{1,0:T(8,128)S(1)}, f32[272,256]{1,0:T(8,128)S(1)}, u32[]{:S(2)}, u32[]{:S(2)}) collective-permute-start(f32[272,256]{1,0:T(8,128)S(1)} %get-tuple-element.53), channel_id=1, source_target_pairs={{0,16},{16,32},{32,48},{48,0},{64,80},{80,96},{96,112},{112,64},{1... | collective-permute-start | bytes 835592 | tf_op jit(solution)/shard_map/ppermute | solution.py:404
  68.6 14.9 %collective-permute-start.5 = (f32[272,256]{1,0:T(8,128)S(1)}, f32[272,256]{1,0:T(8,128)S(1)}, u32[]{:S(2)}, u32[]{:S(2)}) collective-permute-start(f32[272,256]{1,0:T(8,128)S(1)} %get-tuple-element.52), channel_id=1, source_target_pairs={{0,16},{16,32},{32,48},{48,0},{64,80},{80,96},{96,112},{112,64},{1... | collective-permute-start | bytes 835592 | tf_op jit(solution)/shard_map/ppermute | solution.py:404
  70.1 13.3 %collective-permute-start = (f32[272,256]{1,0:T(8,128)S(1)}, f32[272,256]{1,0:T(8,128)S(1)}, u32[]{:S(2)}, u32[]{:S(2)}) collective-permute-start(f32[272,256]{1,0:T(8,128)S(1)} %get-tuple-element.53), channel_id=1, source_target_pairs={{0,48},{16,0},{32,16},{48,32},{64,112},{80,64},{96,80},{112,96},{1... | collective-permute-start | bytes 835592 | tf_op jit(solution)/shard_map/ppermute | solution.py:404
  76.1 11.0 %collective-permute-start.4 = (f32[272,256]{1,0:T(8,128)S(1)}, f32[272,256]{1,0:T(8,128)S(1)}, u32[]{:S(2)}, u32[]{:S(2)}) collective-permute-start(f32[272,256]{1,0:T(8,128)S(1)} %collective-permute-done.1.refs_1_), channel_id=1, source_target_pairs={{0,48},{16,0},{32,16},{48,32},{64,112},{80,64},{96,80},{112,96},{1... | collective-permute-start | bytes 835592 | tf_op jit(solution)/shard_map/ppermute | solution.py:404
  77.5 11.0 %collective-permute-start.3 = (f32[272,256]{1,0:T(8,128)S(1)}, f32[272,256]{1,0:T(8,128)S(1)}, u32[]{:S(2)}, u32[]{:S(2)}) collective-permute-start(f32[272,256]{1,0:T(8,128)S(1)} %collective-permute-done.2.refs_4_), channel_id=1, source_target_pairs={{0,16},{16,32},{32,48},{48,0},{64,80},{80,96},{96,112},{112,64},{1... | collective-permute-start | bytes 835592 | tf_op jit(solution)/shard_map/ppermute | solution.py:404
  90.2 5.2 %collective-permute-start.6 = (f32[32,256]{1,0:T(8,128)S(1)}, f32[32,256]{1,0:T(8,128)S(1)}, u32[]{:S(2)}, u32[]{:S(2)}) collective-permute-start(f32[32,256]{1,0:T(8,128)S(1)} %get-tuple-element.40), channel_id=1, source_target_pairs={{0,64},{2,66},{4,68},{6,70},{8,200},{10,202},{12,204},{14,206},{16... | collective-permute-start | bytes 98312 | tf_op jit(solution)/shard_map/ppermute | solution.py:434
  96.9 5.2 %collective-permute-start.7 = (f32[32,256]{1,0:T(8,128)S(1)}, f32[32,256]{1,0:T(8,128)S(1)}, u32[]{:S(2)}, u32[]{:S(2)}) collective-permute-start(f32[32,256]{1,0:T(8,128)S(1)} %row_step.2), channel_id=1, source_target_pairs={{0,64},{2,66},{4,68},{6,70},{8,200},{10,202},{12,204},{14,206},{16... | collective-permute-start | bytes 98312 | tf_op jit(solution)/shard_map/ppermute | solution.py:444
  103.6 5.2 %collective-permute-start.8 = (f32[32,256]{1,0:T(8,128)S(1)}, f32[32,256]{1,0:T(8,128)S(1)}, u32[]{:S(2)}, u32[]{:S(2)}) collective-permute-start(f32[32,256]{1,0:T(8,128)S(1)} %row_step.3), channel_id=1, source_target_pairs={{0,64},{2,66},{4,68},{6,70},{8,200},{10,202},{12,204},{14,206},{16... | collective-permute-start | bytes 98312 | tf_op jit(solution)/shard_map/ppermute | solution.py:444
  129.7 19.7 %all-to-all-start.2 = ((f32[8,64,256]{2,1,0:T(8,128)}), f32[8,64,256]{2,1,0:T(8,128)S(1)}, u32[]{:S(2)}, u32[]{:S(2)}) async-start(f32[8,64,256]{2,1,0:T(8,128)} %inflow.1), calls=%async_computation.2 | async-start | bytes 1048576 | tf_op jit(solution)/shard_map/all_to_all | solution.py:302
  149.4 1.0 copy-start.5
Sparse Core Ops, SparseCore 0:
  69.1 68.8 reduce-scatter.1

commit v4 on v3

--- a/solution.py
+++ b/solution.py
@@ -8,6 +8,7 @@
 F32 = jnp.float32
 BF16 = jnp.bfloat16
 LIMIT = 48 * 1024 * 1024
+PACK = 16
 
 
 def split(value):
@@ -37,7 +38,7 @@
 
 
 def interface_kernel(
-    first_ref, inject_ref, src_ref, g0_ref, g1_ref, out_ref, high_ref, low_ref, acc_ref
+    place_ref, inject_ref, src_ref, g0_ref, g1_ref, out_ref, high_ref, low_ref, acc_ref
 ):
     step = pl.program_id(0)
     slab = step // 2
@@ -57,7 +58,7 @@
             pieces = []
             for sweep in range(2):
                 pieces.append((cols == rows * 8 + sweep).astype(F32))
-                chosen = targets[sweep] == (first_ref[0] + local).astype(F32)
+                chosen = targets[sweep] == (place_ref[0] + local).astype(F32)
                 for part in range(2):
                     pieces.append(jnp.where(chosen, src_ref[sweep, part], 0.0))
             high, low = split(jnp.concatenate(pieces, axis=0))
@@ -101,25 +102,72 @@
                 ]
 
 
+def packed_columns(place_ref, inject_ref, sweep):
+    modes = inject_ref.shape[1]
+    target = inject_ref[sweep : sweep + 1, :]
+    own = (target == place_ref[0]) | (target == place_ref[0] + 1)
+    own = jnp.broadcast_to(own.astype(F32), (PACK, modes))
+    earlier = lax.broadcasted_iota(jnp.int32, (modes, modes), 0)
+    later = lax.broadcasted_iota(jnp.int32, (modes, modes), 1)
+    rank = mm(own.astype(BF16), (earlier < later).astype(F32).astype(BF16))
+    wanted = lax.broadcasted_iota(jnp.int32, (PACK, modes), 0) + PACK * place_ref[1]
+    return jnp.where(rank == wanted.astype(F32), own, 0.0)
+
+
+def unpacked_rows(place_ref, inject_ref, base_ref, sweep, part):
+    back = packed_columns(place_ref, inject_ref, sweep).T.astype(BF16)
+    start = (2 * sweep + part) * PACK
+    high, low = split(base_ref[start : start + PACK, :])
+    return mm(back, high) + mm(back, low)
+
+
+def select_kernel(place_ref, inject_ref, src_ref, high_ref, low_ref):
+    width = src_ref.shape[3]
+    rows = lax.broadcasted_iota(jnp.int32, (width // 8, width), 0)
+    cols = lax.broadcasted_iota(jnp.int32, (width // 8, width), 1)
+    lead = width // 8
+    for slab in range(2):
+        for sweep in range(2):
+            span = slice(sweep * lead, (sweep + 1) * lead)
+            unit = (cols == rows * 8 + sweep).astype(F32)
+            high_ref[slab, span, :] = unit.astype(BF16)
+            low_ref[slab, span, :] = jnp.zeros_like(unit).astype(BF16)
+            here = inject_ref[sweep : sweep + 1, :] == place_ref[0] + slab
+            pick = jnp.where(here, packed_columns(place_ref, inject_ref, sweep), 0.0).astype(BF16)
+            for part in range(2):
+                start = 2 * lead + (2 * sweep + part) * PACK
+                high, low = split(src_ref[sweep, part])
+                high_ref[slab, start : start + PACK, :] = mm(pick, high).astype(BF16)
+                low_ref[slab, start : start + PACK, :] = mm(pick, low).astype(BF16)
+
+
 def spread_kernel(high_ref, low_ref, g_ref, out_ref, flow_ref):
-    half = high_ref.shape[1] // 2
     lead = g_ref.shape[3] // 8
-    modes = (half - lead) // 2
     total = [0.0] * 4
     for slab in range(2):
         parts = (high_ref[slab], low_ref[slab])
         real = mm3(parts, split(g_ref[slab, 0]), True)
         imag = mm3(parts, split(g_ref[slab, 1]), True)
         for sweep in range(2):
-            base = sweep * half
+            base = sweep * lead
             place = slab * 4 * lead + sweep * 2 * lead
             out_ref[0, place : place + lead, :] = real[base : base + lead]
             out_ref[0, place + lead : place + 2 * lead, :] = imag[base : base + lead]
-            one, two, three = base + lead, base + lead + modes, base + half
+            one = 2 * lead + 2 * sweep * PACK
+            two, three = one + PACK, one + 2 * PACK
             total[2 * sweep] += real[one:two] - imag[two:three]
             total[2 * sweep + 1] += real[two:three] + imag[one:two]
     for item in range(4):
-        flow_ref[0, item * modes : (item + 1) * modes, :] = total[item]
+        flow_ref[0, item * PACK : (item + 1) * PACK, :] = total[item]
+
+
+def expand_kernel(place_ref, inject_ref, base_ref, extra_ref, out_ref):
+    modes = inject_ref.shape[1]
+    for sweep in range(2):
+        for part in range(2):
+            span = slice((2 * sweep + part) * modes, (2 * sweep + part + 1) * modes)
+            rows = unpacked_rows(place_ref, inject_ref, base_ref, sweep, part)
+            out_ref[span, :] = extra_ref[span, :] + rows
 
 
 def coupling_kernel(team_ref, c_ref, x_ref):
@@ -256,7 +304,7 @@
 
 
 def state_kernel(
-    first_ref, inject_ref, inner_ref, high_ref, low_ref, base_ref, left_ref, right_ref
+    place_ref, inject_ref, inner_ref, high_ref, low_ref, base_ref, extra_ref, left_ref, right_ref
 ):
     modes = inject_ref.shape[1]
     width = base_ref.shape[1]
@@ -264,6 +312,11 @@
         target = jnp.broadcast_to(
             inject_ref[sweep : sweep + 1, :].astype(F32), (width, modes)
         ).T
+        bases = []
+        for part in range(2):
+            start = (2 * sweep + part) * modes
+            rows = unpacked_rows(place_ref, inject_ref, base_ref, sweep, part)
+            bases.append(rows + extra_ref[start : start + modes, :])
         for slab in range(2):
             item = slab if sweep == 0 else 1 - slab
             pieces = []
@@ -275,10 +328,9 @@
             by = []
             for part in range(2):
                 by.append(mm3(parts, (high_ref[slab, sweep, part], low_ref[slab, sweep, part])))
-            chosen = target == (first_ref[0] + slab).astype(F32)
+            chosen = target == (place_ref[0] + slab).astype(F32)
             for part in range(2):
-                start = (2 * sweep + part) * modes
-                base = jnp.where(chosen, base_ref[start : start + modes, :], 0.0)
+                base = jnp.where(chosen, bases[part], 0.0)
                 if part == 0:
                     out_ref[slab, part] = base + (by[0][:modes] - by[1][modes:])
                 else:
@@ -314,7 +366,8 @@
     col_index = lax.axis_index("col")
     team = col_index // 4
     member = col_index % 4
-    first = jnp.reshape(slab_index * 2, (1,)).astype(jnp.int32)
+    first = slab_index * 2
+    place = jnp.stack([first, jnp.zeros_like(first)]).astype(jnp.int32)
     position = jnp.where(team == 0, slab_index, slabs - 1 - slab_index)
     info = jnp.stack([team, position // 4, position % 4, slab_index % 4]).astype(jnp.int32)
     stack = 2 * (lead + 2 * modes)
@@ -322,7 +375,7 @@
     sources = jnp.transpose(sources, (0, 1, 3, 2))
     leads = jnp.transpose(leads, (0, 1, 3, 2))
 
-    sent, high, low = pl.pallas_call(
+    sent = pl.pallas_call(
         interface_kernel,
         grid=(4,),
         in_specs=[
@@ -332,41 +385,53 @@
             pl.BlockSpec((1, 1, orbitals, width // 2), lambda step: (step // 2, step % 2, 0, 0)),
             pl.BlockSpec((1, 1, orbitals, width // 2), lambda step: (step // 2, step % 2, 0, 1)),
         ],
-        out_specs=[
-            whole((8, block_rows, size)),
-            whole((2, stack, width)),
-            whole((2, stack, width)),
+        out_specs=whole((8, block_rows, size)),
+        out_shape=jax.ShapeDtypeStruct((8, block_rows, size), F32),
+        scratch_shapes=[
+            pltpu.VMEM((2, stack, width), BF16),
+            pltpu.VMEM((2, stack, width), BF16),
+            pltpu.VMEM((2, 2 * modes, size), F32),
         ],
-        out_shape=[
-            jax.ShapeDtypeStruct((8, block_rows, size), F32),
-            jax.ShapeDtypeStruct((2, stack, width), BF16),
-            jax.ShapeDtypeStruct((2, stack, width), BF16),
-        ],
-        scratch_shapes=[pltpu.VMEM((2, 2 * modes, size), F32)],
         compiler_params=params(),
         name="interface_terms",
-    )(first, inject, sources, diag_inverse, diag_inverse)
+    )(place, inject, sources, diag_inverse, diag_inverse)
+    sent, inject_after = lax.optimization_barrier((sent, inject))
     received = exchange(sent)
 
-    spread, flows = pl.pallas_call(
-        spread_kernel,
-        grid=(8,),
-        in_specs=[
-            whole((2, stack, width)),
-            whole((2, stack, width)),
-            pl.BlockSpec((2, 2, part_rows, width), lambda step: (0, 0, step, 0)),
-        ],
-        out_specs=[
-            pl.BlockSpec((1, 8 * lead, part_rows), lambda step: (step, 0, 0)),
-            pl.BlockSpec((1, 4 * modes, part_rows), lambda step: (step, 0, 0)),
-        ],
-        out_shape=[
-            jax.ShapeDtypeStruct((8, 8 * lead, part_rows), F32),
-            jax.ShapeDtypeStruct((8, 4 * modes, part_rows), F32),
-        ],
-        compiler_params=params(),
-        name="spread_terms",
-    )(high, low, diag_inverse)
+    def chunk_terms(place):
+        terms = jax.ShapeDtypeStruct((2, 2 * lead + 4 * PACK, width), BF16)
+        high, low = pl.pallas_call(
+            select_kernel,
+            in_specs=[SMEM, VMEM, VMEM],
+            out_specs=[VMEM, VMEM],
+            out_shape=[terms, terms],
+            compiler_params=params(),
+            name="select_terms",
+        )(place, inject_after, sources)
+        return pl.pallas_call(
+            spread_kernel,
+            grid=(8,),
+            in_specs=[
+                whole(terms.shape),
+                whole(terms.shape),
+                pl.BlockSpec((2, 2, part_rows, width), lambda step: (0, 0, step, 0)),
+            ],
+            out_specs=[
+                pl.BlockSpec((1, 8 * lead, part_rows), lambda step: (step, 0, 0)),
+                pl.BlockSpec((1, 4 * PACK, part_rows), lambda step: (step, 0, 0)),
+            ],
+            out_shape=[
+                jax.ShapeDtypeStruct((8, 8 * lead, part_rows), F32),
+                jax.ShapeDtypeStruct((8, 4 * PACK, part_rows), F32),
+            ],
+            compiler_params=params(),
+            name="spread_terms",
+        )(high, low, diag_inverse)
+
+    def summed(flows):
+        return lax.psum_scatter(flows, "col", scatter_dimension=0, tiled=False)
+
+    spread, flows = chunk_terms(place)
     turned = pl.pallas_call(
         coupling_kernel,
         in_specs=[SMEM, VMEM],
@@ -377,7 +442,7 @@
     )(info, couplings)
     own_inject = lax.dynamic_slice(inject, (team, member * 16), (1, 16))[0]
     own_inject = jnp.concatenate([own_inject, own_inject])
-    marks = jnp.stack([own_inject == first[0] + team, own_inject == first[0] + 1 - team])
+    marks = jnp.stack([own_inject == first + team, own_inject == first + 1 - team])
     marks = jnp.broadcast_to(marks.astype(F32)[:, :, None], (2, 32, size))
     own_lead = lax.dynamic_slice(leads, (team, 0, member * 16, 0), (1, 2, 16, size))
     own_lead = own_lead.reshape(32, size)
@@ -398,7 +463,7 @@
     )(info, received, turned, marks)
     packed, spread = lax.optimization_barrier((packed, spread))
     rows = exchange(spread)
-    base = lax.psum_scatter(flows, "col", scatter_dimension=0, tiled=False)
+    base = summed(flows)
 
     def turn(value, step):
         return lax.ppermute(
@@ -407,6 +472,9 @@
 
     top, bottom = packed[: size + 16], packed[size + 16 :]
     before_top, after_bottom = turn(top, 1), turn(bottom, -1)
+    before_top, after_bottom, top, bottom = lax.optimization_barrier(
+        (before_top, after_bottom, top, bottom)
+    )
     before_bottom, after_top = turn(bottom, 1), turn(top, -1)
     across_top, across_bottom = turn(before_top, 1), turn(after_bottom, -1)
     pieces = (after_top, after_bottom, across_top, across_bottom, before_top, before_bottom)
@@ -450,7 +518,25 @@
         compiler_params=params(),
         name="inflow",
     )(info, own_lead, flow, *maps, received, turned, flow_a)
-    rows, inner = lax.optimization_barrier((rows, inner))
+    rows, inner, base = lax.optimization_barrier((rows, inner, base))
+
+    owners = jnp.arange(slabs, dtype=jnp.int32)[:, None, None]
+    counts = jnp.sum((inject_after[None] >> 1 == owners).astype(jnp.int32), axis=2)
+    chunks = (jnp.max(counts) + PACK - 1) // PACK
+
+    def more(chunk, extra):
+        place = jnp.stack([first, chunk]).astype(jnp.int32)
+        _, flows = chunk_terms(place)
+        return pl.pallas_call(
+            expand_kernel,
+            in_specs=[SMEM, VMEM, VMEM, VMEM],
+            out_specs=VMEM,
+            out_shape=jax.ShapeDtypeStruct((4 * modes, part_rows), F32),
+            compiler_params=params(),
+            name="expand_terms",
+        )(place, inject, summed(flows), extra)
+
+    extra = lax.fori_loop(1, chunks, more, jnp.zeros((4 * modes, part_rows), F32))
     inner = exchange(inner)
     row_high, row_low = pl.pallas_call(
         arrange_kernel,
@@ -467,12 +553,12 @@
     shape = (2, 2, modes, part_rows)
     left, right = pl.pallas_call(
         state_kernel,
-        in_specs=[SMEM, VMEM, VMEM, VMEM, VMEM, VMEM],
+        in_specs=[SMEM] + [VMEM] * 6,
         out_specs=[VMEM, VMEM],
         out_shape=[jax.ShapeDtypeStruct(shape, F32), jax.ShapeDtypeStruct(shape, F32)],
         compiler_params=params(),
         name="states",
-    )(first, inject, inner, row_high, row_low, base)
+    )(place, inject, inner, row_high, row_low, base, extra)
     return jnp.transpose(left, (0, 1, 3, 2)), jnp.transpose(right, (0, 1, 3, 2))
 
 

time: 160 us -> 151 us (0.944)
  waiting for transfers between devices: 83.5 us -> 72.2 us
    all_to_all x3, waiting for transfers between devices: 50.2 us -> 38.7 us  [exchange(): return lax.all_to_all(value, 'col', split_axis=0, concat_axis=0, tiled=True)]
    ppermute x6, waiting for transfers between devices: 16.3 us -> 19.2 us  [turn(): lax.ppermute(value, 'slab', [(slab, slab // 4 * 4 + (slab + step) % 4) fo...]
    reduce_scatter x1, waiting for transfers between devices: 2.77 us -> 0.01 us  [summed(): return lax.psum_scatter(flows, 'col', scatter_dimension=0, tiled=False)]
    pallas_call x2 -> x3, Pallas kernels: 10.1 us -> 11.1 us  [the longest x1 7.58 us: chunk_terms(): pl.pallas_call(spread_kernel, grid=(8,), in_specs=[whole(terms.shape), wh...]
    unnamed x16 -> x20, local copies, waits for them, and re-layouts: 6.5 us -> 5.58 us
  transfers between devices with their start and end apart: 13 -> 13, of which waited for: 12 -> 12; matrix products, arithmetic and copies ran while one was open for 0% -> 1% of each run, Pallas kernels for 12% -> 13%
where the time goes in v4:
time: 151 us
  waiting for transfers between devices  72.2 us (48%)
  Pallas kernels  30.8 us (20%)
  starting transfers between devices  25.8 us (17%)
  between operations  14.9 us (10%)
  local copies, waits for them, and re-layouts  5.81 us (4%)
    all_to_all x3, waiting for transfers between devices, exchange(): return lax.all_to_all(value, 'col', split_axis=0, concat_axis=0, tiled=True)  38.7 us
    ppermute x6, waiting for transfers between devices, turn(): lax.ppermute(value, 'slab', [(slab, slab // 4 * 4 + (slab + step) % 4) fo...  19.2 us
    all_to_all x3, starting transfers between devices, exchange(): return lax.all_to_all(value, 'col', split_axis=0, concat_axis=0, tiled=True)  16.5 us
    ppermute x3, waiting for transfers between devices, on_device(): flow = lax.ppermute(flow, ('slab', 'col'), pairs)  13.6 us
    pallas_call x1, Pallas kernels, chunk_terms(): pl.pallas_call(spread_kernel, grid=(8,), in_specs=[whole(terms.shape), wh...  7.58 us
    ppermute x6, starting transfers between devices, turn(): lax.ppermute(value, 'slab', [(slab, slab // 4 * 4 + (slab + step) % 4) fo...  7.09 us
    pallas_call x1, Pallas kernels, on_device(): pl.pallas_call(interface_kernel, grid=(4,), in_specs=[SMEM, whole(inject....  6.7 us
    unnamed x20, local copies, waits for them, and re-layouts  5.58 us
  transfers between devices with their start and end apart: 13, of which 12 were waited for; matrix products, arithmetic and copies ran while one was open for 1% of the time, Pallas kernels for 13%

profile of v4, /device:TPU:8, one launch (start us, length us, event | category | flops | bytes accessed | tf_op | source)
XLA Modules:
  0.0 150.6 jit_solution(11552214677499560040)
XLA Ops:
  7.3 6.7 %interface_terms.1 = f32[8,160,256]{2,1,0:T(8,128)} custom-call(s32[2]{0:T(128)S(1)} %pad_add_fusion.1.place_ref, s32[2,64]{1,0:T(2,128)} %inject_ref.4, f32[2,2,64,256]{3,2,1,0:T(8,128)} %bitcast.27, f32[2,2,2048,256]{3,2,1,0:T(8,128)} %g_ref.1, f32[2,2,2048,256]{3,2,1,0:T(8,128)} %g_ref.1), custom_call_target="tpu_custom_call" | custom-call | tf_op jit(solution)/shard_map/interface_terms/pallas_call | solution.py:378
  14.0 8.6 %all-to-all-start = ((f32[8,160,256]{2,1,0:T(8,128)}), f32[8,160,256]{2,1,0:T(8,128)S(1)}, u32[]{:S(2)}, u32[]{:S(2)}) async-start(f32[8,160,256]{2,1,0:T(8,128)} %interface_terms.1), calls=%async_computation.1 | async-start | bytes 2621440 | tf_op jit(solution)/shard_map/all_to_all | solution.py:354
  26.1 7.6 %spread_terms.2 = (f32[8,256,256]{2,1,0:T(8,128)S(1)}, f32[8,64,256]{2,1,0:T(8,128)S(1)}) custom-call(bf16[2,128,256]{2,1,0:T(8,128)(2,1)S(1)} %get-tuple-element.81.high_ref, bf16[2,128,256]{2,1,0:T(8,128)(2,1)S(1)} %get-tuple-element.82.low_ref, f32[2,2,2048,256]{3,2,1,0:T(8,128)} %g_ref.1), custom_call_target="tpu_custom_call" | custom-call | tf_op jit(solution)/shard_map/spread_terms/pallas_call | solution.py:411
  35.9 21.1 %all-to-all-done.recv_ref = f32[8,160,256]{2,1,0:T(8,128)S(1)} async-done(((f32[8,160,256]{2,1,0:T(8,128)}), f32[8,160,256]{2,1,0:T(8,128)S(1)}, u32[]{:S(2)}, u32[]{:S(2)}) %all-to-all-start) | async-done | bytes 1310752 | tf_op jit(solution)/shard_map/all_to_all | solution.py:354
  57.1 2.8 %pair_map.1 = (f32[544,256]{1,0:T(8,128)S(1)}, f32[32,256]{1,0:T(8,128)S(1)}) custom-call(s32[4]{0:T(128)S(1)} %pad_add_fusion.2.team_ref.info_ref, f32[8,160,256]{2,1,0:T(8,128)S(1)} %all-to-all-done.recv_ref, f32[2,512,256]{2,1,0:T(8,128)S(1)} %coupling_rows.1.x_ref, f32[2,32,256]{2,1,0:T(8,128)S(1)} %broadcast_in_dim.4.mask_ref), custom_call_target="tpu_custom_call" | custom-call | tf_op jit(solution)/shard_map/pair_map/pallas_call | solution.py:453
  59.9 4.4 %all-to-all-start.1 = ((f32[8,256,256]{2,1,0:T(8,128)}), f32[8,256,256]{2,1,0:T(8,128)}, u32[]{:S(2)}, u32[]{:S(2)}) async-start(f32[8,256,256]{2,1,0:T(8,128)} %copy-done.1), calls=%async_computation.2 | async-start | bytes 4194304 | tf_op jit(solution)/shard_map/all_to_all | solution.py:354
  65.5 1.6 %collective-permute-start = (f32[272,256]{1,0:T(8,128)S(1)}, f32[272,256]{1,0:T(8,128)S(1)}, u32[]{:S(2)}, u32[]{:S(2)}) collective-permute-start(f32[272,256]{1,0:T(8,128)S(1)} %get-tuple-element.93), channel_id=1, source_target_pairs={{0,16},{16,32},{32,48},{48,0},{64,80},{80,96},{96,112},{112,64},{1... | collective-permute-start | bytes 835592 | tf_op jit(solution)/shard_map/ppermute | solution.py:469
  67.1 6.6 %collective-permute-done.1.refs_1_ = f32[272,256]{1,0:T(8,128)S(1)} collective-permute-done((f32[272,256]{1,0:T(8,128)S(1)}, f32[272,256]{1,0:T(8,128)S(1)}, u32[]{:S(2)}, u32[]{:S(2)}) %collective-permute-start.1) | collective-permute-done | bytes 278560 | tf_op jit(solution)/shard_map/ppermute | solution.py:469
  75.1 3.0 %collective-permute-start.2 = (f32[272,256]{1,0:T(8,128)S(1)}, f32[272,256]{1,0:T(8,128)S(1)}, u32[]{:S(2)}, u32[]{:S(2)}) collective-permute-start(f32[272,256]{1,0:T(8,128)S(1)} %get-tuple-element.93), channel_id=1, source_target_pairs={{0,48},{16,0},{32,16},{48,32},{64,112},{80,64},{96,80},{112,96},{1... | collective-permute-start | bytes 835592 | tf_op jit(solution)/shard_map/ppermute | solution.py:469
  78.1 2.0 %collective-permute-start.4 = (f32[272,256]{1,0:T(8,128)S(1)}, f32[272,256]{1,0:T(8,128)S(1)}, u32[]{:S(2)}, u32[]{:S(2)}) collective-permute-start(f32[272,256]{1,0:T(8,128)S(1)} %collective-permute-done.1.refs_1_), channel_id=1, source_target_pairs={{0,48},{16,0},{32,16},{48,32},{64,112},{80,64},{96,80},{112,96},{1... | collective-permute-start | bytes 835592 | tf_op jit(solution)/shard_map/ppermute | solution.py:469
  80.1 5.1 %collective-permute-done.2.refs_0_ = f32[272,256]{1,0:T(8,128)S(1)} collective-permute-done((f32[272,256]{1,0:T(8,128)S(1)}, f32[272,256]{1,0:T(8,128)S(1)}, u32[]{:S(2)}, u32[]{:S(2)}) %collective-permute-start.2) | collective-permute-done | bytes 278560 | tf_op jit(solution)/shard_map/ppermute | solution.py:469
  85.2 2.5 %collective-permute-done.5.refs_5_ = f32[272,256]{1,0:T(8,128)S(1)} collective-permute-done((f32[272,256]{1,0:T(8,128)S(1)}, f32[272,256]{1,0:T(8,128)S(1)}, u32[]{:S(2)}, u32[]{:S(2)}) %collective-permute-start.5) | collective-permute-done | bytes 278560 | tf_op jit(solution)/shard_map/ppermute | solution.py:469
  89.1 2.2 %collective-permute-done.3.refs_2_ = f32[272,256]{1,0:T(8,128)S(1)} collective-permute-done((f32[272,256]{1,0:T(8,128)S(1)}, f32[272,256]{1,0:T(8,128)S(1)}, u32[]{:S(2)}, u32[]{:S(2)}) %collective-permute-start.3) | collective-permute-done | bytes 278560 | tf_op jit(solution)/shard_map/ppermute | solution.py:469
  91.3 1.8 %gather_maps.1 = (bf16[4,512,256]{2,1,0:T(8,128)(2,1)S(1)}, bf16[4,512,256]{2,1,0:T(8,128)(2,1)S(1)}, f32[4,32,256]{2,1,0:T(8,128)S(1)}, f32[32,256]{1,0:T(8,128)S(1)}) custom-call(s32[4]{0:T(128)S(1)} %pad_add_fusion.2.team_ref.info_ref, f32[32,256]{1,0:T(8,128)S(1)} %bitcast.22, f32[544,256]{1,0:T(8,128)S(1)} %get-tuple-element.92.own_ref, ...), custom_call_target="tpu_custom_call" | custom-call | tf_op jit(solution)/shard_map/gather_maps/pallas_call | solution.py:487
  93.0 1.6 %collective-permute-start.6 = (f32[32,256]{1,0:T(8,128)S(1)}, f32[32,256]{1,0:T(8,128)S(1)}, u32[]{:S(2)}, u32[]{:S(2)}) collective-permute-start(f32[32,256]{1,0:T(8,128)S(1)} %get-tuple-element.97), channel_id=1, source_target_pairs={{0,64},{2,66},{4,68},{6,70},{8,200},{10,202},{12,204},{14,206},{16... | collective-permute-start | bytes 98312 | tf_op jit(solution)/shard_map/ppermute | solution.py:502
  94.6 3.6 %collective-permute-done.6.state_ref = f32[32,256]{1,0:T(8,128)S(1)} collective-permute-done((f32[32,256]{1,0:T(8,128)S(1)}, f32[32,256]{1,0:T(8,128)S(1)}, u32[]{:S(2)}, u32[]{:S(2)}) %collective-permute-start.6) | collective-permute-done | bytes 32800 | tf_op jit(solution)/shard_map/ppermute | solution.py:502
  100.1 4.9 %collective-permute-done.7.state_ref = f32[32,256]{1,0:T(8,128)S(1)} collective-permute-done((f32[32,256]{1,0:T(8,128)S(1)}, f32[32,256]{1,0:T(8,128)S(1)}, u32[]{:S(2)}, u32[]{:S(2)}) %collective-permute-start.7) | collective-permute-done | bytes 32800 | tf_op jit(solution)/shard_map/ppermute | solution.py:512
  106.7 5.1 %collective-permute-done.8.state_ref = f32[32,256]{1,0:T(8,128)S(1)} collective-permute-done((f32[32,256]{1,0:T(8,128)S(1)}, f32[32,256]{1,0:T(8,128)S(1)}, u32[]{:S(2)}, u32[]{:S(2)}) %collective-permute-start.8) | collective-permute-done | bytes 32800 | tf_op jit(solution)/shard_map/ppermute | solution.py:512
  111.8 2.8 %inflow.1 = f32[8,64,256]{2,1,0:T(8,128)} custom-call(s32[4]{0:T(128)S(1)} %pad_add_fusion.2.team_ref.info_ref, f32[32,256]{1,0:T(8,128)S(1)} %bitcast.25, f32[32,256]{1,0:T(8,128)S(1)} %collective-permute-done.8.state_ref, bf16[4,512,256]{2,1,0:T(8,128)(2,1)S(1)} %get-tuple-element.98.high_ref, bf16[4,512,256]{2,1,0:T(8,128)(2,1)S(1)} %get-tuple-element.99.low_ref, ...), custom_call_target="tpu_custom_call" | custom-call | tf_op jit(solution)/shard_map/inflow/pallas_call | solution.py:513
  114.6 6.2 %all-to-all-done.1.recv_ref = f32[8,256,256]{2,1,0:T(8,128)} async-done(((f32[8,256,256]{2,1,0:T(8,128)}), f32[8,256,256]{2,1,0:T(8,128)}, u32[]{:S(2)}, u32[]{:S(2)}) %all-to-all-start.1) | async-done | bytes 2097184 | tf_op jit(solution)/shard_map/all_to_all | solution.py:354
  120.8 3.5 %all-to-all-start.2 = ((f32[8,64,256]{2,1,0:T(8,128)}), f32[8,64,256]{2,1,0:T(8,128)S(1)}, u32[]{:S(2)}, u32[]{:S(2)}) async-start(f32[8,64,256]{2,1,0:T(8,128)} %inflow.1), calls=%async_computation.4 | async-start | bytes 1048576 | tf_op jit(solution)/shard_map/all_to_all | solution.py:354
  125.7 1.9 %arrange_rows.1 = (bf16[2,2,2,256,256]{4,3,2,1,0:T(8,128)(2,1)S(1)}, bf16[2,2,2,256,256]{4,3,2,1,0:T(8,128)(2,1)S(1)}) custom-call(f32[8,256,256]{2,1,0:T(8,128)} %all-to-all-done.1.recv_ref), custom_call_target="tpu_custom_call" | custom-call | tf_op jit(solution)/shard_map/arrange_rows/pallas_call | solution.py:541
  128.7 11.5 %all-to-all-done.2.inner_ref = f32[8,64,256]{2,1,0:T(8,128)S(1)} async-done(((f32[8,64,256]{2,1,0:T(8,128)}), f32[8,64,256]{2,1,0:T(8,128)S(1)}, u32[]{:S(2)}, u32[]{:S(2)}) %all-to-all-start.2) | async-done | bytes 524320 | tf_op jit(solution)/shard_map/all_to_all | solution.py:354
  141.4 2.3 %states.1 = (f32[2,2,64,256]{3,2,1,0:T(8,128)}, f32[2,2,64,256]{3,2,1,0:T(8,128)}) custom-call(s32[2]{0:T(128)S(1)} %pad_add_fusion.1.place_ref, s32[2,64]{1,0:T(2,128)S(1)} %get-tuple-element.242, f32[8,64,256]{2,1,0:T(8,128)S(1)} %all-to-all-done.2.inner_ref, bf16[2,2,2,256,256]{4,3,2,1,0:T(8,128)(2,1)S(1)} %get-tuple-element.105.high_ref, ...), custom_call_target="tpu_custom_call" | custom-call | tf_op jit(solution)/shard_map/states/pallas_call | solution.py:554
  (47 shorter events, 16.6 us)
Async XLA Ops:
  7.2 28.7 %copy-start = (f32[2,2,256,64]{2,3,1,0:T(8,128)S(1)}, f32[2,2,256,64]{2,3,1,0:T(8,128)}, u32[]{:S(2)}) copy-start(f32[2,2,256,64]{2,3,1,0:T(8,128)} %param.11) | copy-start | bytes 786436
  14.0 8.6 %copy-start.8 = (f32[2,2,256,64]{2,3,1,0:T(8,128)S(1)}, f32[2,2,256,64]{2,3,1,0:T(8,128)}, u32[]{:S(2)}) copy-start(f32[2,2,256,64]{2,3,1,0:T(8,128)} %param.9) | copy-start | bytes 786436
  14.0 8.6 %copy-start.10 = (s32[2,64]{1,0:T(2,128)S(1)}, s32[2,64]{1,0:T(2,128)}, u32[]{:S(2)}) copy-start(s32[2,64]{1,0:T(2,128)} %inject_ref.4) | copy-start | bytes 1540
  14.0 43.0 %all-to-all-start = ((f32[8,160,256]{2,1,0:T(8,128)}), f32[8,160,256]{2,1,0:T(8,128)S(1)}, u32[]{:S(2)}, u32[]{:S(2)}) async-start(f32[8,160,256]{2,1,0:T(8,128)} %interface_terms.1), calls=%async_computation.1 | async-start | bytes 2621440 | tf_op jit(solution)/shard_map/all_to_all | solution.py:354
  24.0 1.2 copy-start.3
  33.7 1.3 copy-start.1
  35.0 0.8 copy-start.6
  59.9 60.9 %all-to-all-start.1 = ((f32[8,256,256]{2,1,0:T(8,128)}), f32[8,256,256]{2,1,0:T(8,128)}, u32[]{:S(2)}, u32[]{:S(2)}) async-start(f32[8,256,256]{2,1,0:T(8,128)} %copy-done.1), calls=%async_computation.2 | async-start | bytes 4194304 | tf_op jit(solution)/shard_map/all_to_all | solution.py:354
  64.2 50.4 %reduce-scatter.3.cloned.1.call-start = ((), (), s32[]{:S(2)}) async-start(), calls=%async_computation.5 | async-start | bytes 589824 | tf_op jit(solution)/shard_map/reduce_scatter | solution.py:432
  65.0 8.7 %collective-permute-start.1 = (f32[272,256]{1,0:T(8,128)S(1)}, f32[272,256]{1,0:T(8,128)S(1)}, u32[]{:S(2)}, u32[]{:S(2)}) collective-permute-start(f32[272,256]{1,0:T(8,128)S(1)} %get-tuple-element.96), channel_id=1, source_target_pairs={{0,48},{16,0},{32,16},{48,32},{64,112},{80,64},{96,80},{112,96},{1... | collective-permute-start | bytes 835592 | tf_op jit(solution)/shard_map/ppermute | solution.py:469
  65.5 9.6 %collective-permute-start = (f32[272,256]{1,0:T(8,128)S(1)}, f32[272,256]{1,0:T(8,128)S(1)}, u32[]{:S(2)}, u32[]{:S(2)}) collective-permute-start(f32[272,256]{1,0:T(8,128)S(1)} %get-tuple-element.93), channel_id=1, source_target_pairs={{0,16},{16,32},{32,48},{48,0},{64,80},{80,96},{96,112},{112,64},{1... | collective-permute-start | bytes 835592 | tf_op jit(solution)/shard_map/ppermute | solution.py:469
  75.1 10.1 %collective-permute-start.2 = (f32[272,256]{1,0:T(8,128)S(1)}, f32[272,256]{1,0:T(8,128)S(1)}, u32[]{:S(2)}, u32[]{:S(2)}) collective-permute-start(f32[272,256]{1,0:T(8,128)S(1)} %get-tuple-element.93), channel_id=1, source_target_pairs={{0,48},{16,0},{32,16},{48,32},{64,112},{80,64},{96,80},{112,96},{1... | collective-permute-start | bytes 835592 | tf_op jit(solution)/shard_map/ppermute | solution.py:469
  78.1 9.6 %collective-permute-start.5 = (f32[272,256]{1,0:T(8,128)S(1)}, f32[272,256]{1,0:T(8,128)S(1)}, u32[]{:S(2)}, u32[]{:S(2)}) collective-permute-start(f32[272,256]{1,0:T(8,128)S(1)} %get-tuple-element.96), channel_id=1, source_target_pairs={{0,16},{16,32},{32,48},{48,0},{64,80},{80,96},{96,112},{112,64},{1... | collective-permute-start | bytes 835592 | tf_op jit(solution)/shard_map/ppermute | solution.py:469
  78.1 11.0 %collective-permute-start.4 = (f32[272,256]{1,0:T(8,128)S(1)}, f32[272,256]{1,0:T(8,128)S(1)}, u32[]{:S(2)}, u32[]{:S(2)}) collective-permute-start(f32[272,256]{1,0:T(8,128)S(1)} %collective-permute-done.1.refs_1_), channel_id=1, source_target_pairs={{0,48},{16,0},{32,16},{48,32},{64,112},{80,64},{96,80},{112,96},{1... | collective-permute-start | bytes 835592 | tf_op jit(solution)/shard_map/ppermute | solution.py:469
  80.1 11.2 %collective-permute-start.3 = (f32[272,256]{1,0:T(8,128)S(1)}, f32[272,256]{1,0:T(8,128)S(1)}, u32[]{:S(2)}, u32[]{:S(2)}) collective-permute-start(f32[272,256]{1,0:T(8,128)S(1)} %collective-permute-done.refs_4_), channel_id=1, source_target_pairs={{0,16},{16,32},{32,48},{48,0},{64,80},{80,96},{96,112},{112,64},{1... | collective-permute-start | bytes 835592 | tf_op jit(solution)/shard_map/ppermute | solution.py:469
  93.0 5.2 %collective-permute-start.6 = (f32[32,256]{1,0:T(8,128)S(1)}, f32[32,256]{1,0:T(8,128)S(1)}, u32[]{:S(2)}, u32[]{:S(2)}) collective-permute-start(f32[32,256]{1,0:T(8,128)S(1)} %get-tuple-element.97), channel_id=1, source_target_pairs={{0,64},{2,66},{4,68},{6,70},{8,200},{10,202},{12,204},{14,206},{16... | collective-permute-start | bytes 98312 | tf_op jit(solution)/shard_map/ppermute | solution.py:502
  99.7 5.2 %collective-permute-start.7 = (f32[32,256]{1,0:T(8,128)S(1)}, f32[32,256]{1,0:T(8,128)S(1)}, u32[]{:S(2)}, u32[]{:S(2)}) collective-permute-start(f32[32,256]{1,0:T(8,128)S(1)} %row_step.2), channel_id=1, source_target_pairs={{0,64},{2,66},{4,68},{6,70},{8,200},{10,202},{12,204},{14,206},{16... | collective-permute-start | bytes 98312 | tf_op jit(solution)/shard_map/ppermute | solution.py:512
  106.4 5.4 %collective-permute-start.8 = (f32[32,256]{1,0:T(8,128)S(1)}, f32[32,256]{1,0:T(8,128)S(1)}, u32[]{:S(2)}, u32[]{:S(2)}) collective-permute-start(f32[32,256]{1,0:T(8,128)S(1)} %row_step.3), channel_id=1, source_target_pairs={{0,64},{2,66},{4,68},{6,70},{8,200},{10,202},{12,204},{14,206},{16... | collective-permute-start | bytes 98312 | tf_op jit(solution)/shard_map/ppermute | solution.py:512
  114.6 14.1 %copy-start.9 = (f32[2,2,256,64]{2,3,1,0:T(8,128)S(1)}, f32[2,2,256,64]{2,3,1,0:T(8,128)}, u32[]{:S(2)}) copy-start(f32[2,2,256,64]{2,3,1,0:T(8,128)} %param.9) | copy-start | bytes 786436
  120.8 19.4 %all-to-all-start.2 = ((f32[8,64,256]{2,1,0:T(8,128)}), f32[8,64,256]{2,1,0:T(8,128)S(1)}, u32[]{:S(2)}, u32[]{:S(2)}) async-start(f32[8,64,256]{2,1,0:T(8,128)} %inflow.1), calls=%async_computation.4 | async-start | bytes 1048576 | tf_op jit(solution)/shard_map/all_to_all | solution.py:354
  127.7 1.0 copy-start.4
  128.7 11.5 %copy-start.7 = (f32[1,64,256]{2,1,0:T(8,128)S(1)}, f32[1,64,256]{2,1,0:T(8,128)}, u32[]{:S(2)}) copy-start(f32[1,64,256]{2,1,0:T(8,128)} %reduce-scatter.3.cloned.1.call-done) | copy-start | bytes 196612
  140.2 1.2 copy-start.5
Sparse Core Ops, SparseCore 0:
  67.6 45.8 reduce-scatter.2

commit v5 on v4

--- a/solution.py
+++ b/solution.py
@@ -7,7 +7,8 @@
 
 F32 = jnp.float32
 BF16 = jnp.bfloat16
-LIMIT = 48 * 1024 * 1024
+LIMIT = 24 * 1024 * 1024
+LARGE = 56 * 1024 * 1024
 PACK = 16
 
 
@@ -27,14 +28,23 @@
     return wide[:rows] + (wide[rows:] + mm(left[0], right[1], transposed))
 
 
-def complex_rows(left, right):
-    half = left.shape[0] // 2
-    parts = split(left)
-    by_real = mm3(parts, split(right[0]))
-    by_imag = mm3(parts, split(right[1]))
+def combined(by_real, by_imag):
+    half = by_real.shape[0] // 2
     return jnp.concatenate(
         [by_real[:half] - by_imag[half:], by_imag[:half] + by_real[half:]], axis=0
     )
+
+
+def complex_rows(left, right):
+    parts = split(left)
+    return combined(mm3(parts, split(right[0])), mm3(parts, split(right[1])))
+
+
+def times(left, right):
+    size = right[0].shape[0] // 2
+    by_real = mm3(left, (right[0][:size], right[1][:size]))
+    by_imag = mm3(left, (right[0][size:], right[1][size:]))
+    return combined(by_real, by_imag)
 
 
 def interface_kernel(
@@ -182,7 +192,9 @@
     return jnp.concatenate([ref[block, start : start + count, :] for block in range(8)], axis=0)
 
 
-def pair_map_kernel(team_ref, recv_ref, x_ref, mask_ref, out_ref, qa_ref):
+def pair_map_kernel(
+    team_ref, recv_ref, x_ref, mask_ref, top_ref, bottom_ref, qa_ref, first_ref
+):
     left = team_ref[0] == 0
     size = x_ref.shape[2]
     lead = size // 8
@@ -201,51 +213,41 @@
     def pick(one, two):
         return (jnp.where(left, one[0], two[0]), jnp.where(left, one[1], two[1]))
 
-    def times(one, two):
-        both = complex_rows(jnp.concatenate(one, axis=0), two)
-        return both, (both[:size], both[size:])
-
-    first, _ = times(pick(coupled[0], blocks[0]), pick(blocks[0], coupled[1]))
-    _, second = times(pick(coupled[1], blocks[1]), pick(blocks[1], coupled[0]))
-    out_ref[: 2 * size, :] = complex_rows(first, second)
+    def product(one, two):
+        return complex_rows(jnp.concatenate(one, axis=0), two)
+
+    first = product(pick(coupled[0], blocks[0]), pick(blocks[0], coupled[1]))
+    second = product(pick(coupled[1], blocks[1]), pick(blocks[1], coupled[0]))
+    second = (second[:size], second[size:])
+    first_ref[...] = first
+    half = top_ref.shape[0]
+    both = complex_rows(first, second)
+    top_ref[...] = both[:half]
+    bottom_ref[: 2 * size - half, :] = both[half:]
     flow_a = jnp.where(left, flow_a, complex_rows(flow_a, coupled[1]))
     flow_b = jnp.where(left, flow_b, complex_rows(flow_b, coupled[0]))
-    out_ref[2 * size :, :] = complex_rows(flow_a, second) + flow_b
-
-
-def advance(state, maps, flow):
-    size = maps[0].shape[1]
-    half = state.shape[0] // 2
-    parts = split(state)
-    by_real = mm3(parts, tuple(ref[:size, :] for ref in maps))
-    by_imag = mm3(parts, tuple(ref[size:, :] for ref in maps))
-    moved = jnp.concatenate(
-        [by_real[:half] - by_imag[half:], by_imag[:half] + by_real[half:]], axis=0
-    )
-    return moved + flow
+    bottom_ref[2 * size - half :, :] = complex_rows(flow_a, second) + flow_b
+
+
+def after_kernel(value_ref, other_ref, out_ref):
+    pass
 
 
 def item_of(info_ref, item):
     return jnp.where(info_ref[0] == 0, item, 3 - item)
 
 
-def row_state(info_ref, state, high_ref, low_ref, flow_ref):
-    for item in range(4):
-        index = item_of(info_ref, item)
-        state = advance(state, (high_ref.at[index], low_ref.at[index]), flow_ref[index])
-    return state
-
-
-def gather_kernel(info_ref, lead_ref, own_ref, *refs):
-    pieces, (high_ref, low_ref, flow_ref, out_ref) = refs[:6], refs[6:]
-    size = own_ref.shape[1]
+def entry_state(info_ref, lead_ref, state_ref):
+    return jnp.where(info_ref[1] == 0, lead_ref[...], state_ref[...])
+
+
+def gather_kernel(info_ref, lead_ref, *refs):
+    pieces, (high_ref, low_ref, flow_ref, out_ref) = refs[:8], refs[8:]
+    size = pieces[0].shape[1]
     half = pieces[0].shape[0]
     for shift in range(4):
         place = lax.rem(info_ref[3] + shift, 4)
-        if shift == 0:
-            top, bottom = own_ref[:half, :], own_ref[half:, :]
-        else:
-            top, bottom = pieces[2 * shift - 2][...], pieces[2 * shift - 1][...]
+        top, bottom = pieces[2 * shift][...], pieces[2 * shift + 1][...]
         rest = 2 * size - half
         high, low = split(top)
         high_ref[place, :half, :] = high
@@ -254,46 +256,94 @@
         high_ref[place, half:, :] = high
         low_ref[place, half:, :] = low
         flow_ref[place] = bottom[rest:]
-    out_ref[...] = row_state(info_ref, lead_ref[...], high_ref, low_ref, flow_ref)
+    state = lead_ref[...]
+    for item in range(4):
+        index = item_of(info_ref, item)
+        state = times(split(state), (high_ref[index], low_ref[index])) + flow_ref[index]
+    out_ref[...] = state
+
+
+def row_map_kernel(
+    info_ref, high_ref, low_ref, flow_ref, row_high_ref, row_low_ref, row_flow_ref, half_ref
+):
+    maps, flows = [], []
+    for item in range(4):
+        index = item_of(info_ref, item)
+        maps.append((high_ref[index], low_ref[index]))
+        flows.append(flow_ref[index])
+    size = high_ref.shape[2]
+    early = times(maps[0], maps[1])
+    early_flow = times(split(flows[0]), maps[1]) + flows[1]
+    late = split(times(maps[2], maps[3]))
+    late_flow = times(split(flows[2]), maps[3]) + flows[3]
+    half_ref[: 2 * size, :] = early
+    half_ref[2 * size :, :] = early_flow
+    high, low = split(times(split(early), late))
+    row_high_ref[...] = high
+    row_low_ref[...] = low
+    row_flow_ref[...] = times(split(early_flow), late) + late_flow
 
 
 def row_kernel(info_ref, lead_ref, state_ref, high_ref, low_ref, flow_ref, out_ref):
-    state = jnp.where(info_ref[1] == 0, lead_ref[...], state_ref[...])
-    out_ref[...] = row_state(info_ref, state, high_ref, low_ref, flow_ref)
-
-
-def inflow_kernel(
-    info_ref,
-    lead_ref,
-    state_ref,
-    high_ref,
-    low_ref,
-    flow_ref,
-    recv_ref,
-    x_ref,
-    qa_ref,
-    out_ref,
+    state = entry_state(info_ref, lead_ref, state_ref)
+    out_ref[...] = times(split(state), (high_ref[...], low_ref[...])) + flow_ref[...]
+
+
+def prefix_kernel(
+    info_ref, high_ref, low_ref, flow_ref, half_ref, first_ref, x_ref, qa_ref, out_ref, inner_ref
 ):
+    size = high_ref.shape[2]
+    left = info_ref[0] == 0
+    one, three = item_of(info_ref, 0), item_of(info_ref, 2)
+    rows = lax.broadcasted_iota(jnp.int32, (2 * size + 32, size), 0)
+    cols = lax.broadcasted_iota(jnp.int32, (2 * size + 32, size), 1)
+    half = half_ref[...]
+    third = (high_ref[three], low_ref[three])
+    whole_row = times(split(half[: 2 * size]), third)
+    whole_flow = times(split(half[2 * size :]), third) + flow_ref[three]
+    none = (rows == cols).astype(F32)
+    single = high_ref[one].astype(F32) + low_ref[one].astype(F32)
+    single = jnp.concatenate([single, flow_ref[one]], axis=0)
+    triple = jnp.concatenate([whole_row, whole_flow], axis=0)
+    count = info_ref[2]
+    low_half = jnp.where(count == 0, none, single)
+    out_ref[...] = jnp.where(count < 2, low_half, jnp.where(count == 2, half, triple))
+    second = split(x_ref[1])
+    first = first_ref[...]
+    inner_ref[: 2 * size, :] = jnp.where(left, times(split(first), second), first)
+    inner_ref[2 * size :, :] = times(split(qa_ref[...]), second)
+
+
+def entry_map_kernel(info_ref, prefix_ref, inner_ref, x_ref, high_ref, low_ref, flow_ref):
     size = x_ref.shape[2]
-    lead = size // 8
     left = info_ref[0] == 0
-    state = jnp.where(info_ref[1] == 0, lead_ref[...], state_ref[...])
-    for item in range(3):
-        index = item_of(info_ref, item)
-        later = advance(state, (high_ref.at[index], low_ref.at[index]), flow_ref[index])
-        state = jnp.where(item < info_ref[2], later, state)
-    turned = complex_rows(state, (x_ref[0, :size], x_ref[0, size:]))
-    inner_a = jnp.where(left, turned, state)
-    block = (stacked(recv_ref, 0, lead), stacked(recv_ref, lead, lead))
-    middle = complex_rows(inner_a, block) + qa_ref[...]
-    inner_b = complex_rows(middle, (x_ref[1, :size], x_ref[1, size:]))
-    for dest in range(8):
-        out_ref[dest, :32, :] = inner_a
-        out_ref[dest, 32:, :] = inner_b
-
-
-def arrange_kernel(recv_ref, high_ref, low_ref):
+    prefix, flow = split(prefix_ref[: 2 * size, :]), split(prefix_ref[2 * size :, :])
+    turn = split(x_ref[0])
+    inner = split(inner_ref[: 2 * size, :])
+    item_a = jnp.where(left, times(prefix, turn), prefix_ref[: 2 * size, :])
+    flow_ref[0] = jnp.where(left, times(flow, turn), prefix_ref[2 * size :, :])
+    item_b = times(prefix, inner)
+    flow_ref[1] = times(flow, inner) + inner_ref[2 * size :, :]
+    for item, value in enumerate((item_a, item_b)):
+        high, low = split(value)
+        high_ref[item] = high
+        low_ref[item] = low
+
+
+def inflow_kernel(info_ref, lead_ref, state_ref, high_ref, low_ref, flow_ref, out_ref):
+    state = split(entry_state(info_ref, lead_ref, state_ref))
+    for item in range(2):
+        value = times(state, (high_ref[item], low_ref[item])) + flow_ref[item]
+        for dest in range(8):
+            out_ref[dest, 32 * item : 32 * (item + 1), :] = value
+
+
+def arrange_kernel(
+    place_ref, inject_ref, recv_ref, base_ref, extra_ref, high_ref, low_ref, out_ref
+):
     lead = recv_ref.shape[2] // 8
+    modes = inject_ref.shape[1]
+    width = base_ref.shape[1]
     for slab in range(2):
         for kind in range(4):
             value = stacked(recv_ref, (slab * 4 + kind) * lead, lead)
@@ -301,22 +351,22 @@
             sweep, part = divmod(kind, 2)
             high_ref[slab, sweep, part] = high
             low_ref[slab, sweep, part] = low
-
-
-def state_kernel(
-    place_ref, inject_ref, inner_ref, high_ref, low_ref, base_ref, extra_ref, left_ref, right_ref
-):
-    modes = inject_ref.shape[1]
-    width = base_ref.shape[1]
-    for sweep, out_ref in enumerate((left_ref, right_ref)):
+    for sweep in range(2):
         target = jnp.broadcast_to(
             inject_ref[sweep : sweep + 1, :].astype(F32), (width, modes)
         ).T
-        bases = []
         for part in range(2):
             start = (2 * sweep + part) * modes
             rows = unpacked_rows(place_ref, inject_ref, base_ref, sweep, part)
-            bases.append(rows + extra_ref[start : start + modes, :])
+            rows = rows + extra_ref[start : start + modes, :]
+            for slab in range(2):
+                chosen = target == (place_ref[0] + slab).astype(F32)
+                out_ref[sweep, slab, part] = jnp.where(chosen, rows, 0.0)
+
+
+def state_kernel(inner_ref, high_ref, low_ref, base_ref, left_ref, right_ref):
+    modes = base_ref.shape[3]
+    for sweep, out_ref in enumerate((left_ref, right_ref)):
         for slab in range(2):
             item = slab if sweep == 0 else 1 - slab
             pieces = []
@@ -325,20 +375,18 @@
                 for member in range(4):
                     pieces.append(inner_ref[sweep * 4 + member, start : start + 16, :])
             parts = split(jnp.concatenate(pieces, axis=0))
-            by = []
+            by = [
+                mm3(parts, (high_ref[slab, sweep, part], low_ref[slab, sweep, part]))
+                for part in range(2)
+            ]
+            value = combined(by[0], by[1])
             for part in range(2):
-                by.append(mm3(parts, (high_ref[slab, sweep, part], low_ref[slab, sweep, part])))
-            chosen = target == (place_ref[0] + slab).astype(F32)
-            for part in range(2):
-                base = jnp.where(chosen, bases[part], 0.0)
-                if part == 0:
-                    out_ref[slab, part] = base + (by[0][:modes] - by[1][modes:])
-                else:
-                    out_ref[slab, part] = base + (by[1][:modes] + by[0][modes:])
-
-
-def params(**extra):
-    return pltpu.CompilerParams(vmem_limit_bytes=LIMIT, **extra)
+                rows = value[part * modes : (part + 1) * modes]
+                out_ref[slab, part] = base_ref[sweep, slab, part] + rows
+
+
+def params(limit=LIMIT):
+    return pltpu.CompilerParams(vmem_limit_bytes=limit)
 
 
 def whole(shape):
@@ -348,6 +396,7 @@
 
 SMEM = pl.BlockSpec(memory_space=pltpu.SMEM)
 VMEM = pl.BlockSpec(memory_space=pltpu.VMEM)
+ANY = pl.BlockSpec(memory_space=pl.ANY)
 
 
 def exchange(value):
@@ -392,7 +441,7 @@
             pltpu.VMEM((2, stack, width), BF16),
             pltpu.VMEM((2, 2 * modes, size), F32),
         ],
-        compiler_params=params(),
+        compiler_params=params(LARGE),
         name="interface_terms",
     )(place, inject, sources, diag_inverse, diag_inverse)
     sent, inject_after = lax.optimization_barrier((sent, inject))
@@ -424,7 +473,7 @@
                 jax.ShapeDtypeStruct((8, 8 * lead, part_rows), F32),
                 jax.ShapeDtypeStruct((8, 4 * PACK, part_rows), F32),
             ],
-            compiler_params=params(),
+            compiler_params=params(LARGE),
             name="spread_terms",
         )(high, low, diag_inverse)
 
@@ -446,35 +495,58 @@
     marks = jnp.broadcast_to(marks.astype(F32)[:, :, None], (2, 32, size))
     own_lead = lax.dynamic_slice(leads, (team, 0, member * 16, 0), (1, 2, 16, size))
     own_lead = own_lead.reshape(32, size)
-    received, spread, flows, turned, marks, own_lead = lax.optimization_barrier(
-        (received, spread, flows, turned, marks, own_lead)
-    )
-
-    packed, flow_a = pl.pallas_call(
+    base = summed(flows)
+    owners = jnp.arange(slabs, dtype=jnp.int32)[:, None, None]
+    counts = jnp.sum((inject_after[None] >> 1 == owners).astype(jnp.int32), axis=2)
+    chunks = (jnp.max(counts) + PACK - 1) // PACK
+
+    def more(chunk, extra):
+        place = jnp.stack([first, chunk]).astype(jnp.int32)
+        _, flows = chunk_terms(place)
+        return pl.pallas_call(
+            expand_kernel,
+            in_specs=[SMEM, VMEM, VMEM, VMEM],
+            out_specs=VMEM,
+            out_shape=jax.ShapeDtypeStruct((4 * modes, part_rows), F32),
+            compiler_params=params(),
+            name="expand_terms",
+        )(place, inject, summed(flows), extra)
+
+    extra = lax.fori_loop(1, chunks, more, jnp.zeros((4 * modes, part_rows), F32))
+    received, turned, marks, own_lead, spread, extra = lax.optimization_barrier(
+        (received, turned, marks, own_lead, spread, extra)
+    )
+
+    top, bottom, flow_a, first_map = pl.pallas_call(
         pair_map_kernel,
         in_specs=[SMEM, VMEM, VMEM, VMEM],
-        out_specs=[VMEM, VMEM],
+        out_specs=[VMEM] * 4,
         out_shape=[
-            jax.ShapeDtypeStruct((2 * size + 32, size), F32),
+            jax.ShapeDtypeStruct((size + 16, size), F32),
+            jax.ShapeDtypeStruct((size + 16, size), F32),
             jax.ShapeDtypeStruct((32, size), F32),
+            jax.ShapeDtypeStruct((2 * size, size), F32),
         ],
         compiler_params=params(),
         name="pair_map",
     )(info, received, turned, marks)
-    packed, spread = lax.optimization_barrier((packed, spread))
+
+    spread = pl.pallas_call(
+        after_kernel,
+        in_specs=[ANY, ANY],
+        out_specs=ANY,
+        out_shape=jax.ShapeDtypeStruct(spread.shape, F32),
+        input_output_aliases={0: 0},
+        name="after_pair_map",
+    )(spread, bottom)
     rows = exchange(spread)
-    base = summed(flows)
 
     def turn(value, step):
         return lax.ppermute(
             value, "slab", [(slab, slab // 4 * 4 + (slab + step) % 4) for slab in range(slabs)]
         )
 
-    top, bottom = packed[: size + 16], packed[size + 16 :]
     before_top, after_bottom = turn(top, 1), turn(bottom, -1)
-    before_top, after_bottom, top, bottom = lax.optimization_barrier(
-        (before_top, after_bottom, top, bottom)
-    )
     before_bottom, after_top = turn(bottom, 1), turn(top, -1)
     across_top, across_bottom = turn(before_top, 1), turn(after_bottom, -1)
     pieces = (after_top, after_bottom, across_top, across_bottom, before_top, before_bottom)
@@ -486,12 +558,12 @@
     state_shape = jax.ShapeDtypeStruct((32, size), F32)
     *maps, flow = pl.pallas_call(
         gather_kernel,
-        in_specs=[SMEM] + [VMEM] * 8,
+        in_specs=[SMEM] + [VMEM] * 9,
         out_specs=[VMEM] * 4,
         out_shape=row_maps + [state_shape],
         compiler_params=params(),
         name="gather_maps",
-    )(info, own_lead, packed, *pieces)
+    )(info, own_lead, top, bottom, *pieces)
 
     cols = lax.axis_size("col")
     pairs = []
@@ -499,66 +571,72 @@
         for col in range(cols):
             target = (slab + (4 if col < 4 else -4)) % slabs
             pairs.append((slab * cols + col, target * cols + col))
-    flow = lax.ppermute(flow, ("slab", "col"), pairs)
-    for _ in range(slabs // 4 - 2):
-        flow = pl.pallas_call(
-            row_kernel,
-            in_specs=[SMEM] + [VMEM] * 5,
-            out_specs=VMEM,
-            out_shape=state_shape,
+
+    def local(kernel, name, shapes, *args):
+        single = not isinstance(shapes, list)
+        return pl.pallas_call(
+            kernel,
+            in_specs=[SMEM] + [VMEM] * (len(args) - 1),
+            out_specs=VMEM if single else [VMEM] * len(shapes),
+            out_shape=shapes,
             compiler_params=params(),
-            name="row_step",
-        )(info, own_lead, flow, *maps)
-        flow = lax.ppermute(flow, ("slab", "col"), pairs)
-    inner = pl.pallas_call(
+            name=name,
+        )(*args)
+
+    def hop(value):
+        return lax.ppermute(value, ("slab", "col"), pairs)
+
+    full = jax.ShapeDtypeStruct((2 * size + 32, size), F32)
+    half_map = jax.ShapeDtypeStruct((2 * size, size), BF16)
+    flow = hop(flow)
+    *row_map, half_row = local(
+        row_map_kernel, "row_map", [half_map, half_map, state_shape, full], info, *maps
+    )
+    flow = local(row_kernel, "row_step", state_shape, info, own_lead, flow, *row_map)
+    flow, half_row = lax.optimization_barrier((flow, half_row))
+    flow = hop(flow)
+    prefix, inner_map = local(
+        prefix_kernel, "prefix_map", [full, full], info, *maps, half_row, first_map, turned, flow_a
+    )
+    flow = local(row_kernel, "row_step", state_shape, info, own_lead, flow, *row_map)
+    flow, prefix, inner_map = lax.optimization_barrier((flow, prefix, inner_map))
+    flow = hop(flow)
+    two_maps = [
+        jax.ShapeDtypeStruct((2, 2 * size, size), BF16),
+        jax.ShapeDtypeStruct((2, 2 * size, size), BF16),
+        jax.ShapeDtypeStruct((2, 32, size), F32),
+    ]
+    entry = local(entry_map_kernel, "entry_map", two_maps, info, prefix, inner_map, turned)
+    inner = local(
         inflow_kernel,
-        in_specs=[SMEM] + [VMEM] * 8,
-        out_specs=VMEM,
-        out_shape=jax.ShapeDtypeStruct((8, 64, size), F32),
-        compiler_params=params(),
-        name="inflow",
-    )(info, own_lead, flow, *maps, received, turned, flow_a)
+        "inflow",
+        jax.ShapeDtypeStruct((8, 64, size), F32),
+        info,
+        own_lead,
+        flow,
+        *entry,
+    )
     rows, inner, base = lax.optimization_barrier((rows, inner, base))
 
-    owners = jnp.arange(slabs, dtype=jnp.int32)[:, None, None]
-    counts = jnp.sum((inject_after[None] >> 1 == owners).astype(jnp.int32), axis=2)
-    chunks = (jnp.max(counts) + PACK - 1) // PACK
-
-    def more(chunk, extra):
-        place = jnp.stack([first, chunk]).astype(jnp.int32)
-        _, flows = chunk_terms(place)
-        return pl.pallas_call(
-            expand_kernel,
-            in_specs=[SMEM, VMEM, VMEM, VMEM],
-            out_specs=VMEM,
-            out_shape=jax.ShapeDtypeStruct((4 * modes, part_rows), F32),
-            compiler_params=params(),
-            name="expand_terms",
-        )(place, inject, summed(flows), extra)
-
-    extra = lax.fori_loop(1, chunks, more, jnp.zeros((4 * modes, part_rows), F32))
     inner = exchange(inner)
-    row_high, row_low = pl.pallas_call(
-        arrange_kernel,
-        in_specs=[VMEM],
-        out_specs=[VMEM, VMEM],
-        out_shape=[
-            jax.ShapeDtypeStruct((2, 2, 2, size, part_rows), BF16),
-            jax.ShapeDtypeStruct((2, 2, 2, size, part_rows), BF16),
-        ],
-        compiler_params=params(),
-        name="arrange_rows",
-    )(rows)
+    arranged = [
+        jax.ShapeDtypeStruct((2, 2, 2, size, part_rows), BF16),
+        jax.ShapeDtypeStruct((2, 2, 2, size, part_rows), BF16),
+        jax.ShapeDtypeStruct((2, 2, 2, modes, part_rows), F32),
+    ]
+    arranged = local(
+        arrange_kernel, "arrange_rows", arranged, place, inject, rows, base, extra
+    )
 
     shape = (2, 2, modes, part_rows)
     left, right = pl.pallas_call(
         state_kernel,
-        in_specs=[SMEM] + [VMEM] * 6,
+        in_specs=[VMEM] * 4,
         out_specs=[VMEM, VMEM],
         out_shape=[jax.ShapeDtypeStruct(shape, F32), jax.ShapeDtypeStruct(shape, F32)],
         compiler_params=params(),
         name="states",
-    )(place, inject, inner, row_high, row_low, base, extra)
+    )(inner, *arranged)
     return jnp.transpose(left, (0, 1, 3, 2)), jnp.transpose(right, (0, 1, 3, 2))
 
 

time: 151 us -> 153 us (1.013)
  Pallas kernels: 30.8 us -> 35.7 us
  waiting for transfers between devices: 72.2 us -> 68.3 us
    reduce_scatter x1, waiting for transfers between devices: 0.01 us -> 12.4 us  [summed(): return lax.psum_scatter(flows, 'col', scatter_dimension=0, tiled=False)]
    ppermute x3, waiting for transfers between devices: 13.6 us -> 6.22 us  [hop(): return lax.ppermute(value, ('slab', 'col'), pairs)]
    all_to_all x3, waiting for transfers between devices: 38.7 us -> 33.4 us  [exchange(): return lax.all_to_all(value, 'col', split_axis=0, concat_axis=0, tiled=True)]
    pallas_call x6 -> x10, Pallas kernels: 11.7 us -> 15.4 us  [the longest x7 12.3 us: local(): pl.pallas_call(kernel, in_specs=[SMEM] + [VMEM] * (len(args) - 1), out_sp...]
    ppermute x6, waiting for transfers between devices: 19.2 us -> 15.7 us  [turn(): lax.ppermute(value, 'slab', [(slab, slab // 4 * 4 + (slab + step) % 4) fo...]
    unnamed x20 -> x26, local copies, waits for them, and re-layouts: 5.58 us -> 4.2 us
  transfers between devices with their start and end apart: 13 -> 13, of which waited for: 12 -> 11; matrix products, arithmetic and copies ran while one was open for 1% -> 1% of each run, Pallas kernels for 13% -> 16%
where the time goes in v5:
time: 153 us; the launch traced here: 152 us
  waiting for transfers between devices  68.3 us (45%)
  Pallas kernels  35.7 us (23%)
  starting transfers between devices  25.7 us (17%)
  between operations  16.3 us (11%)
  local copies, waits for them, and re-layouts  4.37 us (3%)
    all_to_all x3, waiting for transfers between devices, exchange(): return lax.all_to_all(value, 'col', split_axis=0, concat_axis=0, tiled=True)  33.4 us
    all_to_all x3, starting transfers between devices, exchange(): return lax.all_to_all(value, 'col', split_axis=0, concat_axis=0, tiled=True)  16.6 us
    ppermute x6, waiting for transfers between devices, turn(): lax.ppermute(value, 'slab', [(slab, slab // 4 * 4 + (slab + step) % 4) fo...  15.7 us
    reduce_scatter x1, waiting for transfers between devices, summed(): return lax.psum_scatter(flows, 'col', scatter_dimension=0, tiled=False)  12.4 us
    pallas_call x7, Pallas kernels, local(): pl.pallas_call(kernel, in_specs=[SMEM] + [VMEM] * (len(args) - 1), out_sp...  12.3 us
    pallas_call x1, Pallas kernels, chunk_terms(): pl.pallas_call(spread_kernel, grid=(8,), in_specs=[whole(terms.shape), wh...  8.73 us
    pallas_call x1, Pallas kernels, on_device(): pl.pallas_call(interface_kernel, grid=(4,), in_specs=[SMEM, whole(inject....  6.72 us
    ppermute x3, waiting for transfers between devices, hop(): return lax.ppermute(value, ('slab', 'col'), pairs)  6.22 us
  transfers between devices with their start and end apart: 13, of which 11 were waited for; matrix products, arithmetic and copies ran while one was open for 1% of the time, Pallas kernels for 16%

profile of v5, /device:TPU:8, one launch (start us, length us, event | category | flops | bytes accessed | tf_op | source)
XLA Modules:
  0.0 151.9 jit_solution(2842071629331569022)
XLA Ops:
  8.6 6.7 %interface_terms.1 = f32[8,160,256]{2,1,0:T(8,128)} custom-call(s32[2]{0:T(128)} %pad_add_fusion.1.place_ref, s32[2,64]{1,0:T(2,128)} %inject_ref.4, f32[2,2,64,256]{3,2,1,0:T(8,128)} %bitcast.27, f32[2,2,2048,256]{3,2,1,0:T(8,128)} %g_ref.1, f32[2,2,2048,256]{3,2,1,0:T(8,128)} %g_ref.1), custom_call_target="tpu_custom_call" | custom-call | tf_op jit(solution)/shard_map/interface_terms/pallas_call | solution.py:427
  15.3 8.6 %all-to-all-start = ((f32[8,160,256]{2,1,0:T(8,128)}), f32[8,160,256]{2,1,0:T(8,128)S(1)}, u32[]{:S(2)}, u32[]{:S(2)}) async-start(f32[8,160,256]{2,1,0:T(8,128)} %interface_terms.1), calls=%async_computation.1 | async-start | bytes 2621440 | tf_op jit(solution)/shard_map/all_to_all | solution.py:403
  29.6 8.7 %spread_terms.2 = (f32[8,256,256]{2,1,0:T(8,128)}, f32[8,64,256]{2,1,0:T(8,128)}) custom-call(bf16[2,128,256]{2,1,0:T(8,128)(2,1)} %copy-done.9, bf16[2,128,256]{2,1,0:T(8,128)(2,1)} %copy-done.10, f32[2,2,2048,256]{3,2,1,0:T(8,128)} %g_ref.1), custom_call_target="tpu_custom_call" | custom-call | tf_op jit(solution)/shard_map/spread_terms/pallas_call | solution.py:460
  38.5 19.9 %all-to-all-done.recv_ref = f32[8,160,256]{2,1,0:T(8,128)S(1)} async-done(((f32[8,160,256]{2,1,0:T(8,128)}), f32[8,160,256]{2,1,0:T(8,128)S(1)}, u32[]{:S(2)}, u32[]{:S(2)}) %all-to-all-start) | async-done | bytes 1310752 | tf_op jit(solution)/shard_map/all_to_all | solution.py:403
  58.5 2.8 %pair_map.1 = (f32[272,256]{1,0:T(8,128)S(1)}, f32[272,256]{1,0:T(8,128)S(1)}, f32[32,256]{1,0:T(8,128)S(1)}, f32[512,256]{1,0:T(8,128)S(1)}) custom-call(s32[4]{0:T(128)S(1)} %pad_add_fusion.2.team_ref.info_ref, f32[8,160,256]{2,1,0:T(8,128)S(1)} %all-to-all-done.recv_ref, f32[2,512,256]{2,1,0:T(8,128)S(1)} %coupling_rows.1.x_ref, ...), custom_call_target="tpu_custom_call" | custom-call | tf_op jit(solution)/shard_map/pair_map/pallas_call | solution.py:520
  62.7 4.5 %all-to-all-start.1 = ((f32[8,256,256]{2,1,0:T(8,128)}), f32[8,256,256]{2,1,0:T(8,128)}, u32[]{:S(2)}, u32[]{:S(2)}) async-start(f32[8,256,256]{2,1,0:T(8,128)} %after_pair_map.1), calls=%async_computation.2 | async-start | bytes 4194304 | tf_op jit(solution)/shard_map/all_to_all | solution.py:403
  67.8 1.7 %collective-permute-start.2 = (f32[272,256]{1,0:T(8,128)S(1)}, f32[272,256]{1,0:T(8,128)S(1)}, u32[]{:S(2)}, u32[]{:S(2)}) collective-permute-start(f32[272,256]{1,0:T(8,128)S(1)} %copy-done.8), channel_id=1, source_target_pairs={{0,16},{16,32},{32,48},{48,0},{64,80},{80,96},{96,112},{112,64},{1... | collective-permute-start | bytes 835592 | tf_op jit(solution)/shard_map/ppermute | solution.py:545
  69.9 1.7 %collective-permute-start = (f32[272,256]{1,0:T(8,128)S(1)}, f32[272,256]{1,0:T(8,128)S(1)}, u32[]{:S(2)}, u32[]{:S(2)}) collective-permute-start(f32[272,256]{1,0:T(8,128)S(1)} %copy-done.8), channel_id=1, source_target_pairs={{0,48},{16,0},{32,16},{48,32},{64,112},{80,64},{96,80},{112,96},{1... | collective-permute-start | bytes 835592 | tf_op jit(solution)/shard_map/ppermute | solution.py:545
  71.9 5.5 %collective-permute-done.2.refs_6_ = f32[272,256]{1,0:T(8,128)S(1)} collective-permute-done((f32[272,256]{1,0:T(8,128)S(1)}, f32[272,256]{1,0:T(8,128)S(1)}, u32[]{:S(2)}, u32[]{:S(2)}) %collective-permute-start.2) | collective-permute-done | bytes 278560 | tf_op jit(solution)/shard_map/ppermute | solution.py:545
  77.3 1.6 %collective-permute-start.3 = (f32[272,256]{1,0:T(8,128)S(1)}, f32[272,256]{1,0:T(8,128)S(1)}, u32[]{:S(2)}, u32[]{:S(2)}) collective-permute-start(f32[272,256]{1,0:T(8,128)S(1)} %collective-permute-done.2.refs_6_), channel_id=1, source_target_pairs={{0,16},{16,32},{32,48},{48,0},{64,80},{80,96},{96,112},{112,64},{1... | collective-permute-start | bytes 835592 | tf_op jit(solution)/shard_map/ppermute | solution.py:545
  79.4 5.5 %collective-permute-done.refs_2_ = f32[272,256]{1,0:T(8,128)S(1)} collective-permute-done((f32[272,256]{1,0:T(8,128)S(1)}, f32[272,256]{1,0:T(8,128)S(1)}, u32[]{:S(2)}, u32[]{:S(2)}) %collective-permute-start) | collective-permute-done | bytes 278560 | tf_op jit(solution)/shard_map/ppermute | solution.py:545
  84.9 3.4 %collective-permute-done.3.refs_4_ = f32[272,256]{1,0:T(8,128)S(1)} collective-permute-done((f32[272,256]{1,0:T(8,128)S(1)}, f32[272,256]{1,0:T(8,128)S(1)}, u32[]{:S(2)}, u32[]{:S(2)}) %collective-permute-start.3) | collective-permute-done | bytes 278560 | tf_op jit(solution)/shard_map/ppermute | solution.py:545
  89.6 1.7 %gather_maps.1 = (bf16[4,512,256]{2,1,0:T(8,128)(2,1)S(1)}, bf16[4,512,256]{2,1,0:T(8,128)(2,1)S(1)}, f32[4,32,256]{2,1,0:T(8,128)S(1)}, f32[32,256]{1,0:T(8,128)S(1)}) custom-call(s32[4]{0:T(128)S(1)} %pad_add_fusion.2.team_ref.info_ref, f32[32,256]{1,0:T(8,128)S(1)} %bitcast.22, f32[272,256]{1,0:T(8,128)S(1)} %copy-done.8, f32[272,256]{1,0:T(8,128)S(1)} %copy-done.5, ...), custom_call_target="tpu_custom_call" | custom-call | tf_op jit(solution)/shard_map/gather_maps/pallas_call | solution.py:559
  91.4 1.8 %collective-permute-start.6 = (f32[32,256]{1,0:T(8,128)S(1)}, f32[32,256]{1,0:T(8,128)S(1)}, u32[]{:S(2)}, u32[]{:S(2)}) collective-permute-start(f32[32,256]{1,0:T(8,128)S(1)} %get-tuple-element.103), channel_id=1, source_target_pairs={{0,64},{2,66},{4,68},{6,70},{8,200},{10,202},{12,204},{14,206},{16... | collective-permute-start | bytes 98312 | tf_op jit(solution)/shard_map/ppermute | solution.py:587
  93.2 3.2 %row_map.1 = (bf16[512,256]{1,0:T(8,128)(2,1)S(1)}, bf16[512,256]{1,0:T(8,128)(2,1)S(1)}, f32[32,256]{1,0:T(8,128)S(1)}, f32[544,256]{1,0:T(8,128)S(1)}) custom-call(s32[4]{0:T(128)S(1)} %pad_add_fusion.2.team_ref.info_ref, bf16[4,512,256]{2,1,0:T(8,128)(2,1)S(1)} %get-tuple-element.104.high_ref, bf16[4,512,256]{2,1,0:T(8,128)(2,1)S(1)} %get-tuple-element.105.low_ref, ...), custom_call_target="tpu_custom_call" | custom-call | tf_op jit(solution)/shard_map/row_map/pallas_call | solution.py:577
  98.6 1.7 %prefix_map.1 = (f32[544,256]{1,0:T(8,128)S(1)}, f32[544,256]{1,0:T(8,128)S(1)}) custom-call(s32[4]{0:T(128)S(1)} %pad_add_fusion.2.team_ref.info_ref, bf16[4,512,256]{2,1,0:T(8,128)(2,1)S(1)} %get-tuple-element.104.high_ref, bf16[4,512,256]{2,1,0:T(8,128)(2,1)S(1)} %get-tuple-element.105.low_ref, f32[4,32,256]{2,1,0:T(8,128)S(1)} %get-tuple-element.106.flow_ref, ...), custom_call_target="tpu_custom_call" | custom-call | tf_op jit(solution)/shard_map/prefix_map/pallas_call | solution.py:577
  100.4 2.3 %collective-permute-done.7.state_ref = f32[32,256]{1,0:T(8,128)S(1)} collective-permute-done((f32[32,256]{1,0:T(8,128)S(1)}, f32[32,256]{1,0:T(8,128)S(1)}, u32[]{:S(2)}, u32[]{:S(2)}) %collective-permute-start.7) | collective-permute-done | bytes 32800 | tf_op jit(solution)/shard_map/ppermute | solution.py:587
  103.5 1.7 %entry_map.1 = (bf16[2,512,256]{2,1,0:T(8,128)(2,1)S(1)}, bf16[2,512,256]{2,1,0:T(8,128)(2,1)S(1)}, f32[2,32,256]{2,1,0:T(8,128)S(1)}) custom-call(s32[4]{0:T(128)S(1)} %pad_add_fusion.2.team_ref.info_ref, f32[544,256]{1,0:T(8,128)S(1)} %get-tuple-element.118.prefix_ref, f32[544,256]{1,0:T(8,128)S(1)} %get-tuple-element.119.inner_ref, ...), custom_call_target="tpu_custom_call" | custom-call | tf_op jit(solution)/shard_map/entry_map/pallas_call | solution.py:577
  105.2 3.4 %collective-permute-done.8.state_ref = f32[32,256]{1,0:T(8,128)S(1)} collective-permute-done((f32[32,256]{1,0:T(8,128)S(1)}, f32[32,256]{1,0:T(8,128)S(1)}, u32[]{:S(2)}, u32[]{:S(2)}) %collective-permute-start.8) | collective-permute-done | bytes 32800 | tf_op jit(solution)/shard_map/ppermute | solution.py:587
  108.6 1.7 %inflow.1 = f32[8,64,256]{2,1,0:T(8,128)} custom-call(s32[4]{0:T(128)S(1)} %pad_add_fusion.2.team_ref.info_ref, f32[32,256]{1,0:T(8,128)S(1)} %bitcast.25, f32[32,256]{1,0:T(8,128)S(1)} %collective-permute-done.8.state_ref, bf16[2,512,256]{2,1,0:T(8,128)(2,1)S(1)} %get-tuple-element.120.high_ref, bf16[2,512,256]{2,1,0:T(8,128)(2,1)S(1)} %get-tuple-element.121.low_ref, ...), custom_call_target="tpu_custom_call" | custom-call | tf_op jit(solution)/shard_map/inflow/pallas_call | solution.py:577
  110.2 12.4 %reduce-scatter.3.cloned.1.call-done = f32[1,64,256]{2,1,0:T(8,128)} async-done(((f32[8,64,256]{2,1,0:T(8,128)}), f32[1,64,256]{2,1,0:T(8,128)}) %reduce-scatter.3.cloned.1.call-update) | async-done | bytes 65552 | tf_op jit(solution)/shard_map/reduce_scatter | solution.py:481
  123.7 3.5 %all-to-all-start.2 = ((f32[8,64,256]{2,1,0:T(8,128)}), f32[8,64,256]{2,1,0:T(8,128)S(1)}, u32[]{:S(2)}, u32[]{:S(2)}) async-start(f32[8,64,256]{2,1,0:T(8,128)} %inflow.1), calls=%async_computation.4 | async-start | bytes 1048576 | tf_op jit(solution)/shard_map/all_to_all | solution.py:403
  128.1 2.6 %arrange_rows.1 = (bf16[2,2,2,256,256]{4,3,2,1,0:T(8,128)(2,1)S(1)}, bf16[2,2,2,256,256]{4,3,2,1,0:T(8,128)(2,1)S(1)}, f32[2,2,2,64,256]{4,3,2,1,0:T(8,128)S(1)}) custom-call(s32[2]{0:T(128)S(1)} %copy-done.12, s32[2,64]{1,0:T(2,128)S(1)} %get-tuple-element.266, f32[8,256,256]{2,1,0:T(8,128)} %all-to-all-done.1.recv_ref, f32[64,256]{1,0:T(8,128)S(1)} %bitcast.26, ...), custom_call_target="tpu_custom_call" | custom-call | tf_op jit(solution)/shard_map/arrange_rows/pallas_call | solution.py:577
  130.7 12.4 %all-to-all-done.2.inner_ref = f32[8,64,256]{2,1,0:T(8,128)S(1)} async-done(((f32[8,64,256]{2,1,0:T(8,128)}), f32[8,64,256]{2,1,0:T(8,128)S(1)}, u32[]{:S(2)}, u32[]{:S(2)}) %all-to-all-start.2) | async-done | bytes 524320 | tf_op jit(solution)/shard_map/all_to_all | solution.py:403
  (56 shorter events, 16.6 us)
Async XLA Ops:
  8.0 30.4 %copy-start = (f32[2,2,256,64]{2,3,1,0:T(8,128)S(1)}, f32[2,2,256,64]{2,3,1,0:T(8,128)}, u32[]{:S(2)}) copy-start(f32[2,2,256,64]{2,3,1,0:T(8,128)} %param.11) | copy-start | bytes 786436
  15.3 8.6 %copy-start.15 = (s32[2,64]{1,0:T(2,128)S(1)}, s32[2,64]{1,0:T(2,128)}, u32[]{:S(2)}) copy-start(s32[2,64]{1,0:T(2,128)} %inject_ref.4) | copy-start | bytes 1540
  15.3 10.1 %copy-start.12 = (s32[2]{0:T(128)S(1)}, s32[2]{0:T(128)}, u32[]{:S(2)}) copy-start(s32[2]{0:T(128)} %pad_add_fusion.1.place_ref) | copy-start | bytes 28
  15.3 10.1 %copy-start.13 = (f32[2,2,256,64]{2,3,1,0:T(8,128)S(1)}, f32[2,2,256,64]{2,3,1,0:T(8,128)}, u32[]{:S(2)}) copy-start(f32[2,2,256,64]{2,3,1,0:T(8,128)} %param.9) | copy-start | bytes 786436
  15.3 43.0 %all-to-all-start = ((f32[8,160,256]{2,1,0:T(8,128)}), f32[8,160,256]{2,1,0:T(8,128)S(1)}, u32[]{:S(2)}, u32[]{:S(2)}) async-start(f32[8,160,256]{2,1,0:T(8,128)} %interface_terms.1), calls=%async_computation.1 | async-start | bytes 2621440 | tf_op jit(solution)/shard_map/all_to_all | solution.py:403
  27.3 2.3 %copy-start.10 = (bf16[2,128,256]{2,1,0:T(8,128)(2,1)}, bf16[2,128,256]{2,1,0:T(8,128)(2,1)S(1)}, u32[]{:S(2)}) copy-start(bf16[2,128,256]{2,1,0:T(8,128)(2,1)S(1)} %get-tuple-element.93.low_ref) | copy-start | bytes 393220
  27.4 1.2 copy-start.6
  38.5 20.0 %copy-start.14 = (f32[256,256]{1,0:T(8,128)}, f32[256,256]{1,0:T(8,128)S(1)}, u32[]{:S(2)}) copy-start(f32[256,256]{1,0:T(8,128)S(1)} %get-tuple-element.127.extra_ref) | copy-start | bytes 786436
  61.2 0.7 copy-start.4
  62.7 5.1 %copy-start.8 = (f32[272,256]{1,0:T(8,128)S(1)}, f32[272,256]{1,0:T(8,128)}, u32[]{:S(2)}) copy-start(f32[272,256]{1,0:T(8,128)} %copy-done.7) | copy-start | bytes 835588
  62.7 6.7 %copy-start.5 = (f32[272,256]{1,0:T(8,128)S(1)}, f32[272,256]{1,0:T(8,128)}, u32[]{:S(2)}) copy-start(f32[272,256]{1,0:T(8,128)} %copy-done.4) | copy-start | bytes 835588
  62.7 61.1 %all-to-all-start.1 = ((f32[8,256,256]{2,1,0:T(8,128)}), f32[8,256,256]{2,1,0:T(8,128)}, u32[]{:S(2)}, u32[]{:S(2)}) async-start(f32[8,256,256]{2,1,0:T(8,128)} %after_pair_map.1), calls=%async_computation.2 | async-start | bytes 4194304 | tf_op jit(solution)/shard_map/all_to_all | solution.py:403
  67.2 55.5 %reduce-scatter.3.cloned.1.call-start = ((), (), s32[]{:S(2)}) async-start(), calls=%async_computation.5 | async-start | bytes 589824 | tf_op jit(solution)/shard_map/reduce_scatter | solution.py:481
  67.8 9.6 %collective-permute-start.2 = (f32[272,256]{1,0:T(8,128)S(1)}, f32[272,256]{1,0:T(8,128)S(1)}, u32[]{:S(2)}, u32[]{:S(2)}) collective-permute-start(f32[272,256]{1,0:T(8,128)S(1)} %copy-done.8), channel_id=1, source_target_pairs={{0,16},{16,32},{32,48},{48,0},{64,80},{80,96},{96,112},{112,64},{1... | collective-permute-start | bytes 835592 | tf_op jit(solution)/shard_map/ppermute | solution.py:545
  69.4 9.6 %collective-permute-start.1 = (f32[272,256]{1,0:T(8,128)S(1)}, f32[272,256]{1,0:T(8,128)S(1)}, u32[]{:S(2)}, u32[]{:S(2)}) collective-permute-start(f32[272,256]{1,0:T(8,128)S(1)} %copy-done.5), channel_id=1, source_target_pairs={{0,48},{16,0},{32,16},{48,32},{64,112},{80,64},{96,80},{112,96},{1... | collective-permute-start | bytes 835592 | tf_op jit(solution)/shard_map/ppermute | solution.py:545
  69.9 15.1 %collective-permute-start = (f32[272,256]{1,0:T(8,128)S(1)}, f32[272,256]{1,0:T(8,128)S(1)}, u32[]{:S(2)}, u32[]{:S(2)}) collective-permute-start(f32[272,256]{1,0:T(8,128)S(1)} %copy-done.8), channel_id=1, source_target_pairs={{0,48},{16,0},{32,16},{48,32},{64,112},{80,64},{96,80},{112,96},{1... | collective-permute-start | bytes 835592 | tf_op jit(solution)/shard_map/ppermute | solution.py:545
  71.5 13.4 %collective-permute-start.5 = (f32[272,256]{1,0:T(8,128)S(1)}, f32[272,256]{1,0:T(8,128)S(1)}, u32[]{:S(2)}, u32[]{:S(2)}) collective-permute-start(f32[272,256]{1,0:T(8,128)S(1)} %copy-done.5), channel_id=1, source_target_pairs={{0,16},{16,32},{32,48},{48,0},{64,80},{80,96},{96,112},{112,64},{1... | collective-permute-start | bytes 835592 | tf_op jit(solution)/shard_map/ppermute | solution.py:545
  77.3 11.0 %collective-permute-start.3 = (f32[272,256]{1,0:T(8,128)S(1)}, f32[272,256]{1,0:T(8,128)S(1)}, u32[]{:S(2)}, u32[]{:S(2)}) collective-permute-start(f32[272,256]{1,0:T(8,128)S(1)} %collective-permute-done.2.refs_6_), channel_id=1, source_target_pairs={{0,16},{16,32},{32,48},{48,0},{64,80},{80,96},{96,112},{112,64},{1... | collective-permute-start | bytes 835592 | tf_op jit(solution)/shard_map/ppermute | solution.py:545
  79.0 10.7 %collective-permute-start.4 = (f32[272,256]{1,0:T(8,128)S(1)}, f32[272,256]{1,0:T(8,128)S(1)}, u32[]{:S(2)}, u32[]{:S(2)}) collective-permute-start(f32[272,256]{1,0:T(8,128)S(1)} %collective-permute-done.1.refs_3_), channel_id=1, source_target_pairs={{0,48},{16,0},{32,16},{48,32},{64,112},{80,64},{96,80},{112,96},{1... | collective-permute-start | bytes 835592 | tf_op jit(solution)/shard_map/ppermute | solution.py:545
  91.4 5.4 %collective-permute-start.6 = (f32[32,256]{1,0:T(8,128)S(1)}, f32[32,256]{1,0:T(8,128)S(1)}, u32[]{:S(2)}, u32[]{:S(2)}) collective-permute-start(f32[32,256]{1,0:T(8,128)S(1)} %get-tuple-element.103), channel_id=1, source_target_pairs={{0,64},{2,66},{4,68},{6,70},{8,200},{10,202},{12,204},{14,206},{16... | collective-permute-start | bytes 98312 | tf_op jit(solution)/shard_map/ppermute | solution.py:587
  97.5 5.2 %collective-permute-start.7 = (f32[32,256]{1,0:T(8,128)S(1)}, f32[32,256]{1,0:T(8,128)S(1)}, u32[]{:S(2)}, u32[]{:S(2)}) collective-permute-start(f32[32,256]{1,0:T(8,128)S(1)} %row_step.2), channel_id=1, source_target_pairs={{0,64},{2,66},{4,68},{6,70},{8,200},{10,202},{12,204},{14,206},{16... | collective-permute-start | bytes 98312 | tf_op jit(solution)/shard_map/ppermute | solution.py:587
  103.4 5.2 %collective-permute-start.8 = (f32[32,256]{1,0:T(8,128)S(1)}, f32[32,256]{1,0:T(8,128)S(1)}, u32[]{:S(2)}, u32[]{:S(2)}) collective-permute-start(f32[32,256]{1,0:T(8,128)S(1)} %row_step.3), channel_id=1, source_target_pairs={{0,64},{2,66},{4,68},{6,70},{8,200},{10,202},{12,204},{14,206},{16... | collective-permute-start | bytes 98312 | tf_op jit(solution)/shard_map/ppermute | solution.py:587
  123.7 19.4 %all-to-all-start.2 = ((f32[8,64,256]{2,1,0:T(8,128)}), f32[8,64,256]{2,1,0:T(8,128)S(1)}, u32[]{:S(2)}, u32[]{:S(2)}) async-start(f32[8,64,256]{2,1,0:T(8,128)} %inflow.1), calls=%async_computation.4 | async-start | bytes 1048576 | tf_op jit(solution)/shard_map/all_to_all | solution.py:403
  127.2 0.8 copy-start.11
  (2 other events, 1.4 us)
Sparse Core Ops, SparseCore 1:
  70.1 52.5 reduce-scatter.2

commit v6 on v5

--- a/solution.py
+++ b/solution.py
@@ -151,7 +151,7 @@
                 low_ref[slab, start : start + PACK, :] = mm(pick, low).astype(BF16)
 
 
-def spread_kernel(high_ref, low_ref, g_ref, out_ref, flow_ref):
+def spread_kernel(high_ref, low_ref, g_ref, early_ref, late_ref, flow_ref):
     lead = g_ref.shape[3] // 8
     total = [0.0] * 4
     for slab in range(2):
@@ -161,6 +161,9 @@
         for sweep in range(2):
             base = sweep * lead
             place = slab * 4 * lead + sweep * 2 * lead
+            out_ref = early_ref
+            if slab == 1 and sweep == 1:
+                out_ref, place = late_ref, 0
             out_ref[0, place : place + lead, :] = real[base : base + lead]
             out_ref[0, place + lead : place + 2 * lead, :] = imag[base : base + lead]
             one = 2 * lead + 2 * sweep * PACK
@@ -227,10 +230,6 @@
     flow_a = jnp.where(left, flow_a, complex_rows(flow_a, coupled[1]))
     flow_b = jnp.where(left, flow_b, complex_rows(flow_b, coupled[0]))
     bottom_ref[2 * size - half :, :] = complex_rows(flow_a, second) + flow_b
-
-
-def after_kernel(value_ref, other_ref, out_ref):
-    pass
 
 
 def item_of(info_ref, item):
@@ -330,7 +329,10 @@
         low_ref[item] = low
 
 
-def inflow_kernel(info_ref, lead_ref, state_ref, high_ref, low_ref, flow_ref, out_ref):
+def inflow_kernel(
+    info_ref, lead_ref, state_ref, high_ref, low_ref, flow_ref, spread_ref, out_ref
+):
+    out_ref[:, 64:, :] = spread_ref[...]
     state = split(entry_state(info_ref, lead_ref, state_ref))
     for item in range(2):
         value = times(state, (high_ref[item], low_ref[item])) + flow_ref[item]
@@ -338,51 +340,42 @@
             out_ref[dest, 32 * item : 32 * (item + 1), :] = value
 
 
-def arrange_kernel(
-    place_ref, inject_ref, recv_ref, base_ref, extra_ref, high_ref, low_ref, out_ref
+def state_kernel(
+    place_ref, inject_ref, last_ref, rows_ref, base_ref, extra_ref, left_ref, right_ref
 ):
-    lead = recv_ref.shape[2] // 8
     modes = inject_ref.shape[1]
     width = base_ref.shape[1]
-    for slab in range(2):
-        for kind in range(4):
-            value = stacked(recv_ref, (slab * 4 + kind) * lead, lead)
-            high, low = split(value)
-            sweep, part = divmod(kind, 2)
-            high_ref[slab, sweep, part] = high
-            low_ref[slab, sweep, part] = low
-    for sweep in range(2):
+    lead = rows_ref.shape[1] // 6
+    for sweep, out_ref in enumerate((left_ref, right_ref)):
         target = jnp.broadcast_to(
             inject_ref[sweep : sweep + 1, :].astype(F32), (width, modes)
         ).T
+        bases = []
         for part in range(2):
             start = (2 * sweep + part) * modes
             rows = unpacked_rows(place_ref, inject_ref, base_ref, sweep, part)
-            rows = rows + extra_ref[start : start + modes, :]
-            for slab in range(2):
-                chosen = target == (place_ref[0] + slab).astype(F32)
-                out_ref[sweep, slab, part] = jnp.where(chosen, rows, 0.0)
-
-
-def state_kernel(inner_ref, high_ref, low_ref, base_ref, left_ref, right_ref):
-    modes = base_ref.shape[3]
-    for sweep, out_ref in enumerate((left_ref, right_ref)):
+            bases.append(rows + extra_ref[start : start + modes, :])
         for slab in range(2):
             item = slab if sweep == 0 else 1 - slab
             pieces = []
             for part in range(2):
                 start = item * 32 + part * 16
                 for member in range(4):
-                    pieces.append(inner_ref[sweep * 4 + member, start : start + 16, :])
+                    pieces.append(last_ref[sweep * 4 + member, start : start + 16, :])
             parts = split(jnp.concatenate(pieces, axis=0))
-            by = [
-                mm3(parts, (high_ref[slab, sweep, part], low_ref[slab, sweep, part]))
-                for part in range(2)
-            ]
+            by = []
+            for part in range(2):
+                kind = 2 * sweep + part
+                if slab == 1 and sweep == 1:
+                    matrix = stacked(last_ref, 64 + part * lead, lead)
+                else:
+                    matrix = stacked(rows_ref, (4 * slab + kind) * lead, lead)
+                by.append(mm3(parts, split(matrix)))
             value = combined(by[0], by[1])
+            chosen = target == (place_ref[0] + slab).astype(F32)
             for part in range(2):
                 rows = value[part * modes : (part + 1) * modes]
-                out_ref[slab, part] = base_ref[sweep, slab, part] + rows
+                out_ref[slab, part] = jnp.where(chosen, bases[part], 0.0) + rows
 
 
 def params(limit=LIMIT):
@@ -396,7 +389,6 @@
 
 SMEM = pl.BlockSpec(memory_space=pltpu.SMEM)
 VMEM = pl.BlockSpec(memory_space=pltpu.VMEM)
-ANY = pl.BlockSpec(memory_space=pl.ANY)
 
 
 def exchange(value):
@@ -466,11 +458,13 @@
                 pl.BlockSpec((2, 2, part_rows, width), lambda step: (0, 0, step, 0)),
             ],
             out_specs=[
-                pl.BlockSpec((1, 8 * lead, part_rows), lambda step: (step, 0, 0)),
+                pl.BlockSpec((1, 6 * lead, part_rows), lambda step: (step, 0, 0)),
+                pl.BlockSpec((1, 2 * lead, part_rows), lambda step: (step, 0, 0)),
                 pl.BlockSpec((1, 4 * PACK, part_rows), lambda step: (step, 0, 0)),
             ],
             out_shape=[
-                jax.ShapeDtypeStruct((8, 8 * lead, part_rows), F32),
+                jax.ShapeDtypeStruct((8, 6 * lead, part_rows), F32),
+                jax.ShapeDtypeStruct((8, 2 * lead, part_rows), F32),
                 jax.ShapeDtypeStruct((8, 4 * PACK, part_rows), F32),
             ],
             compiler_params=params(LARGE),
@@ -480,7 +474,7 @@
     def summed(flows):
         return lax.psum_scatter(flows, "col", scatter_dimension=0, tiled=False)
 
-    spread, flows = chunk_terms(place)
+    early, late, flows = chunk_terms(place)
     turned = pl.pallas_call(
         coupling_kernel,
         in_specs=[SMEM, VMEM],
@@ -502,7 +496,7 @@
 
     def more(chunk, extra):
         place = jnp.stack([first, chunk]).astype(jnp.int32)
-        _, flows = chunk_terms(place)
+        flows = chunk_terms(place)[2]
         return pl.pallas_call(
             expand_kernel,
             in_specs=[SMEM, VMEM, VMEM, VMEM],
@@ -513,9 +507,10 @@
         )(place, inject, summed(flows), extra)
 
     extra = lax.fori_loop(1, chunks, more, jnp.zeros((4 * modes, part_rows), F32))
-    received, turned, marks, own_lead, spread, extra = lax.optimization_barrier(
-        (received, turned, marks, own_lead, spread, extra)
-    )
+    received, turned, marks, own_lead, early, extra = lax.optimization_barrier(
+        (received, turned, marks, own_lead, early, extra)
+    )
+    rows = exchange(early)
 
     top, bottom, flow_a, first_map = pl.pallas_call(
         pair_map_kernel,
@@ -530,16 +525,6 @@
         compiler_params=params(),
         name="pair_map",
     )(info, received, turned, marks)
-
-    spread = pl.pallas_call(
-        after_kernel,
-        in_specs=[ANY, ANY],
-        out_specs=ANY,
-        out_shape=jax.ShapeDtypeStruct(spread.shape, F32),
-        input_output_aliases={0: 0},
-        name="after_pair_map",
-    )(spread, bottom)
-    rows = exchange(spread)
 
     def turn(value, step):
         return lax.ppermute(
@@ -607,36 +592,24 @@
         jax.ShapeDtypeStruct((2, 32, size), F32),
     ]
     entry = local(entry_map_kernel, "entry_map", two_maps, info, prefix, inner_map, turned)
-    inner = local(
+    last = local(
         inflow_kernel,
         "inflow",
-        jax.ShapeDtypeStruct((8, 64, size), F32),
+        jax.ShapeDtypeStruct((8, 64 + 2 * lead, size), F32),
         info,
         own_lead,
         flow,
         *entry,
-    )
-    rows, inner, base = lax.optimization_barrier((rows, inner, base))
-
-    inner = exchange(inner)
-    arranged = [
-        jax.ShapeDtypeStruct((2, 2, 2, size, part_rows), BF16),
-        jax.ShapeDtypeStruct((2, 2, 2, size, part_rows), BF16),
-        jax.ShapeDtypeStruct((2, 2, 2, modes, part_rows), F32),
-    ]
-    arranged = local(
-        arrange_kernel, "arrange_rows", arranged, place, inject, rows, base, extra
-    )
-
-    shape = (2, 2, modes, part_rows)
-    left, right = pl.pallas_call(
-        state_kernel,
-        in_specs=[VMEM] * 4,
-        out_specs=[VMEM, VMEM],
-        out_shape=[jax.ShapeDtypeStruct(shape, F32), jax.ShapeDtypeStruct(shape, F32)],
-        compiler_params=params(),
-        name="states",
-    )(inner, *arranged)
+        late,
+    )
+    rows, base, last = lax.optimization_barrier((rows, base, last))
+    last = exchange(last)
+    last, rows, base, extra, inject = lax.optimization_barrier((last, rows, base, extra, inject))
+
+    shape = jax.ShapeDtypeStruct((2, 2, modes, part_rows), F32)
+    left, right = local(
+        state_kernel, "states", [shape, shape], place, inject, last, rows, base, extra
+    )
     return jnp.transpose(left, (0, 1, 3, 2)), jnp.transpose(right, (0, 1, 3, 2))
 
 

time: 153 us -> 153 us (level)
  blocking collectives: 0 us -> 29.5 us
  waiting for transfers between devices: 68.3 us -> 45.3 us
  starting transfers between devices: 25.7 us -> 21.3 us
  Pallas kernels: 35.7 us -> 33.4 us
    all_to_all x0 -> x1, blocking collectives: none -> 29.5 us  [exchange(): return lax.all_to_all(value, 'col', split_axis=0, concat_axis=0, tiled=True)]
    all_to_all x3 -> x2, waiting for transfers between devices: 33.4 us -> 19.9 us  [exchange(): return lax.all_to_all(value, 'col', split_axis=0, concat_axis=0, tiled=True)]
    reduce_scatter x1, waiting for transfers between devices: 12.4 us -> 2.83 us  [summed(): return lax.psum_scatter(flows, 'col', scatter_dimension=0, tiled=False)]
    all_to_all x3 -> x2, starting transfers between devices: 16.6 us -> 12.2 us  [exchange(): return lax.all_to_all(value, 'col', split_axis=0, concat_axis=0, tiled=True)]
    unnamed x26 -> x22, local copies, waits for them, and re-layouts: 4.2 us -> 4.31 us
  transfers between devices with their start and end apart: 13 -> 12, of which waited for: 11 -> 9; matrix products, arithmetic and copies ran while one was open for 1% -> 1% of each run, Pallas kernels for 16% -> 16%
where the time goes in v6:
time: 153 us; the launch traced here: 152 us
  waiting for transfers between devices  45.3 us (30%)
  Pallas kernels  33.4 us (22%)
  blocking collectives  29.5 us (19%)
  starting transfers between devices  21.3 us (14%)
  between operations  16.3 us (11%)
  local copies, waits for them, and re-layouts  4.48 us (3%)
    all_to_all x1, blocking collectives, exchange(): return lax.all_to_all(value, 'col', split_axis=0, concat_axis=0, tiled=True)  29.5 us
    all_to_all x2, waiting for transfers between devices, exchange(): return lax.all_to_all(value, 'col', split_axis=0, concat_axis=0, tiled=True)  19.9 us
    ppermute x6, waiting for transfers between devices, turn(): lax.ppermute(value, 'slab', [(slab, slab // 4 * 4 + (slab + step) % 4) fo...  15.7 us
    all_to_all x2, starting transfers between devices, exchange(): return lax.all_to_all(value, 'col', split_axis=0, concat_axis=0, tiled=True)  12.2 us
    pallas_call x7, Pallas kernels, local(): pl.pallas_call(kernel, in_specs=[SMEM] + [VMEM] * (len(args) - 1), out_sp...  11.4 us
    pallas_call x1, Pallas kernels, chunk_terms(): pl.pallas_call(spread_kernel, grid=(8,), in_specs=[whole(terms.shape), wh...  8.72 us
    pallas_call x1, Pallas kernels, on_device(): pl.pallas_call(interface_kernel, grid=(4,), in_specs=[SMEM, whole(inject....  6.67 us
    ppermute x3, waiting for transfers between devices, hop(): return lax.ppermute(value, ('slab', 'col'), pairs)  6.22 us
  transfers between devices with their start and end apart: 12, of which 9 were waited for; matrix products, arithmetic and copies ran while one was open for 1% of the time, Pallas kernels for 16%

profile of v6, /device:TPU:8, one launch (start us, length us, event | category | flops | bytes accessed | tf_op | source)
XLA Modules:
  0.0 151.7 jit_solution(18330750890621354128)
XLA Ops:
  8.6 6.7 %interface_terms.1 = f32[8,160,256]{2,1,0:T(8,128)} custom-call(s32[2]{0:T(128)} %pad_add_fusion.1.place_ref, s32[2,64]{1,0:T(2,128)} %inject_ref.3, f32[2,2,64,256]{3,2,1,0:T(8,128)} %bitcast.27, f32[2,2,2048,256]{3,2,1,0:T(8,128)} %g_ref.1, f32[2,2,2048,256]{3,2,1,0:T(8,128)} %g_ref.1), custom_call_target="tpu_custom_call" | custom-call | tf_op jit(solution)/shard_map/interface_terms/pallas_call | solution.py:419
  15.3 8.6 %all-to-all-start = ((f32[8,160,256]{2,1,0:T(8,128)}), f32[8,160,256]{2,1,0:T(8,128)S(1)}, u32[]{:S(2)}, u32[]{:S(2)}) async-start(f32[8,160,256]{2,1,0:T(8,128)} %interface_terms.1), calls=%async_computation.1 | async-start | bytes 2621440 | tf_op jit(solution)/shard_map/all_to_all | solution.py:395
  29.5 8.7 %spread_terms.2 = (f32[8,192,256]{2,1,0:T(8,128)}, f32[8,64,256]{2,1,0:T(8,128)}, f32[8,64,256]{2,1,0:T(8,128)}) custom-call(bf16[2,128,256]{2,1,0:T(8,128)(2,1)} %copy-done.8, bf16[2,128,256]{2,1,0:T(8,128)(2,1)} %copy-done.9, f32[2,2,2048,256]{3,2,1,0:T(8,128)} %g_ref.1), custom_call_target="tpu_custom_call" | custom-call | tf_op jit(solution)/shard_map/spread_terms/pallas_call | solution.py:452
  38.4 19.9 %all-to-all-done.recv_ref = f32[8,160,256]{2,1,0:T(8,128)S(1)} async-done(((f32[8,160,256]{2,1,0:T(8,128)}), f32[8,160,256]{2,1,0:T(8,128)S(1)}, u32[]{:S(2)}, u32[]{:S(2)}) %all-to-all-start) | async-done | bytes 1310752 | tf_op jit(solution)/shard_map/all_to_all | solution.py:395
  59.5 3.6 %all-to-all-start.1 = ((f32[8,192,256]{2,1,0:T(8,128)}), f32[8,192,256]{2,1,0:T(8,128)S(1)}, u32[]{:S(2)}, u32[]{:S(2)}) async-start(f32[8,192,256]{2,1,0:T(8,128)} %get-tuple-element.99), calls=%async_computation.2 | async-start | bytes 3145728 | tf_op jit(solution)/shard_map/all_to_all | solution.py:395
  63.7 1.3 copy-done.2
  65.0 2.8 %pair_map.1 = (f32[272,256]{1,0:T(8,128)S(1)}, f32[272,256]{1,0:T(8,128)S(1)}, f32[32,256]{1,0:T(8,128)S(1)}, f32[512,256]{1,0:T(8,128)S(1)}) custom-call(s32[4]{0:T(128)S(1)} %pad_add_fusion.2.team_ref.info_ref, f32[8,160,256]{2,1,0:T(8,128)S(1)} %copy-done.2, f32[2,512,256]{2,1,0:T(8,128)S(1)} %coupling_rows.1.x_ref, ...), custom_call_target="tpu_custom_call" | custom-call | tf_op jit(solution)/shard_map/pair_map/pallas_call | solution.py:515
  67.7 1.7 %collective-permute-start.2 = (f32[272,256]{1,0:T(8,128)S(1)}, f32[272,256]{1,0:T(8,128)S(1)}, u32[]{:S(2)}, u32[]{:S(2)}) collective-permute-start(f32[272,256]{1,0:T(8,128)S(1)} %get-tuple-element.105.refs_0_), channel_id=1, source_target_pairs={{0,16},{16,32},{32,48},{48,0},{64,80},{80,96},{96,112},{112,64},{1... | collective-permute-start | bytes 835592 | tf_op jit(solution)/shard_map/ppermute | solution.py:530
  69.8 1.7 %collective-permute-start = (f32[272,256]{1,0:T(8,128)S(1)}, f32[272,256]{1,0:T(8,128)S(1)}, u32[]{:S(2)}, u32[]{:S(2)}) collective-permute-start(f32[272,256]{1,0:T(8,128)S(1)} %get-tuple-element.105.refs_0_), channel_id=1, source_target_pairs={{0,48},{16,0},{32,16},{48,32},{64,112},{80,64},{96,80},{112,96},{1... | collective-permute-start | bytes 835592 | tf_op jit(solution)/shard_map/ppermute | solution.py:530
  71.9 5.5 %collective-permute-done.2.refs_6_ = f32[272,256]{1,0:T(8,128)S(1)} collective-permute-done((f32[272,256]{1,0:T(8,128)S(1)}, f32[272,256]{1,0:T(8,128)S(1)}, u32[]{:S(2)}, u32[]{:S(2)}) %collective-permute-start.2) | collective-permute-done | bytes 278560 | tf_op jit(solution)/shard_map/ppermute | solution.py:530
  77.3 1.6 %collective-permute-start.3 = (f32[272,256]{1,0:T(8,128)S(1)}, f32[272,256]{1,0:T(8,128)S(1)}, u32[]{:S(2)}, u32[]{:S(2)}) collective-permute-start(f32[272,256]{1,0:T(8,128)S(1)} %collective-permute-done.2.refs_6_), channel_id=1, source_target_pairs={{0,16},{16,32},{32,48},{48,0},{64,80},{80,96},{96,112},{112,64},{1... | collective-permute-start | bytes 835592 | tf_op jit(solution)/shard_map/ppermute | solution.py:530
  79.4 5.5 %collective-permute-done.refs_2_ = f32[272,256]{1,0:T(8,128)S(1)} collective-permute-done((f32[272,256]{1,0:T(8,128)S(1)}, f32[272,256]{1,0:T(8,128)S(1)}, u32[]{:S(2)}, u32[]{:S(2)}) %collective-permute-start) | collective-permute-done | bytes 278560 | tf_op jit(solution)/shard_map/ppermute | solution.py:530
  84.9 3.4 %collective-permute-done.3.refs_4_ = f32[272,256]{1,0:T(8,128)S(1)} collective-permute-done((f32[272,256]{1,0:T(8,128)S(1)}, f32[272,256]{1,0:T(8,128)S(1)}, u32[]{:S(2)}, u32[]{:S(2)}) %collective-permute-start.3) | collective-permute-done | bytes 278560 | tf_op jit(solution)/shard_map/ppermute | solution.py:530
  88.3 1.3 collective-permute-done.4.refs_5_
  89.6 1.7 %gather_maps.1 = (bf16[4,512,256]{2,1,0:T(8,128)(2,1)S(1)}, bf16[4,512,256]{2,1,0:T(8,128)(2,1)S(1)}, f32[4,32,256]{2,1,0:T(8,128)S(1)}, f32[32,256]{1,0:T(8,128)S(1)}) custom-call(s32[4]{0:T(128)S(1)} %pad_add_fusion.2.team_ref.info_ref, f32[32,256]{1,0:T(8,128)S(1)} %bitcast.22, f32[272,256]{1,0:T(8,128)S(1)} %get-tuple-element.105.refs_0_, ...), custom_call_target="tpu_custom_call" | custom-call | tf_op jit(solution)/shard_map/gather_maps/pallas_call | solution.py:544
  91.4 1.8 %collective-permute-start.6 = (f32[32,256]{1,0:T(8,128)S(1)}, f32[32,256]{1,0:T(8,128)S(1)}, u32[]{:S(2)}, u32[]{:S(2)}) collective-permute-start(f32[32,256]{1,0:T(8,128)S(1)} %get-tuple-element.107), channel_id=1, source_target_pairs={{0,64},{2,66},{4,68},{6,70},{8,200},{10,202},{12,204},{14,206},{16... | collective-permute-start | bytes 98312 | tf_op jit(solution)/shard_map/ppermute | solution.py:572
  93.1 3.2 %row_map.1 = (bf16[512,256]{1,0:T(8,128)(2,1)S(1)}, bf16[512,256]{1,0:T(8,128)(2,1)S(1)}, f32[32,256]{1,0:T(8,128)S(1)}, f32[544,256]{1,0:T(8,128)S(1)}) custom-call(s32[4]{0:T(128)S(1)} %pad_add_fusion.2.team_ref.info_ref, bf16[4,512,256]{2,1,0:T(8,128)(2,1)S(1)} %get-tuple-element.108.high_ref, bf16[4,512,256]{2,1,0:T(8,128)(2,1)S(1)} %get-tuple-element.109.low_ref, ...), custom_call_target="tpu_custom_call" | custom-call | tf_op jit(solution)/shard_map/row_map/pallas_call | solution.py:562
  98.6 1.7 %prefix_map.1 = (f32[544,256]{1,0:T(8,128)S(1)}, f32[544,256]{1,0:T(8,128)S(1)}) custom-call(s32[4]{0:T(128)S(1)} %pad_add_fusion.2.team_ref.info_ref, bf16[4,512,256]{2,1,0:T(8,128)(2,1)S(1)} %get-tuple-element.108.high_ref, bf16[4,512,256]{2,1,0:T(8,128)(2,1)S(1)} %get-tuple-element.109.low_ref, f32[4,32,256]{2,1,0:T(8,128)S(1)} %get-tuple-element.110.flow_ref, ...), custom_call_target="tpu_custom_call" | custom-call | tf_op jit(solution)/shard_map/prefix_map/pallas_call | solution.py:562
  100.3 2.3 %collective-permute-done.7.state_ref = f32[32,256]{1,0:T(8,128)S(1)} collective-permute-done((f32[32,256]{1,0:T(8,128)S(1)}, f32[32,256]{1,0:T(8,128)S(1)}, u32[]{:S(2)}, u32[]{:S(2)}) %collective-permute-start.7) | collective-permute-done | bytes 32800 | tf_op jit(solution)/shard_map/ppermute | solution.py:572
  103.4 1.7 %entry_map.1 = (bf16[2,512,256]{2,1,0:T(8,128)(2,1)S(1)}, bf16[2,512,256]{2,1,0:T(8,128)(2,1)S(1)}, f32[2,32,256]{2,1,0:T(8,128)S(1)}) custom-call(s32[4]{0:T(128)S(1)} %pad_add_fusion.2.team_ref.info_ref, f32[544,256]{1,0:T(8,128)S(1)} %get-tuple-element.122.prefix_ref, f32[544,256]{1,0:T(8,128)S(1)} %get-tuple-element.123.inner_ref, ...), custom_call_target="tpu_custom_call" | custom-call | tf_op jit(solution)/shard_map/entry_map/pallas_call | solution.py:562
  105.1 3.4 %collective-permute-done.8.state_ref = f32[32,256]{1,0:T(8,128)S(1)} collective-permute-done((f32[32,256]{1,0:T(8,128)S(1)}, f32[32,256]{1,0:T(8,128)S(1)}, u32[]{:S(2)}, u32[]{:S(2)}) %collective-permute-start.8) | collective-permute-done | bytes 32800 | tf_op jit(solution)/shard_map/ppermute | solution.py:572
  109.5 2.8 %reduce-scatter.3.cloned.1.call-done = f32[1,64,256]{2,1,0:T(8,128)} async-done(((f32[8,64,256]{2,1,0:T(8,128)}), f32[1,64,256]{2,1,0:T(8,128)}) %reduce-scatter.3.cloned.1.call-update) | async-done | bytes 65552 | tf_op jit(solution)/shard_map/reduce_scatter | solution.py:475
  112.3 29.5 %all_to_all.15.last_ref = f32[8,128,256]{2,1,0:T(8,128)S(1)} all-to-all(f32[8,128,256]{2,1,0:T(8,128)S(1)} %inflow.1), channel_id=1, replica_groups=mesh['slab'=16,'col'=8,'energy'=2] {'col'}, dimensions={0} | all-to-all | bytes 2097152 | tf_op jit(solution)/shard_map/all_to_all | solution.py:395
  141.8 2.5 %states.1 = (f32[2,2,64,256]{3,2,1,0:T(8,128)}, f32[2,2,64,256]{3,2,1,0:T(8,128)}) custom-call(s32[2]{0:T(128)S(1)} %copy-done.11, s32[2,64]{1,0:T(2,128)S(1)} %get-tuple-element.272, f32[8,128,256]{2,1,0:T(8,128)S(1)} %all_to_all.15.last_ref, f32[8,192,256]{2,1,0:T(8,128)S(1)} %all-to-all-done.1.rows_ref, f32[64,256]{1,0:T(8,128)S(1)} %bitcast.26, ...), custom_call_target="tpu_custom_call" | custom-call | tf_op jit(solution)/shard_map/states/pallas_call | solution.py:562
  (49 shorter events, 12.6 us)
Async XLA Ops:
  8.0 30.3 %copy-start = (f32[2,2,256,64]{2,3,1,0:T(8,128)S(1)}, f32[2,2,256,64]{2,3,1,0:T(8,128)}, u32[]{:S(2)}) copy-start(f32[2,2,256,64]{2,3,1,0:T(8,128)} %param.11) | copy-start | bytes 786436
  15.3 8.6 %copy-start.13 = (s32[2,64]{1,0:T(2,128)S(1)}, s32[2,64]{1,0:T(2,128)}, u32[]{:S(2)}) copy-start(s32[2,64]{1,0:T(2,128)} %inject_ref.3) | copy-start | bytes 1540
  15.3 10.1 %copy-start.11 = (s32[2]{0:T(128)S(1)}, s32[2]{0:T(128)}, u32[]{:S(2)}) copy-start(s32[2]{0:T(128)} %pad_add_fusion.1.place_ref) | copy-start | bytes 28
  15.3 10.1 %copy-start.12 = (f32[2,2,256,64]{2,3,1,0:T(8,128)S(1)}, f32[2,2,256,64]{2,3,1,0:T(8,128)}, u32[]{:S(2)}) copy-start(f32[2,2,256,64]{2,3,1,0:T(8,128)} %param.9) | copy-start | bytes 786436
  15.3 43.0 %all-to-all-start = ((f32[8,160,256]{2,1,0:T(8,128)}), f32[8,160,256]{2,1,0:T(8,128)S(1)}, u32[]{:S(2)}, u32[]{:S(2)}) async-start(f32[8,160,256]{2,1,0:T(8,128)} %interface_terms.1), calls=%async_computation.1 | async-start | bytes 2621440 | tf_op jit(solution)/shard_map/all_to_all | solution.py:395
  26.5 0.7 copy-start.8
  27.2 2.3 %copy-start.9 = (bf16[2,128,256]{2,1,0:T(8,128)(2,1)}, bf16[2,128,256]{2,1,0:T(8,128)(2,1)S(1)}, u32[]{:S(2)}) copy-start(bf16[2,128,256]{2,1,0:T(8,128)(2,1)S(1)} %get-tuple-element.96.low_ref) | copy-start | bytes 393220
  27.4 1.2 copy-start.6
  58.3 1.1 copy-start.1
  59.5 52.8 %all-to-all-start.1 = ((f32[8,192,256]{2,1,0:T(8,128)}), f32[8,192,256]{2,1,0:T(8,128)S(1)}, u32[]{:S(2)}, u32[]{:S(2)}) async-start(f32[8,192,256]{2,1,0:T(8,128)} %get-tuple-element.99), calls=%async_computation.2 | async-start | bytes 3145728 | tf_op jit(solution)/shard_map/all_to_all | solution.py:395
  63.1 49.2 %reduce-scatter.3.cloned.1.call-start = ((), (), s32[]{:S(2)}) async-start(), calls=%async_computation.5 | async-start | bytes 589824 | tf_op jit(solution)/shard_map/reduce_scatter | solution.py:475
  63.6 1.3 copy-start.2
  67.7 9.6 %collective-permute-start.2 = (f32[272,256]{1,0:T(8,128)S(1)}, f32[272,256]{1,0:T(8,128)S(1)}, u32[]{:S(2)}, u32[]{:S(2)}) collective-permute-start(f32[272,256]{1,0:T(8,128)S(1)} %get-tuple-element.105.refs_0_), channel_id=1, source_target_pairs={{0,16},{16,32},{32,48},{48,0},{64,80},{80,96},{96,112},{112,64},{1... | collective-permute-start | bytes 835592 | tf_op jit(solution)/shard_map/ppermute | solution.py:530
  69.4 9.6 %collective-permute-start.1 = (f32[272,256]{1,0:T(8,128)S(1)}, f32[272,256]{1,0:T(8,128)S(1)}, u32[]{:S(2)}, u32[]{:S(2)}) collective-permute-start(f32[272,256]{1,0:T(8,128)S(1)} %get-tuple-element.106.refs_1_), channel_id=1, source_target_pairs={{0,48},{16,0},{32,16},{48,32},{64,112},{80,64},{96,80},{112,96},{1... | collective-permute-start | bytes 835592 | tf_op jit(solution)/shard_map/ppermute | solution.py:530
  69.8 15.1 %collective-permute-start = (f32[272,256]{1,0:T(8,128)S(1)}, f32[272,256]{1,0:T(8,128)S(1)}, u32[]{:S(2)}, u32[]{:S(2)}) collective-permute-start(f32[272,256]{1,0:T(8,128)S(1)} %get-tuple-element.105.refs_0_), channel_id=1, source_target_pairs={{0,48},{16,0},{32,16},{48,32},{64,112},{80,64},{96,80},{112,96},{1... | collective-permute-start | bytes 835592 | tf_op jit(solution)/shard_map/ppermute | solution.py:530
  71.5 13.4 %collective-permute-start.5 = (f32[272,256]{1,0:T(8,128)S(1)}, f32[272,256]{1,0:T(8,128)S(1)}, u32[]{:S(2)}, u32[]{:S(2)}) collective-permute-start(f32[272,256]{1,0:T(8,128)S(1)} %get-tuple-element.106.refs_1_), channel_id=1, source_target_pairs={{0,16},{16,32},{32,48},{48,0},{64,80},{80,96},{96,112},{112,64},{1... | collective-permute-start | bytes 835592 | tf_op jit(solution)/shard_map/ppermute | solution.py:530
  77.3 11.0 %collective-permute-start.3 = (f32[272,256]{1,0:T(8,128)S(1)}, f32[272,256]{1,0:T(8,128)S(1)}, u32[]{:S(2)}, u32[]{:S(2)}) collective-permute-start(f32[272,256]{1,0:T(8,128)S(1)} %collective-permute-done.2.refs_6_), channel_id=1, source_target_pairs={{0,16},{16,32},{32,48},{48,0},{64,80},{80,96},{96,112},{112,64},{1... | collective-permute-start | bytes 835592 | tf_op jit(solution)/shard_map/ppermute | solution.py:530
  79.0 10.7 %collective-permute-start.4 = (f32[272,256]{1,0:T(8,128)S(1)}, f32[272,256]{1,0:T(8,128)S(1)}, u32[]{:S(2)}, u32[]{:S(2)}) collective-permute-start(f32[272,256]{1,0:T(8,128)S(1)} %collective-permute-done.1.refs_3_), channel_id=1, source_target_pairs={{0,48},{16,0},{32,16},{48,32},{64,112},{80,64},{96,80},{112,96},{1... | collective-permute-start | bytes 835592 | tf_op jit(solution)/shard_map/ppermute | solution.py:530
  91.4 5.4 %collective-permute-start.6 = (f32[32,256]{1,0:T(8,128)S(1)}, f32[32,256]{1,0:T(8,128)S(1)}, u32[]{:S(2)}, u32[]{:S(2)}) collective-permute-start(f32[32,256]{1,0:T(8,128)S(1)} %get-tuple-element.107), channel_id=1, source_target_pairs={{0,64},{2,66},{4,68},{6,70},{8,200},{10,202},{12,204},{14,206},{16... | collective-permute-start | bytes 98312 | tf_op jit(solution)/shard_map/ppermute | solution.py:572
  97.5 5.2 %collective-permute-start.7 = (f32[32,256]{1,0:T(8,128)S(1)}, f32[32,256]{1,0:T(8,128)S(1)}, u32[]{:S(2)}, u32[]{:S(2)}) collective-permute-start(f32[32,256]{1,0:T(8,128)S(1)} %row_step.2), channel_id=1, source_target_pairs={{0,64},{2,66},{4,68},{6,70},{8,200},{10,202},{12,204},{14,206},{16... | collective-permute-start | bytes 98312 | tf_op jit(solution)/shard_map/ppermute | solution.py:572
  100.3 8.2 %copy-start.7 = (f32[8,64,256]{2,1,0:T(8,128)S(1)}, f32[8,64,256]{2,1,0:T(8,128)}, u32[]{:S(2)}) copy-start(f32[8,64,256]{2,1,0:T(8,128)} %get-tuple-element.127.spread_ref) | copy-start | bytes 1572868
  103.4 5.2 %collective-permute-start.8 = (f32[32,256]{1,0:T(8,128)S(1)}, f32[32,256]{1,0:T(8,128)S(1)}, u32[]{:S(2)}, u32[]{:S(2)}) collective-permute-start(f32[32,256]{1,0:T(8,128)S(1)} %row_step.3), channel_id=1, source_target_pairs={{0,64},{2,66},{4,68},{6,70},{8,200},{10,202},{12,204},{14,206},{16... | collective-permute-start | bytes 98312 | tf_op jit(solution)/shard_map/ppermute | solution.py:572
  112.3 29.5 %copy-start.10 = (f32[1,64,256]{2,1,0:T(8,128)S(1)}, f32[1,64,256]{2,1,0:T(8,128)}, u32[]{:S(2)}) copy-start(f32[1,64,256]{2,1,0:T(8,128)} %reduce-scatter.3.cloned.1.call-done) | copy-start | bytes 196612
Sparse Core Ops, SparseCore 1:
  66.0 46.2 reduce-scatter.2

commit v7 on v6

--- a/solution.py
+++ b/solution.py
@@ -10,6 +10,7 @@
 LIMIT = 24 * 1024 * 1024
 LARGE = 56 * 1024 * 1024
 PACK = 16
+NEAR = (1, 7, 2)
 
 
 def split(value):
@@ -151,25 +152,31 @@
                 low_ref[slab, start : start + PACK, :] = mm(pick, low).astype(BF16)
 
 
-def spread_kernel(high_ref, low_ref, g_ref, early_ref, late_ref, flow_ref):
+def spread_kernel(order_ref, high_ref, low_ref, g_ref, *refs):
+    early_refs, (late_ref, flow_ref) = refs[:8], refs[8:]
+    step = pl.program_id(0)
     lead = g_ref.shape[3] // 8
     total = [0.0] * 4
+    pieces = []
     for slab in range(2):
         parts = (high_ref[slab], low_ref[slab])
         real = mm3(parts, split(g_ref[slab, 0]), True)
         imag = mm3(parts, split(g_ref[slab, 1]), True)
         for sweep in range(2):
-            base = sweep * lead
-            place = slab * 4 * lead + sweep * 2 * lead
-            out_ref = early_ref
-            if slab == 1 and sweep == 1:
-                out_ref, place = late_ref, 0
-            out_ref[0, place : place + lead, :] = real[base : base + lead]
-            out_ref[0, place + lead : place + 2 * lead, :] = imag[base : base + lead]
+            span = slice(sweep * lead, (sweep + 1) * lead)
+            pieces += [real[span], imag[span]]
             one = 2 * lead + 2 * sweep * PACK
             two, three = one + PACK, one + 2 * PACK
             total[2 * sweep] += real[one:two] - imag[two:three]
             total[2 * sweep + 1] += real[two:three] + imag[one:two]
+    early = jnp.concatenate(pieces[:6], axis=0)
+    for away in range(8):
+
+        @pl.when(step == away)
+        def _(away=away):
+            early_refs[away][...] = early
+
+    late_ref[0] = jnp.concatenate(pieces[6:], axis=0)
     for item in range(4):
         flow_ref[0, item * PACK : (item + 1) * PACK, :] = total[item]
 
@@ -341,11 +348,17 @@
 
 
 def state_kernel(
-    place_ref, inject_ref, last_ref, rows_ref, base_ref, extra_ref, left_ref, right_ref
+    place_ref, inject_ref, last_ref, base_ref, extra_ref, *refs
 ):
+    piece_refs, (left_ref, right_ref, rows_ref) = refs[:8], refs[8:]
     modes = inject_ref.shape[1]
     width = base_ref.shape[1]
-    lead = rows_ref.shape[1] // 6
+    lead = piece_refs[0].shape[0] // 6
+    for away in range(8):
+        source = lax.rem(place_ref[2] + 8 - away, 8)
+        for kind in range(6):
+            span = pl.ds(pl.multiple_of(source * lead, lead), lead)
+            rows_ref[kind, span, :] = piece_refs[away][kind * lead : (kind + 1) * lead, :]
     for sweep, out_ref in enumerate((left_ref, right_ref)):
         target = jnp.broadcast_to(
             inject_ref[sweep : sweep + 1, :].astype(F32), (width, modes)
@@ -369,7 +382,7 @@
                 if slab == 1 and sweep == 1:
                     matrix = stacked(last_ref, 64 + part * lead, lead)
                 else:
-                    matrix = stacked(rows_ref, (4 * slab + kind) * lead, lead)
+                    matrix = rows_ref[4 * slab + kind]
                 by.append(mm3(parts, split(matrix)))
             value = combined(by[0], by[1])
             chosen = target == (place_ref[0] + slab).astype(F32)
@@ -408,7 +421,7 @@
     team = col_index // 4
     member = col_index % 4
     first = slab_index * 2
-    place = jnp.stack([first, jnp.zeros_like(first)]).astype(jnp.int32)
+    place = jnp.stack([first, jnp.zeros_like(first), col_index]).astype(jnp.int32)
     position = jnp.where(team == 0, slab_index, slabs - 1 - slab_index)
     info = jnp.stack([team, position // 4, position % 4, slab_index % 4]).astype(jnp.int32)
     stack = 2 * (lead + 2 * modes)
@@ -439,6 +452,8 @@
     sent, inject_after = lax.optimization_barrier((sent, inject))
     received = exchange(sent)
 
+    ring = (col_index + jnp.arange(8, dtype=jnp.int32)) % 8
+
     def chunk_terms(place):
         terms = jax.ShapeDtypeStruct((2, 2 * lead + 4 * PACK, width), BF16)
         high, low = pl.pallas_call(
@@ -451,30 +466,34 @@
         )(place, inject_after, sources)
         return pl.pallas_call(
             spread_kernel,
-            grid=(8,),
-            in_specs=[
-                whole(terms.shape),
-                whole(terms.shape),
-                pl.BlockSpec((2, 2, part_rows, width), lambda step: (0, 0, step, 0)),
-            ],
-            out_specs=[
-                pl.BlockSpec((1, 6 * lead, part_rows), lambda step: (step, 0, 0)),
-                pl.BlockSpec((1, 2 * lead, part_rows), lambda step: (step, 0, 0)),
-                pl.BlockSpec((1, 4 * PACK, part_rows), lambda step: (step, 0, 0)),
-            ],
-            out_shape=[
-                jax.ShapeDtypeStruct((8, 6 * lead, part_rows), F32),
-                jax.ShapeDtypeStruct((8, 2 * lead, part_rows), F32),
-                jax.ShapeDtypeStruct((8, 4 * PACK, part_rows), F32),
+            grid_spec=pltpu.PrefetchScalarGridSpec(
+                num_scalar_prefetch=1,
+                grid=(8,),
+                in_specs=[
+                    whole(terms.shape),
+                    whole(terms.shape),
+                    pl.BlockSpec(
+                        (2, 2, part_rows, width), lambda step, order: (0, 0, order[step], 0)
+                    ),
+                ],
+                out_specs=[whole((6 * lead, part_rows))] * 8
+                + [
+                    pl.BlockSpec((1, rows, part_rows), lambda step, order: (order[step], 0, 0))
+                    for rows in (2 * lead, 4 * PACK)
+                ],
+            ),
+            out_shape=[jax.ShapeDtypeStruct((6 * lead, part_rows), F32)] * 8
+            + [
+                jax.ShapeDtypeStruct((8, rows, part_rows), F32) for rows in (2 * lead, 4 * PACK)
             ],
             compiler_params=params(LARGE),
             name="spread_terms",
-        )(high, low, diag_inverse)
+        )(ring, high, low, diag_inverse)
 
     def summed(flows):
         return lax.psum_scatter(flows, "col", scatter_dimension=0, tiled=False)
 
-    early, late, flows = chunk_terms(place)
+    *early, late, flows = chunk_terms(place)
     turned = pl.pallas_call(
         coupling_kernel,
         in_specs=[SMEM, VMEM],
@@ -496,7 +515,7 @@
 
     def more(chunk, extra):
         place = jnp.stack([first, chunk]).astype(jnp.int32)
-        flows = chunk_terms(place)[2]
+        flows = chunk_terms(place)[9]
         return pl.pallas_call(
             expand_kernel,
             in_specs=[SMEM, VMEM, VMEM, VMEM],
@@ -510,7 +529,11 @@
     received, turned, marks, own_lead, early, extra = lax.optimization_barrier(
         (received, turned, marks, own_lead, early, extra)
     )
-    rows = exchange(early)
+
+    def further(away):
+        return lax.ppermute(early[away], "col", [(col, (col + away) % 8) for col in range(8)])
+
+    rows = [early[0]] + [further(away) for away in range(1, 8)]
 
     top, bottom, flow_a, first_map = pl.pallas_call(
         pair_map_kernel,
@@ -535,6 +558,9 @@
     before_bottom, after_top = turn(bottom, 1), turn(top, -1)
     across_top, across_bottom = turn(before_top, 1), turn(after_bottom, -1)
     pieces = (after_top, after_bottom, across_top, across_bottom, before_top, before_bottom)
+    pieces, near = lax.optimization_barrier((pieces, [rows[away] for away in NEAR]))
+    for away, value in zip(NEAR, near):
+        rows[away] = value
     row_maps = [
         jax.ShapeDtypeStruct((4, 2 * size, size), BF16),
         jax.ShapeDtypeStruct((4, 2 * size, size), BF16),
@@ -607,9 +633,15 @@
     last, rows, base, extra, inject = lax.optimization_barrier((last, rows, base, extra, inject))
 
     shape = jax.ShapeDtypeStruct((2, 2, modes, part_rows), F32)
-    left, right = local(
-        state_kernel, "states", [shape, shape], place, inject, last, rows, base, extra
-    )
+    left, right = pl.pallas_call(
+        state_kernel,
+        in_specs=[SMEM] + [VMEM] * 12,
+        out_specs=[VMEM, VMEM],
+        out_shape=[shape, shape],
+        scratch_shapes=[pltpu.VMEM((6, size, part_rows), F32)],
+        compiler_params=params(),
+        name="states",
+    )(place, inject, last, base, extra, *rows)
     return jnp.transpose(left, (0, 1, 3, 2)), jnp.transpose(right, (0, 1, 3, 2))
 
 

time: 153 us -> 164 us (1.072)
  starting transfers between devices: 21.3 us -> 26.9 us
  blocking collectives: 29.5 us -> 32.9 us
  waiting for transfers between devices: 45.3 us -> 48 us
  local copies, waits for them, and re-layouts: 4.48 us -> 2.78 us
    ppermute x0 -> x7, waiting for transfers between devices: none -> 24.1 us  [further(): lax.ppermute(early[away], 'col', [(col, (col + away) % 8) for col in rang...]
    ppermute x6, waiting for transfers between devices: 15.7 us -> 0.02 us  [turn(): lax.ppermute(value, 'slab', [(slab, slab // 4 * 4 + (slab + step) % 4) fo...]
    ppermute x0 -> x7, starting transfers between devices: none -> 8.43 us  [further(): lax.ppermute(early[away], 'col', [(col, (col + away) % 8) for col in rang...]
    all_to_all x2 -> x1, starting transfers between devices: 12.2 us -> 8.61 us  [exchange(): return lax.all_to_all(value, 'col', split_axis=0, concat_axis=0, tiled=True)]
    pallas_call x1 -> x2, Pallas kernels: 8.72 us -> 12.3 us  [the longest x1 9.88 us: chunk_terms(): pl.pallas_call(spread_kernel, grid_spec=pltpu.PrefetchScalarGridSpec(num_...]
    all_to_all x1, blocking collectives: 29.5 us -> 32.9 us  [exchange(): return lax.all_to_all(value, 'col', split_axis=0, concat_axis=0, tiled=True)]
    all_to_all x2 -> x1, waiting for transfers between devices: 19.9 us -> 17 us  [exchange(): return lax.all_to_all(value, 'col', split_axis=0, concat_axis=0, tiled=True)]
    reduce_scatter x1, waiting for transfers between devices: 2.83 us -> 0.03 us  [summed(): return lax.psum_scatter(flows, 'col', scatter_dimension=0, tiled=False)]
  transfers between devices with their start and end apart: 12 -> 18, of which waited for: 9 -> 7; matrix products, arithmetic and copies ran while one was open for 1% -> 1% of each run, Pallas kernels for 16% -> 16%
where the time goes in v7:
time: 164 us
  waiting for transfers between devices  48 us (29%)
  Pallas kernels  34.5 us (21%)
  blocking collectives  32.9 us (20%)
  starting transfers between devices  26.9 us (16%)
  between operations  16.4 us (10%)
  local copies, waits for them, and re-layouts  2.78 us (2%)
  other arithmetic  2.09 us (1%)
    all_to_all x1, blocking collectives, exchange(): return lax.all_to_all(value, 'col', split_axis=0, concat_axis=0, tiled=True)  32.9 us
    ppermute x7, waiting for transfers between devices, further(): lax.ppermute(early[away], 'col', [(col, (col + away) % 8) for col in rang...  24.1 us
    all_to_all x1, waiting for transfers between devices, exchange(): return lax.all_to_all(value, 'col', split_axis=0, concat_axis=0, tiled=True)  17 us
    pallas_call x1, Pallas kernels, chunk_terms(): pl.pallas_call(spread_kernel, grid_spec=pltpu.PrefetchScalarGridSpec(num_...  9.88 us
    pallas_call x6, Pallas kernels, local(): pl.pallas_call(kernel, in_specs=[SMEM] + [VMEM] * (len(args) - 1), out_sp...  8.94 us
    all_to_all x1, starting transfers between devices, exchange(): return lax.all_to_all(value, 'col', split_axis=0, concat_axis=0, tiled=True)  8.61 us
    ppermute x7, starting transfers between devices, further(): lax.ppermute(early[away], 'col', [(col, (col + away) % 8) for col in rang...  8.43 us
    ppermute x6, starting transfers between devices, turn(): lax.ppermute(value, 'slab', [(slab, slab // 4 * 4 + (slab + step) % 4) fo...  7.06 us
  transfers between devices with their start and end apart: 18, of which 7 were waited for; matrix products, arithmetic and copies ran while one was open for 1% of the time, Pallas kernels for 16%

profile of v7, /device:TPU:8, one launch (start us, length us, event | category | flops | bytes accessed | tf_op | source)
XLA Modules:
  0.0 163.7 jit_solution(10859565951101788420)
XLA Ops:
  8.6 6.7 %interface_terms.1 = f32[8,160,256]{2,1,0:T(8,128)} custom-call(s32[3]{0:T(128)} %pad_add_fusion.1.place_ref, s32[2,64]{1,0:T(2,128)} %inject_ref.3, f32[2,2,64,256]{3,2,1,0:T(8,128)} %bitcast.28, f32[2,2,2048,256]{3,2,1,0:T(8,128)} %g_ref.1, f32[2,2,2048,256]{3,2,1,0:T(8,128)} %g_ref.1), custom_call_target="tpu_custom_call" | custom-call | tf_op jit(solution)/shard_map/interface_terms/pallas_call | solution.py:432
  15.3 8.6 %all-to-all-start = ((f32[8,160,256]{2,1,0:T(8,128)}), f32[8,160,256]{2,1,0:T(8,128)S(1)}, u32[]{:S(2)}, u32[]{:S(2)}) async-start(f32[8,160,256]{2,1,0:T(8,128)} %interface_terms.1), calls=%async_computation.1 | async-start | bytes 2621440 | tf_op jit(solution)/shard_map/all_to_all | solution.py:408
  28.5 9.9 %spread_terms.2 = (f32[192,256]{1,0:T(8,128)}, f32[192,256]{1,0:T(8,128)}, f32[192,256]{1,0:T(8,128)}, f32[192,256]{1,0:T(8,128)}, f32[192,256]{1,0:T(8,128)}, /...) custom-call(s32[8]{0:T(128)} %and_select_fusion.1.order_ref, ...), custom_call_target="tpu_custom_call" | custom-call | tf_op jit(solution)/shard_map/spread_terms/pallas_call | solution.py:467
  39.2 1.2 copy-done.4
  41.5 17.0 %all-to-all-done.recv_ref = f32[8,160,256]{2,1,0:T(8,128)S(1)} async-done(((f32[8,160,256]{2,1,0:T(8,128)}), f32[8,160,256]{2,1,0:T(8,128)S(1)}, u32[]{:S(2)}, u32[]{:S(2)}) %all-to-all-start) | async-done | bytes 1310752 | tf_op jit(solution)/shard_map/all_to_all | solution.py:408
  58.5 2.8 %pair_map.1 = (f32[272,256]{1,0:T(8,128)S(1)}, f32[272,256]{1,0:T(8,128)S(1)}, f32[32,256]{1,0:T(8,128)S(1)}, f32[512,256]{1,0:T(8,128)S(1)}) custom-call(s32[4]{0:T(128)S(1)} %pad_add_fusion.2.team_ref.info_ref, f32[8,160,256]{2,1,0:T(8,128)S(1)} %all-to-all-done.recv_ref, f32[2,512,256]{2,1,0:T(8,128)S(1)} %coupling_rows.1.x_ref, ...), custom_call_target="tpu_custom_call" | custom-call | tf_op jit(solution)/shard_map/pair_map/pallas_call | solution.py:538
  61.3 1.6 collective-permute-start.2
  63.9 2.8 %collective-permute-start.7 = (f32[192,256]{1,0:T(8,128)S(1)}, f32[192,256]{1,0:T(8,128)S(1)}, u32[]{:S(2)}, u32[]{:S(2)}) collective-permute-start(f32[192,256]{1,0:T(8,128)S(1)} %copy-done.15), channel_id=1, source_target_pairs={{0,14},{2,0},{4,2},{6,4},{8,6},{10,8},{12,10},{14,12},{1,15},{3,1}... | collective-permute-start | bytes 589832 | tf_op jit(solution)/shard_map/ppermute | solution.py:534
  66.7 1.7 %collective-permute-start = (f32[272,256]{1,0:T(8,128)S(1)}, f32[272,256]{1,0:T(8,128)S(1)}, u32[]{:S(2)}, u32[]{:S(2)}) collective-permute-start(f32[272,256]{1,0:T(8,128)S(1)} %get-tuple-element.152.refs_0_), channel_id=1, source_target_pairs={{0,48},{16,0},{32,16},{48,32},{64,112},{80,64},{96,80},{112,96},{1... | collective-permute-start | bytes 835592 | tf_op jit(solution)/shard_map/ppermute | solution.py:553
  68.3 3.2 %collective-permute-done.6.refs_1_ = f32[192,256]{1,0:T(8,128)S(1)} collective-permute-done((f32[192,256]{1,0:T(8,128)S(1)}, f32[192,256]{1,0:T(8,128)S(1)}, u32[]{:S(2)}, u32[]{:S(2)}) %collective-permute-start.6) | collective-permute-done | bytes 196640 | tf_op jit(solution)/shard_map/ppermute | solution.py:534
  71.5 1.3 collective-permute-start.5
  73.6 1.3 collective-permute-start.4
  74.9 15.4 %collective-permute-done.8.refs_2_ = f32[192,256]{1,0:T(8,128)S(1)} collective-permute-done((f32[192,256]{1,0:T(8,128)S(1)}, f32[192,256]{1,0:T(8,128)S(1)}, u32[]{:S(2)}, u32[]{:S(2)}) %collective-permute-start.8) | collective-permute-done | bytes 196640 | tf_op jit(solution)/shard_map/ppermute | solution.py:534
  90.4 5.1 %collective-permute-start.11 = (f32[192,256]{1,0:T(8,128)}, f32[192,256]{1,0:T(8,128)S(1)}, u32[]{:S(2)}, u32[]{:S(2)}) collective-permute-start(f32[192,256]{1,0:T(8,128)} %get-tuple-element.161), channel_id=1, source_target_pairs={{0,10},{2,12},{4,14},{6,0},{8,2},{10,4},{12,6},{14,8},{1,11},{3,13... | collective-permute-start | bytes 589832 | tf_op jit(solution)/shard_map/ppermute | solution.py:534
  95.5 1.7 %gather_maps.1 = (bf16[4,512,256]{2,1,0:T(8,128)(2,1)S(1)}, bf16[4,512,256]{2,1,0:T(8,128)(2,1)S(1)}, f32[4,32,256]{2,1,0:T(8,128)S(1)}, f32[32,256]{1,0:T(8,128)S(1)}) custom-call(s32[4]{0:T(128)S(1)} %pad_add_fusion.2.team_ref.info_ref, f32[32,256]{1,0:T(8,128)S(1)} %bitcast.23, f32[272,256]{1,0:T(8,128)S(1)} %get-tuple-element.152.refs_0_, ...), custom_call_target="tpu_custom_call" | custom-call | tf_op jit(solution)/shard_map/gather_maps/pallas_call | solution.py:570
  97.2 1.6 %collective-permute-start.13 = (f32[32,256]{1,0:T(8,128)S(1)}, f32[32,256]{1,0:T(8,128)S(1)}, u32[]{:S(2)}, u32[]{:S(2)}) collective-permute-start(f32[32,256]{1,0:T(8,128)S(1)} %get-tuple-element.172), channel_id=1, source_target_pairs={{0,64},{2,66},{4,68},{6,70},{8,200},{10,202},{12,204},{14,206},{16... | collective-permute-start | bytes 98312 | tf_op jit(solution)/shard_map/ppermute | solution.py:598
  98.9 3.2 %row_map.1 = (bf16[512,256]{1,0:T(8,128)(2,1)S(1)}, bf16[512,256]{1,0:T(8,128)(2,1)S(1)}, f32[32,256]{1,0:T(8,128)S(1)}, f32[544,256]{1,0:T(8,128)S(1)}) custom-call(s32[4]{0:T(128)S(1)} %pad_add_fusion.2.team_ref.info_ref, bf16[4,512,256]{2,1,0:T(8,128)(2,1)S(1)} %get-tuple-element.173.high_ref, bf16[4,512,256]{2,1,0:T(8,128)(2,1)S(1)} %get-tuple-element.174.low_ref, ...), custom_call_target="tpu_custom_call" | custom-call | tf_op jit(solution)/shard_map/row_map/pallas_call | solution.py:588
  104.3 1.7 %prefix_map.1 = (f32[544,256]{1,0:T(8,128)S(1)}, f32[544,256]{1,0:T(8,128)S(1)}) custom-call(s32[4]{0:T(128)S(1)} %pad_add_fusion.2.team_ref.info_ref, bf16[4,512,256]{2,1,0:T(8,128)(2,1)S(1)} %get-tuple-element.173.high_ref, bf16[4,512,256]{2,1,0:T(8,128)(2,1)S(1)} %get-tuple-element.174.low_ref, f32[4,32,256]{2,1,0:T(8,128)S(1)} %get-tuple-element.175.flow_ref, ...), custom_call_target="tpu_custom_call" | custom-call | tf_op jit(solution)/shard_map/prefix_map/pallas_call | solution.py:588
  106.0 2.5 %collective-permute-done.14.state_ref = f32[32,256]{1,0:T(8,128)S(1)} collective-permute-done((f32[32,256]{1,0:T(8,128)S(1)}, f32[32,256]{1,0:T(8,128)S(1)}, u32[]{:S(2)}, u32[]{:S(2)}) %collective-permute-start.14) | collective-permute-done | bytes 32800 | tf_op jit(solution)/shard_map/ppermute | solution.py:598
  109.3 1.7 %entry_map.1 = (bf16[2,512,256]{2,1,0:T(8,128)(2,1)S(1)}, bf16[2,512,256]{2,1,0:T(8,128)(2,1)S(1)}, f32[2,32,256]{2,1,0:T(8,128)S(1)}) custom-call(s32[4]{0:T(128)S(1)} %pad_add_fusion.2.team_ref.info_ref, f32[544,256]{1,0:T(8,128)S(1)} %get-tuple-element.187.prefix_ref, f32[544,256]{1,0:T(8,128)S(1)} %get-tuple-element.188.inner_ref, ...), custom_call_target="tpu_custom_call" | custom-call | tf_op jit(solution)/shard_map/entry_map/pallas_call | solution.py:588
  111.0 3.4 %collective-permute-done.15.state_ref = f32[32,256]{1,0:T(8,128)S(1)} collective-permute-done((f32[32,256]{1,0:T(8,128)S(1)}, f32[32,256]{1,0:T(8,128)S(1)}, u32[]{:S(2)}, u32[]{:S(2)}) %collective-permute-start.15) | collective-permute-done | bytes 32800 | tf_op jit(solution)/shard_map/ppermute | solution.py:598
  115.4 5.5 %collective-permute-done.12.refs_6_ = f32[192,256]{1,0:T(8,128)S(1)} collective-permute-done((f32[192,256]{1,0:T(8,128)S(1)}, f32[192,256]{1,0:T(8,128)S(1)}, u32[]{:S(2)}, u32[]{:S(2)}) %collective-permute-start.12) | collective-permute-done | bytes 196640 | tf_op jit(solution)/shard_map/ppermute | solution.py:534
  120.9 32.9 %all_to_all.10.last_ref = f32[8,128,256]{2,1,0:T(8,128)S(1)} all-to-all(f32[8,128,256]{2,1,0:T(8,128)S(1)} %inflow.1), channel_id=1, replica_groups=mesh['slab'=16,'col'=8,'energy'=2] {'col'}, dimensions={0} | all-to-all | bytes 2097152 | tf_op jit(solution)/shard_map/all_to_all | solution.py:408
  153.8 2.4 %states.1 = (f32[2,2,64,256]{3,2,1,0:T(8,128)}, f32[2,2,64,256]{3,2,1,0:T(8,128)}) custom-call(s32[3]{0:T(128)S(1)} %copy-done.10, s32[2,64]{1,0:T(2,128)S(1)} %get-tuple-element.391, f32[8,128,256]{2,1,0:T(8,128)S(1)} %all_to_all.10.last_ref, f32[64,256]{1,0:T(8,128)S(1)} %bitcast.27, f32[256,256]{1,0:T(8,128)S(1)} %get-tuple-element.207.extra_ref, ...), custom_call_target="tpu_custom_call" | custom-call | tf_op jit(solution)/shard_map/states/pallas_call | solution.py:636
  (68 shorter events, 12.0 us)
Async XLA Ops:
  8.0 33.4 %copy-start = (f32[2,2,256,64]{2,3,1,0:T(8,128)S(1)}, f32[2,2,256,64]{2,3,1,0:T(8,128)}, u32[]{:S(2)}) copy-start(f32[2,2,256,64]{2,3,1,0:T(8,128)} %param.11) | copy-start | bytes 786436
  15.3 43.2 %all-to-all-start = ((f32[8,160,256]{2,1,0:T(8,128)}), f32[8,160,256]{2,1,0:T(8,128)S(1)}, u32[]{:S(2)}, u32[]{:S(2)}) async-start(f32[8,160,256]{2,1,0:T(8,128)} %interface_terms.1), calls=%async_computation.1 | async-start | bytes 2621440 | tf_op jit(solution)/shard_map/all_to_all | solution.py:408
  38.4 76.9 %reduce-scatter.3.cloned.1.call-start = ((), (), s32[]{:S(2)}) async-start(), calls=%async_computation.4 | async-start | bytes 589824 | tf_op jit(solution)/shard_map/reduce_scatter | solution.py:494
  41.3 22.6 %copy-start.15 = (f32[192,256]{1,0:T(8,128)S(1)}, f32[192,256]{1,0:T(8,128)}, u32[]{:S(2)}) copy-start(f32[192,256]{1,0:T(8,128)} %get-tuple-element.155) | copy-start | bytes 589828
  41.3 32.3 %copy-start.14 = (f32[192,256]{1,0:T(8,128)S(1)}, f32[192,256]{1,0:T(8,128)}, u32[]{:S(2)}) copy-start(f32[192,256]{1,0:T(8,128)} %get-tuple-element.156) | copy-start | bytes 589828
  41.3 54.1 %copy-start.13 = (f32[192,256]{1,0:T(8,128)S(1)}, f32[192,256]{1,0:T(8,128)}, u32[]{:S(2)}) copy-start(f32[192,256]{1,0:T(8,128)} %get-tuple-element.162) | copy-start | bytes 589828
  61.3 11.5 %collective-permute-start.2 = (f32[272,256]{1,0:T(8,128)S(1)}, f32[272,256]{1,0:T(8,128)S(1)}, u32[]{:S(2)}, u32[]{:S(2)}) collective-permute-start(f32[272,256]{1,0:T(8,128)S(1)} %get-tuple-element.152.refs_0_), channel_id=1, source_target_pairs={{0,16},{16,32},{32,48},{48,0},{64,80},{80,96},{96,112},{112,64},{1... | collective-permute-start | bytes 835592 | tf_op jit(solution)/shard_map/ppermute | solution.py:553
  62.9 8.6 %collective-permute-start.6 = (f32[192,256]{1,0:T(8,128)S(1)}, f32[192,256]{1,0:T(8,128)S(1)}, u32[]{:S(2)}, u32[]{:S(2)}) collective-permute-start(f32[192,256]{1,0:T(8,128)S(1)} %copy-done.16), channel_id=1, source_target_pairs={{0,2},{2,4},{4,6},{6,8},{8,10},{10,12},{12,14},{14,0},{1,3},{3,5},... | collective-permute-start | bytes 589832 | tf_op jit(solution)/shard_map/ppermute | solution.py:534
  63.4 10.2 %collective-permute-start.1 = (f32[272,256]{1,0:T(8,128)S(1)}, f32[272,256]{1,0:T(8,128)S(1)}, u32[]{:S(2)}, u32[]{:S(2)}) collective-permute-start(f32[272,256]{1,0:T(8,128)S(1)} %get-tuple-element.153.refs_1_), channel_id=1, source_target_pairs={{0,48},{16,0},{32,16},{48,32},{64,112},{80,64},{96,80},{112,96},{1... | collective-permute-start | bytes 835592 | tf_op jit(solution)/shard_map/ppermute | solution.py:553
  63.9 9.7 %collective-permute-start.7 = (f32[192,256]{1,0:T(8,128)S(1)}, f32[192,256]{1,0:T(8,128)S(1)}, u32[]{:S(2)}, u32[]{:S(2)}) collective-permute-start(f32[192,256]{1,0:T(8,128)S(1)} %copy-done.15), channel_id=1, source_target_pairs={{0,14},{2,0},{4,2},{6,4},{8,6},{10,8},{12,10},{14,12},{1,15},{3,1}... | collective-permute-start | bytes 589832 | tf_op jit(solution)/shard_map/ppermute | solution.py:534
  66.7 23.7 %collective-permute-start = (f32[272,256]{1,0:T(8,128)S(1)}, f32[272,256]{1,0:T(8,128)S(1)}, u32[]{:S(2)}, u32[]{:S(2)}) collective-permute-start(f32[272,256]{1,0:T(8,128)S(1)} %get-tuple-element.152.refs_0_), channel_id=1, source_target_pairs={{0,48},{16,0},{32,16},{48,32},{64,112},{80,64},{96,80},{112,96},{1... | collective-permute-start | bytes 835592 | tf_op jit(solution)/shard_map/ppermute | solution.py:553
  71.5 18.8 %collective-permute-start.5 = (f32[272,256]{1,0:T(8,128)S(1)}, f32[272,256]{1,0:T(8,128)S(1)}, u32[]{:S(2)}, u32[]{:S(2)}) collective-permute-start(f32[272,256]{1,0:T(8,128)S(1)} %get-tuple-element.153.refs_1_), channel_id=1, source_target_pairs={{0,16},{16,32},{32,48},{48,0},{64,80},{80,96},{96,112},{112,64},{1... | collective-permute-start | bytes 835592 | tf_op jit(solution)/shard_map/ppermute | solution.py:553
  72.8 22.7 %collective-permute-start.3 = (f32[272,256]{1,0:T(8,128)S(1)}, f32[272,256]{1,0:T(8,128)S(1)}, u32[]{:S(2)}, u32[]{:S(2)}) collective-permute-start(f32[272,256]{1,0:T(8,128)S(1)} %collective-permute-done.2.refs_6_), channel_id=1, source_target_pairs={{0,16},{16,32},{32,48},{48,0},{64,80},{80,96},{96,112},{112,64},{1... | collective-permute-start | bytes 835592 | tf_op jit(solution)/shard_map/ppermute | solution.py:553
  73.6 16.7 %collective-permute-start.8 = (f32[192,256]{1,0:T(8,128)S(1)}, f32[192,256]{1,0:T(8,128)S(1)}, u32[]{:S(2)}, u32[]{:S(2)}) collective-permute-start(f32[192,256]{1,0:T(8,128)S(1)} %copy-done.14), channel_id=1, source_target_pairs={{0,4},{2,6},{4,8},{6,10},{8,12},{10,14},{12,0},{14,2},{1,5},{3,7},... | collective-permute-start | bytes 589832 | tf_op jit(solution)/shard_map/ppermute | solution.py:534
  73.6 21.8 %collective-permute-start.4 = (f32[272,256]{1,0:T(8,128)S(1)}, f32[272,256]{1,0:T(8,128)S(1)}, u32[]{:S(2)}, u32[]{:S(2)}) collective-permute-start(f32[272,256]{1,0:T(8,128)S(1)} %collective-permute-done.1.refs_3_), channel_id=1, source_target_pairs={{0,48},{16,0},{32,16},{48,32},{64,112},{80,64},{96,80},{112,96},{1... | collective-permute-start | bytes 835592 | tf_op jit(solution)/shard_map/ppermute | solution.py:553
  90.3 25.0 %collective-permute-start.9 = (f32[192,256]{1,0:T(8,128)}, f32[192,256]{1,0:T(8,128)S(1)}, u32[]{:S(2)}, u32[]{:S(2)}) collective-permute-start(f32[192,256]{1,0:T(8,128)} %get-tuple-element.159), channel_id=1, source_target_pairs={{0,6},{2,8},{4,10},{6,12},{8,14},{10,0},{12,2},{14,4},{1,7},{3,9},... | collective-permute-start | bytes 589832 | tf_op jit(solution)/shard_map/ppermute | solution.py:534
  90.3 25.0 %collective-permute-start.10 = (f32[192,256]{1,0:T(8,128)}, f32[192,256]{1,0:T(8,128)S(1)}, u32[]{:S(2)}, u32[]{:S(2)}) collective-permute-start(f32[192,256]{1,0:T(8,128)} %get-tuple-element.160), channel_id=1, source_target_pairs={{0,8},{2,10},{4,12},{6,14},{8,0},{10,2},{12,4},{14,6},{1,9},{3,11}... | collective-permute-start | bytes 589832 | tf_op jit(solution)/shard_map/ppermute | solution.py:534
  90.4 25.0 %collective-permute-start.11 = (f32[192,256]{1,0:T(8,128)}, f32[192,256]{1,0:T(8,128)S(1)}, u32[]{:S(2)}, u32[]{:S(2)}) collective-permute-start(f32[192,256]{1,0:T(8,128)} %get-tuple-element.161), channel_id=1, source_target_pairs={{0,10},{2,12},{4,14},{6,0},{8,2},{10,4},{12,6},{14,8},{1,11},{3,13... | collective-permute-start | bytes 589832 | tf_op jit(solution)/shard_map/ppermute | solution.py:534
  95.5 25.4 %collective-permute-start.12 = (f32[192,256]{1,0:T(8,128)S(1)}, f32[192,256]{1,0:T(8,128)S(1)}, u32[]{:S(2)}, u32[]{:S(2)}) collective-permute-start(f32[192,256]{1,0:T(8,128)S(1)} %copy-done.13), channel_id=1, source_target_pairs={{0,12},{2,14},{4,0},{6,2},{8,4},{10,6},{12,8},{14,10},{1,13},{3,15... | collective-permute-start | bytes 589832 | tf_op jit(solution)/shard_map/ppermute | solution.py:534
  97.2 5.2 %collective-permute-start.13 = (f32[32,256]{1,0:T(8,128)S(1)}, f32[32,256]{1,0:T(8,128)S(1)}, u32[]{:S(2)}, u32[]{:S(2)}) collective-permute-start(f32[32,256]{1,0:T(8,128)S(1)} %get-tuple-element.172), channel_id=1, source_target_pairs={{0,64},{2,66},{4,68},{6,70},{8,200},{10,202},{12,204},{14,206},{16... | collective-permute-start | bytes 98312 | tf_op jit(solution)/shard_map/ppermute | solution.py:598
  103.2 5.3 %collective-permute-start.14 = (f32[32,256]{1,0:T(8,128)S(1)}, f32[32,256]{1,0:T(8,128)S(1)}, u32[]{:S(2)}, u32[]{:S(2)}) collective-permute-start(f32[32,256]{1,0:T(8,128)S(1)} %row_step.2), channel_id=1, source_target_pairs={{0,64},{2,66},{4,68},{6,70},{8,200},{10,202},{12,204},{14,206},{16... | collective-permute-start | bytes 98312 | tf_op jit(solution)/shard_map/ppermute | solution.py:598
  109.2 5.2 %collective-permute-start.15 = (f32[32,256]{1,0:T(8,128)S(1)}, f32[32,256]{1,0:T(8,128)S(1)}, u32[]{:S(2)}, u32[]{:S(2)}) collective-permute-start(f32[32,256]{1,0:T(8,128)S(1)} %row_step.3), channel_id=1, source_target_pairs={{0,64},{2,66},{4,68},{6,70},{8,200},{10,202},{12,204},{14,206},{16... | collective-permute-start | bytes 98312 | tf_op jit(solution)/shard_map/ppermute | solution.py:598
  115.3 38.6 %copy-start.6 = (f32[192,256]{1,0:T(8,128)S(1)}, f32[192,256]{1,0:T(8,128)}, u32[]{:S(2)}) copy-start(f32[192,256]{1,0:T(8,128)} %get-tuple-element.208.refs_0_) | copy-start | bytes 589828
  115.3 38.5 %copy-start.9 = (f32[1,64,256]{2,1,0:T(8,128)S(1)}, f32[1,64,256]{2,1,0:T(8,128)}, u32[]{:S(2)}) copy-start(f32[1,64,256]{2,1,0:T(8,128)} %reduce-scatter.3.cloned.1.call-done) | copy-start | bytes 196612
  (8 other events, 44.1 us)
Sparse Core Ops, SparseCore 1:
  41.4 40.0 reduce-scatter.2

commit v8 on v6

--- a/solution.py
+++ b/solution.py
@@ -160,10 +160,8 @@
         imag = mm3(parts, split(g_ref[slab, 1]), True)
         for sweep in range(2):
             base = sweep * lead
-            place = slab * 4 * lead + sweep * 2 * lead
-            out_ref = early_ref
-            if slab == 1 and sweep == 1:
-                out_ref, place = late_ref, 0
+            place = sweep * 2 * lead
+            out_ref = (early_ref, late_ref)[slab]
             out_ref[0, place : place + lead, :] = real[base : base + lead]
             out_ref[0, place + lead : place + 2 * lead, :] = imag[base : base + lead]
             one = 2 * lead + 2 * sweep * PACK
@@ -345,7 +343,7 @@
 ):
     modes = inject_ref.shape[1]
     width = base_ref.shape[1]
-    lead = rows_ref.shape[1] // 6
+    lead = rows_ref.shape[1] // 4
     for sweep, out_ref in enumerate((left_ref, right_ref)):
         target = jnp.broadcast_to(
             inject_ref[sweep : sweep + 1, :].astype(F32), (width, modes)
@@ -366,10 +364,10 @@
             by = []
             for part in range(2):
                 kind = 2 * sweep + part
-                if slab == 1 and sweep == 1:
-                    matrix = stacked(last_ref, 64 + part * lead, lead)
+                if slab == 0:
+                    matrix = stacked(rows_ref, kind * lead, lead)
                 else:
-                    matrix = stacked(rows_ref, (4 * slab + kind) * lead, lead)
+                    matrix = stacked(last_ref, 64 + kind * lead, lead)
                 by.append(mm3(parts, split(matrix)))
             value = combined(by[0], by[1])
             chosen = target == (place_ref[0] + slab).astype(F32)
@@ -458,13 +456,13 @@
                 pl.BlockSpec((2, 2, part_rows, width), lambda step: (0, 0, step, 0)),
             ],
             out_specs=[
-                pl.BlockSpec((1, 6 * lead, part_rows), lambda step: (step, 0, 0)),
-                pl.BlockSpec((1, 2 * lead, part_rows), lambda step: (step, 0, 0)),
+                pl.BlockSpec((1, 4 * lead, part_rows), lambda step: (step, 0, 0)),
+                pl.BlockSpec((1, 4 * lead, part_rows), lambda step: (step, 0, 0)),
                 pl.BlockSpec((1, 4 * PACK, part_rows), lambda step: (step, 0, 0)),
             ],
             out_shape=[
-                jax.ShapeDtypeStruct((8, 6 * lead, part_rows), F32),
-                jax.ShapeDtypeStruct((8, 2 * lead, part_rows), F32),
+                jax.ShapeDtypeStruct((8, 4 * lead, part_rows), F32),
+                jax.ShapeDtypeStruct((8, 4 * lead, part_rows), F32),
                 jax.ShapeDtypeStruct((8, 4 * PACK, part_rows), F32),
             ],
             compiler_params=params(LARGE),
@@ -535,6 +533,7 @@
     before_bottom, after_top = turn(bottom, 1), turn(top, -1)
     across_top, across_bottom = turn(before_top, 1), turn(after_bottom, -1)
     pieces = (after_top, after_bottom, across_top, across_bottom, before_top, before_bottom)
+    pieces, base = lax.optimization_barrier((pieces, base))
     row_maps = [
         jax.ShapeDtypeStruct((4, 2 * size, size), BF16),
         jax.ShapeDtypeStruct((4, 2 * size, size), BF16),
@@ -547,6 +546,7 @@
         out_specs=[VMEM] * 4,
         out_shape=row_maps + [state_shape],
         compiler_params=params(),
+        cost_estimate=pl.CostEstimate(flops=30000000000, bytes_accessed=0, transcendentals=0),
         name="gather_maps",
     )(info, own_lead, top, bottom, *pieces)
 
@@ -581,7 +581,15 @@
     flow, half_row = lax.optimization_barrier((flow, half_row))
     flow = hop(flow)
     prefix, inner_map = local(
-        prefix_kernel, "prefix_map", [full, full], info, *maps, half_row, first_map, turned, flow_a
+        prefix_kernel,
+        "prefix_map",
+        [full, full],
+        info,
+        *maps,
+        half_row,
+        first_map,
+        turned,
+        flow_a,
     )
     flow = local(row_kernel, "row_step", state_shape, info, own_lead, flow, *row_map)
     flow, prefix, inner_map = lax.optimization_barrier((flow, prefix, inner_map))
@@ -595,14 +603,14 @@
     last = local(
         inflow_kernel,
         "inflow",
-        jax.ShapeDtypeStruct((8, 64 + 2 * lead, size), F32),
+        jax.ShapeDtypeStruct((8, 64 + 4 * lead, size), F32),
         info,
         own_lead,
         flow,
         *entry,
         late,
     )
-    rows, base, last = lax.optimization_barrier((rows, base, last))
+    rows, last = lax.optimization_barrier((rows, last))
     last = exchange(last)
     last, rows, base, extra, inject = lax.optimization_barrier((last, rows, base, extra, inject))
 

time: 153 us -> 158 us (1.033); the launches traced: 152 us -> 155 us
  blocking collectives: 29.5 us -> 39.9 us
  waiting for transfers between devices: 45.3 us -> 37.9 us
  Pallas kernels: 33.4 us -> 35.1 us
  local copies, waits for them, and re-layouts: 4.48 us -> 2.78 us
    all_to_all x1, blocking collectives: 29.5 us -> 39.9 us  [exchange(): return lax.all_to_all(value, 'col', split_axis=0, concat_axis=0, tiled=True)]
    ppermute x6, waiting for transfers between devices: 15.7 us -> 11.3 us  [turn(): lax.ppermute(value, 'slab', [(slab, slab // 4 * 4 + (slab + step) % 4) fo...]
    reduce_scatter x1, waiting for transfers between devices: 2.83 us -> 1.11 us  [summed(): return lax.psum_scatter(flows, 'col', scatter_dimension=0, tiled=False)]
    unnamed x22, local copies, waits for them, and re-layouts: 4.31 us -> 2.6 us
  transfers between devices with their start and end apart: 12 -> 12, of which waited for: 9 -> 10; matrix products, arithmetic and copies ran while one was open for 1% -> 1% of each run, Pallas kernels for 16% -> 17%
where the time goes in v8:
time: 158 us; the launch traced here: 155 us
  blocking collectives  39.9 us (25%)
  waiting for transfers between devices  37.9 us (24%)
  Pallas kernels  35.1 us (22%)
  starting transfers between devices  21.2 us (13%)
  between operations  16.4 us (10%)
  local copies, waits for them, and re-layouts  2.78 us (2%)
    all_to_all x1, blocking collectives, exchange(): return lax.all_to_all(value, 'col', split_axis=0, concat_axis=0, tiled=True)  39.9 us
    all_to_all x2, waiting for transfers between devices, exchange(): return lax.all_to_all(value, 'col', split_axis=0, concat_axis=0, tiled=True)  18.7 us
    all_to_all x2, starting transfers between devices, exchange(): return lax.all_to_all(value, 'col', split_axis=0, concat_axis=0, tiled=True)  12.2 us
    pallas_call x7, Pallas kernels, local(): pl.pallas_call(kernel, in_specs=[SMEM] + [VMEM] * (len(args) - 1), out_sp...  11.4 us
    ppermute x6, waiting for transfers between devices, turn(): lax.ppermute(value, 'slab', [(slab, slab // 4 * 4 + (slab + step) % 4) fo...  11.3 us
    pallas_call x1, Pallas kernels, chunk_terms(): pl.pallas_call(spread_kernel, grid=(8,), in_specs=[whole(terms.shape), wh...  8.71 us
    pallas_call x1, Pallas kernels, on_device(): pl.pallas_call(interface_kernel, grid=(4,), in_specs=[SMEM, whole(inject....  6.69 us
    ppermute x3, waiting for transfers between devices, hop(): return lax.ppermute(value, ('slab', 'col'), pairs)  6.21 us
  transfers between devices with their start and end apart: 12, of which 10 were waited for; matrix products, arithmetic and copies ran while one was open for 1% of the time, Pallas kernels for 17%

profile of v8, /device:TPU:8, one launch (start us, length us, event | category | flops | bytes accessed | tf_op | source)
XLA Modules:
  0.0 154.7 jit_solution(13153734553723706802)
XLA Ops:
  8.6 6.7 %interface_terms.1 = f32[8,160,256]{2,1,0:T(8,128)} custom-call(s32[2]{0:T(128)} %pad_add_fusion.1.place_ref, s32[2,64]{1,0:T(2,128)} %inject_ref.3, f32[2,2,64,256]{3,2,1,0:T(8,128)} %bitcast.27, f32[2,2,2048,256]{3,2,1,0:T(8,128)} %g_ref.1, f32[2,2,2048,256]{3,2,1,0:T(8,128)} %g_ref.1), custom_call_target="tpu_custom_call" | custom-call | tf_op jit(solution)/shard_map/interface_terms/pallas_call | solution.py:417
  15.3 8.6 %all-to-all-start = ((f32[8,160,256]{2,1,0:T(8,128)}), f32[8,160,256]{2,1,0:T(8,128)S(1)}, u32[]{:S(2)}, u32[]{:S(2)}) async-start(f32[8,160,256]{2,1,0:T(8,128)} %interface_terms.1), calls=%async_computation.1 | async-start | bytes 2621440 | tf_op jit(solution)/shard_map/all_to_all | solution.py:393
  25.4 1.2 select_terms.2
  27.9 8.7 %spread_terms.2 = (f32[8,128,256]{2,1,0:T(8,128)}, f32[8,128,256]{2,1,0:T(8,128)}, f32[8,64,256]{2,1,0:T(8,128)}) custom-call(bf16[2,128,256]{2,1,0:T(8,128)(2,1)} %copy-done.6, bf16[2,128,256]{2,1,0:T(8,128)(2,1)} %copy-done.7, f32[2,2,2048,256]{3,2,1,0:T(8,128)} %g_ref.1), custom_call_target="tpu_custom_call" | custom-call | tf_op jit(solution)/shard_map/spread_terms/pallas_call | solution.py:450
  37.5 1.2 copy-done.4
  39.7 18.7 %all-to-all-done.recv_ref = f32[8,160,256]{2,1,0:T(8,128)S(1)} async-done(((f32[8,160,256]{2,1,0:T(8,128)}), f32[8,160,256]{2,1,0:T(8,128)S(1)}, u32[]{:S(2)}, u32[]{:S(2)}) %all-to-all-start) | async-done | bytes 1310752 | tf_op jit(solution)/shard_map/all_to_all | solution.py:393
  58.5 3.5 %pair_map.1 = (f32[272,256]{1,0:T(8,128)}, f32[272,256]{1,0:T(8,128)}, f32[32,256]{1,0:T(8,128)S(1)}, f32[512,256]{1,0:T(8,128)S(1)}) custom-call(s32[4]{0:T(128)S(1)} %pad_add_fusion.2.team_ref.info_ref, f32[8,160,256]{2,1,0:T(8,128)S(1)} %all-to-all-done.recv_ref, f32[2,512,256]{2,1,0:T(8,128)S(1)} %coupling_rows.1.x_ref, ...), custom_call_target="tpu_custom_call" | custom-call | tf_op jit(solution)/shard_map/pair_map/pallas_call | solution.py:513
  62.0 1.6 %collective-permute-start.2 = (f32[272,256]{1,0:T(8,128)}, f32[272,256]{1,0:T(8,128)S(1)}, u32[]{:S(2)}, u32[]{:S(2)}) collective-permute-start(f32[272,256]{1,0:T(8,128)} %get-tuple-element.110.refs_0_), channel_id=1, source_target_pairs={{0,16},{16,32},{32,48},{48,0},{64,80},{80,96},{96,112},{112,64},{1... | collective-permute-start | bytes 835592 | tf_op jit(solution)/shard_map/ppermute | solution.py:528
  64.0 1.6 %collective-permute-start = (f32[272,256]{1,0:T(8,128)}, f32[272,256]{1,0:T(8,128)}, u32[]{:S(2)}, u32[]{:S(2)}) collective-permute-start(f32[272,256]{1,0:T(8,128)} %get-tuple-element.110.refs_0_), channel_id=1, source_target_pairs={{0,48},{16,0},{32,16},{48,32},{64,112},{80,64},{96,80},{112,96},{1... | collective-permute-start | bytes 835592 | tf_op jit(solution)/shard_map/ppermute | solution.py:528
  66.1 5.7 %collective-permute-done.2.refs_6_ = f32[272,256]{1,0:T(8,128)S(1)} collective-permute-done((f32[272,256]{1,0:T(8,128)}, f32[272,256]{1,0:T(8,128)S(1)}, u32[]{:S(2)}, u32[]{:S(2)}) %collective-permute-start.2) | collective-permute-done | bytes 278560 | tf_op jit(solution)/shard_map/ppermute | solution.py:528
  71.7 1.6 %collective-permute-start.3 = (f32[272,256]{1,0:T(8,128)S(1)}, f32[272,256]{1,0:T(8,128)}, u32[]{:S(2)}, u32[]{:S(2)}) collective-permute-start(f32[272,256]{1,0:T(8,128)S(1)} %collective-permute-done.2.refs_6_), channel_id=1, source_target_pairs={{0,16},{16,32},{32,48},{48,0},{64,80},{80,96},{96,112},{112,64},{1... | collective-permute-start | bytes 835592 | tf_op jit(solution)/shard_map/ppermute | solution.py:528
  73.9 3.6 %all-to-all-start.1 = ((f32[8,128,256]{2,1,0:T(8,128)}), f32[8,128,256]{2,1,0:T(8,128)S(1)}, u32[]{:S(2)}, u32[]{:S(2)}) async-start(f32[8,128,256]{2,1,0:T(8,128)} %get-tuple-element.105), calls=%async_computation.2 | async-start | bytes 2097152 | tf_op jit(solution)/shard_map/all_to_all | solution.py:393
  77.5 1.1 reduce-scatter.3.cloned.1.call-done
  79.4 3.3 %collective-permute-done.3.refs_4_ = f32[272,256]{1,0:T(8,128)} collective-permute-done((f32[272,256]{1,0:T(8,128)S(1)}, f32[272,256]{1,0:T(8,128)}, u32[]{:S(2)}, u32[]{:S(2)}) %collective-permute-start.3) | collective-permute-done | bytes 278560 | tf_op jit(solution)/shard_map/ppermute | solution.py:528
  82.8 1.3 collective-permute-done.4.refs_5_
  84.1 2.7 %gather_maps.1 = (bf16[4,512,256]{2,1,0:T(8,128)(2,1)S(1)}, bf16[4,512,256]{2,1,0:T(8,128)(2,1)S(1)}, f32[4,32,256]{2,1,0:T(8,128)S(1)}, f32[32,256]{1,0:T(8,128)S(1)}) custom-call(s32[4]{0:T(128)S(1)} %pad_add_fusion.2.team_ref.info_ref, f32[32,256]{1,0:T(8,128)S(1)} %bitcast.22, f32[272,256]{1,0:T(8,128)} %get-tuple-element.110.refs_0_, ...), custom_call_target="tpu_custom_call" | custom-call | flops 30000001024 | tf_op jit(solution)/shard_map/gather_maps/pallas_call | solution.py:543
  86.8 1.8 %collective-permute-start.6 = (f32[32,256]{1,0:T(8,128)S(1)}, f32[32,256]{1,0:T(8,128)S(1)}, u32[]{:S(2)}, u32[]{:S(2)}) collective-permute-start(f32[32,256]{1,0:T(8,128)S(1)} %get-tuple-element.119), channel_id=1, source_target_pairs={{0,64},{2,66},{4,68},{6,70},{8,200},{10,202},{12,204},{14,206},{16... | collective-permute-start | bytes 98312 | tf_op jit(solution)/shard_map/ppermute | solution.py:572
  88.5 3.2 %row_map.1 = (bf16[512,256]{1,0:T(8,128)(2,1)S(1)}, bf16[512,256]{1,0:T(8,128)(2,1)S(1)}, f32[32,256]{1,0:T(8,128)S(1)}, f32[544,256]{1,0:T(8,128)S(1)}) custom-call(s32[4]{0:T(128)S(1)} %pad_add_fusion.2.team_ref.info_ref, bf16[4,512,256]{2,1,0:T(8,128)(2,1)S(1)} %get-tuple-element.120.high_ref, bf16[4,512,256]{2,1,0:T(8,128)(2,1)S(1)} %get-tuple-element.121.low_ref, ...), custom_call_target="tpu_custom_call" | custom-call | tf_op jit(solution)/shard_map/row_map/pallas_call | solution.py:562
  94.0 1.7 %prefix_map.1 = (f32[544,256]{1,0:T(8,128)S(1)}, f32[544,256]{1,0:T(8,128)S(1)}) custom-call(s32[4]{0:T(128)S(1)} %pad_add_fusion.2.team_ref.info_ref, bf16[4,512,256]{2,1,0:T(8,128)(2,1)S(1)} %get-tuple-element.120.high_ref, bf16[4,512,256]{2,1,0:T(8,128)(2,1)S(1)} %get-tuple-element.121.low_ref, f32[4,32,256]{2,1,0:T(8,128)S(1)} %get-tuple-element.122.flow_ref, ...), custom_call_target="tpu_custom_call" | custom-call | tf_op jit(solution)/shard_map/prefix_map/pallas_call | solution.py:562
  95.7 2.3 %collective-permute-done.7.state_ref = f32[32,256]{1,0:T(8,128)S(1)} collective-permute-done((f32[32,256]{1,0:T(8,128)S(1)}, f32[32,256]{1,0:T(8,128)S(1)}, u32[]{:S(2)}, u32[]{:S(2)}) %collective-permute-start.7) | collective-permute-done | bytes 32800 | tf_op jit(solution)/shard_map/ppermute | solution.py:572
  98.8 1.7 %entry_map.1 = (bf16[2,512,256]{2,1,0:T(8,128)(2,1)S(1)}, bf16[2,512,256]{2,1,0:T(8,128)(2,1)S(1)}, f32[2,32,256]{2,1,0:T(8,128)S(1)}) custom-call(s32[4]{0:T(128)S(1)} %pad_add_fusion.2.team_ref.info_ref, f32[544,256]{1,0:T(8,128)S(1)} %get-tuple-element.134.prefix_ref, f32[544,256]{1,0:T(8,128)S(1)} %get-tuple-element.135.inner_ref, ...), custom_call_target="tpu_custom_call" | custom-call | tf_op jit(solution)/shard_map/entry_map/pallas_call | solution.py:562
  100.5 3.4 %collective-permute-done.8.state_ref = f32[32,256]{1,0:T(8,128)S(1)} collective-permute-done((f32[32,256]{1,0:T(8,128)S(1)}, f32[32,256]{1,0:T(8,128)S(1)}, u32[]{:S(2)}, u32[]{:S(2)}) %collective-permute-start.8) | collective-permute-done | bytes 32800 | tf_op jit(solution)/shard_map/ppermute | solution.py:572
  104.9 39.9 %all_to_all.15.last_ref = f32[8,192,256]{2,1,0:T(8,128)S(1)} all-to-all(f32[8,192,256]{2,1,0:T(8,128)S(1)} %inflow.1), channel_id=1, replica_groups=mesh['slab'=16,'col'=8,'energy'=2] {'col'}, dimensions={0} | all-to-all | bytes 3145728 | tf_op jit(solution)/shard_map/all_to_all | solution.py:393
  144.8 2.5 %states.1 = (f32[2,2,64,256]{3,2,1,0:T(8,128)}, f32[2,2,64,256]{3,2,1,0:T(8,128)}) custom-call(s32[2]{0:T(128)S(1)} %copy-done.9, s32[2,64]{1,0:T(2,128)S(1)} %get-tuple-element.274, f32[8,192,256]{2,1,0:T(8,128)S(1)} %all_to_all.15.last_ref, f32[8,128,256]{2,1,0:T(8,128)S(1)} %all-to-all-done.1.rows_ref, f32[64,256]{1,0:T(8,128)S(1)} %bitcast.26, ...), custom_call_target="tpu_custom_call" | custom-call | tf_op jit(solution)/shard_map/states/pallas_call | solution.py:562
  (49 shorter events, 10.8 us)
Async XLA Ops:
  8.0 31.7 %copy-start = (f32[2,2,256,64]{2,3,1,0:T(8,128)S(1)}, f32[2,2,256,64]{2,3,1,0:T(8,128)}, u32[]{:S(2)}) copy-start(f32[2,2,256,64]{2,3,1,0:T(8,128)} %param.11) | copy-start | bytes 786436
  15.3 8.6 %copy-start.13 = (s32[2,64]{1,0:T(2,128)S(1)}, s32[2,64]{1,0:T(2,128)}, u32[]{:S(2)}) copy-start(s32[2,64]{1,0:T(2,128)} %inject_ref.3) | copy-start | bytes 1540
  15.3 10.0 %copy-start.9 = (s32[2]{0:T(128)S(1)}, s32[2]{0:T(128)}, u32[]{:S(2)}) copy-start(s32[2]{0:T(128)} %pad_add_fusion.1.place_ref) | copy-start | bytes 28
  15.3 10.1 %copy-start.10 = (f32[2,2,256,64]{2,3,1,0:T(8,128)S(1)}, f32[2,2,256,64]{2,3,1,0:T(8,128)}, u32[]{:S(2)}) copy-start(f32[2,2,256,64]{2,3,1,0:T(8,128)} %param.9) | copy-start | bytes 786436
  15.3 43.1 %all-to-all-start = ((f32[8,160,256]{2,1,0:T(8,128)}), f32[8,160,256]{2,1,0:T(8,128)S(1)}, u32[]{:S(2)}, u32[]{:S(2)}) async-start(f32[8,160,256]{2,1,0:T(8,128)} %interface_terms.1), calls=%async_computation.1 | async-start | bytes 2621440 | tf_op jit(solution)/shard_map/all_to_all | solution.py:393
  26.6 0.7 copy-start.6
  27.2 0.7 copy-start.7
  36.6 0.7 copy-start.11
  36.7 41.9 %reduce-scatter.3.cloned.1.call-start = ((), (), s32[]{:S(2)}) async-start(), calls=%async_computation.5 | async-start | bytes 589824 | tf_op jit(solution)/shard_map/reduce_scatter | solution.py:473
  37.5 1.2 copy-start.4
  62.0 9.7 %collective-permute-start.2 = (f32[272,256]{1,0:T(8,128)}, f32[272,256]{1,0:T(8,128)S(1)}, u32[]{:S(2)}, u32[]{:S(2)}) collective-permute-start(f32[272,256]{1,0:T(8,128)} %get-tuple-element.110.refs_0_), channel_id=1, source_target_pairs={{0,16},{16,32},{32,48},{48,0},{64,80},{80,96},{96,112},{112,64},{1... | collective-permute-start | bytes 835592 | tf_op jit(solution)/shard_map/ppermute | solution.py:528
  63.6 9.9 %collective-permute-start.1 = (f32[272,256]{1,0:T(8,128)}, f32[272,256]{1,0:T(8,128)}, u32[]{:S(2)}, u32[]{:S(2)}) collective-permute-start(f32[272,256]{1,0:T(8,128)} %get-tuple-element.111.refs_1_), channel_id=1, source_target_pairs={{0,48},{16,0},{32,16},{48,32},{64,112},{80,64},{96,80},{112,96},{1... | collective-permute-start | bytes 835592 | tf_op jit(solution)/shard_map/ppermute | solution.py:528
  64.0 15.4 %collective-permute-start = (f32[272,256]{1,0:T(8,128)}, f32[272,256]{1,0:T(8,128)}, u32[]{:S(2)}, u32[]{:S(2)}) collective-permute-start(f32[272,256]{1,0:T(8,128)} %get-tuple-element.110.refs_0_), channel_id=1, source_target_pairs={{0,48},{16,0},{32,16},{48,32},{64,112},{80,64},{96,80},{112,96},{1... | collective-permute-start | bytes 835592 | tf_op jit(solution)/shard_map/ppermute | solution.py:528
  65.7 13.8 %collective-permute-start.5 = (f32[272,256]{1,0:T(8,128)}, f32[272,256]{1,0:T(8,128)}, u32[]{:S(2)}, u32[]{:S(2)}) collective-permute-start(f32[272,256]{1,0:T(8,128)} %get-tuple-element.111.refs_1_), channel_id=1, source_target_pairs={{0,16},{16,32},{32,48},{48,0},{64,80},{80,96},{96,112},{112,64},{1... | collective-permute-start | bytes 835592 | tf_op jit(solution)/shard_map/ppermute | solution.py:528
  71.7 11.0 %collective-permute-start.3 = (f32[272,256]{1,0:T(8,128)S(1)}, f32[272,256]{1,0:T(8,128)}, u32[]{:S(2)}, u32[]{:S(2)}) collective-permute-start(f32[272,256]{1,0:T(8,128)S(1)} %collective-permute-done.2.refs_6_), channel_id=1, source_target_pairs={{0,16},{16,32},{32,48},{48,0},{64,80},{80,96},{96,112},{112,64},{1... | collective-permute-start | bytes 835592 | tf_op jit(solution)/shard_map/ppermute | solution.py:528
  73.5 10.6 %collective-permute-start.4 = (f32[272,256]{1,0:T(8,128)}, f32[272,256]{1,0:T(8,128)}, u32[]{:S(2)}, u32[]{:S(2)}) collective-permute-start(f32[272,256]{1,0:T(8,128)} %collective-permute-done.1.refs_3_), channel_id=1, source_target_pairs={{0,48},{16,0},{32,16},{48,32},{64,112},{80,64},{96,80},{112,96},{1... | collective-permute-start | bytes 835592 | tf_op jit(solution)/shard_map/ppermute | solution.py:528
  73.9 31.0 %all-to-all-start.1 = ((f32[8,128,256]{2,1,0:T(8,128)}), f32[8,128,256]{2,1,0:T(8,128)S(1)}, u32[]{:S(2)}, u32[]{:S(2)}) async-start(f32[8,128,256]{2,1,0:T(8,128)} %get-tuple-element.105), calls=%async_computation.2 | async-start | bytes 2097152 | tf_op jit(solution)/shard_map/all_to_all | solution.py:393
  86.8 5.4 %collective-permute-start.6 = (f32[32,256]{1,0:T(8,128)S(1)}, f32[32,256]{1,0:T(8,128)S(1)}, u32[]{:S(2)}, u32[]{:S(2)}) collective-permute-start(f32[32,256]{1,0:T(8,128)S(1)} %get-tuple-element.119), channel_id=1, source_target_pairs={{0,64},{2,66},{4,68},{6,70},{8,200},{10,202},{12,204},{14,206},{16... | collective-permute-start | bytes 98312 | tf_op jit(solution)/shard_map/ppermute | solution.py:572
  92.9 5.2 %collective-permute-start.7 = (f32[32,256]{1,0:T(8,128)S(1)}, f32[32,256]{1,0:T(8,128)S(1)}, u32[]{:S(2)}, u32[]{:S(2)}) collective-permute-start(f32[32,256]{1,0:T(8,128)S(1)} %row_step.2), channel_id=1, source_target_pairs={{0,64},{2,66},{4,68},{6,70},{8,200},{10,202},{12,204},{14,206},{16... | collective-permute-start | bytes 98312 | tf_op jit(solution)/shard_map/ppermute | solution.py:572
  95.7 8.2 %copy-start.5 = (f32[8,128,256]{2,1,0:T(8,128)S(1)}, f32[8,128,256]{2,1,0:T(8,128)}, u32[]{:S(2)}) copy-start(f32[8,128,256]{2,1,0:T(8,128)} %get-tuple-element.139.spread_ref) | copy-start | bytes 3145732
  98.8 5.2 %collective-permute-start.8 = (f32[32,256]{1,0:T(8,128)S(1)}, f32[32,256]{1,0:T(8,128)S(1)}, u32[]{:S(2)}, u32[]{:S(2)}) collective-permute-start(f32[32,256]{1,0:T(8,128)S(1)} %row_step.3), channel_id=1, source_target_pairs={{0,64},{2,66},{4,68},{6,70},{8,200},{10,202},{12,204},{14,206},{16... | collective-permute-start | bytes 98312 | tf_op jit(solution)/shard_map/ppermute | solution.py:572
  104.9 39.9 %copy-start.8 = (f32[1,64,256]{2,1,0:T(8,128)S(1)}, f32[1,64,256]{2,1,0:T(8,128)}, u32[]{:S(2)}) copy-start(f32[1,64,256]{2,1,0:T(8,128)} %reduce-scatter.3.cloned.1.call-done) | copy-start | bytes 196612
  104.9 39.9 %copy-start.12 = (f32[256,256]{1,0:T(8,128)S(1)}, f32[256,256]{1,0:T(8,128)}, u32[]{:S(2)}) copy-start(f32[256,256]{1,0:T(8,128)} %copy-done.11) | copy-start | bytes 786436
Sparse Core Ops, SparseCore 1:
  39.6 38.9 reduce-scatter.2

commit v9 on v8

--- a/solution.py
+++ b/solution.py
@@ -10,6 +10,7 @@
 LIMIT = 24 * 1024 * 1024
 LARGE = 56 * 1024 * 1024
 PACK = 16
+LANES = 128
 
 
 def split(value):
@@ -86,9 +87,14 @@
         picked = pl.ds(sweep * half, half)
         term = mm3((high_ref[slab, picked, :], low_ref[slab, picked, :]), split(rows), True)
         order = slab if sweep == 0 else 1 - slab
-        place = pl.ds(pl.multiple_of((order * 2 + plane) * lead, lead), lead)
-        for member in range(4):
-            out_ref[sweep * 4 + member, place, :] = term[:lead]
+        rows, lanes = out_ref.shape[1] // 2, out_ref.shape[2]
+        for side in range(2):
+            place = (order * 2 + plane) * lead + side * rows
+            place = pl.ds(pl.multiple_of(place, 8), lead)
+            for member in range(4):
+                out_ref[sweep * 4 + member, place, :] = term[
+                    :lead, side * lanes : (side + 1) * lanes
+                ]
         real, imag = term[lead : lead + modes], term[lead + modes :]
 
         @pl.when(plane == 0)
@@ -107,9 +113,7 @@
             sweep, member = divmod(dest, 4)
             for part in range(2):
                 start = part * modes + member * 16
-                out_ref[dest, 4 * lead + part * 16 : 4 * lead + (part + 1) * 16, :] = acc_ref[
-                    sweep, start : start + 16, :
-                ]
+                put(out_ref, dest, 4 * lead + part * 16, acc_ref[sweep, start : start + 16, :])
 
 
 def packed_columns(place_ref, inject_ref, sweep):
@@ -162,8 +166,8 @@
             base = sweep * lead
             place = sweep * 2 * lead
             out_ref = (early_ref, late_ref)[slab]
-            out_ref[0, place : place + lead, :] = real[base : base + lead]
-            out_ref[0, place + lead : place + 2 * lead, :] = imag[base : base + lead]
+            put(out_ref, 0, place, real[base : base + lead])
+            put(out_ref, 0, place + lead, imag[base : base + lead])
             one = 2 * lead + 2 * sweep * PACK
             two, three = one + PACK, one + 2 * PACK
             total[2 * sweep] += real[one:two] - imag[two:three]
@@ -189,8 +193,20 @@
         x_ref[slab, size:] = jnp.where(left, c_ref[slab, 1].T, -c_ref[slab, 1])
 
 
+def put(ref, dest, start, value):
+    rows, lanes = ref.shape[1] // 2, ref.shape[2]
+    ref[dest, start : start + value.shape[0], :] = value[:, :lanes]
+    ref[dest, rows + start : rows + start + value.shape[0], :] = value[:, lanes:]
+
+
+def taken(ref, source, start, count):
+    rows = ref.shape[1] // 2
+    halves = [ref[source, base + start : base + start + count, :] for base in (0, rows)]
+    return jnp.concatenate(halves, axis=1)
+
+
 def stacked(ref, start, count):
-    return jnp.concatenate([ref[block, start : start + count, :] for block in range(8)], axis=0)
+    return jnp.concatenate([taken(ref, block, start, count) for block in range(8)], axis=0)
 
 
 def pair_map_kernel(
@@ -204,9 +220,9 @@
         (stacked(recv_ref, 2 * item * lead, lead), stacked(recv_ref, (2 * item + 1) * lead, lead))
         for item in range(2)
     ]
-    flow = recv_ref[0, 4 * lead :, :]
+    flow = taken(recv_ref, 0, 4 * lead, 32)
     for block in range(1, 8):
-        flow = flow + recv_ref[block, 4 * lead :, :]
+        flow = flow + taken(recv_ref, block, 4 * lead, 32)
     flow_a = jnp.where(mask_ref[0] != 0, flow, 0.0)
     flow_b = jnp.where(mask_ref[1] != 0, flow, 0.0)
     qa_ref[...] = flow_a
@@ -221,13 +237,15 @@
     second = product(pick(coupled[1], blocks[1]), pick(blocks[1], coupled[0]))
     second = (second[:size], second[size:])
     first_ref[...] = first
-    half = top_ref.shape[0]
+    lanes = size // 2
     both = complex_rows(first, second)
-    top_ref[...] = both[:half]
-    bottom_ref[: 2 * size - half, :] = both[half:]
     flow_a = jnp.where(left, flow_a, complex_rows(flow_a, coupled[1]))
     flow_b = jnp.where(left, flow_b, complex_rows(flow_b, coupled[0]))
-    bottom_ref[2 * size - half :, :] = complex_rows(flow_a, second) + flow_b
+    flow = complex_rows(flow_a, second) + flow_b
+    for side, out_ref in enumerate((top_ref, bottom_ref)):
+        span = slice(side * lanes, (side + 1) * lanes)
+        out_ref[: 2 * size, :] = both[:, span]
+        out_ref[2 * size :, :] = flow[:, span]
 
 
 def item_of(info_ref, item):
@@ -240,19 +258,17 @@
 
 def gather_kernel(info_ref, lead_ref, *refs):
     pieces, (high_ref, low_ref, flow_ref, out_ref) = refs[:8], refs[8:]
-    size = pieces[0].shape[1]
-    half = pieces[0].shape[0]
+    lanes = pieces[0].shape[1]
+    count = 4 * lanes
     for shift in range(4):
         place = lax.rem(info_ref[3] + shift, 4)
-        top, bottom = pieces[2 * shift][...], pieces[2 * shift + 1][...]
-        rest = 2 * size - half
-        high, low = split(top)
-        high_ref[place, :half, :] = high
-        low_ref[place, :half, :] = low
-        high, low = split(bottom[:rest])
-        high_ref[place, half:, :] = high
-        low_ref[place, half:, :] = low
-        flow_ref[place] = bottom[rest:]
+        for side in range(2):
+            piece = pieces[2 * shift + side]
+            span = slice(side * lanes, (side + 1) * lanes)
+            high, low = split(piece[:count, :])
+            high_ref[place, :, span] = high
+            low_ref[place, :, span] = low
+            flow_ref[place, :, span] = piece[count:, :]
     state = lead_ref[...]
     for item in range(4):
         index = item_of(info_ref, item)
@@ -330,12 +346,16 @@
 def inflow_kernel(
     info_ref, lead_ref, state_ref, high_ref, low_ref, flow_ref, spread_ref, out_ref
 ):
-    out_ref[:, 64:, :] = spread_ref[...]
+    rows, late = out_ref.shape[1] // 2, spread_ref.shape[1] // 2
+    for side in range(2):
+        out_ref[:, side * rows + 64 : (side + 1) * rows, :] = spread_ref[
+            :, side * late : (side + 1) * late, :
+        ]
     state = split(entry_state(info_ref, lead_ref, state_ref))
     for item in range(2):
         value = times(state, (high_ref[item], low_ref[item])) + flow_ref[item]
         for dest in range(8):
-            out_ref[dest, 32 * item : 32 * (item + 1), :] = value
+            put(out_ref, dest, 32 * item, value)
 
 
 def state_kernel(
@@ -343,7 +363,7 @@
 ):
     modes = inject_ref.shape[1]
     width = base_ref.shape[1]
-    lead = rows_ref.shape[1] // 4
+    lead = rows_ref.shape[1] // 8
     for sweep, out_ref in enumerate((left_ref, right_ref)):
         target = jnp.broadcast_to(
             inject_ref[sweep : sweep + 1, :].astype(F32), (width, modes)
@@ -359,7 +379,7 @@
             for part in range(2):
                 start = item * 32 + part * 16
                 for member in range(4):
-                    pieces.append(last_ref[sweep * 4 + member, start : start + 16, :])
+                    pieces.append(taken(last_ref, sweep * 4 + member, start, 16))
             parts = split(jnp.concatenate(pieces, axis=0))
             by = []
             for part in range(2):
@@ -424,8 +444,8 @@
             pl.BlockSpec((1, 1, orbitals, width // 2), lambda step: (step // 2, step % 2, 0, 0)),
             pl.BlockSpec((1, 1, orbitals, width // 2), lambda step: (step // 2, step % 2, 0, 1)),
         ],
-        out_specs=whole((8, block_rows, size)),
-        out_shape=jax.ShapeDtypeStruct((8, block_rows, size), F32),
+        out_specs=whole((8, 2 * block_rows, LANES)),
+        out_shape=jax.ShapeDtypeStruct((8, 2 * block_rows, LANES), F32),
         scratch_shapes=[
             pltpu.VMEM((2, stack, width), BF16),
             pltpu.VMEM((2, stack, width), BF16),
@@ -456,13 +476,13 @@
                 pl.BlockSpec((2, 2, part_rows, width), lambda step: (0, 0, step, 0)),
             ],
             out_specs=[
-                pl.BlockSpec((1, 4 * lead, part_rows), lambda step: (step, 0, 0)),
-                pl.BlockSpec((1, 4 * lead, part_rows), lambda step: (step, 0, 0)),
+                pl.BlockSpec((1, 8 * lead, LANES), lambda step: (step, 0, 0)),
+                pl.BlockSpec((1, 8 * lead, LANES), lambda step: (step, 0, 0)),
                 pl.BlockSpec((1, 4 * PACK, part_rows), lambda step: (step, 0, 0)),
             ],
             out_shape=[
-                jax.ShapeDtypeStruct((8, 4 * lead, part_rows), F32),
-                jax.ShapeDtypeStruct((8, 4 * lead, part_rows), F32),
+                jax.ShapeDtypeStruct((8, 8 * lead, LANES), F32),
+                jax.ShapeDtypeStruct((8, 8 * lead, LANES), F32),
                 jax.ShapeDtypeStruct((8, 4 * PACK, part_rows), F32),
             ],
             compiler_params=params(LARGE),
@@ -515,8 +535,8 @@
         in_specs=[SMEM, VMEM, VMEM, VMEM],
         out_specs=[VMEM] * 4,
         out_shape=[
-            jax.ShapeDtypeStruct((size + 16, size), F32),
-            jax.ShapeDtypeStruct((size + 16, size), F32),
+            jax.ShapeDtypeStruct((2 * size + 32, size // 2), F32),
+            jax.ShapeDtypeStruct((2 * size + 32, size // 2), F32),
             jax.ShapeDtypeStruct((32, size), F32),
             jax.ShapeDtypeStruct((2 * size, size), F32),
         ],
@@ -603,7 +623,7 @@
     last = local(
         inflow_kernel,
         "inflow",
-        jax.ShapeDtypeStruct((8, 64 + 4 * lead, size), F32),
+        jax.ShapeDtypeStruct((8, 2 * (64 + 4 * lead), LANES), F32),
         info,
         own_lead,
         flow,

time: 158 us -> 158 us (level)
  no operation moved by 1% of the time
where the time goes in v9:
time: 158 us; the launch traced here: 155 us
  blocking collectives  39.7 us (25%)
  waiting for transfers between devices  37.9 us (24%)
  Pallas kernels  35.3 us (22%)
  starting transfers between devices  21.2 us (13%)
  between operations  16.4 us (10%)
  local copies, waits for them, and re-layouts  2.78 us (2%)
    all_to_all x1, blocking collectives, exchange(): return lax.all_to_all(value, 'col', split_axis=0, concat_axis=0, tiled=True)  39.7 us
    all_to_all x2, waiting for transfers between devices, exchange(): return lax.all_to_all(value, 'col', split_axis=0, concat_axis=0, tiled=True)  18.7 us
    all_to_all x2, starting transfers between devices, exchange(): return lax.all_to_all(value, 'col', split_axis=0, concat_axis=0, tiled=True)  12.2 us
    pallas_call x7, Pallas kernels, local(): pl.pallas_call(kernel, in_specs=[SMEM] + [VMEM] * (len(args) - 1), out_sp...  11.4 us
    ppermute x6, waiting for transfers between devices, turn(): lax.ppermute(value, 'slab', [(slab, slab // 4 * 4 + (slab + step) % 4) fo...  11.4 us
    pallas_call x1, Pallas kernels, chunk_terms(): pl.pallas_call(spread_kernel, grid=(8,), in_specs=[whole(terms.shape), wh...  8.71 us
    pallas_call x1, Pallas kernels, on_device(): pl.pallas_call(interface_kernel, grid=(4,), in_specs=[SMEM, whole(inject....  6.69 us
    ppermute x3, waiting for transfers between devices, hop(): return lax.ppermute(value, ('slab', 'col'), pairs)  6.22 us
  transfers between devices with their start and end apart: 12, of which 10 were waited for; matrix products, arithmetic and copies ran while one was open for 1% of the time, Pallas kernels for 17%

profile of v9, /device:TPU:8, one launch (start us, length us, event | category | flops | bytes accessed | tf_op | source)
XLA Modules:
  0.0 154.7 jit_solution(11461445435209919262)
XLA Ops:
  8.6 6.7 %interface_terms.1 = f32[8,320,128]{2,1,0:T(8,128)} custom-call(s32[2]{0:T(128)} %pad_add_fusion.1.place_ref, s32[2,64]{1,0:T(2,128)} %inject_ref.3, f32[2,2,64,256]{3,2,1,0:T(8,128)} %bitcast.27, f32[2,2,2048,256]{3,2,1,0:T(8,128)} %g_ref.1, f32[2,2,2048,256]{3,2,1,0:T(8,128)} %g_ref.1), custom_call_target="tpu_custom_call" | custom-call | tf_op jit(solution)/shard_map/interface_terms/pallas_call | solution.py:437
  15.3 8.6 %all-to-all-start = ((f32[8,320,128]{2,1,0:T(8,128)}), f32[8,320,128]{2,1,0:T(8,128)S(1)}, u32[]{:S(2)}, u32[]{:S(2)}) async-start(f32[8,320,128]{2,1,0:T(8,128)} %interface_terms.1), calls=%async_computation.1 | async-start | bytes 2621440 | tf_op jit(solution)/shard_map/all_to_all | solution.py:413
  25.4 1.2 select_terms.2
  27.9 8.7 %spread_terms.2 = (f32[8,256,128]{2,1,0:T(8,128)}, f32[8,256,128]{2,1,0:T(8,128)}, f32[8,64,256]{2,1,0:T(8,128)}) custom-call(bf16[2,128,256]{2,1,0:T(8,128)(2,1)} %copy-done.6, bf16[2,128,256]{2,1,0:T(8,128)(2,1)} %copy-done.7, f32[2,2,2048,256]{3,2,1,0:T(8,128)} %g_ref.1), custom_call_target="tpu_custom_call" | custom-call | tf_op jit(solution)/shard_map/spread_terms/pallas_call | solution.py:470
  37.5 1.2 copy-done.4
  39.7 18.7 %all-to-all-done.recv_ref = f32[8,320,128]{2,1,0:T(8,128)S(1)} async-done(((f32[8,320,128]{2,1,0:T(8,128)}), f32[8,320,128]{2,1,0:T(8,128)S(1)}, u32[]{:S(2)}, u32[]{:S(2)}) %all-to-all-start) | async-done | bytes 1310752 | tf_op jit(solution)/shard_map/all_to_all | solution.py:413
  58.5 3.6 %pair_map.1 = (f32[544,128]{1,0:T(8,128)}, f32[544,128]{1,0:T(8,128)}, f32[32,256]{1,0:T(8,128)S(1)}, f32[512,256]{1,0:T(8,128)S(1)}) custom-call(s32[4]{0:T(128)S(1)} %pad_add_fusion.2.team_ref.info_ref, f32[8,320,128]{2,1,0:T(8,128)S(1)} %all-to-all-done.recv_ref, f32[2,512,256]{2,1,0:T(8,128)S(1)} %coupling_rows.1.x_ref, ...), custom_call_target="tpu_custom_call" | custom-call | tf_op jit(solution)/shard_map/pair_map/pallas_call | solution.py:533
  62.1 1.6 %collective-permute-start.2 = (f32[544,128]{1,0:T(8,128)}, f32[544,128]{1,0:T(8,128)S(1)}, u32[]{:S(2)}, u32[]{:S(2)}) collective-permute-start(f32[544,128]{1,0:T(8,128)} %get-tuple-element.110.refs_0_), channel_id=1, source_target_pairs={{0,16},{16,32},{32,48},{48,0},{64,80},{80,96},{96,112},{112,64},{1... | collective-permute-start | bytes 835592 | tf_op jit(solution)/shard_map/ppermute | solution.py:548
  64.1 1.6 %collective-permute-start = (f32[544,128]{1,0:T(8,128)}, f32[544,128]{1,0:T(8,128)}, u32[]{:S(2)}, u32[]{:S(2)}) collective-permute-start(f32[544,128]{1,0:T(8,128)} %get-tuple-element.110.refs_0_), channel_id=1, source_target_pairs={{0,48},{16,0},{32,16},{48,32},{64,112},{80,64},{96,80},{112,96},{1... | collective-permute-start | bytes 835592 | tf_op jit(solution)/shard_map/ppermute | solution.py:548
  66.1 5.7 %collective-permute-done.2.refs_6_ = f32[544,128]{1,0:T(8,128)S(1)} collective-permute-done((f32[544,128]{1,0:T(8,128)}, f32[544,128]{1,0:T(8,128)S(1)}, u32[]{:S(2)}, u32[]{:S(2)}) %collective-permute-start.2) | collective-permute-done | bytes 278560 | tf_op jit(solution)/shard_map/ppermute | solution.py:548
  71.8 1.6 %collective-permute-start.3 = (f32[544,128]{1,0:T(8,128)S(1)}, f32[544,128]{1,0:T(8,128)}, u32[]{:S(2)}, u32[]{:S(2)}) collective-permute-start(f32[544,128]{1,0:T(8,128)S(1)} %collective-permute-done.2.refs_6_), channel_id=1, source_target_pairs={{0,16},{16,32},{32,48},{48,0},{64,80},{80,96},{96,112},{112,64},{1... | collective-permute-start | bytes 835592 | tf_op jit(solution)/shard_map/ppermute | solution.py:548
  74.0 3.6 %all-to-all-start.1 = ((f32[8,256,128]{2,1,0:T(8,128)}), f32[8,256,128]{2,1,0:T(8,128)S(1)}, u32[]{:S(2)}, u32[]{:S(2)}) async-start(f32[8,256,128]{2,1,0:T(8,128)} %get-tuple-element.105), calls=%async_computation.2 | async-start | bytes 2097152 | tf_op jit(solution)/shard_map/all_to_all | solution.py:413
  79.5 3.3 %collective-permute-done.3.refs_4_ = f32[544,128]{1,0:T(8,128)} collective-permute-done((f32[544,128]{1,0:T(8,128)S(1)}, f32[544,128]{1,0:T(8,128)}, u32[]{:S(2)}, u32[]{:S(2)}) %collective-permute-start.3) | collective-permute-done | bytes 278560 | tf_op jit(solution)/shard_map/ppermute | solution.py:548
  82.8 1.3 collective-permute-done.4.refs_5_
  84.1 2.8 %gather_maps.1 = (bf16[4,512,256]{2,1,0:T(8,128)(2,1)S(1)}, bf16[4,512,256]{2,1,0:T(8,128)(2,1)S(1)}, f32[4,32,256]{2,1,0:T(8,128)S(1)}, f32[32,256]{1,0:T(8,128)S(1)}) custom-call(s32[4]{0:T(128)S(1)} %pad_add_fusion.2.team_ref.info_ref, f32[32,256]{1,0:T(8,128)S(1)} %bitcast.22, f32[544,128]{1,0:T(8,128)} %get-tuple-element.110.refs_0_, ...), custom_call_target="tpu_custom_call" | custom-call | flops 30000001024 | tf_op jit(solution)/shard_map/gather_maps/pallas_call | solution.py:563
  87.0 1.8 %collective-permute-start.6 = (f32[32,256]{1,0:T(8,128)S(1)}, f32[32,256]{1,0:T(8,128)S(1)}, u32[]{:S(2)}, u32[]{:S(2)}) collective-permute-start(f32[32,256]{1,0:T(8,128)S(1)} %get-tuple-element.119), channel_id=1, source_target_pairs={{0,64},{2,66},{4,68},{6,70},{8,200},{10,202},{12,204},{14,206},{16... | collective-permute-start | bytes 98312 | tf_op jit(solution)/shard_map/ppermute | solution.py:592
  88.7 3.2 %row_map.1 = (bf16[512,256]{1,0:T(8,128)(2,1)S(1)}, bf16[512,256]{1,0:T(8,128)(2,1)S(1)}, f32[32,256]{1,0:T(8,128)S(1)}, f32[544,256]{1,0:T(8,128)S(1)}) custom-call(s32[4]{0:T(128)S(1)} %pad_add_fusion.2.team_ref.info_ref, bf16[4,512,256]{2,1,0:T(8,128)(2,1)S(1)} %get-tuple-element.120.high_ref, bf16[4,512,256]{2,1,0:T(8,128)(2,1)S(1)} %get-tuple-element.121.low_ref, ...), custom_call_target="tpu_custom_call" | custom-call | tf_op jit(solution)/shard_map/row_map/pallas_call | solution.py:582
  93.1 1.1 collective-permute-start.7
  94.2 1.7 %prefix_map.1 = (f32[544,256]{1,0:T(8,128)S(1)}, f32[544,256]{1,0:T(8,128)S(1)}) custom-call(s32[4]{0:T(128)S(1)} %pad_add_fusion.2.team_ref.info_ref, bf16[4,512,256]{2,1,0:T(8,128)(2,1)S(1)} %get-tuple-element.120.high_ref, bf16[4,512,256]{2,1,0:T(8,128)(2,1)S(1)} %get-tuple-element.121.low_ref, f32[4,32,256]{2,1,0:T(8,128)S(1)} %get-tuple-element.122.flow_ref, ...), custom_call_target="tpu_custom_call" | custom-call | tf_op jit(solution)/shard_map/prefix_map/pallas_call | solution.py:582
  95.9 2.3 %collective-permute-done.7.state_ref = f32[32,256]{1,0:T(8,128)S(1)} collective-permute-done((f32[32,256]{1,0:T(8,128)S(1)}, f32[32,256]{1,0:T(8,128)S(1)}, u32[]{:S(2)}, u32[]{:S(2)}) %collective-permute-start.7) | collective-permute-done | bytes 32800 | tf_op jit(solution)/shard_map/ppermute | solution.py:592
  99.0 1.7 %entry_map.1 = (bf16[2,512,256]{2,1,0:T(8,128)(2,1)S(1)}, bf16[2,512,256]{2,1,0:T(8,128)(2,1)S(1)}, f32[2,32,256]{2,1,0:T(8,128)S(1)}) custom-call(s32[4]{0:T(128)S(1)} %pad_add_fusion.2.team_ref.info_ref, f32[544,256]{1,0:T(8,128)S(1)} %get-tuple-element.134.prefix_ref, f32[544,256]{1,0:T(8,128)S(1)} %get-tuple-element.135.inner_ref, ...), custom_call_target="tpu_custom_call" | custom-call | tf_op jit(solution)/shard_map/entry_map/pallas_call | solution.py:582
  100.7 3.4 %collective-permute-done.8.state_ref = f32[32,256]{1,0:T(8,128)S(1)} collective-permute-done((f32[32,256]{1,0:T(8,128)S(1)}, f32[32,256]{1,0:T(8,128)S(1)}, u32[]{:S(2)}, u32[]{:S(2)}) %collective-permute-start.8) | collective-permute-done | bytes 32800 | tf_op jit(solution)/shard_map/ppermute | solution.py:592
  105.1 39.7 %all_to_all.15.last_ref = f32[8,384,128]{2,1,0:T(8,128)S(1)} all-to-all(f32[8,384,128]{2,1,0:T(8,128)S(1)} %inflow.1), channel_id=1, replica_groups=mesh['slab'=16,'col'=8,'energy'=2] {'col'}, dimensions={0} | all-to-all | bytes 3145728 | tf_op jit(solution)/shard_map/all_to_all | solution.py:413
  144.8 2.4 %states.1 = (f32[2,2,64,256]{3,2,1,0:T(8,128)}, f32[2,2,64,256]{3,2,1,0:T(8,128)}) custom-call(s32[2]{0:T(128)S(1)} %copy-done.9, s32[2,64]{1,0:T(2,128)S(1)} %get-tuple-element.274, f32[8,384,128]{2,1,0:T(8,128)S(1)} %all_to_all.15.last_ref, f32[8,256,128]{2,1,0:T(8,128)S(1)} %all-to-all-done.1.rows_ref, f32[64,256]{1,0:T(8,128)S(1)} %bitcast.26, ...), custom_call_target="tpu_custom_call" | custom-call | tf_op jit(solution)/shard_map/states/pallas_call | solution.py:582
  (49 shorter events, 10.8 us)
Async XLA Ops:
  8.0 31.7 %copy-start = (f32[2,2,256,64]{2,3,1,0:T(8,128)S(1)}, f32[2,2,256,64]{2,3,1,0:T(8,128)}, u32[]{:S(2)}) copy-start(f32[2,2,256,64]{2,3,1,0:T(8,128)} %param.11) | copy-start | bytes 786436
  15.3 8.6 %copy-start.13 = (s32[2,64]{1,0:T(2,128)S(1)}, s32[2,64]{1,0:T(2,128)}, u32[]{:S(2)}) copy-start(s32[2,64]{1,0:T(2,128)} %inject_ref.3) | copy-start | bytes 1540
  15.3 10.0 %copy-start.9 = (s32[2]{0:T(128)S(1)}, s32[2]{0:T(128)}, u32[]{:S(2)}) copy-start(s32[2]{0:T(128)} %pad_add_fusion.1.place_ref) | copy-start | bytes 28
  15.3 10.1 %copy-start.10 = (f32[2,2,256,64]{2,3,1,0:T(8,128)S(1)}, f32[2,2,256,64]{2,3,1,0:T(8,128)}, u32[]{:S(2)}) copy-start(f32[2,2,256,64]{2,3,1,0:T(8,128)} %param.9) | copy-start | bytes 786436
  15.3 43.1 %all-to-all-start = ((f32[8,320,128]{2,1,0:T(8,128)}), f32[8,320,128]{2,1,0:T(8,128)S(1)}, u32[]{:S(2)}, u32[]{:S(2)}) async-start(f32[8,320,128]{2,1,0:T(8,128)} %interface_terms.1), calls=%async_computation.1 | async-start | bytes 2621440 | tf_op jit(solution)/shard_map/all_to_all | solution.py:413
  26.6 0.7 copy-start.6
  27.2 0.7 copy-start.7
  36.6 0.7 copy-start.11
  36.7 41.9 %reduce-scatter.3.cloned.1.call-start = ((), (), s32[]{:S(2)}) async-start(), calls=%async_computation.5 | async-start | bytes 589824 | tf_op jit(solution)/shard_map/reduce_scatter | solution.py:493
  37.5 1.2 copy-start.4
  62.1 9.7 %collective-permute-start.2 = (f32[544,128]{1,0:T(8,128)}, f32[544,128]{1,0:T(8,128)S(1)}, u32[]{:S(2)}, u32[]{:S(2)}) collective-permute-start(f32[544,128]{1,0:T(8,128)} %get-tuple-element.110.refs_0_), channel_id=1, source_target_pairs={{0,16},{16,32},{32,48},{48,0},{64,80},{80,96},{96,112},{112,64},{1... | collective-permute-start | bytes 835592 | tf_op jit(solution)/shard_map/ppermute | solution.py:548
  63.6 9.9 %collective-permute-start.1 = (f32[544,128]{1,0:T(8,128)}, f32[544,128]{1,0:T(8,128)}, u32[]{:S(2)}, u32[]{:S(2)}) collective-permute-start(f32[544,128]{1,0:T(8,128)} %get-tuple-element.111.refs_1_), channel_id=1, source_target_pairs={{0,48},{16,0},{32,16},{48,32},{64,112},{80,64},{96,80},{112,96},{1... | collective-permute-start | bytes 835592 | tf_op jit(solution)/shard_map/ppermute | solution.py:548
  64.1 15.4 %collective-permute-start = (f32[544,128]{1,0:T(8,128)}, f32[544,128]{1,0:T(8,128)}, u32[]{:S(2)}, u32[]{:S(2)}) collective-permute-start(f32[544,128]{1,0:T(8,128)} %get-tuple-element.110.refs_0_), channel_id=1, source_target_pairs={{0,48},{16,0},{32,16},{48,32},{64,112},{80,64},{96,80},{112,96},{1... | collective-permute-start | bytes 835592 | tf_op jit(solution)/shard_map/ppermute | solution.py:548
  65.7 13.8 %collective-permute-start.5 = (f32[544,128]{1,0:T(8,128)}, f32[544,128]{1,0:T(8,128)}, u32[]{:S(2)}, u32[]{:S(2)}) collective-permute-start(f32[544,128]{1,0:T(8,128)} %get-tuple-element.111.refs_1_), channel_id=1, source_target_pairs={{0,16},{16,32},{32,48},{48,0},{64,80},{80,96},{96,112},{112,64},{1... | collective-permute-start | bytes 835592 | tf_op jit(solution)/shard_map/ppermute | solution.py:548
  71.8 11.0 %collective-permute-start.3 = (f32[544,128]{1,0:T(8,128)S(1)}, f32[544,128]{1,0:T(8,128)}, u32[]{:S(2)}, u32[]{:S(2)}) collective-permute-start(f32[544,128]{1,0:T(8,128)S(1)} %collective-permute-done.2.refs_6_), channel_id=1, source_target_pairs={{0,16},{16,32},{32,48},{48,0},{64,80},{80,96},{96,112},{112,64},{1... | collective-permute-start | bytes 835592 | tf_op jit(solution)/shard_map/ppermute | solution.py:548
  73.5 10.6 %collective-permute-start.4 = (f32[544,128]{1,0:T(8,128)}, f32[544,128]{1,0:T(8,128)}, u32[]{:S(2)}, u32[]{:S(2)}) collective-permute-start(f32[544,128]{1,0:T(8,128)} %collective-permute-done.1.refs_3_), channel_id=1, source_target_pairs={{0,48},{16,0},{32,16},{48,32},{64,112},{80,64},{96,80},{112,96},{1... | collective-permute-start | bytes 835592 | tf_op jit(solution)/shard_map/ppermute | solution.py:548
  74.0 31.1 %all-to-all-start.1 = ((f32[8,256,128]{2,1,0:T(8,128)}), f32[8,256,128]{2,1,0:T(8,128)S(1)}, u32[]{:S(2)}, u32[]{:S(2)}) async-start(f32[8,256,128]{2,1,0:T(8,128)} %get-tuple-element.105), calls=%async_computation.2 | async-start | bytes 2097152 | tf_op jit(solution)/shard_map/all_to_all | solution.py:413
  87.0 5.4 %collective-permute-start.6 = (f32[32,256]{1,0:T(8,128)S(1)}, f32[32,256]{1,0:T(8,128)S(1)}, u32[]{:S(2)}, u32[]{:S(2)}) collective-permute-start(f32[32,256]{1,0:T(8,128)S(1)} %get-tuple-element.119), channel_id=1, source_target_pairs={{0,64},{2,66},{4,68},{6,70},{8,200},{10,202},{12,204},{14,206},{16... | collective-permute-start | bytes 98312 | tf_op jit(solution)/shard_map/ppermute | solution.py:592
  93.1 5.2 %collective-permute-start.7 = (f32[32,256]{1,0:T(8,128)S(1)}, f32[32,256]{1,0:T(8,128)S(1)}, u32[]{:S(2)}, u32[]{:S(2)}) collective-permute-start(f32[32,256]{1,0:T(8,128)S(1)} %row_step.2), channel_id=1, source_target_pairs={{0,64},{2,66},{4,68},{6,70},{8,200},{10,202},{12,204},{14,206},{16... | collective-permute-start | bytes 98312 | tf_op jit(solution)/shard_map/ppermute | solution.py:592
  95.9 8.2 %copy-start.5 = (f32[8,256,128]{2,1,0:T(8,128)S(1)}, f32[8,256,128]{2,1,0:T(8,128)}, u32[]{:S(2)}) copy-start(f32[8,256,128]{2,1,0:T(8,128)} %get-tuple-element.139.spread_ref) | copy-start | bytes 3145732
  99.0 5.2 %collective-permute-start.8 = (f32[32,256]{1,0:T(8,128)S(1)}, f32[32,256]{1,0:T(8,128)S(1)}, u32[]{:S(2)}, u32[]{:S(2)}) collective-permute-start(f32[32,256]{1,0:T(8,128)S(1)} %row_step.3), channel_id=1, source_target_pairs={{0,64},{2,66},{4,68},{6,70},{8,200},{10,202},{12,204},{14,206},{16... | collective-permute-start | bytes 98312 | tf_op jit(solution)/shard_map/ppermute | solution.py:592
  105.1 39.8 %copy-start.8 = (f32[1,64,256]{2,1,0:T(8,128)S(1)}, f32[1,64,256]{2,1,0:T(8,128)}, u32[]{:S(2)}) copy-start(f32[1,64,256]{2,1,0:T(8,128)} %reduce-scatter.3.cloned.1.call-done) | copy-start | bytes 196612
  105.1 39.7 %copy-start.12 = (f32[256,256]{1,0:T(8,128)S(1)}, f32[256,256]{1,0:T(8,128)}, u32[]{:S(2)}) copy-start(f32[256,256]{1,0:T(8,128)} %copy-done.11) | copy-start | bytes 786436
Sparse Core Ops, SparseCore 1:
  39.6 38.9 reduce-scatter.2

commit v10 on v9

--- a/solution.py
+++ b/solution.py
@@ -155,7 +155,7 @@
                 low_ref[slab, start : start + PACK, :] = mm(pick, low).astype(BF16)
 
 
-def spread_kernel(high_ref, low_ref, g_ref, early_ref, late_ref, flow_ref):
+def spread_kernel(high_ref, low_ref, g_ref, out_ref, flow_ref):
     lead = g_ref.shape[3] // 8
     total = [0.0] * 4
     for slab in range(2):
@@ -164,8 +164,7 @@
         imag = mm3(parts, split(g_ref[slab, 1]), True)
         for sweep in range(2):
             base = sweep * lead
-            place = sweep * 2 * lead
-            out_ref = (early_ref, late_ref)[slab]
+            place = slab * 4 * lead + sweep * 2 * lead
             put(out_ref, 0, place, real[base : base + lead])
             put(out_ref, 0, place + lead, imag[base : base + lead])
             one = 2 * lead + 2 * sweep * PACK
@@ -343,14 +342,7 @@
         low_ref[item] = low
 
 
-def inflow_kernel(
-    info_ref, lead_ref, state_ref, high_ref, low_ref, flow_ref, spread_ref, out_ref
-):
-    rows, late = out_ref.shape[1] // 2, spread_ref.shape[1] // 2
-    for side in range(2):
-        out_ref[:, side * rows + 64 : (side + 1) * rows, :] = spread_ref[
-            :, side * late : (side + 1) * late, :
-        ]
+def inflow_kernel(info_ref, lead_ref, state_ref, high_ref, low_ref, flow_ref, out_ref):
     state = split(entry_state(info_ref, lead_ref, state_ref))
     for item in range(2):
         value = times(state, (high_ref[item], low_ref[item])) + flow_ref[item]
@@ -358,21 +350,34 @@
             put(out_ref, dest, 32 * item, value)
 
 
-def state_kernel(
-    place_ref, inject_ref, last_ref, rows_ref, base_ref, extra_ref, left_ref, right_ref
+def arrange_kernel(
+    place_ref, inject_ref, recv_ref, base_ref, extra_ref, high_ref, low_ref, out_ref
 ):
+    lead = recv_ref.shape[1] // 16
     modes = inject_ref.shape[1]
     width = base_ref.shape[1]
-    lead = rows_ref.shape[1] // 8
-    for sweep, out_ref in enumerate((left_ref, right_ref)):
+    for slab in range(2):
+        for kind in range(4):
+            high, low = split(stacked(recv_ref, (slab * 4 + kind) * lead, lead))
+            sweep, part = divmod(kind, 2)
+            high_ref[slab, sweep, part] = high
+            low_ref[slab, sweep, part] = low
+    for sweep in range(2):
         target = jnp.broadcast_to(
             inject_ref[sweep : sweep + 1, :].astype(F32), (width, modes)
         ).T
-        bases = []
         for part in range(2):
             start = (2 * sweep + part) * modes
             rows = unpacked_rows(place_ref, inject_ref, base_ref, sweep, part)
-            bases.append(rows + extra_ref[start : start + modes, :])
+            rows = rows + extra_ref[start : start + modes, :]
+            for slab in range(2):
+                chosen = target == (place_ref[0] + slab).astype(F32)
+                out_ref[sweep, slab, part] = jnp.where(chosen, rows, 0.0)
+
+
+def state_kernel(last_ref, high_ref, low_ref, base_ref, left_ref, right_ref):
+    modes = base_ref.shape[3]
+    for sweep, out_ref in enumerate((left_ref, right_ref)):
         for slab in range(2):
             item = slab if sweep == 0 else 1 - slab
             pieces = []
@@ -381,19 +386,14 @@
                 for member in range(4):
                     pieces.append(taken(last_ref, sweep * 4 + member, start, 16))
             parts = split(jnp.concatenate(pieces, axis=0))
-            by = []
-            for part in range(2):
-                kind = 2 * sweep + part
-                if slab == 0:
-                    matrix = stacked(rows_ref, kind * lead, lead)
-                else:
-                    matrix = stacked(last_ref, 64 + kind * lead, lead)
-                by.append(mm3(parts, split(matrix)))
+            by = [
+                mm3(parts, (high_ref[slab, sweep, part], low_ref[slab, sweep, part]))
+                for part in range(2)
+            ]
             value = combined(by[0], by[1])
-            chosen = target == (place_ref[0] + slab).astype(F32)
             for part in range(2):
                 rows = value[part * modes : (part + 1) * modes]
-                out_ref[slab, part] = jnp.where(chosen, bases[part], 0.0) + rows
+                out_ref[slab, part] = base_ref[sweep, slab, part] + rows
 
 
 def params(limit=LIMIT):
@@ -476,13 +476,11 @@
                 pl.BlockSpec((2, 2, part_rows, width), lambda step: (0, 0, step, 0)),
             ],
             out_specs=[
-                pl.BlockSpec((1, 8 * lead, LANES), lambda step: (step, 0, 0)),
-                pl.BlockSpec((1, 8 * lead, LANES), lambda step: (step, 0, 0)),
+                pl.BlockSpec((1, 16 * lead, LANES), lambda step: (step, 0, 0)),
                 pl.BlockSpec((1, 4 * PACK, part_rows), lambda step: (step, 0, 0)),
             ],
             out_shape=[
-                jax.ShapeDtypeStruct((8, 8 * lead, LANES), F32),
-                jax.ShapeDtypeStruct((8, 8 * lead, LANES), F32),
+                jax.ShapeDtypeStruct((8, 16 * lead, LANES), F32),
                 jax.ShapeDtypeStruct((8, 4 * PACK, part_rows), F32),
             ],
             compiler_params=params(LARGE),
@@ -492,7 +490,7 @@
     def summed(flows):
         return lax.psum_scatter(flows, "col", scatter_dimension=0, tiled=False)
 
-    early, late, flows = chunk_terms(place)
+    spread, flows = chunk_terms(place)
     turned = pl.pallas_call(
         coupling_kernel,
         in_specs=[SMEM, VMEM],
@@ -514,7 +512,7 @@
 
     def more(chunk, extra):
         place = jnp.stack([first, chunk]).astype(jnp.int32)
-        flows = chunk_terms(place)[2]
+        flows = chunk_terms(place)[1]
         return pl.pallas_call(
             expand_kernel,
             in_specs=[SMEM, VMEM, VMEM, VMEM],
@@ -525,10 +523,10 @@
         )(place, inject, summed(flows), extra)
 
     extra = lax.fori_loop(1, chunks, more, jnp.zeros((4 * modes, part_rows), F32))
-    received, turned, marks, own_lead, early, extra = lax.optimization_barrier(
-        (received, turned, marks, own_lead, early, extra)
-    )
-    rows = exchange(early)
+    received, turned, marks, own_lead, spread, extra = lax.optimization_barrier(
+        (received, turned, marks, own_lead, spread, extra)
+    )
+    rows = exchange(spread)
 
     top, bottom, flow_a, first_map = pl.pallas_call(
         pair_map_kernel,
@@ -553,7 +551,6 @@
     before_bottom, after_top = turn(bottom, 1), turn(top, -1)
     across_top, across_bottom = turn(before_top, 1), turn(after_bottom, -1)
     pieces = (after_top, after_bottom, across_top, across_bottom, before_top, before_bottom)
-    pieces, base = lax.optimization_barrier((pieces, base))
     row_maps = [
         jax.ShapeDtypeStruct((4, 2 * size, size), BF16),
         jax.ShapeDtypeStruct((4, 2 * size, size), BF16),
@@ -566,7 +563,6 @@
         out_specs=[VMEM] * 4,
         out_shape=row_maps + [state_shape],
         compiler_params=params(),
-        cost_estimate=pl.CostEstimate(flops=30000000000, bytes_accessed=0, transcendentals=0),
         name="gather_maps",
     )(info, own_lead, top, bottom, *pieces)
 
@@ -623,21 +619,32 @@
     last = local(
         inflow_kernel,
         "inflow",
-        jax.ShapeDtypeStruct((8, 2 * (64 + 4 * lead), LANES), F32),
+        jax.ShapeDtypeStruct((8, 2 * 64, LANES), F32),
         info,
         own_lead,
         flow,
         *entry,
-        late,
-    )
-    rows, last = lax.optimization_barrier((rows, last))
+    )
+    rows, base, last = lax.optimization_barrier((rows, base, last))
     last = exchange(last)
-    last, rows, base, extra, inject = lax.optimization_barrier((last, rows, base, extra, inject))
+    arranged = [
+        jax.ShapeDtypeStruct((2, 2, 2, size, part_rows), BF16),
+        jax.ShapeDtypeStruct((2, 2, 2, size, part_rows), BF16),
+        jax.ShapeDtypeStruct((2, 2, 2, modes, part_rows), F32),
+    ]
+    arranged = local(
+        arrange_kernel, "arrange_rows", arranged, place, inject, rows, base, extra
+    )
 
     shape = jax.ShapeDtypeStruct((2, 2, modes, part_rows), F32)
-    left, right = local(
-        state_kernel, "states", [shape, shape], place, inject, last, rows, base, extra
-    )
+    left, right = pl.pallas_call(
+        state_kernel,
+        in_specs=[VMEM] * 4,
+        out_specs=[VMEM, VMEM],
+        out_shape=[shape, shape],
+        compiler_params=params(),
+        name="states",
+    )(last, *arranged)
     return jnp.transpose(left, (0, 1, 3, 2)), jnp.transpose(right, (0, 1, 3, 2))
 
 

time: 158 us -> 148 us (0.937); the launches traced: 155 us -> 148 us
  blocking collectives: 39.7 us -> 0 us
  waiting for transfers between devices: 37.9 us -> 65.4 us
  starting transfers between devices: 21.2 us -> 25.6 us
    all_to_all x1 -> x0, blocking collectives: 39.7 us -> none  [exchange(): return lax.all_to_all(value, 'col', split_axis=0, concat_axis=0, tiled=True)]
    all_to_all x2 -> x3, waiting for transfers between devices: 18.7 us -> 39.2 us  [exchange(): return lax.all_to_all(value, 'col', split_axis=0, concat_axis=0, tiled=True)]
    ppermute x6, waiting for transfers between devices: 11.4 us -> 15.7 us  [turn(): lax.ppermute(value, 'slab', [(slab, slab // 4 * 4 + (slab + step) % 4) fo...]
    all_to_all x2 -> x3, starting transfers between devices: 12.2 us -> 16.5 us  [exchange(): return lax.all_to_all(value, 'col', split_axis=0, concat_axis=0, tiled=True)]
    reduce_scatter x1, waiting for transfers between devices: 1.05 us -> 3.64 us  [summed(): return lax.psum_scatter(flows, 'col', scatter_dimension=0, tiled=False)]
  transfers between devices with their start and end apart: 12 -> 13, of which waited for: 10 -> 11; matrix products, arithmetic and copies ran while one was open for 1% -> 1% of each run, Pallas kernels for 17% -> 19%
where the time goes in v10:
time: 148 us
  waiting for transfers between devices  65.4 us (44%)
  Pallas kernels  35.8 us (24%)
  starting transfers between devices  25.6 us (17%)
  between operations  16.3 us (11%)
  local copies, waits for them, and re-layouts  2.95 us (2%)
  other arithmetic  1.51 us (1%)
    all_to_all x3, waiting for transfers between devices, exchange(): return lax.all_to_all(value, 'col', split_axis=0, concat_axis=0, tiled=True)  39.2 us
    all_to_all x3, starting transfers between devices, exchange(): return lax.all_to_all(value, 'col', split_axis=0, concat_axis=0, tiled=True)  16.5 us
    ppermute x6, waiting for transfers between devices, turn(): lax.ppermute(value, 'slab', [(slab, slab // 4 * 4 + (slab + step) % 4) fo...  15.7 us
    pallas_call x7, Pallas kernels, local(): pl.pallas_call(kernel, in_specs=[SMEM] + [VMEM] * (len(args) - 1), out_sp...  12.4 us
    pallas_call x1, Pallas kernels, chunk_terms(): pl.pallas_call(spread_kernel, grid=(8,), in_specs=[whole(terms.shape), wh...  8.75 us
    pallas_call x1, Pallas kernels, on_device(): pl.pallas_call(interface_kernel, grid=(4,), in_specs=[SMEM, whole(inject....  6.73 us
    ppermute x3, waiting for transfers between devices, hop(): return lax.ppermute(value, ('slab', 'col'), pairs)  6.23 us
    ppermute x6, starting transfers between devices, turn(): lax.ppermute(value, 'slab', [(slab, slab // 4 * 4 + (slab + step) % 4) fo...  6.15 us
  transfers between devices with their start and end apart: 13, of which 11 were waited for; matrix products, arithmetic and copies ran while one was open for 1% of the time, Pallas kernels for 19%

profile of v10, /device:TPU:8, one launch (start us, length us, event | category | flops | bytes accessed | tf_op | source)
XLA Modules:
  0.0 147.5 jit_solution(4021217299604267961)
XLA Ops:
  8.6 6.7 %interface_terms.1 = f32[8,320,128]{2,1,0:T(8,128)} custom-call(s32[2]{0:T(128)} %pad_add_fusion.1.place_ref, s32[2,64]{1,0:T(2,128)} %inject_ref.4, f32[2,2,64,256]{3,2,1,0:T(8,128)} %bitcast.27, f32[2,2,2048,256]{3,2,1,0:T(8,128)} %g_ref.1, f32[2,2,2048,256]{3,2,1,0:T(8,128)} %g_ref.1), custom_call_target="tpu_custom_call" | custom-call | tf_op jit(solution)/shard_map/interface_terms/pallas_call | solution.py:437
  15.3 8.6 %all-to-all-start = ((f32[8,320,128]{2,1,0:T(8,128)}), f32[8,320,128]{2,1,0:T(8,128)S(1)}, u32[]{:S(2)}, u32[]{:S(2)}) async-start(f32[8,320,128]{2,1,0:T(8,128)} %interface_terms.1), calls=%async_computation.1 | async-start | bytes 2621440 | tf_op jit(solution)/shard_map/all_to_all | solution.py:413
  29.6 8.8 %spread_terms.2 = (f32[8,512,128]{2,1,0:T(8,128)}, f32[8,64,256]{2,1,0:T(8,128)}) custom-call(bf16[2,128,256]{2,1,0:T(8,128)(2,1)} %copy-done.5, bf16[2,128,256]{2,1,0:T(8,128)(2,1)} %copy-done.6, f32[2,2,2048,256]{3,2,1,0:T(8,128)} %g_ref.1), custom_call_target="tpu_custom_call" | custom-call | tf_op jit(solution)/shard_map/spread_terms/pallas_call | solution.py:470
  38.5 19.9 %all-to-all-done.recv_ref = f32[8,320,128]{2,1,0:T(8,128)S(1)} async-done(((f32[8,320,128]{2,1,0:T(8,128)}), f32[8,320,128]{2,1,0:T(8,128)S(1)}, u32[]{:S(2)}, u32[]{:S(2)}) %all-to-all-start) | async-done | bytes 1310752 | tf_op jit(solution)/shard_map/all_to_all | solution.py:413
  58.5 4.4 %all-to-all-start.1 = ((f32[8,512,128]{2,1,0:T(8,128)}), f32[8,512,128]{2,1,0:T(8,128)}, u32[]{:S(2)}, u32[]{:S(2)}) async-start(f32[8,512,128]{2,1,0:T(8,128)} %get-tuple-element.96), calls=%async_computation.2 | async-start | bytes 4194304 | tf_op jit(solution)/shard_map/all_to_all | solution.py:413
  63.4 2.8 %pair_map.1 = (f32[544,128]{1,0:T(8,128)S(1)}, f32[544,128]{1,0:T(8,128)S(1)}, f32[32,256]{1,0:T(8,128)S(1)}, f32[512,256]{1,0:T(8,128)S(1)}) custom-call(s32[4]{0:T(128)S(1)} %pad_add_fusion.2.team_ref.info_ref, f32[8,320,128]{2,1,0:T(8,128)S(1)} %all-to-all-done.recv_ref, f32[2,512,256]{2,1,0:T(8,128)S(1)} %coupling_rows.1.x_ref, ...), custom_call_target="tpu_custom_call" | custom-call | tf_op jit(solution)/shard_map/pair_map/pallas_call | solution.py:531
  66.2 1.7 %collective-permute-start.2 = (f32[544,128]{1,0:T(8,128)S(1)}, f32[544,128]{1,0:T(8,128)S(1)}, u32[]{:S(2)}, u32[]{:S(2)}) collective-permute-start(f32[544,128]{1,0:T(8,128)S(1)} %get-tuple-element.102.refs_0_), channel_id=1, source_target_pairs={{0,16},{16,32},{32,48},{48,0},{64,80},{80,96},{96,112},{112,64},{1... | collective-permute-start | bytes 835592 | tf_op jit(solution)/shard_map/ppermute | solution.py:546
  68.3 1.7 %collective-permute-start = (f32[544,128]{1,0:T(8,128)S(1)}, f32[544,128]{1,0:T(8,128)S(1)}, u32[]{:S(2)}, u32[]{:S(2)}) collective-permute-start(f32[544,128]{1,0:T(8,128)S(1)} %get-tuple-element.102.refs_0_), channel_id=1, source_target_pairs={{0,48},{16,0},{32,16},{48,32},{64,112},{80,64},{96,80},{112,96},{1... | collective-permute-start | bytes 835592 | tf_op jit(solution)/shard_map/ppermute | solution.py:546
  70.3 5.5 %collective-permute-done.2.refs_6_ = f32[544,128]{1,0:T(8,128)S(1)} collective-permute-done((f32[544,128]{1,0:T(8,128)S(1)}, f32[544,128]{1,0:T(8,128)S(1)}, u32[]{:S(2)}, u32[]{:S(2)}) %collective-permute-start.2) | collective-permute-done | bytes 278560 | tf_op jit(solution)/shard_map/ppermute | solution.py:546
  77.8 5.5 %collective-permute-done.refs_2_ = f32[544,128]{1,0:T(8,128)S(1)} collective-permute-done((f32[544,128]{1,0:T(8,128)S(1)}, f32[544,128]{1,0:T(8,128)S(1)}, u32[]{:S(2)}, u32[]{:S(2)}) %collective-permute-start) | collective-permute-done | bytes 278560 | tf_op jit(solution)/shard_map/ppermute | solution.py:546
  83.4 3.4 %collective-permute-done.3.refs_4_ = f32[544,128]{1,0:T(8,128)S(1)} collective-permute-done((f32[544,128]{1,0:T(8,128)S(1)}, f32[544,128]{1,0:T(8,128)S(1)}, u32[]{:S(2)}, u32[]{:S(2)}) %collective-permute-start.3) | collective-permute-done | bytes 278560 | tf_op jit(solution)/shard_map/ppermute | solution.py:546
  88.1 1.9 %gather_maps.1 = (bf16[4,512,256]{2,1,0:T(8,128)(2,1)S(1)}, bf16[4,512,256]{2,1,0:T(8,128)(2,1)S(1)}, f32[4,32,256]{2,1,0:T(8,128)S(1)}, f32[32,256]{1,0:T(8,128)S(1)}) custom-call(s32[4]{0:T(128)S(1)} %pad_add_fusion.2.team_ref.info_ref, f32[32,256]{1,0:T(8,128)S(1)} %bitcast.22, f32[544,128]{1,0:T(8,128)S(1)} %get-tuple-element.102.refs_0_, ...), custom_call_target="tpu_custom_call" | custom-call | tf_op jit(solution)/shard_map/gather_maps/pallas_call | solution.py:560
  89.9 1.8 %collective-permute-start.6 = (f32[32,256]{1,0:T(8,128)S(1)}, f32[32,256]{1,0:T(8,128)S(1)}, u32[]{:S(2)}, u32[]{:S(2)}) collective-permute-start(f32[32,256]{1,0:T(8,128)S(1)} %get-tuple-element.104), channel_id=1, source_target_pairs={{0,64},{2,66},{4,68},{6,70},{8,200},{10,202},{12,204},{14,206},{16... | collective-permute-start | bytes 98312 | tf_op jit(solution)/shard_map/ppermute | solution.py:588
  91.7 3.2 %row_map.1 = (bf16[512,256]{1,0:T(8,128)(2,1)S(1)}, bf16[512,256]{1,0:T(8,128)(2,1)S(1)}, f32[32,256]{1,0:T(8,128)S(1)}, f32[544,256]{1,0:T(8,128)S(1)}) custom-call(s32[4]{0:T(128)S(1)} %pad_add_fusion.2.team_ref.info_ref, bf16[4,512,256]{2,1,0:T(8,128)(2,1)S(1)} %get-tuple-element.105.high_ref, bf16[4,512,256]{2,1,0:T(8,128)(2,1)S(1)} %get-tuple-element.106.low_ref, ...), custom_call_target="tpu_custom_call" | custom-call | tf_op jit(solution)/shard_map/row_map/pallas_call | solution.py:578
  97.2 1.7 %prefix_map.1 = (f32[544,256]{1,0:T(8,128)S(1)}, f32[544,256]{1,0:T(8,128)S(1)}) custom-call(s32[4]{0:T(128)S(1)} %pad_add_fusion.2.team_ref.info_ref, bf16[4,512,256]{2,1,0:T(8,128)(2,1)S(1)} %get-tuple-element.105.high_ref, bf16[4,512,256]{2,1,0:T(8,128)(2,1)S(1)} %get-tuple-element.106.low_ref, f32[4,32,256]{2,1,0:T(8,128)S(1)} %get-tuple-element.107.flow_ref, ...), custom_call_target="tpu_custom_call" | custom-call | tf_op jit(solution)/shard_map/prefix_map/pallas_call | solution.py:578
  98.9 2.3 %collective-permute-done.7.state_ref = f32[32,256]{1,0:T(8,128)S(1)} collective-permute-done((f32[32,256]{1,0:T(8,128)S(1)}, f32[32,256]{1,0:T(8,128)S(1)}, u32[]{:S(2)}, u32[]{:S(2)}) %collective-permute-start.7) | collective-permute-done | bytes 32800 | tf_op jit(solution)/shard_map/ppermute | solution.py:588
  102.0 1.7 %entry_map.1 = (bf16[2,512,256]{2,1,0:T(8,128)(2,1)S(1)}, bf16[2,512,256]{2,1,0:T(8,128)(2,1)S(1)}, f32[2,32,256]{2,1,0:T(8,128)S(1)}) custom-call(s32[4]{0:T(128)S(1)} %pad_add_fusion.2.team_ref.info_ref, f32[544,256]{1,0:T(8,128)S(1)} %get-tuple-element.119.prefix_ref, f32[544,256]{1,0:T(8,128)S(1)} %get-tuple-element.120.inner_ref, ...), custom_call_target="tpu_custom_call" | custom-call | tf_op jit(solution)/shard_map/entry_map/pallas_call | solution.py:578
  103.7 3.4 %collective-permute-done.8.state_ref = f32[32,256]{1,0:T(8,128)S(1)} collective-permute-done((f32[32,256]{1,0:T(8,128)S(1)}, f32[32,256]{1,0:T(8,128)S(1)}, u32[]{:S(2)}, u32[]{:S(2)}) %collective-permute-start.8) | collective-permute-done | bytes 32800 | tf_op jit(solution)/shard_map/ppermute | solution.py:588
  107.1 1.7 %inflow.1 = f32[8,128,128]{2,1,0:T(8,128)} custom-call(s32[4]{0:T(128)S(1)} %pad_add_fusion.2.team_ref.info_ref, f32[32,256]{1,0:T(8,128)S(1)} %bitcast.25, f32[32,256]{1,0:T(8,128)S(1)} %collective-permute-done.8.state_ref, bf16[2,512,256]{2,1,0:T(8,128)(2,1)S(1)} %get-tuple-element.121.high_ref, bf16[2,512,256]{2,1,0:T(8,128)(2,1)S(1)} %get-tuple-element.122.low_ref, ...), custom_call_target="tpu_custom_call" | custom-call | tf_op jit(solution)/shard_map/inflow/pallas_call | solution.py:578
  108.8 3.6 %reduce-scatter.3.cloned.1.call-done = f32[1,64,256]{2,1,0:T(8,128)} async-done(((f32[8,64,256]{2,1,0:T(8,128)}), f32[1,64,256]{2,1,0:T(8,128)}) %reduce-scatter.3.cloned.1.call-update) | async-done | bytes 65552 | tf_op jit(solution)/shard_map/reduce_scatter | solution.py:491
  112.5 6.9 %all-to-all-done.1.recv_ref = f32[8,512,128]{2,1,0:T(8,128)} async-done(((f32[8,512,128]{2,1,0:T(8,128)}), f32[8,512,128]{2,1,0:T(8,128)}, u32[]{:S(2)}, u32[]{:S(2)}) %all-to-all-start.1) | async-done | bytes 2097184 | tf_op jit(solution)/shard_map/all_to_all | solution.py:413
  119.4 3.5 %all-to-all-start.2 = ((f32[8,128,128]{2,1,0:T(8,128)}), f32[8,128,128]{2,1,0:T(8,128)S(1)}, u32[]{:S(2)}, u32[]{:S(2)}) async-start(f32[8,128,128]{2,1,0:T(8,128)} %inflow.1), calls=%async_computation.4 | async-start | bytes 1048576 | tf_op jit(solution)/shard_map/all_to_all | solution.py:413
  123.7 2.6 %arrange_rows.1 = (bf16[2,2,2,256,256]{4,3,2,1,0:T(8,128)(2,1)S(1)}, bf16[2,2,2,256,256]{4,3,2,1,0:T(8,128)(2,1)S(1)}, f32[2,2,2,64,256]{4,3,2,1,0:T(8,128)S(1)}) custom-call(s32[2]{0:T(128)S(1)} %copy-done.8, s32[2,64]{1,0:T(2,128)S(1)} %get-tuple-element.266, f32[8,512,128]{2,1,0:T(8,128)} %all-to-all-done.1.recv_ref, f32[64,256]{1,0:T(8,128)S(1)} %bitcast.26, ...), custom_call_target="tpu_custom_call" | custom-call | tf_op jit(solution)/shard_map/arrange_rows/pallas_call | solution.py:578
  126.4 12.4 %all-to-all-done.2.last_ref = f32[8,128,128]{2,1,0:T(8,128)S(1)} async-done(((f32[8,128,128]{2,1,0:T(8,128)}), f32[8,128,128]{2,1,0:T(8,128)S(1)}, u32[]{:S(2)}, u32[]{:S(2)}) %all-to-all-start.2) | async-done | bytes 524320 | tf_op jit(solution)/shard_map/all_to_all | solution.py:413
  (47 shorter events, 15.6 us)
Async XLA Ops:
  8.0 30.4 %copy-start = (f32[2,2,256,64]{2,3,1,0:T(8,128)S(1)}, f32[2,2,256,64]{2,3,1,0:T(8,128)}, u32[]{:S(2)}) copy-start(f32[2,2,256,64]{2,3,1,0:T(8,128)} %param.11) | copy-start | bytes 786436
  15.3 8.6 %copy-start.11 = (s32[2,64]{1,0:T(2,128)S(1)}, s32[2,64]{1,0:T(2,128)}, u32[]{:S(2)}) copy-start(s32[2,64]{1,0:T(2,128)} %inject_ref.4) | copy-start | bytes 1540
  15.3 10.1 %copy-start.8 = (s32[2]{0:T(128)S(1)}, s32[2]{0:T(128)}, u32[]{:S(2)}) copy-start(s32[2]{0:T(128)} %pad_add_fusion.1.place_ref) | copy-start | bytes 28
  15.3 10.1 %copy-start.9 = (f32[2,2,256,64]{2,3,1,0:T(8,128)S(1)}, f32[2,2,256,64]{2,3,1,0:T(8,128)}, u32[]{:S(2)}) copy-start(f32[2,2,256,64]{2,3,1,0:T(8,128)} %param.9) | copy-start | bytes 786436
  15.3 43.0 %all-to-all-start = ((f32[8,320,128]{2,1,0:T(8,128)}), f32[8,320,128]{2,1,0:T(8,128)S(1)}, u32[]{:S(2)}, u32[]{:S(2)}) async-start(f32[8,320,128]{2,1,0:T(8,128)} %interface_terms.1), calls=%async_computation.1 | async-start | bytes 2621440 | tf_op jit(solution)/shard_map/all_to_all | solution.py:413
  26.6 0.7 copy-start.5
  27.3 2.3 %copy-start.6 = (bf16[2,128,256]{2,1,0:T(8,128)(2,1)}, bf16[2,128,256]{2,1,0:T(8,128)(2,1)S(1)}, u32[]{:S(2)}) copy-start(bf16[2,128,256]{2,1,0:T(8,128)(2,1)S(1)} %get-tuple-element.93.low_ref) | copy-start | bytes 393220
  27.4 1.2 copy-start.4
  38.5 20.0 %copy-start.10 = (f32[256,256]{1,0:T(8,128)}, f32[256,256]{1,0:T(8,128)S(1)}, u32[]{:S(2)}) copy-start(f32[256,256]{1,0:T(8,128)S(1)} %get-tuple-element.127.extra_ref) | copy-start | bytes 786436
  58.5 60.9 %all-to-all-start.1 = ((f32[8,512,128]{2,1,0:T(8,128)}), f32[8,512,128]{2,1,0:T(8,128)}, u32[]{:S(2)}, u32[]{:S(2)}) async-start(f32[8,512,128]{2,1,0:T(8,128)} %get-tuple-element.96), calls=%async_computation.2 | async-start | bytes 4194304 | tf_op jit(solution)/shard_map/all_to_all | solution.py:413
  62.8 49.6 %reduce-scatter.3.cloned.1.call-start = ((), (), s32[]{:S(2)}) async-start(), calls=%async_computation.5 | async-start | bytes 589824 | tf_op jit(solution)/shard_map/reduce_scatter | solution.py:491
  66.2 9.6 %collective-permute-start.2 = (f32[544,128]{1,0:T(8,128)S(1)}, f32[544,128]{1,0:T(8,128)S(1)}, u32[]{:S(2)}, u32[]{:S(2)}) collective-permute-start(f32[544,128]{1,0:T(8,128)S(1)} %get-tuple-element.102.refs_0_), channel_id=1, source_target_pairs={{0,16},{16,32},{32,48},{48,0},{64,80},{80,96},{96,112},{112,64},{1... | collective-permute-start | bytes 835592 | tf_op jit(solution)/shard_map/ppermute | solution.py:546
  67.8 9.6 %collective-permute-start.1 = (f32[544,128]{1,0:T(8,128)S(1)}, f32[544,128]{1,0:T(8,128)S(1)}, u32[]{:S(2)}, u32[]{:S(2)}) collective-permute-start(f32[544,128]{1,0:T(8,128)S(1)} %get-tuple-element.103.refs_1_), channel_id=1, source_target_pairs={{0,48},{16,0},{32,16},{48,32},{64,112},{80,64},{96,80},{112,96},{1... | collective-permute-start | bytes 835592 | tf_op jit(solution)/shard_map/ppermute | solution.py:546
  68.3 15.1 %collective-permute-start = (f32[544,128]{1,0:T(8,128)S(1)}, f32[544,128]{1,0:T(8,128)S(1)}, u32[]{:S(2)}, u32[]{:S(2)}) collective-permute-start(f32[544,128]{1,0:T(8,128)S(1)} %get-tuple-element.102.refs_0_), channel_id=1, source_target_pairs={{0,48},{16,0},{32,16},{48,32},{64,112},{80,64},{96,80},{112,96},{1... | collective-permute-start | bytes 835592 | tf_op jit(solution)/shard_map/ppermute | solution.py:546
  70.0 13.4 %collective-permute-start.5 = (f32[544,128]{1,0:T(8,128)S(1)}, f32[544,128]{1,0:T(8,128)S(1)}, u32[]{:S(2)}, u32[]{:S(2)}) collective-permute-start(f32[544,128]{1,0:T(8,128)S(1)} %get-tuple-element.103.refs_1_), channel_id=1, source_target_pairs={{0,16},{16,32},{32,48},{48,0},{64,80},{80,96},{96,112},{112,64},{1... | collective-permute-start | bytes 835592 | tf_op jit(solution)/shard_map/ppermute | solution.py:546
  75.8 11.0 %collective-permute-start.3 = (f32[544,128]{1,0:T(8,128)S(1)}, f32[544,128]{1,0:T(8,128)S(1)}, u32[]{:S(2)}, u32[]{:S(2)}) collective-permute-start(f32[544,128]{1,0:T(8,128)S(1)} %collective-permute-done.2.refs_6_), channel_id=1, source_target_pairs={{0,16},{16,32},{32,48},{48,0},{64,80},{80,96},{96,112},{112,64},{1... | collective-permute-start | bytes 835592 | tf_op jit(solution)/shard_map/ppermute | solution.py:546
  77.4 10.7 %collective-permute-start.4 = (f32[544,128]{1,0:T(8,128)S(1)}, f32[544,128]{1,0:T(8,128)S(1)}, u32[]{:S(2)}, u32[]{:S(2)}) collective-permute-start(f32[544,128]{1,0:T(8,128)S(1)} %collective-permute-done.1.refs_3_), channel_id=1, source_target_pairs={{0,48},{16,0},{32,16},{48,32},{64,112},{80,64},{96,80},{112,96},{1... | collective-permute-start | bytes 835592 | tf_op jit(solution)/shard_map/ppermute | solution.py:546
  89.9 5.4 %collective-permute-start.6 = (f32[32,256]{1,0:T(8,128)S(1)}, f32[32,256]{1,0:T(8,128)S(1)}, u32[]{:S(2)}, u32[]{:S(2)}) collective-permute-start(f32[32,256]{1,0:T(8,128)S(1)} %get-tuple-element.104), channel_id=1, source_target_pairs={{0,64},{2,66},{4,68},{6,70},{8,200},{10,202},{12,204},{14,206},{16... | collective-permute-start | bytes 98312 | tf_op jit(solution)/shard_map/ppermute | solution.py:588
  96.1 5.2 %collective-permute-start.7 = (f32[32,256]{1,0:T(8,128)S(1)}, f32[32,256]{1,0:T(8,128)S(1)}, u32[]{:S(2)}, u32[]{:S(2)}) collective-permute-start(f32[32,256]{1,0:T(8,128)S(1)} %row_step.2), channel_id=1, source_target_pairs={{0,64},{2,66},{4,68},{6,70},{8,200},{10,202},{12,204},{14,206},{16... | collective-permute-start | bytes 98312 | tf_op jit(solution)/shard_map/ppermute | solution.py:588
  102.0 5.2 %collective-permute-start.8 = (f32[32,256]{1,0:T(8,128)S(1)}, f32[32,256]{1,0:T(8,128)S(1)}, u32[]{:S(2)}, u32[]{:S(2)}) collective-permute-start(f32[32,256]{1,0:T(8,128)S(1)} %row_step.3), channel_id=1, source_target_pairs={{0,64},{2,66},{4,68},{6,70},{8,200},{10,202},{12,204},{14,206},{16... | collective-permute-start | bytes 98312 | tf_op jit(solution)/shard_map/ppermute | solution.py:588
  119.4 19.4 %all-to-all-start.2 = ((f32[8,128,128]{2,1,0:T(8,128)}), f32[8,128,128]{2,1,0:T(8,128)S(1)}, u32[]{:S(2)}, u32[]{:S(2)}) async-start(f32[8,128,128]{2,1,0:T(8,128)} %inflow.1), calls=%async_computation.4 | async-start | bytes 1048576 | tf_op jit(solution)/shard_map/all_to_all | solution.py:413
  122.9 0.8 copy-start.7
Sparse Core Ops, SparseCore 1:
  65.8 46.6 reduce-scatter.2

commit v11 on v10

--- a/solution.py
+++ b/solution.py
@@ -11,6 +11,7 @@
 LARGE = 56 * 1024 * 1024
 PACK = 16
 LANES = 128
+SHARE = 32
 
 
 def split(value):
@@ -49,8 +50,9 @@
 
 
 def interface_kernel(
-    place_ref, inject_ref, src_ref, g0_ref, g1_ref, out_ref, high_ref, low_ref, acc_ref
+    place_ref, inject_ref, src_ref, g0_ref, g1_ref, *refs
 ):
+    out_refs, (high_ref, low_ref, acc_ref, columns_ref) = refs[:4], refs[4:]
     step = pl.program_id(0)
     slab = step // 2
     plane = step % 2
@@ -87,14 +89,8 @@
         picked = pl.ds(sweep * half, half)
         term = mm3((high_ref[slab, picked, :], low_ref[slab, picked, :]), split(rows), True)
         order = slab if sweep == 0 else 1 - slab
-        rows, lanes = out_ref.shape[1] // 2, out_ref.shape[2]
-        for side in range(2):
-            place = (order * 2 + plane) * lead + side * rows
-            place = pl.ds(pl.multiple_of(place, 8), lead)
-            for member in range(4):
-                out_ref[sweep * 4 + member, place, :] = term[
-                    :lead, side * lanes : (side + 1) * lanes
-                ]
+        span = pl.ds(pl.multiple_of((order * 2 + plane) * lead, lead), lead)
+        columns_ref[sweep, span, :] = term[:lead]
         real, imag = term[lead : lead + modes], term[lead + modes :]
 
         @pl.when(plane == 0)
@@ -109,11 +105,14 @@
 
     @pl.when(step == 3)
     def _():
-        for dest in range(8):
-            sweep, member = divmod(dest, 4)
+        for turn, out_ref in enumerate(out_refs):
+            worker = lax.rem((place_ref[2] + 1) // 2 + turn, 4)
+            sweep, half = lax.rem(worker, 2), worker // 2
+            out_ref[: 4 * lead, :] = columns_ref[sweep]
             for part in range(2):
-                start = part * modes + member * 16
-                put(out_ref, dest, 4 * lead + part * 16, acc_ref[sweep, start : start + 16, :])
+                start = pl.multiple_of(part * modes + half * SHARE, 8)
+                place = 4 * lead + part * SHARE
+                out_ref[place : place + SHARE, :] = acc_ref[sweep, pl.ds(start, SHARE), :]
 
 
 def packed_columns(place_ref, inject_ref, sweep):
@@ -208,20 +207,20 @@
     return jnp.concatenate([taken(ref, block, start, count) for block in range(8)], axis=0)
 
 
-def pair_map_kernel(
-    team_ref, recv_ref, x_ref, mask_ref, top_ref, bottom_ref, qa_ref, first_ref
-):
-    left = team_ref[0] == 0
+def pair_map_kernel(info_ref, x_ref, mask_ref, *refs):
+    recv_refs, (top_ref, bottom_ref, qa_ref, first_ref, block_ref) = refs[:8], refs[8:]
+    left = info_ref[0] == 0
     size = x_ref.shape[2]
     lead = size // 8
     coupled = [(x_ref[slab, :size], x_ref[slab, size:]) for slab in range(2)]
-    blocks = [
-        (stacked(recv_ref, 2 * item * lead, lead), stacked(recv_ref, (2 * item + 1) * lead, lead))
-        for item in range(2)
-    ]
-    flow = taken(recv_ref, 0, 4 * lead, 32)
-    for block in range(1, 8):
-        flow = flow + taken(recv_ref, block, 4 * lead, 32)
+    flow = 0.0
+    for away, recv_ref in enumerate(recv_refs):
+        source = lax.rem(info_ref[4] + 8 - away, 8)
+        span = pl.ds(pl.multiple_of(source * lead, lead), lead)
+        for item in range(4):
+            block_ref[item, span, :] = recv_ref[item * lead : (item + 1) * lead, :]
+        flow = flow + recv_ref[4 * lead :, :]
+    blocks = [(block_ref[2 * item], block_ref[2 * item + 1]) for item in range(2)]
     flow_a = jnp.where(mask_ref[0] != 0, flow, 0.0)
     flow_b = jnp.where(mask_ref[1] != 0, flow, 0.0)
     qa_ref[...] = flow_a
@@ -307,8 +306,8 @@
     size = high_ref.shape[2]
     left = info_ref[0] == 0
     one, three = item_of(info_ref, 0), item_of(info_ref, 2)
-    rows = lax.broadcasted_iota(jnp.int32, (2 * size + 32, size), 0)
-    cols = lax.broadcasted_iota(jnp.int32, (2 * size + 32, size), 1)
+    rows = lax.broadcasted_iota(jnp.int32, (2 * size + 2 * SHARE, size), 0)
+    cols = lax.broadcasted_iota(jnp.int32, (2 * size + 2 * SHARE, size), 1)
     half = half_ref[...]
     third = (high_ref[three], low_ref[three])
     whole_row = times(split(half[: 2 * size]), third)
@@ -346,8 +345,7 @@
     state = split(entry_state(info_ref, lead_ref, state_ref))
     for item in range(2):
         value = times(state, (high_ref[item], low_ref[item])) + flow_ref[item]
-        for dest in range(8):
-            put(out_ref, dest, 32 * item, value)
+        out_ref[2 * SHARE * item : 2 * SHARE * (item + 1), :] = value
 
 
 def arrange_kernel(
@@ -375,16 +373,24 @@
                 out_ref[sweep, slab, part] = jnp.where(chosen, rows, 0.0)
 
 
-def state_kernel(last_ref, high_ref, low_ref, base_ref, left_ref, right_ref):
+def state_kernel(place_ref, high_ref, low_ref, base_ref, *refs):
+    recv_refs, (left_ref, right_ref, inner_ref) = refs[:8], refs[8:]
     modes = base_ref.shape[3]
+    for away, recv_ref in enumerate(recv_refs):
+        source = lax.rem(place_ref[2] + 8 - away, 8)
+
+        @pl.when(lax.rem(source, 2) == 0)
+        def _(source=source, recv_ref=recv_ref):
+            inner_ref[source // 2] = recv_ref[...]
+
     for sweep, out_ref in enumerate((left_ref, right_ref)):
         for slab in range(2):
             item = slab if sweep == 0 else 1 - slab
             pieces = []
             for part in range(2):
-                start = item * 32 + part * 16
-                for member in range(4):
-                    pieces.append(taken(last_ref, sweep * 4 + member, start, 16))
+                start = (item * 2 + part) * SHARE
+                for half in range(2):
+                    pieces.append(inner_ref[sweep + 2 * half, start : start + SHARE, :])
             parts = split(jnp.concatenate(pieces, axis=0))
             by = [
                 mm3(parts, (high_ref[slab, sweep, part], low_ref[slab, sweep, part]))
@@ -423,14 +429,15 @@
     slabs = lax.axis_size("slab")
     slab_index = lax.axis_index("slab")
     col_index = lax.axis_index("col")
-    team = col_index // 4
-    member = col_index % 4
+    team = col_index // 2 % 2
+    member = col_index // 4
     first = slab_index * 2
-    place = jnp.stack([first, jnp.zeros_like(first)]).astype(jnp.int32)
+    place = jnp.stack([first, jnp.zeros_like(first), col_index]).astype(jnp.int32)
     position = jnp.where(team == 0, slab_index, slabs - 1 - slab_index)
-    info = jnp.stack([team, position // 4, position % 4, slab_index % 4]).astype(jnp.int32)
+    info = [team, position // 4, position % 4, slab_index % 4, col_index]
+    info = jnp.stack(info).astype(jnp.int32)
     stack = 2 * (lead + 2 * modes)
-    block_rows = 4 * lead + 32
+    block = jax.ShapeDtypeStruct((4 * lead + 2 * SHARE, size), F32)
     sources = jnp.transpose(sources, (0, 1, 3, 2))
     leads = jnp.transpose(leads, (0, 1, 3, 2))
 
@@ -444,18 +451,28 @@
             pl.BlockSpec((1, 1, orbitals, width // 2), lambda step: (step // 2, step % 2, 0, 0)),
             pl.BlockSpec((1, 1, orbitals, width // 2), lambda step: (step // 2, step % 2, 0, 1)),
         ],
-        out_specs=whole((8, 2 * block_rows, LANES)),
-        out_shape=jax.ShapeDtypeStruct((8, 2 * block_rows, LANES), F32),
+        out_specs=[whole(block.shape)] * 4,
+        out_shape=[block] * 4,
         scratch_shapes=[
             pltpu.VMEM((2, stack, width), BF16),
             pltpu.VMEM((2, stack, width), BF16),
             pltpu.VMEM((2, 2 * modes, size), F32),
+            pltpu.VMEM((2, 4 * lead, size), F32),
         ],
         compiler_params=params(LARGE),
         name="interface_terms",
     )(place, inject, sources, diag_inverse, diag_inverse)
-    sent, inject_after = lax.optimization_barrier((sent, inject))
-    received = exchange(sent)
+    received = [sent[0]] + [
+        lax.ppermute(
+            sent[away // 2],
+            "col",
+            [(col, (col + away) % 8) for col in range(8) if (col + away) % 2 == 0],
+        )
+        for away in range(1, 8)
+    ]
+    received[1], received[7], inject_after = lax.optimization_barrier(
+        (received[1], received[7], inject)
+    )
 
     def chunk_terms(place):
         terms = jax.ShapeDtypeStruct((2, 2 * lead + 4 * PACK, width), BF16)
@@ -499,12 +516,12 @@
         compiler_params=params(),
         name="coupling_rows",
     )(info, couplings)
-    own_inject = lax.dynamic_slice(inject, (team, member * 16), (1, 16))[0]
+    own_inject = lax.dynamic_slice(inject, (team, member * SHARE), (1, SHARE))[0]
     own_inject = jnp.concatenate([own_inject, own_inject])
     marks = jnp.stack([own_inject == first + team, own_inject == first + 1 - team])
-    marks = jnp.broadcast_to(marks.astype(F32)[:, :, None], (2, 32, size))
-    own_lead = lax.dynamic_slice(leads, (team, 0, member * 16, 0), (1, 2, 16, size))
-    own_lead = own_lead.reshape(32, size)
+    marks = jnp.broadcast_to(marks.astype(F32)[:, :, None], (2, 2 * SHARE, size))
+    own_lead = lax.dynamic_slice(leads, (team, 0, member * SHARE, 0), (1, 2, SHARE, size))
+    own_lead = own_lead.reshape(2 * SHARE, size)
     base = summed(flows)
     owners = jnp.arange(slabs, dtype=jnp.int32)[:, None, None]
     counts = jnp.sum((inject_after[None] >> 1 == owners).astype(jnp.int32), axis=2)
@@ -530,17 +547,18 @@
 
     top, bottom, flow_a, first_map = pl.pallas_call(
         pair_map_kernel,
-        in_specs=[SMEM, VMEM, VMEM, VMEM],
+        in_specs=[SMEM] + [VMEM] * 10,
         out_specs=[VMEM] * 4,
         out_shape=[
-            jax.ShapeDtypeStruct((2 * size + 32, size // 2), F32),
-            jax.ShapeDtypeStruct((2 * size + 32, size // 2), F32),
-            jax.ShapeDtypeStruct((32, size), F32),
+            jax.ShapeDtypeStruct((2 * size + 2 * SHARE, size // 2), F32),
+            jax.ShapeDtypeStruct((2 * size + 2 * SHARE, size // 2), F32),
+            jax.ShapeDtypeStruct((2 * SHARE, size), F32),
             jax.ShapeDtypeStruct((2 * size, size), F32),
         ],
+        scratch_shapes=[pltpu.VMEM((4, size, size), F32)],
         compiler_params=params(),
         name="pair_map",
-    )(info, received, turned, marks)
+    )(info, turned, marks, *received)
 
     def turn(value, step):
         return lax.ppermute(
@@ -554,9 +572,9 @@
     row_maps = [
         jax.ShapeDtypeStruct((4, 2 * size, size), BF16),
         jax.ShapeDtypeStruct((4, 2 * size, size), BF16),
-        jax.ShapeDtypeStruct((4, 32, size), F32),
+        jax.ShapeDtypeStruct((4, 2 * SHARE, size), F32),
     ]
-    state_shape = jax.ShapeDtypeStruct((32, size), F32)
+    state_shape = jax.ShapeDtypeStruct((2 * SHARE, size), F32)
     *maps, flow = pl.pallas_call(
         gather_kernel,
         in_specs=[SMEM] + [VMEM] * 9,
@@ -570,7 +588,7 @@
     pairs = []
     for slab in range(slabs):
         for col in range(cols):
-            target = (slab + (4 if col < 4 else -4)) % slabs
+            target = (slab + (4 if col // 2 % 2 == 0 else -4)) % slabs
             pairs.append((slab * cols + col, target * cols + col))
 
     def local(kernel, name, shapes, *args):
@@ -587,7 +605,7 @@
     def hop(value):
         return lax.ppermute(value, ("slab", "col"), pairs)
 
-    full = jax.ShapeDtypeStruct((2 * size + 32, size), F32)
+    full = jax.ShapeDtypeStruct((2 * size + 2 * SHARE, size), F32)
     half_map = jax.ShapeDtypeStruct((2 * size, size), BF16)
     flow = hop(flow)
     *row_map, half_row = local(
@@ -613,20 +631,23 @@
     two_maps = [
         jax.ShapeDtypeStruct((2, 2 * size, size), BF16),
         jax.ShapeDtypeStruct((2, 2 * size, size), BF16),
-        jax.ShapeDtypeStruct((2, 32, size), F32),
+        jax.ShapeDtypeStruct((2, 2 * SHARE, size), F32),
     ]
     entry = local(entry_map_kernel, "entry_map", two_maps, info, prefix, inner_map, turned)
     last = local(
         inflow_kernel,
         "inflow",
-        jax.ShapeDtypeStruct((8, 2 * 64, LANES), F32),
+        jax.ShapeDtypeStruct((4 * SHARE, size), F32),
         info,
         own_lead,
         flow,
         *entry,
     )
     rows, base, last = lax.optimization_barrier((rows, base, last))
-    last = exchange(last)
+    last = [last] + [
+        lax.ppermute(last, "col", [(col, (col + away) % 8) for col in range(0, 8, 2)])
+        for away in range(1, 8)
+    ]
     arranged = [
         jax.ShapeDtypeStruct((2, 2, 2, size, part_rows), BF16),
         jax.ShapeDtypeStruct((2, 2, 2, size, part_rows), BF16),
@@ -639,12 +660,13 @@
     shape = jax.ShapeDtypeStruct((2, 2, modes, part_rows), F32)
     left, right = pl.pallas_call(
         state_kernel,
-        in_specs=[VMEM] * 4,
+        in_specs=[SMEM] + [VMEM] * 11,
         out_specs=[VMEM, VMEM],
         out_shape=[shape, shape],
+        scratch_shapes=[pltpu.VMEM((4, 4 * SHARE, size), F32)],
         compiler_params=params(),
         name="states",
-    )(last, *arranged)
+    )(place, *arranged, *last)
     return jnp.transpose(left, (0, 1, 3, 2)), jnp.transpose(right, (0, 1, 3, 2))
 
 

time: 148 us -> 167 us (1.13)
  starting transfers between devices: 25.6 us -> 54.2 us
  waiting for transfers between devices: 65.4 us -> 54.1 us
    ppermute x0 -> x14, starting transfers between devices: none -> 40.8 us  [the longest x7 21.8 us: on_device(): lax.ppermute(sent[away // 2], 'col', [(col, (col + away) % 8) for col in...]
    all_to_all x3 -> x1, waiting for transfers between devices: 39.2 us -> 7.56 us  [exchange(): return lax.all_to_all(value, 'col', split_axis=0, concat_axis=0, tiled=True)]
    ppermute x0 -> x14, waiting for transfers between devices: none -> 20.7 us  [the longest x7 15.3 us: on_device(): lax.ppermute(sent[away // 2], 'col', [(col, (col + away) % 8) for col in...]
    all_to_all x3 -> x1, starting transfers between devices: 16.5 us -> 4.51 us  [exchange(): return lax.all_to_all(value, 'col', split_axis=0, concat_axis=0, tiled=True)]
    reduce_scatter x1, waiting for transfers between devices: 3.64 us -> 1.45 us  [summed(): return lax.psum_scatter(flows, 'col', scatter_dimension=0, tiled=False)]
  transfers between devices with their start and end apart: 13 -> 25, of which waited for: 11 -> 13; matrix products, arithmetic and copies ran while one was open for 1% -> 1% of each run, Pallas kernels for 19% -> 17%
where the time goes in v11:
time: 167 us; the launch traced here: 165 us
  starting transfers between devices  54.2 us (32%)
  waiting for transfers between devices  54.1 us (32%)
  Pallas kernels  36.3 us (22%)
  between operations  16.6 us (10%)
  local copies, waits for them, and re-layouts  2.47 us (1%)
    ppermute x7, starting transfers between devices, on_device(): lax.ppermute(sent[away // 2], 'col', [(col, (col + away) % 8) for col in...  21.8 us
    ppermute x7, starting transfers between devices, on_device(): lax.ppermute(last, 'col', [(col, (col + away) % 8) for col in range(0, 8,...  19 us
    ppermute x6, waiting for transfers between devices, turn(): lax.ppermute(value, 'slab', [(slab, slab // 4 * 4 + (slab + step) % 4) fo...  16.5 us
    ppermute x7, waiting for transfers between devices, on_device(): lax.ppermute(sent[away // 2], 'col', [(col, (col + away) % 8) for col in...  15.3 us
    pallas_call x7, Pallas kernels, local(): pl.pallas_call(kernel, in_specs=[SMEM] + [VMEM] * (len(args) - 1), out_sp...  11.7 us
    pallas_call x1, Pallas kernels, chunk_terms(): pl.pallas_call(spread_kernel, grid=(8,), in_specs=[whole(terms.shape), wh...  8.72 us
    all_to_all x1, waiting for transfers between devices, exchange(): return lax.all_to_all(value, 'col', split_axis=0, concat_axis=0, tiled=True)  7.56 us
    ppermute x3, waiting for transfers between devices, hop(): return lax.ppermute(value, ('slab', 'col'), pairs)  7.49 us
  transfers between devices with their start and end apart: 25, of which 13 were waited for; matrix products, arithmetic and copies ran while one was open for 1% of the time, Pallas kernels for 17%

profile of v11, /device:TPU:8, one launch (start us, length us, event | category | flops | bytes accessed | tf_op | source)
XLA Modules:
  0.0 165.2 jit_solution(11928039387073805498)
XLA Ops:
  8.6 6.7 %interface_terms.1 = (f32[192,256]{1,0:T(8,128)}, f32[192,256]{1,0:T(8,128)}, f32[192,256]{1,0:T(8,128)}, f32[192,256]{1,0:T(8,128)}) custom-call(s32[3]{0:T(128)} %pad_add_fusion.1.place_ref, s32[2,64]{1,0:T(2,128)} %inject_ref.4, f32[2,2,64,256]{3,2,1,0:T(8,128)} %bitcast.28, f32[2,2,2048,256]{3,2,1,0:T(8,128)} %g_ref.1, f32[2,2,2048,256]{3,2,1,0:T(8,128)} %g_ref.1), custom_call_target="tpu_custom_call" | custom-call | tf_op jit(solution)/shard_map/interface_terms/pallas_call | solution.py:444
  15.3 8.3 %collective-permute-start.6 = (f32[192,256]{1,0:T(8,128)}, f32[192,256]{1,0:T(8,128)S(1)}, u32[]{:S(2)}, u32[]{:S(2)}) collective-permute-start(f32[192,256]{1,0:T(8,128)} %get-tuple-element.103), channel_id=1, source_target_pairs={{0,12},{4,0},{8,4},{12,8},{1,13},{5,1},{9,5},{13,9},{16,28},{20,16... | collective-permute-start | bytes 589832 | tf_op jit(solution)/shard_map/ppermute | solution.py:466
  26.3 1.9 %collective-permute-start.2 = (f32[192,256]{1,0:T(8,128)}, f32[192,256]{1,0:T(8,128)S(1)}, u32[]{:S(2)}, u32[]{:S(2)}) collective-permute-start(f32[192,256]{1,0:T(8,128)} %get-tuple-element.105), channel_id=1, source_target_pairs={{0,4},{4,8},{8,12},{12,0},{1,5},{5,9},{9,13},{13,1},{16,20},{20,24... | collective-permute-start | bytes 589832 | tf_op jit(solution)/shard_map/ppermute | solution.py:466
  30.8 15.3 %collective-permute-done.refs_1_ = f32[192,256]{1,0:T(8,128)S(1)} collective-permute-done((f32[192,256]{1,0:T(8,128)}, f32[192,256]{1,0:T(8,128)S(1)}, u32[]{:S(2)}, u32[]{:S(2)}) %collective-permute-start) | collective-permute-done | bytes 196640 | tf_op jit(solution)/shard_map/ppermute | solution.py:466
  47.4 6.4 %collective-permute-start.4 = (f32[192,256]{1,0:T(8,128)}, f32[192,256]{1,0:T(8,128)S(1)}, u32[]{:S(2)}, u32[]{:S(2)}) collective-permute-start(f32[192,256]{1,0:T(8,128)} %get-tuple-element.106), channel_id=1, source_target_pairs={{0,8},{4,12},{8,0},{12,4},{1,9},{5,13},{9,1},{13,5},{16,24},{20,28... | collective-permute-start | bytes 589832 | tf_op jit(solution)/shard_map/ppermute | solution.py:466
  58.1 8.7 %spread_terms.2 = (f32[8,512,128]{2,1,0:T(8,128)}, f32[8,64,256]{2,1,0:T(8,128)}) custom-call(bf16[2,128,256]{2,1,0:T(8,128)(2,1)} %copy-done.8, bf16[2,128,256]{2,1,0:T(8,128)(2,1)} %copy-done.9, f32[2,2,2048,256]{3,2,1,0:T(8,128)} %g_ref.1), custom_call_target="tpu_custom_call" | custom-call | tf_op jit(solution)/shard_map/spread_terms/pallas_call | solution.py:487
  67.1 4.5 %all-to-all-start = ((f32[8,512,128]{2,1,0:T(8,128)}), f32[8,512,128]{2,1,0:T(8,128)}, u32[]{:S(2)}, u32[]{:S(2)}) async-start(f32[8,512,128]{2,1,0:T(8,128)} %get-tuple-element.113), calls=%async_computation.1 | async-start | bytes 4194304 | tf_op jit(solution)/shard_map/all_to_all | solution.py:419
  72.2 2.9 %pair_map.1 = (f32[576,128]{1,0:T(8,128)S(1)}, f32[576,128]{1,0:T(8,128)S(1)}, f32[64,256]{1,0:T(8,128)S(1)}, f32[512,256]{1,0:T(8,128)S(1)}) custom-call(s32[5]{0:T(128)S(1)} %stack.46.team_ref.info_ref, f32[2,512,256]{2,1,0:T(8,128)S(1)} %coupling_rows.1.x_ref, f32[2,64,256]{2,1,0:T(8,128)S(1)} %broadcast_in_dim.4.mask_ref, f32[192,256]{1,0:T(8,128)S(1)} %copy-done.5, ...), custom_call_target="tpu_custom_call" | custom-call | tf_op jit(solution)/shard_map/pair_map/pallas_call | solution.py:548
  79.2 5.9 %collective-permute-done.9.refs_6_ = f32[576,128]{1,0:T(8,128)S(1)} collective-permute-done((f32[576,128]{1,0:T(8,128)S(1)}, f32[576,128]{1,0:T(8,128)S(1)}, u32[]{:S(2)}, u32[]{:S(2)}) %collective-permute-start.9) | collective-permute-done | bytes 294944 | tf_op jit(solution)/shard_map/ppermute | solution.py:564
  87.1 5.9 %collective-permute-done.7.refs_2_ = f32[576,128]{1,0:T(8,128)S(1)} collective-permute-done((f32[576,128]{1,0:T(8,128)S(1)}, f32[576,128]{1,0:T(8,128)S(1)}, u32[]{:S(2)}, u32[]{:S(2)}) %collective-permute-start.7) | collective-permute-done | bytes 294944 | tf_op jit(solution)/shard_map/ppermute | solution.py:564
  93.0 3.4 %collective-permute-done.10.refs_4_ = f32[576,128]{1,0:T(8,128)S(1)} collective-permute-done((f32[576,128]{1,0:T(8,128)S(1)}, f32[576,128]{1,0:T(8,128)S(1)}, u32[]{:S(2)}, u32[]{:S(2)}) %collective-permute-start.10) | collective-permute-done | bytes 294944 | tf_op jit(solution)/shard_map/ppermute | solution.py:564
  97.7 1.9 %gather_maps.1 = (bf16[4,512,256]{2,1,0:T(8,128)(2,1)S(1)}, bf16[4,512,256]{2,1,0:T(8,128)(2,1)S(1)}, f32[4,64,256]{2,1,0:T(8,128)S(1)}, f32[64,256]{1,0:T(8,128)S(1)}) custom-call(s32[5]{0:T(128)S(1)} %stack.46.team_ref.info_ref, f32[64,256]{1,0:T(8,128)S(1)} %bitcast.23, f32[576,128]{1,0:T(8,128)S(1)} %get-tuple-element.126.refs_0_, ...), custom_call_target="tpu_custom_call" | custom-call | tf_op jit(solution)/shard_map/gather_maps/pallas_call | solution.py:578
  99.6 1.8 %collective-permute-start.13 = (f32[64,256]{1,0:T(8,128)S(1)}, f32[64,256]{1,0:T(8,128)S(1)}, u32[]{:S(2)}, u32[]{:S(2)}) collective-permute-start(f32[64,256]{1,0:T(8,128)S(1)} %get-tuple-element.128), channel_id=1, source_target_pairs={{0,64},{2,66},{4,196},{6,198},{8,72},{10,74},{12,204},{14,206},{16... | collective-permute-start | bytes 196616 | tf_op jit(solution)/shard_map/ppermute | solution.py:606
  101.4 3.2 %row_map.1 = (bf16[512,256]{1,0:T(8,128)(2,1)S(1)}, bf16[512,256]{1,0:T(8,128)(2,1)S(1)}, f32[64,256]{1,0:T(8,128)S(1)}, f32[576,256]{1,0:T(8,128)S(1)}) custom-call(s32[5]{0:T(128)S(1)} %stack.46.team_ref.info_ref, bf16[4,512,256]{2,1,0:T(8,128)(2,1)S(1)} %get-tuple-element.129.high_ref, bf16[4,512,256]{2,1,0:T(8,128)(2,1)S(1)} %get-tuple-element.130.low_ref, ...), custom_call_target="tpu_custom_call" | custom-call | tf_op jit(solution)/shard_map/row_map/pallas_call | solution.py:596
  106.9 1.7 %prefix_map.1 = (f32[576,256]{1,0:T(8,128)S(1)}, f32[576,256]{1,0:T(8,128)S(1)}) custom-call(s32[5]{0:T(128)S(1)} %stack.46.team_ref.info_ref, bf16[4,512,256]{2,1,0:T(8,128)(2,1)S(1)} %get-tuple-element.129.high_ref, bf16[4,512,256]{2,1,0:T(8,128)(2,1)S(1)} %get-tuple-element.130.low_ref, f32[4,64,256]{2,1,0:T(8,128)S(1)} %get-tuple-element.131.flow_ref, ...), custom_call_target="tpu_custom_call" | custom-call | tf_op jit(solution)/shard_map/prefix_map/pallas_call | solution.py:596
  108.7 3.0 %collective-permute-done.14.state_ref = f32[64,256]{1,0:T(8,128)S(1)} collective-permute-done((f32[64,256]{1,0:T(8,128)S(1)}, f32[64,256]{1,0:T(8,128)S(1)}, u32[]{:S(2)}, u32[]{:S(2)}) %collective-permute-start.14) | collective-permute-done | bytes 65568 | tf_op jit(solution)/shard_map/ppermute | solution.py:606
  114.2 3.7 %collective-permute-done.15.state_ref = f32[64,256]{1,0:T(8,128)S(1)} collective-permute-done((f32[64,256]{1,0:T(8,128)S(1)}, f32[64,256]{1,0:T(8,128)S(1)}, u32[]{:S(2)}, u32[]{:S(2)}) %collective-permute-start.15) | collective-permute-done | bytes 65568 | tf_op jit(solution)/shard_map/ppermute | solution.py:606
  120.3 7.6 %all-to-all-done.recv_ref = f32[8,512,128]{2,1,0:T(8,128)} async-done(((f32[8,512,128]{2,1,0:T(8,128)}), f32[8,512,128]{2,1,0:T(8,128)}, u32[]{:S(2)}, u32[]{:S(2)}) %all-to-all-start) | async-done | bytes 2097184 | tf_op jit(solution)/shard_map/all_to_all | solution.py:419
  129.1 3.6 %collective-permute-start.21 = (f32[128,256]{1,0:T(8,128)S(1)}, f32[128,256]{1,0:T(8,128)S(1)}, u32[]{:S(2)}, u32[]{:S(2)}) collective-permute-start(f32[128,256]{1,0:T(8,128)S(1)} %inflow.1.refs_0_), channel_id=1, source_target_pairs={{0,12},{4,0},{8,4},{12,8},{1,13},{5,1},{9,5},{13,9},{16,28},{20,16... | collective-permute-start | bytes 393224 | tf_op jit(solution)/shard_map/ppermute | solution.py:648
  134.1 6.5 %collective-permute-start.19 = (f32[128,256]{1,0:T(8,128)S(1)}, f32[128,256]{1,0:T(8,128)S(1)}, u32[]{:S(2)}, u32[]{:S(2)}) collective-permute-start(f32[128,256]{1,0:T(8,128)S(1)} %inflow.1.refs_0_), channel_id=1, source_target_pairs={{0,8},{4,12},{8,0},{12,4},{1,9},{5,13},{9,1},{13,5},{16,24},{20,28... | collective-permute-start | bytes 393224 | tf_op jit(solution)/shard_map/ppermute | solution.py:648
  141.9 3.8 %collective-permute-start.17 = (f32[128,256]{1,0:T(8,128)S(1)}, f32[128,256]{1,0:T(8,128)S(1)}, u32[]{:S(2)}, u32[]{:S(2)}) collective-permute-start(f32[128,256]{1,0:T(8,128)S(1)} %inflow.1.refs_0_), channel_id=1, source_target_pairs={{0,4},{4,8},{8,12},{12,0},{1,5},{5,9},{9,13},{13,1},{16,20},{20,24... | collective-permute-start | bytes 393224 | tf_op jit(solution)/shard_map/ppermute | solution.py:648
  147.8 2.6 %arrange_rows.1 = (bf16[2,2,2,256,256]{4,3,2,1,0:T(8,128)(2,1)S(1)}, bf16[2,2,2,256,256]{4,3,2,1,0:T(8,128)(2,1)S(1)}, f32[2,2,2,64,256]{4,3,2,1,0:T(8,128)S(1)}) custom-call(s32[3]{0:T(128)S(1)} %copy-done.11, s32[2,64]{1,0:T(2,128)S(1)} %get-tuple-element.308, f32[8,512,128]{2,1,0:T(8,128)} %all-to-all-done.recv_ref, f32[64,256]{1,0:T(8,128)S(1)} %bitcast.27, ...), custom_call_target="tpu_custom_call" | custom-call | tf_op jit(solution)/shard_map/arrange_rows/pallas_call | solution.py:596
  151.0 4.1 %collective-permute-done.17.refs_2_ = f32[128,256]{1,0:T(8,128)S(1)} collective-permute-done((f32[128,256]{1,0:T(8,128)S(1)}, f32[128,256]{1,0:T(8,128)S(1)}, u32[]{:S(2)}, u32[]{:S(2)}) %collective-permute-start.17) | collective-permute-done | bytes 131104 | tf_op jit(solution)/shard_map/ppermute | solution.py:648
  155.8 2.0 %states.1 = (f32[2,2,64,256]{3,2,1,0:T(8,128)}, f32[2,2,64,256]{3,2,1,0:T(8,128)}) custom-call(s32[3]{0:T(128)S(1)} %copy-done.11, bf16[2,2,2,256,256]{4,3,2,1,0:T(8,128)(2,1)S(1)} %get-tuple-element.151.high_ref, bf16[2,2,2,256,256]{4,3,2,1,0:T(8,128)(2,1)S(1)} %get-tuple-element.152.low_ref, f32[2,2,2,64,256]{4,3,2,1,0:T(8,128)S(1)} %get-tuple-element.153.base_ref, ...), custom_call_target="tpu_custom_call" | custom-call | tf_op jit(solution)/shard_map/states/pallas_call | solution.py:661
  (75 shorter events, 33.2 us)
Async XLA Ops:
  15.3 51.6 %collective-permute-start.6 = (f32[192,256]{1,0:T(8,128)}, f32[192,256]{1,0:T(8,128)S(1)}, u32[]{:S(2)}, u32[]{:S(2)}) collective-permute-start(f32[192,256]{1,0:T(8,128)} %get-tuple-element.103), channel_id=1, source_target_pairs={{0,12},{4,0},{8,4},{12,8},{1,13},{5,1},{9,5},{13,9},{16,28},{20,16... | collective-permute-start | bytes 589832 | tf_op jit(solution)/shard_map/ppermute | solution.py:466
  23.7 23.7 %collective-permute-start.1 = (f32[192,256]{1,0:T(8,128)}, f32[192,256]{1,0:T(8,128)S(1)}, u32[]{:S(2)}, u32[]{:S(2)}) collective-permute-start(f32[192,256]{1,0:T(8,128)} %get-tuple-element.103), channel_id=1, source_target_pairs={{2,0},{6,4},{10,8},{14,12},{3,1},{7,5},{11,9},{15,13},{18,16},{22,... | collective-permute-start | bytes 589832 | tf_op jit(solution)/shard_map/ppermute | solution.py:466
  25.0 42.0 %collective-permute-start.3 = (f32[192,256]{1,0:T(8,128)}, f32[192,256]{1,0:T(8,128)S(1)}, u32[]{:S(2)}, u32[]{:S(2)}) collective-permute-start(f32[192,256]{1,0:T(8,128)} %get-tuple-element.105), channel_id=1, source_target_pairs={{2,8},{6,12},{10,0},{14,4},{3,9},{7,13},{11,1},{15,5},{18,24},{22,... | collective-permute-start | bytes 589832 | tf_op jit(solution)/shard_map/ppermute | solution.py:466
  26.3 40.7 %collective-permute-start.2 = (f32[192,256]{1,0:T(8,128)}, f32[192,256]{1,0:T(8,128)S(1)}, u32[]{:S(2)}, u32[]{:S(2)}) collective-permute-start(f32[192,256]{1,0:T(8,128)} %get-tuple-element.105), channel_id=1, source_target_pairs={{0,4},{4,8},{8,12},{12,0},{1,5},{5,9},{9,13},{13,1},{16,20},{20,24... | collective-permute-start | bytes 589832 | tf_op jit(solution)/shard_map/ppermute | solution.py:466
  28.2 17.9 %collective-permute-start = (f32[192,256]{1,0:T(8,128)}, f32[192,256]{1,0:T(8,128)S(1)}, u32[]{:S(2)}, u32[]{:S(2)}) collective-permute-start(f32[192,256]{1,0:T(8,128)} %get-tuple-element.118.refs_0_), channel_id=1, source_target_pairs={{2,4},{6,8},{10,12},{14,0},{3,5},{7,9},{11,13},{15,1},{18,20},{22,... | collective-permute-start | bytes 589832 | tf_op jit(solution)/shard_map/ppermute | solution.py:466
  46.1 20.9 %collective-permute-start.5 = (f32[192,256]{1,0:T(8,128)}, f32[192,256]{1,0:T(8,128)S(1)}, u32[]{:S(2)}, u32[]{:S(2)}) collective-permute-start(f32[192,256]{1,0:T(8,128)} %get-tuple-element.106), channel_id=1, source_target_pairs={{2,12},{6,0},{10,4},{14,8},{3,13},{7,1},{11,5},{15,9},{18,28},{22,... | collective-permute-start | bytes 589832 | tf_op jit(solution)/shard_map/ppermute | solution.py:466
  47.4 19.6 %collective-permute-start.4 = (f32[192,256]{1,0:T(8,128)}, f32[192,256]{1,0:T(8,128)S(1)}, u32[]{:S(2)}, u32[]{:S(2)}) collective-permute-start(f32[192,256]{1,0:T(8,128)} %get-tuple-element.106), channel_id=1, source_target_pairs={{0,8},{4,12},{8,0},{12,4},{1,9},{5,13},{9,1},{13,5},{16,24},{20,28... | collective-permute-start | bytes 589832 | tf_op jit(solution)/shard_map/ppermute | solution.py:466
  67.1 60.8 %all-to-all-start = ((f32[8,512,128]{2,1,0:T(8,128)}), f32[8,512,128]{2,1,0:T(8,128)}, u32[]{:S(2)}, u32[]{:S(2)}) async-start(f32[8,512,128]{2,1,0:T(8,128)} %get-tuple-element.113), calls=%async_computation.1 | async-start | bytes 4194304 | tf_op jit(solution)/shard_map/all_to_all | solution.py:419
  71.6 48.7 %reduce-scatter.3.cloned.1.call-start = ((), (), s32[]{:S(2)}) async-start(), calls=%async_computation.3 | async-start | bytes 589824 | tf_op jit(solution)/shard_map/reduce_scatter | solution.py:508
  75.0 10.0 %collective-permute-start.9 = (f32[576,128]{1,0:T(8,128)S(1)}, f32[576,128]{1,0:T(8,128)S(1)}, u32[]{:S(2)}, u32[]{:S(2)}) collective-permute-start(f32[576,128]{1,0:T(8,128)S(1)} %get-tuple-element.126.refs_0_), channel_id=1, source_target_pairs={{0,16},{16,32},{32,48},{48,0},{64,80},{80,96},{96,112},{112,64},{1... | collective-permute-start | bytes 884744 | tf_op jit(solution)/shard_map/ppermute | solution.py:564
  76.7 9.9 %collective-permute-start.8 = (f32[576,128]{1,0:T(8,128)S(1)}, f32[576,128]{1,0:T(8,128)S(1)}, u32[]{:S(2)}, u32[]{:S(2)}) collective-permute-start(f32[576,128]{1,0:T(8,128)S(1)} %get-tuple-element.127.refs_1_), channel_id=1, source_target_pairs={{0,48},{16,0},{32,16},{48,32},{64,112},{80,64},{96,80},{112,96},{1... | collective-permute-start | bytes 884744 | tf_op jit(solution)/shard_map/ppermute | solution.py:564
  77.1 15.8 %collective-permute-start.7 = (f32[576,128]{1,0:T(8,128)S(1)}, f32[576,128]{1,0:T(8,128)S(1)}, u32[]{:S(2)}, u32[]{:S(2)}) collective-permute-start(f32[576,128]{1,0:T(8,128)S(1)} %get-tuple-element.126.refs_0_), channel_id=1, source_target_pairs={{0,48},{16,0},{32,16},{48,32},{64,112},{80,64},{96,80},{112,96},{1... | collective-permute-start | bytes 884744 | tf_op jit(solution)/shard_map/ppermute | solution.py:564
  78.8 14.2 %collective-permute-start.12 = (f32[576,128]{1,0:T(8,128)S(1)}, f32[576,128]{1,0:T(8,128)S(1)}, u32[]{:S(2)}, u32[]{:S(2)}) collective-permute-start(f32[576,128]{1,0:T(8,128)S(1)} %get-tuple-element.127.refs_1_), channel_id=1, source_target_pairs={{0,16},{16,32},{32,48},{48,0},{64,80},{80,96},{96,112},{112,64},{1... | collective-permute-start | bytes 884744 | tf_op jit(solution)/shard_map/ppermute | solution.py:564
  85.0 11.3 %collective-permute-start.10 = (f32[576,128]{1,0:T(8,128)S(1)}, f32[576,128]{1,0:T(8,128)S(1)}, u32[]{:S(2)}, u32[]{:S(2)}) collective-permute-start(f32[576,128]{1,0:T(8,128)S(1)} %collective-permute-done.9.refs_6_), channel_id=1, source_target_pairs={{0,16},{16,32},{32,48},{48,0},{64,80},{80,96},{96,112},{112,64},{1... | collective-permute-start | bytes 884744 | tf_op jit(solution)/shard_map/ppermute | solution.py:564
  86.7 11.0 %collective-permute-start.11 = (f32[576,128]{1,0:T(8,128)S(1)}, f32[576,128]{1,0:T(8,128)S(1)}, u32[]{:S(2)}, u32[]{:S(2)}) collective-permute-start(f32[576,128]{1,0:T(8,128)S(1)} %collective-permute-done.8.refs_3_), channel_id=1, source_target_pairs={{0,48},{16,0},{32,16},{48,32},{64,112},{80,64},{96,80},{112,96},{1... | collective-permute-start | bytes 884744 | tf_op jit(solution)/shard_map/ppermute | solution.py:564
  99.6 5.7 %collective-permute-start.13 = (f32[64,256]{1,0:T(8,128)S(1)}, f32[64,256]{1,0:T(8,128)S(1)}, u32[]{:S(2)}, u32[]{:S(2)}) collective-permute-start(f32[64,256]{1,0:T(8,128)S(1)} %get-tuple-element.128), channel_id=1, source_target_pairs={{0,64},{2,66},{4,196},{6,198},{8,72},{10,74},{12,204},{14,206},{16... | collective-permute-start | bytes 196616 | tf_op jit(solution)/shard_map/ppermute | solution.py:606
  106.1 5.6 %collective-permute-start.14 = (f32[64,256]{1,0:T(8,128)S(1)}, f32[64,256]{1,0:T(8,128)S(1)}, u32[]{:S(2)}, u32[]{:S(2)}) collective-permute-start(f32[64,256]{1,0:T(8,128)S(1)} %row_step.2), channel_id=1, source_target_pairs={{0,64},{2,66},{4,196},{6,198},{8,72},{10,74},{12,204},{14,206},{16... | collective-permute-start | bytes 196616 | tf_op jit(solution)/shard_map/ppermute | solution.py:606
  127.8 14.0 %collective-permute-start.22 = (f32[128,256]{1,0:T(8,128)S(1)}, f32[128,256]{1,0:T(8,128)S(1)}, u32[]{:S(2)}, u32[]{:S(2)}) collective-permute-start(f32[128,256]{1,0:T(8,128)S(1)} %inflow.1.refs_0_), channel_id=1, source_target_pairs={{0,14},{4,2},{8,6},{12,10},{1,15},{5,3},{9,7},{13,11},{16,30},{20,... | collective-permute-start | bytes 393224 | tf_op jit(solution)/shard_map/ppermute | solution.py:648
  129.1 16.5 %collective-permute-start.21 = (f32[128,256]{1,0:T(8,128)S(1)}, f32[128,256]{1,0:T(8,128)S(1)}, u32[]{:S(2)}, u32[]{:S(2)}) collective-permute-start(f32[128,256]{1,0:T(8,128)S(1)} %inflow.1.refs_0_), channel_id=1, source_target_pairs={{0,12},{4,0},{8,4},{12,8},{1,13},{5,1},{9,5},{13,9},{16,28},{20,16... | collective-permute-start | bytes 393224 | tf_op jit(solution)/shard_map/ppermute | solution.py:648
  132.8 17.7 %collective-permute-start.20 = (f32[128,256]{1,0:T(8,128)S(1)}, f32[128,256]{1,0:T(8,128)S(1)}, u32[]{:S(2)}, u32[]{:S(2)}) collective-permute-start(f32[128,256]{1,0:T(8,128)S(1)} %inflow.1.refs_0_), channel_id=1, source_target_pairs={{0,10},{4,14},{8,2},{12,6},{1,11},{5,15},{9,3},{13,7},{16,26},{20,... | collective-permute-start | bytes 393224 | tf_op jit(solution)/shard_map/ppermute | solution.py:648
  134.1 16.4 %collective-permute-start.19 = (f32[128,256]{1,0:T(8,128)S(1)}, f32[128,256]{1,0:T(8,128)S(1)}, u32[]{:S(2)}, u32[]{:S(2)}) collective-permute-start(f32[128,256]{1,0:T(8,128)S(1)} %inflow.1.refs_0_), channel_id=1, source_target_pairs={{0,8},{4,12},{8,0},{12,4},{1,9},{5,13},{9,1},{13,5},{16,24},{20,28... | collective-permute-start | bytes 393224 | tf_op jit(solution)/shard_map/ppermute | solution.py:648
  140.6 10.5 %collective-permute-start.18 = (f32[128,256]{1,0:T(8,128)S(1)}, f32[128,256]{1,0:T(8,128)S(1)}, u32[]{:S(2)}, u32[]{:S(2)}) collective-permute-start(f32[128,256]{1,0:T(8,128)S(1)} %inflow.1.refs_0_), channel_id=1, source_target_pairs={{0,6},{4,10},{8,14},{12,2},{1,7},{5,11},{9,15},{13,3},{16,22},{20,... | collective-permute-start | bytes 393224 | tf_op jit(solution)/shard_map/ppermute | solution.py:648
  141.9 13.2 %collective-permute-start.17 = (f32[128,256]{1,0:T(8,128)S(1)}, f32[128,256]{1,0:T(8,128)S(1)}, u32[]{:S(2)}, u32[]{:S(2)}) collective-permute-start(f32[128,256]{1,0:T(8,128)S(1)} %inflow.1.refs_0_), channel_id=1, source_target_pairs={{0,4},{4,8},{8,12},{12,0},{1,5},{5,9},{9,13},{13,1},{16,20},{20,24... | collective-permute-start | bytes 393224 | tf_op jit(solution)/shard_map/ppermute | solution.py:648
  145.7 10.1 %collective-permute-start.16 = (f32[128,256]{1,0:T(8,128)S(1)}, f32[128,256]{1,0:T(8,128)S(1)}, u32[]{:S(2)}, u32[]{:S(2)}) collective-permute-start(f32[128,256]{1,0:T(8,128)S(1)} %inflow.1.refs_0_), channel_id=1, source_target_pairs={{0,2},{4,6},{8,10},{12,14},{1,3},{5,7},{9,11},{13,15},{16,18},{20,... | collective-permute-start | bytes 393224 | tf_op jit(solution)/shard_map/ppermute | solution.py:648
  (12 other events, 152.2 us)
Sparse Core Ops, SparseCore 1:
  74.6 45.7 reduce-scatter.2

commit v12 on v10

--- a/solution.py
+++ b/solution.py
@@ -48,72 +48,67 @@
     return combined(by_real, by_imag)
 
 
-def interface_kernel(
-    place_ref, inject_ref, src_ref, g0_ref, g1_ref, out_ref, high_ref, low_ref, acc_ref
-):
-    step = pl.program_id(0)
-    slab = step // 2
-    plane = step % 2
-    modes = src_ref.shape[2]
-    width = src_ref.shape[3]
-
-    @pl.when(step == 0)
-    def _():
-        rows = lax.broadcasted_iota(jnp.int32, (width // 8, width), 0)
-        cols = lax.broadcasted_iota(jnp.int32, (width // 8, width), 1)
-        targets = [
-            jnp.broadcast_to(inject_ref[sweep : sweep + 1, :].astype(F32), (width, modes)).T
-            for sweep in range(2)
-        ]
-        for local in range(2):
-            pieces = []
+def interface_kernel(inject_ref, src_hbm, g_hbm, out_ref, g_ref, src_ref, sems, src_sem):
+    first = lax.axis_index("slab") * 2
+    modes, width = src_ref.shape[2], src_ref.shape[3]
+    lanes = width // 2
+    lead = width // 8
+    fetch_src = pltpu.make_async_copy(src_hbm, src_ref, src_sem)
+    fetch_src.start()
+    fetches = {}
+    for slab in range(2):
+        for plane in range(2):
+            for side in range(2):
+                fetch = pltpu.make_async_copy(
+                    g_hbm.at[slab, plane, :, side * lanes : (side + 1) * lanes],
+                    g_ref.at[slab, plane, side],
+                    sems.at[slab, plane, side],
+                )
+                fetch.start()
+                fetches[slab, plane, side] = fetch
+    rows = lax.broadcasted_iota(jnp.int32, (lead, width), 0)
+    cols = lax.broadcasted_iota(jnp.int32, (lead, width), 1)
+    targets = [
+        jnp.broadcast_to(inject_ref[sweep : sweep + 1, :].astype(F32), (width, modes)).T
+        for sweep in range(2)
+    ]
+    fetch_src.wait()
+    count = g_ref.shape[3] // 8
+    total = [0.0] * 4
+    for slab in range(2):
+        chosen = [target == (first + slab).astype(F32) for target in targets]
+        left = []
+        for sweep in range(2):
+            unit = (cols == rows * 8 + sweep).astype(F32)
+            source = [jnp.where(chosen[sweep], src_ref[sweep, part], 0.0) for part in range(2)]
+            left.append(split(jnp.concatenate([unit] + source, axis=0)))
+        for plane in range(2):
+            for side in range(2):
+                fetches[slab, plane, side].wait()
             for sweep in range(2):
-                pieces.append((cols == rows * 8 + sweep).astype(F32))
-                chosen = targets[sweep] == (place_ref[0] + local).astype(F32)
-                for part in range(2):
-                    pieces.append(jnp.where(chosen, src_ref[sweep, part], 0.0))
-            high, low = split(jnp.concatenate(pieces, axis=0))
-            high_ref[local] = high
-            low_ref[local] = low
-        acc_ref[...] = jnp.zeros_like(acc_ref)
-
-    half = high_ref.shape[1] // 2
-    lead = width // 8
-    count = g0_ref.shape[2] // 8
-    for sweep in range(2):
-        rows = jnp.concatenate(
-            [ref[0, 0, pl.ds(1 - sweep, count, stride=8), :] for ref in (g0_ref, g1_ref)], axis=1
-        )
-        picked = pl.ds(sweep * half, half)
-        term = mm3((high_ref[slab, picked, :], low_ref[slab, picked, :]), split(rows), True)
-        order = slab if sweep == 0 else 1 - slab
-        rows, lanes = out_ref.shape[1] // 2, out_ref.shape[2]
-        for side in range(2):
-            place = (order * 2 + plane) * lead + side * rows
-            place = pl.ds(pl.multiple_of(place, 8), lead)
-            for member in range(4):
-                out_ref[sweep * 4 + member, place, :] = term[
-                    :lead, side * lanes : (side + 1) * lanes
-                ]
-        real, imag = term[lead : lead + modes], term[lead + modes :]
-
-        @pl.when(plane == 0)
-        def _():
-            acc_ref[sweep, :modes] += real
-            acc_ref[sweep, modes:] += imag
-
-        @pl.when(plane == 1)
-        def _():
-            acc_ref[sweep, :modes] -= imag
-            acc_ref[sweep, modes:] += real
-
-    @pl.when(step == 3)
-    def _():
-        for dest in range(8):
-            sweep, member = divmod(dest, 4)
-            for part in range(2):
-                start = part * modes + member * 16
-                put(out_ref, dest, 4 * lead + part * 16, acc_ref[sweep, start : start + 16, :])
+                picked = jnp.concatenate(
+                    [
+                        g_ref[slab, plane, side, pl.ds(1 - sweep, count, stride=8), :]
+                        for side in range(2)
+                    ],
+                    axis=1,
+                )
+                term = mm3(left[sweep], split(picked), True)
+                order = slab if sweep == 0 else 1 - slab
+                for member in range(4):
+                    put(out_ref, sweep * 4 + member, (order * 2 + plane) * lead, term[:lead])
+                real, imag = term[lead : lead + modes], term[lead + modes :]
+                if plane == 0:
+                    total[2 * sweep] += real
+                    total[2 * sweep + 1] += imag
+                else:
+                    total[2 * sweep] -= imag
+                    total[2 * sweep + 1] += real
+    for dest in range(8):
+        sweep, member = divmod(dest, 4)
+        for part in range(2):
+            piece = total[2 * sweep + part][member * 16 : (member + 1) * 16]
+            put(out_ref, dest, 4 * lead + part * 16, piece)
 
 
 def packed_columns(place_ref, inject_ref, sweep):
@@ -407,6 +402,7 @@
 
 SMEM = pl.BlockSpec(memory_space=pltpu.SMEM)
 VMEM = pl.BlockSpec(memory_space=pltpu.VMEM)
+ANY = pl.BlockSpec(memory_space=pl.ANY)
 
 
 def exchange(value):
@@ -429,31 +425,25 @@
     place = jnp.stack([first, jnp.zeros_like(first)]).astype(jnp.int32)
     position = jnp.where(team == 0, slab_index, slabs - 1 - slab_index)
     info = jnp.stack([team, position // 4, position % 4, slab_index % 4]).astype(jnp.int32)
-    stack = 2 * (lead + 2 * modes)
     block_rows = 4 * lead + 32
     sources = jnp.transpose(sources, (0, 1, 3, 2))
     leads = jnp.transpose(leads, (0, 1, 3, 2))
 
     sent = pl.pallas_call(
         interface_kernel,
-        grid=(4,),
-        in_specs=[
-            SMEM,
-            whole(inject.shape),
-            whole(sources.shape),
-            pl.BlockSpec((1, 1, orbitals, width // 2), lambda step: (step // 2, step % 2, 0, 0)),
-            pl.BlockSpec((1, 1, orbitals, width // 2), lambda step: (step // 2, step % 2, 0, 1)),
-        ],
+        grid=(1,),
+        in_specs=[whole(inject.shape), ANY, ANY],
         out_specs=whole((8, 2 * block_rows, LANES)),
         out_shape=jax.ShapeDtypeStruct((8, 2 * block_rows, LANES), F32),
         scratch_shapes=[
-            pltpu.VMEM((2, stack, width), BF16),
-            pltpu.VMEM((2, stack, width), BF16),
-            pltpu.VMEM((2, 2 * modes, size), F32),
+            pltpu.VMEM((2, 2, 2, orbitals, width // 2), F32),
+            pltpu.VMEM(sources.shape, F32),
+            pltpu.SemaphoreType.DMA((2, 2, 2)),
+            pltpu.SemaphoreType.DMA,
         ],
         compiler_params=params(LARGE),
         name="interface_terms",
-    )(place, inject, sources, diag_inverse, diag_inverse)
+    )(inject, sources, diag_inverse)
     sent, inject_after = lax.optimization_barrier((sent, inject))
     received = exchange(sent)
 

time: 148 us -> 148 us (level)
  no operation moved by 1% of the time
where the time goes in v12:
time: 148 us; the launch traced here: 147 us
  waiting for transfers between devices  65.4 us (44%)
  Pallas kernels  35.6 us (24%)
  starting transfers between devices  25.6 us (17%)
  between operations  16.3 us (11%)
  local copies, waits for them, and re-layouts  2.95 us (2%)
    all_to_all x3, waiting for transfers between devices, exchange(): return lax.all_to_all(value, 'col', split_axis=0, concat_axis=0, tiled=True)  39.8 us
    all_to_all x3, starting transfers between devices, exchange(): return lax.all_to_all(value, 'col', split_axis=0, concat_axis=0, tiled=True)  16.5 us
    ppermute x6, waiting for transfers between devices, turn(): lax.ppermute(value, 'slab', [(slab, slab // 4 * 4 + (slab + step) % 4) fo...  15.7 us
    pallas_call x7, Pallas kernels, local(): pl.pallas_call(kernel, in_specs=[SMEM] + [VMEM] * (len(args) - 1), out_sp...  12.3 us
    pallas_call x1, Pallas kernels, chunk_terms(): pl.pallas_call(spread_kernel, grid=(8,), in_specs=[whole(terms.shape), wh...  8.73 us
    pallas_call x1, Pallas kernels, on_device(): pl.pallas_call(interface_kernel, grid=(1,), in_specs=[whole(inject.shape)...  6.56 us
    ppermute x3, waiting for transfers between devices, hop(): return lax.ppermute(value, ('slab', 'col'), pairs)  6.3 us
    ppermute x6, starting transfers between devices, turn(): lax.ppermute(value, 'slab', [(slab, slab // 4 * 4 + (slab + step) % 4) fo...  6.15 us
  transfers between devices with their start and end apart: 13, of which 11 were waited for; matrix products, arithmetic and copies ran while one was open for 1% of the time, Pallas kernels for 19%

profile of v12, /device:TPU:8, one launch (start us, length us, event | category | flops | bytes accessed | tf_op | source)
XLA Modules:
  0.0 146.8 jit_solution(26178711714578525)
XLA Ops:
  8.0 6.6 %interface_terms.1 = f32[8,320,128]{2,1,0:T(8,128)} custom-call(s32[2,64]{1,0:T(2,128)} %inject_ref.4, f32[2,2,64,256]{3,2,1,0:T(8,128)} %bitcast.27, f32[2,2,2048,256]{3,2,1,0:T(8,128)} %g_ref.1), custom_call_target="tpu_custom_call" | custom-call | tf_op jit(solution)/shard_map/interface_terms/pallas_call | solution.py:432
  14.6 8.6 %all-to-all-start = ((f32[8,320,128]{2,1,0:T(8,128)}), f32[8,320,128]{2,1,0:T(8,128)S(1)}, u32[]{:S(2)}, u32[]{:S(2)}) async-start(f32[8,320,128]{2,1,0:T(8,128)} %interface_terms.1), calls=%async_computation.1 | async-start | bytes 2621440 | tf_op jit(solution)/shard_map/all_to_all | solution.py:409
  28.9 8.7 %spread_terms.2 = (f32[8,512,128]{2,1,0:T(8,128)}, f32[8,64,256]{2,1,0:T(8,128)}) custom-call(bf16[2,128,256]{2,1,0:T(8,128)(2,1)} %copy-done.5, bf16[2,128,256]{2,1,0:T(8,128)(2,1)} %copy-done.6, f32[2,2,2048,256]{3,2,1,0:T(8,128)} %g_ref.1), custom_call_target="tpu_custom_call" | custom-call | tf_op jit(solution)/shard_map/spread_terms/pallas_call | solution.py:460
  37.8 19.8 %all-to-all-done.recv_ref = f32[8,320,128]{2,1,0:T(8,128)S(1)} async-done(((f32[8,320,128]{2,1,0:T(8,128)}), f32[8,320,128]{2,1,0:T(8,128)S(1)}, u32[]{:S(2)}, u32[]{:S(2)}) %all-to-all-start) | async-done | bytes 1310752 | tf_op jit(solution)/shard_map/all_to_all | solution.py:409
  57.7 4.4 %all-to-all-start.1 = ((f32[8,512,128]{2,1,0:T(8,128)}), f32[8,512,128]{2,1,0:T(8,128)}, u32[]{:S(2)}, u32[]{:S(2)}) async-start(f32[8,512,128]{2,1,0:T(8,128)} %get-tuple-element.96), calls=%async_computation.2 | async-start | bytes 4194304 | tf_op jit(solution)/shard_map/all_to_all | solution.py:409
  62.7 2.8 %pair_map.1 = (f32[544,128]{1,0:T(8,128)S(1)}, f32[544,128]{1,0:T(8,128)S(1)}, f32[32,256]{1,0:T(8,128)S(1)}, f32[512,256]{1,0:T(8,128)S(1)}) custom-call(s32[4]{0:T(128)S(1)} %pad_add_fusion.1.team_ref.info_ref, f32[8,320,128]{2,1,0:T(8,128)S(1)} %all-to-all-done.recv_ref, f32[2,512,256]{2,1,0:T(8,128)S(1)} %coupling_rows.1.x_ref, ...), custom_call_target="tpu_custom_call" | custom-call | tf_op jit(solution)/shard_map/pair_map/pallas_call | solution.py:521
  65.4 1.7 %collective-permute-start.2 = (f32[544,128]{1,0:T(8,128)S(1)}, f32[544,128]{1,0:T(8,128)S(1)}, u32[]{:S(2)}, u32[]{:S(2)}) collective-permute-start(f32[544,128]{1,0:T(8,128)S(1)} %get-tuple-element.102.refs_0_), channel_id=1, source_target_pairs={{0,16},{16,32},{32,48},{48,0},{64,80},{80,96},{96,112},{112,64},{1... | collective-permute-start | bytes 835592 | tf_op jit(solution)/shard_map/ppermute | solution.py:536
  67.5 1.7 %collective-permute-start = (f32[544,128]{1,0:T(8,128)S(1)}, f32[544,128]{1,0:T(8,128)S(1)}, u32[]{:S(2)}, u32[]{:S(2)}) collective-permute-start(f32[544,128]{1,0:T(8,128)S(1)} %get-tuple-element.102.refs_0_), channel_id=1, source_target_pairs={{0,48},{16,0},{32,16},{48,32},{64,112},{80,64},{96,80},{112,96},{1... | collective-permute-start | bytes 835592 | tf_op jit(solution)/shard_map/ppermute | solution.py:536
  69.6 5.5 %collective-permute-done.2.refs_6_ = f32[544,128]{1,0:T(8,128)S(1)} collective-permute-done((f32[544,128]{1,0:T(8,128)S(1)}, f32[544,128]{1,0:T(8,128)S(1)}, u32[]{:S(2)}, u32[]{:S(2)}) %collective-permute-start.2) | collective-permute-done | bytes 278560 | tf_op jit(solution)/shard_map/ppermute | solution.py:536
  77.1 5.5 %collective-permute-done.refs_2_ = f32[544,128]{1,0:T(8,128)S(1)} collective-permute-done((f32[544,128]{1,0:T(8,128)S(1)}, f32[544,128]{1,0:T(8,128)S(1)}, u32[]{:S(2)}, u32[]{:S(2)}) %collective-permute-start) | collective-permute-done | bytes 278560 | tf_op jit(solution)/shard_map/ppermute | solution.py:536
  82.6 3.4 %collective-permute-done.3.refs_4_ = f32[544,128]{1,0:T(8,128)S(1)} collective-permute-done((f32[544,128]{1,0:T(8,128)S(1)}, f32[544,128]{1,0:T(8,128)S(1)}, u32[]{:S(2)}, u32[]{:S(2)}) %collective-permute-start.3) | collective-permute-done | bytes 278560 | tf_op jit(solution)/shard_map/ppermute | solution.py:536
  87.3 1.9 %gather_maps.1 = (bf16[4,512,256]{2,1,0:T(8,128)(2,1)S(1)}, bf16[4,512,256]{2,1,0:T(8,128)(2,1)S(1)}, f32[4,32,256]{2,1,0:T(8,128)S(1)}, f32[32,256]{1,0:T(8,128)S(1)}) custom-call(s32[4]{0:T(128)S(1)} %pad_add_fusion.1.team_ref.info_ref, f32[32,256]{1,0:T(8,128)S(1)} %bitcast.22, f32[544,128]{1,0:T(8,128)S(1)} %get-tuple-element.102.refs_0_, ...), custom_call_target="tpu_custom_call" | custom-call | tf_op jit(solution)/shard_map/gather_maps/pallas_call | solution.py:550
  89.2 1.8 %collective-permute-start.6 = (f32[32,256]{1,0:T(8,128)S(1)}, f32[32,256]{1,0:T(8,128)S(1)}, u32[]{:S(2)}, u32[]{:S(2)}) collective-permute-start(f32[32,256]{1,0:T(8,128)S(1)} %get-tuple-element.104), channel_id=1, source_target_pairs={{0,64},{2,66},{4,68},{6,70},{8,200},{10,202},{12,204},{14,206},{16... | collective-permute-start | bytes 98312 | tf_op jit(solution)/shard_map/ppermute | solution.py:578
  91.0 3.1 %row_map.1 = (bf16[512,256]{1,0:T(8,128)(2,1)S(1)}, bf16[512,256]{1,0:T(8,128)(2,1)S(1)}, f32[32,256]{1,0:T(8,128)S(1)}, f32[544,256]{1,0:T(8,128)S(1)}) custom-call(s32[4]{0:T(128)S(1)} %pad_add_fusion.1.team_ref.info_ref, bf16[4,512,256]{2,1,0:T(8,128)(2,1)S(1)} %get-tuple-element.105.high_ref, bf16[4,512,256]{2,1,0:T(8,128)(2,1)S(1)} %get-tuple-element.106.low_ref, ...), custom_call_target="tpu_custom_call" | custom-call | tf_op jit(solution)/shard_map/row_map/pallas_call | solution.py:568
  96.4 1.7 %prefix_map.1 = (f32[544,256]{1,0:T(8,128)S(1)}, f32[544,256]{1,0:T(8,128)S(1)}) custom-call(s32[4]{0:T(128)S(1)} %pad_add_fusion.1.team_ref.info_ref, bf16[4,512,256]{2,1,0:T(8,128)(2,1)S(1)} %get-tuple-element.105.high_ref, bf16[4,512,256]{2,1,0:T(8,128)(2,1)S(1)} %get-tuple-element.106.low_ref, f32[4,32,256]{2,1,0:T(8,128)S(1)} %get-tuple-element.107.flow_ref, ...), custom_call_target="tpu_custom_call" | custom-call | tf_op jit(solution)/shard_map/prefix_map/pallas_call | solution.py:568
  98.1 2.4 %collective-permute-done.7.state_ref = f32[32,256]{1,0:T(8,128)S(1)} collective-permute-done((f32[32,256]{1,0:T(8,128)S(1)}, f32[32,256]{1,0:T(8,128)S(1)}, u32[]{:S(2)}, u32[]{:S(2)}) %collective-permute-start.7) | collective-permute-done | bytes 32800 | tf_op jit(solution)/shard_map/ppermute | solution.py:578
  101.3 1.7 %entry_map.1 = (bf16[2,512,256]{2,1,0:T(8,128)(2,1)S(1)}, bf16[2,512,256]{2,1,0:T(8,128)(2,1)S(1)}, f32[2,32,256]{2,1,0:T(8,128)S(1)}) custom-call(s32[4]{0:T(128)S(1)} %pad_add_fusion.1.team_ref.info_ref, f32[544,256]{1,0:T(8,128)S(1)} %get-tuple-element.119.prefix_ref, f32[544,256]{1,0:T(8,128)S(1)} %get-tuple-element.120.inner_ref, ...), custom_call_target="tpu_custom_call" | custom-call | tf_op jit(solution)/shard_map/entry_map/pallas_call | solution.py:568
  103.0 3.4 %collective-permute-done.8.state_ref = f32[32,256]{1,0:T(8,128)S(1)} collective-permute-done((f32[32,256]{1,0:T(8,128)S(1)}, f32[32,256]{1,0:T(8,128)S(1)}, u32[]{:S(2)}, u32[]{:S(2)}) %collective-permute-start.8) | collective-permute-done | bytes 32800 | tf_op jit(solution)/shard_map/ppermute | solution.py:578
  106.4 1.7 %inflow.1 = f32[8,128,128]{2,1,0:T(8,128)} custom-call(s32[4]{0:T(128)S(1)} %pad_add_fusion.1.team_ref.info_ref, f32[32,256]{1,0:T(8,128)S(1)} %bitcast.25, f32[32,256]{1,0:T(8,128)S(1)} %collective-permute-done.8.state_ref, bf16[2,512,256]{2,1,0:T(8,128)(2,1)S(1)} %get-tuple-element.121.high_ref, bf16[2,512,256]{2,1,0:T(8,128)(2,1)S(1)} %get-tuple-element.122.low_ref, ...), custom_call_target="tpu_custom_call" | custom-call | tf_op jit(solution)/shard_map/inflow/pallas_call | solution.py:568
  108.1 3.0 %reduce-scatter.3.cloned.1.call-done = f32[1,64,256]{2,1,0:T(8,128)} async-done(((f32[8,64,256]{2,1,0:T(8,128)}), f32[1,64,256]{2,1,0:T(8,128)}) %reduce-scatter.3.cloned.1.call-update) | async-done | bytes 65552 | tf_op jit(solution)/shard_map/reduce_scatter | solution.py:481
  111.1 7.6 %all-to-all-done.1.recv_ref = f32[8,512,128]{2,1,0:T(8,128)} async-done(((f32[8,512,128]{2,1,0:T(8,128)}), f32[8,512,128]{2,1,0:T(8,128)}, u32[]{:S(2)}, u32[]{:S(2)}) %all-to-all-start.1) | async-done | bytes 2097184 | tf_op jit(solution)/shard_map/all_to_all | solution.py:409
  118.7 3.5 %all-to-all-start.2 = ((f32[8,128,128]{2,1,0:T(8,128)}), f32[8,128,128]{2,1,0:T(8,128)S(1)}, u32[]{:S(2)}, u32[]{:S(2)}) async-start(f32[8,128,128]{2,1,0:T(8,128)} %inflow.1), calls=%async_computation.4 | async-start | bytes 1048576 | tf_op jit(solution)/shard_map/all_to_all | solution.py:409
  123.0 2.6 %arrange_rows.1 = (bf16[2,2,2,256,256]{4,3,2,1,0:T(8,128)(2,1)S(1)}, bf16[2,2,2,256,256]{4,3,2,1,0:T(8,128)(2,1)S(1)}, f32[2,2,2,64,256]{4,3,2,1,0:T(8,128)S(1)}) custom-call(s32[2]{0:T(128)S(1)} %pad_add_fusion.3.place_ref, s32[2,64]{1,0:T(2,128)S(1)} %get-tuple-element.266, f32[8,512,128]{2,1,0:T(8,128)} %all-to-all-done.1.recv_ref, ...), custom_call_target="tpu_custom_call" | custom-call | tf_op jit(solution)/shard_map/arrange_rows/pallas_call | solution.py:568
  125.7 12.4 %all-to-all-done.2.last_ref = f32[8,128,128]{2,1,0:T(8,128)S(1)} async-done(((f32[8,128,128]{2,1,0:T(8,128)}), f32[8,128,128]{2,1,0:T(8,128)S(1)}, u32[]{:S(2)}, u32[]{:S(2)}) %all-to-all-start.2) | async-done | bytes 524320 | tf_op jit(solution)/shard_map/all_to_all | solution.py:409
  (45 shorter events, 15.1 us)
Async XLA Ops:
  8.0 29.7 %copy-start = (f32[2,2,256,64]{2,3,1,0:T(8,128)S(1)}, f32[2,2,256,64]{2,3,1,0:T(8,128)}, u32[]{:S(2)}) copy-start(f32[2,2,256,64]{2,3,1,0:T(8,128)} %param.11) | copy-start | bytes 786436
  14.6 8.6 %copy-start.10 = (s32[2,64]{1,0:T(2,128)S(1)}, s32[2,64]{1,0:T(2,128)}, u32[]{:S(2)}) copy-start(s32[2,64]{1,0:T(2,128)} %inject_ref.4) | copy-start | bytes 1540
  14.6 10.2 %copy-start.8 = (f32[2,2,256,64]{2,3,1,0:T(8,128)S(1)}, f32[2,2,256,64]{2,3,1,0:T(8,128)}, u32[]{:S(2)}) copy-start(f32[2,2,256,64]{2,3,1,0:T(8,128)} %param.9) | copy-start | bytes 786436
  14.6 43.0 %all-to-all-start = ((f32[8,320,128]{2,1,0:T(8,128)}), f32[8,320,128]{2,1,0:T(8,128)S(1)}, u32[]{:S(2)}, u32[]{:S(2)}) async-start(f32[8,320,128]{2,1,0:T(8,128)} %interface_terms.1), calls=%async_computation.1 | async-start | bytes 2621440 | tf_op jit(solution)/shard_map/all_to_all | solution.py:409
  26.0 0.7 copy-start.5
  26.6 2.3 %copy-start.6 = (bf16[2,128,256]{2,1,0:T(8,128)(2,1)}, bf16[2,128,256]{2,1,0:T(8,128)(2,1)S(1)}, u32[]{:S(2)}) copy-start(bf16[2,128,256]{2,1,0:T(8,128)(2,1)S(1)} %get-tuple-element.93.low_ref) | copy-start | bytes 393220
  26.8 1.2 copy-start.4
  37.8 19.9 %copy-start.9 = (f32[256,256]{1,0:T(8,128)}, f32[256,256]{1,0:T(8,128)S(1)}, u32[]{:S(2)}) copy-start(f32[256,256]{1,0:T(8,128)S(1)} %get-tuple-element.127.extra_ref) | copy-start | bytes 786436
  57.7 60.9 %all-to-all-start.1 = ((f32[8,512,128]{2,1,0:T(8,128)}), f32[8,512,128]{2,1,0:T(8,128)}, u32[]{:S(2)}, u32[]{:S(2)}) async-start(f32[8,512,128]{2,1,0:T(8,128)} %get-tuple-element.96), calls=%async_computation.2 | async-start | bytes 4194304 | tf_op jit(solution)/shard_map/all_to_all | solution.py:409
  62.1 49.0 %reduce-scatter.3.cloned.1.call-start = ((), (), s32[]{:S(2)}) async-start(), calls=%async_computation.5 | async-start | bytes 589824 | tf_op jit(solution)/shard_map/reduce_scatter | solution.py:481
  65.4 9.6 %collective-permute-start.2 = (f32[544,128]{1,0:T(8,128)S(1)}, f32[544,128]{1,0:T(8,128)S(1)}, u32[]{:S(2)}, u32[]{:S(2)}) collective-permute-start(f32[544,128]{1,0:T(8,128)S(1)} %get-tuple-element.102.refs_0_), channel_id=1, source_target_pairs={{0,16},{16,32},{32,48},{48,0},{64,80},{80,96},{96,112},{112,64},{1... | collective-permute-start | bytes 835592 | tf_op jit(solution)/shard_map/ppermute | solution.py:536
  67.1 9.6 %collective-permute-start.1 = (f32[544,128]{1,0:T(8,128)S(1)}, f32[544,128]{1,0:T(8,128)S(1)}, u32[]{:S(2)}, u32[]{:S(2)}) collective-permute-start(f32[544,128]{1,0:T(8,128)S(1)} %get-tuple-element.103.refs_1_), channel_id=1, source_target_pairs={{0,48},{16,0},{32,16},{48,32},{64,112},{80,64},{96,80},{112,96},{1... | collective-permute-start | bytes 835592 | tf_op jit(solution)/shard_map/ppermute | solution.py:536
  67.5 15.1 %collective-permute-start = (f32[544,128]{1,0:T(8,128)S(1)}, f32[544,128]{1,0:T(8,128)S(1)}, u32[]{:S(2)}, u32[]{:S(2)}) collective-permute-start(f32[544,128]{1,0:T(8,128)S(1)} %get-tuple-element.102.refs_0_), channel_id=1, source_target_pairs={{0,48},{16,0},{32,16},{48,32},{64,112},{80,64},{96,80},{112,96},{1... | collective-permute-start | bytes 835592 | tf_op jit(solution)/shard_map/ppermute | solution.py:536
  69.2 13.4 %collective-permute-start.5 = (f32[544,128]{1,0:T(8,128)S(1)}, f32[544,128]{1,0:T(8,128)S(1)}, u32[]{:S(2)}, u32[]{:S(2)}) collective-permute-start(f32[544,128]{1,0:T(8,128)S(1)} %get-tuple-element.103.refs_1_), channel_id=1, source_target_pairs={{0,16},{16,32},{32,48},{48,0},{64,80},{80,96},{96,112},{112,64},{1... | collective-permute-start | bytes 835592 | tf_op jit(solution)/shard_map/ppermute | solution.py:536
  75.0 11.0 %collective-permute-start.3 = (f32[544,128]{1,0:T(8,128)S(1)}, f32[544,128]{1,0:T(8,128)S(1)}, u32[]{:S(2)}, u32[]{:S(2)}) collective-permute-start(f32[544,128]{1,0:T(8,128)S(1)} %collective-permute-done.2.refs_6_), channel_id=1, source_target_pairs={{0,16},{16,32},{32,48},{48,0},{64,80},{80,96},{96,112},{112,64},{1... | collective-permute-start | bytes 835592 | tf_op jit(solution)/shard_map/ppermute | solution.py:536
  76.7 10.7 %collective-permute-start.4 = (f32[544,128]{1,0:T(8,128)S(1)}, f32[544,128]{1,0:T(8,128)S(1)}, u32[]{:S(2)}, u32[]{:S(2)}) collective-permute-start(f32[544,128]{1,0:T(8,128)S(1)} %collective-permute-done.1.refs_3_), channel_id=1, source_target_pairs={{0,48},{16,0},{32,16},{48,32},{64,112},{80,64},{96,80},{112,96},{1... | collective-permute-start | bytes 835592 | tf_op jit(solution)/shard_map/ppermute | solution.py:536
  89.2 5.4 %collective-permute-start.6 = (f32[32,256]{1,0:T(8,128)S(1)}, f32[32,256]{1,0:T(8,128)S(1)}, u32[]{:S(2)}, u32[]{:S(2)}) collective-permute-start(f32[32,256]{1,0:T(8,128)S(1)} %get-tuple-element.104), channel_id=1, source_target_pairs={{0,64},{2,66},{4,68},{6,70},{8,200},{10,202},{12,204},{14,206},{16... | collective-permute-start | bytes 98312 | tf_op jit(solution)/shard_map/ppermute | solution.py:578
  95.3 5.2 %collective-permute-start.7 = (f32[32,256]{1,0:T(8,128)S(1)}, f32[32,256]{1,0:T(8,128)S(1)}, u32[]{:S(2)}, u32[]{:S(2)}) collective-permute-start(f32[32,256]{1,0:T(8,128)S(1)} %row_step.2), channel_id=1, source_target_pairs={{0,64},{2,66},{4,68},{6,70},{8,200},{10,202},{12,204},{14,206},{16... | collective-permute-start | bytes 98312 | tf_op jit(solution)/shard_map/ppermute | solution.py:578
  101.2 5.2 %collective-permute-start.8 = (f32[32,256]{1,0:T(8,128)S(1)}, f32[32,256]{1,0:T(8,128)S(1)}, u32[]{:S(2)}, u32[]{:S(2)}) collective-permute-start(f32[32,256]{1,0:T(8,128)S(1)} %row_step.3), channel_id=1, source_target_pairs={{0,64},{2,66},{4,68},{6,70},{8,200},{10,202},{12,204},{14,206},{16... | collective-permute-start | bytes 98312 | tf_op jit(solution)/shard_map/ppermute | solution.py:578
  118.7 19.4 %all-to-all-start.2 = ((f32[8,128,128]{2,1,0:T(8,128)}), f32[8,128,128]{2,1,0:T(8,128)S(1)}, u32[]{:S(2)}, u32[]{:S(2)}) async-start(f32[8,128,128]{2,1,0:T(8,128)} %inflow.1), calls=%async_computation.4 | async-start | bytes 1048576 | tf_op jit(solution)/shard_map/all_to_all | solution.py:409
  122.2 0.8 copy-start.7
Sparse Core Ops, SparseCore 1:
  65.1 45.9 reduce-scatter.2

commit v13 on v12

--- a/solution.py
+++ b/solution.py
@@ -66,22 +66,24 @@
                 )
                 fetch.start()
                 fetches[slab, plane, side] = fetch
-    rows = lax.broadcasted_iota(jnp.int32, (lead, width), 0)
-    cols = lax.broadcasted_iota(jnp.int32, (lead, width), 1)
-    targets = [
-        jnp.broadcast_to(inject_ref[sweep : sweep + 1, :].astype(F32), (width, modes)).T
+    rows = lax.broadcasted_iota(jnp.int32, (width, lead), 0)
+    cols = lax.broadcasted_iota(jnp.int32, (width, lead), 1)
+    fetch_src.wait()
+    columns = [
+        jnp.concatenate([src_ref[sweep, part] for part in range(2)], axis=0).T
         for sweep in range(2)
     ]
-    fetch_src.wait()
     count = g_ref.shape[3] // 8
-    total = [0.0] * 4
+    sums = [[0.0, 0.0], [0.0, 0.0]]
+    picks = [{}, {}]
     for slab in range(2):
-        chosen = [target == (first + slab).astype(F32) for target in targets]
-        left = []
+        right = []
         for sweep in range(2):
-            unit = (cols == rows * 8 + sweep).astype(F32)
-            source = [jnp.where(chosen[sweep], src_ref[sweep, part], 0.0) for part in range(2)]
-            left.append(split(jnp.concatenate([unit] + source, axis=0)))
+            target = inject_ref[sweep : sweep + 1, :]
+            chosen = jnp.concatenate([target, target], axis=1) == first + slab
+            unit = (rows == cols * 8 + sweep).astype(F32)
+            source = jnp.where(chosen, columns[sweep], 0.0)
+            right.append(split(jnp.concatenate([source, unit], axis=1)))
         for plane in range(2):
             for side in range(2):
                 fetches[slab, plane, side].wait()
@@ -93,22 +95,21 @@
                     ],
                     axis=1,
                 )
-                term = mm3(left[sweep], split(picked), True)
-                order = slab if sweep == 0 else 1 - slab
-                for member in range(4):
-                    put(out_ref, sweep * 4 + member, (order * 2 + plane) * lead, term[:lead])
-                real, imag = term[lead : lead + modes], term[lead + modes :]
-                if plane == 0:
-                    total[2 * sweep] += real
-                    total[2 * sweep + 1] += imag
-                else:
-                    total[2 * sweep] -= imag
-                    total[2 * sweep + 1] += real
-    for dest in range(8):
-        sweep, member = divmod(dest, 4)
-        for part in range(2):
-            piece = total[2 * sweep + part][member * 16 : (member + 1) * 16]
-            put(out_ref, dest, 4 * lead + part * 16, piece)
+                term = mm3(split(picked), right[sweep])
+                sums[sweep][plane] += term[:, : 2 * modes]
+                picks[sweep][slab, plane] = term[:, 2 * modes :]
+    for sweep in range(2):
+        slabs = (0, 1) if sweep == 0 else (1, 0)
+        block = [picks[sweep][slab, plane] for slab in slabs for plane in range(2)]
+        block = jnp.concatenate(block, axis=1).T
+        by_real, by_imag = sums[sweep][0].T, sums[sweep][1].T
+        total = (by_real[:modes] - by_imag[modes:], by_real[modes:] + by_imag[:modes])
+        for member in range(4):
+            dest = sweep * 4 + member
+            put(out_ref, dest, 0, block)
+            for part in range(2):
+                piece = total[part][member * 16 : (member + 1) * 16]
+                put(out_ref, dest, 4 * lead + part * 16, piece)
 
 
 def packed_columns(place_ref, inject_ref, sweep):

time: 148 us -> 148 us (level)
  no operation moved by 1% of the time
where the time goes in v13:
time: 148 us; the launch traced here: 147 us
  waiting for transfers between devices  65.4 us (44%)
  Pallas kernels  36.1 us (24%)
  starting transfers between devices  25.5 us (17%)
  between operations  16.3 us (11%)
  local copies, waits for them, and re-layouts  2.95 us (2%)
    all_to_all x3, waiting for transfers between devices, exchange(): return lax.all_to_all(value, 'col', split_axis=0, concat_axis=0, tiled=True)  39.2 us
    all_to_all x3, starting transfers between devices, exchange(): return lax.all_to_all(value, 'col', split_axis=0, concat_axis=0, tiled=True)  16.5 us
    ppermute x6, waiting for transfers between devices, turn(): lax.ppermute(value, 'slab', [(slab, slab // 4 * 4 + (slab + step) % 4) fo...  15.7 us
    pallas_call x7, Pallas kernels, local(): pl.pallas_call(kernel, in_specs=[SMEM] + [VMEM] * (len(args) - 1), out_sp...  12.3 us
    pallas_call x1, Pallas kernels, chunk_terms(): pl.pallas_call(spread_kernel, grid=(8,), in_specs=[whole(terms.shape), wh...  8.72 us
    pallas_call x1, Pallas kernels, on_device(): pl.pallas_call(interface_kernel, grid=(1,), in_specs=[whole(inject.shape)...  7.11 us
    ppermute x3, waiting for transfers between devices, hop(): return lax.ppermute(value, ('slab', 'col'), pairs)  6.31 us
    ppermute x6, starting transfers between devices, turn(): lax.ppermute(value, 'slab', [(slab, slab // 4 * 4 + (slab + step) % 4) fo...  6.16 us
  transfers between devices with their start and end apart: 13, of which 11 were waited for; matrix products, arithmetic and copies ran while one was open for 1% of the time, Pallas kernels for 19%

profile of v13, /device:TPU:8, one launch (start us, length us, event | category | flops | bytes accessed | tf_op | source)
XLA Modules:
  0.0 147.3 jit_solution(6048758867510097302)
XLA Ops:
  8.0 7.1 %interface_terms.1 = f32[8,320,128]{2,1,0:T(8,128)} custom-call(s32[2,64]{1,0:T(2,128)} %inject_ref.4, f32[2,2,64,256]{3,2,1,0:T(8,128)} %bitcast.27, f32[2,2,2048,256]{3,2,1,0:T(8,128)} %g_ref.1), custom_call_target="tpu_custom_call" | custom-call | tf_op jit(solution)/shard_map/interface_terms/pallas_call | solution.py:433
  15.2 8.6 %all-to-all-start = ((f32[8,320,128]{2,1,0:T(8,128)}), f32[8,320,128]{2,1,0:T(8,128)S(1)}, u32[]{:S(2)}, u32[]{:S(2)}) async-start(f32[8,320,128]{2,1,0:T(8,128)} %interface_terms.1), calls=%async_computation.1 | async-start | bytes 2621440 | tf_op jit(solution)/shard_map/all_to_all | solution.py:410
  29.5 8.7 %spread_terms.2 = (f32[8,512,128]{2,1,0:T(8,128)}, f32[8,64,256]{2,1,0:T(8,128)}) custom-call(bf16[2,128,256]{2,1,0:T(8,128)(2,1)} %copy-done.5, bf16[2,128,256]{2,1,0:T(8,128)(2,1)} %copy-done.6, f32[2,2,2048,256]{3,2,1,0:T(8,128)} %g_ref.1), custom_call_target="tpu_custom_call" | custom-call | tf_op jit(solution)/shard_map/spread_terms/pallas_call | solution.py:461
  38.4 19.8 %all-to-all-done.recv_ref = f32[8,320,128]{2,1,0:T(8,128)S(1)} async-done(((f32[8,320,128]{2,1,0:T(8,128)}), f32[8,320,128]{2,1,0:T(8,128)S(1)}, u32[]{:S(2)}, u32[]{:S(2)}) %all-to-all-start) | async-done | bytes 1310752 | tf_op jit(solution)/shard_map/all_to_all | solution.py:410
  58.3 4.4 %all-to-all-start.1 = ((f32[8,512,128]{2,1,0:T(8,128)}), f32[8,512,128]{2,1,0:T(8,128)}, u32[]{:S(2)}, u32[]{:S(2)}) async-start(f32[8,512,128]{2,1,0:T(8,128)} %get-tuple-element.96), calls=%async_computation.2 | async-start | bytes 4194304 | tf_op jit(solution)/shard_map/all_to_all | solution.py:410
  63.2 2.8 %pair_map.1 = (f32[544,128]{1,0:T(8,128)S(1)}, f32[544,128]{1,0:T(8,128)S(1)}, f32[32,256]{1,0:T(8,128)S(1)}, f32[512,256]{1,0:T(8,128)S(1)}) custom-call(s32[4]{0:T(128)S(1)} %pad_add_fusion.1.team_ref.info_ref, f32[8,320,128]{2,1,0:T(8,128)S(1)} %all-to-all-done.recv_ref, f32[2,512,256]{2,1,0:T(8,128)S(1)} %coupling_rows.1.x_ref, ...), custom_call_target="tpu_custom_call" | custom-call | tf_op jit(solution)/shard_map/pair_map/pallas_call | solution.py:522
  66.0 1.6 %collective-permute-start.2 = (f32[544,128]{1,0:T(8,128)S(1)}, f32[544,128]{1,0:T(8,128)S(1)}, u32[]{:S(2)}, u32[]{:S(2)}) collective-permute-start(f32[544,128]{1,0:T(8,128)S(1)} %get-tuple-element.102.refs_0_), channel_id=1, source_target_pairs={{0,16},{16,32},{32,48},{48,0},{64,80},{80,96},{96,112},{112,64},{1... | collective-permute-start | bytes 835592 | tf_op jit(solution)/shard_map/ppermute | solution.py:537
  68.1 1.6 %collective-permute-start = (f32[544,128]{1,0:T(8,128)S(1)}, f32[544,128]{1,0:T(8,128)S(1)}, u32[]{:S(2)}, u32[]{:S(2)}) collective-permute-start(f32[544,128]{1,0:T(8,128)S(1)} %get-tuple-element.102.refs_0_), channel_id=1, source_target_pairs={{0,48},{16,0},{32,16},{48,32},{64,112},{80,64},{96,80},{112,96},{1... | collective-permute-start | bytes 835592 | tf_op jit(solution)/shard_map/ppermute | solution.py:537
  70.1 5.5 %collective-permute-done.2.refs_6_ = f32[544,128]{1,0:T(8,128)S(1)} collective-permute-done((f32[544,128]{1,0:T(8,128)S(1)}, f32[544,128]{1,0:T(8,128)S(1)}, u32[]{:S(2)}, u32[]{:S(2)}) %collective-permute-start.2) | collective-permute-done | bytes 278560 | tf_op jit(solution)/shard_map/ppermute | solution.py:537
  77.7 5.5 %collective-permute-done.refs_2_ = f32[544,128]{1,0:T(8,128)S(1)} collective-permute-done((f32[544,128]{1,0:T(8,128)S(1)}, f32[544,128]{1,0:T(8,128)S(1)}, u32[]{:S(2)}, u32[]{:S(2)}) %collective-permute-start) | collective-permute-done | bytes 278560 | tf_op jit(solution)/shard_map/ppermute | solution.py:537
  83.2 3.4 %collective-permute-done.3.refs_4_ = f32[544,128]{1,0:T(8,128)S(1)} collective-permute-done((f32[544,128]{1,0:T(8,128)S(1)}, f32[544,128]{1,0:T(8,128)S(1)}, u32[]{:S(2)}, u32[]{:S(2)}) %collective-permute-start.3) | collective-permute-done | bytes 278560 | tf_op jit(solution)/shard_map/ppermute | solution.py:537
  87.9 1.9 %gather_maps.1 = (bf16[4,512,256]{2,1,0:T(8,128)(2,1)S(1)}, bf16[4,512,256]{2,1,0:T(8,128)(2,1)S(1)}, f32[4,32,256]{2,1,0:T(8,128)S(1)}, f32[32,256]{1,0:T(8,128)S(1)}) custom-call(s32[4]{0:T(128)S(1)} %pad_add_fusion.1.team_ref.info_ref, f32[32,256]{1,0:T(8,128)S(1)} %bitcast.22, f32[544,128]{1,0:T(8,128)S(1)} %get-tuple-element.102.refs_0_, ...), custom_call_target="tpu_custom_call" | custom-call | tf_op jit(solution)/shard_map/gather_maps/pallas_call | solution.py:551
  89.8 1.8 %collective-permute-start.6 = (f32[32,256]{1,0:T(8,128)S(1)}, f32[32,256]{1,0:T(8,128)S(1)}, u32[]{:S(2)}, u32[]{:S(2)}) collective-permute-start(f32[32,256]{1,0:T(8,128)S(1)} %get-tuple-element.104), channel_id=1, source_target_pairs={{0,64},{2,66},{4,68},{6,70},{8,200},{10,202},{12,204},{14,206},{16... | collective-permute-start | bytes 98312 | tf_op jit(solution)/shard_map/ppermute | solution.py:579
  91.5 3.1 %row_map.1 = (bf16[512,256]{1,0:T(8,128)(2,1)S(1)}, bf16[512,256]{1,0:T(8,128)(2,1)S(1)}, f32[32,256]{1,0:T(8,128)S(1)}, f32[544,256]{1,0:T(8,128)S(1)}) custom-call(s32[4]{0:T(128)S(1)} %pad_add_fusion.1.team_ref.info_ref, bf16[4,512,256]{2,1,0:T(8,128)(2,1)S(1)} %get-tuple-element.105.high_ref, bf16[4,512,256]{2,1,0:T(8,128)(2,1)S(1)} %get-tuple-element.106.low_ref, ...), custom_call_target="tpu_custom_call" | custom-call | tf_op jit(solution)/shard_map/row_map/pallas_call | solution.py:569
  97.0 1.7 %prefix_map.1 = (f32[544,256]{1,0:T(8,128)S(1)}, f32[544,256]{1,0:T(8,128)S(1)}) custom-call(s32[4]{0:T(128)S(1)} %pad_add_fusion.1.team_ref.info_ref, bf16[4,512,256]{2,1,0:T(8,128)(2,1)S(1)} %get-tuple-element.105.high_ref, bf16[4,512,256]{2,1,0:T(8,128)(2,1)S(1)} %get-tuple-element.106.low_ref, f32[4,32,256]{2,1,0:T(8,128)S(1)} %get-tuple-element.107.flow_ref, ...), custom_call_target="tpu_custom_call" | custom-call | tf_op jit(solution)/shard_map/prefix_map/pallas_call | solution.py:569
  98.7 2.4 %collective-permute-done.7.state_ref = f32[32,256]{1,0:T(8,128)S(1)} collective-permute-done((f32[32,256]{1,0:T(8,128)S(1)}, f32[32,256]{1,0:T(8,128)S(1)}, u32[]{:S(2)}, u32[]{:S(2)}) %collective-permute-start.7) | collective-permute-done | bytes 32800 | tf_op jit(solution)/shard_map/ppermute | solution.py:579
  101.8 1.7 %entry_map.1 = (bf16[2,512,256]{2,1,0:T(8,128)(2,1)S(1)}, bf16[2,512,256]{2,1,0:T(8,128)(2,1)S(1)}, f32[2,32,256]{2,1,0:T(8,128)S(1)}) custom-call(s32[4]{0:T(128)S(1)} %pad_add_fusion.1.team_ref.info_ref, f32[544,256]{1,0:T(8,128)S(1)} %get-tuple-element.119.prefix_ref, f32[544,256]{1,0:T(8,128)S(1)} %get-tuple-element.120.inner_ref, ...), custom_call_target="tpu_custom_call" | custom-call | tf_op jit(solution)/shard_map/entry_map/pallas_call | solution.py:569
  103.5 3.4 %collective-permute-done.8.state_ref = f32[32,256]{1,0:T(8,128)S(1)} collective-permute-done((f32[32,256]{1,0:T(8,128)S(1)}, f32[32,256]{1,0:T(8,128)S(1)}, u32[]{:S(2)}, u32[]{:S(2)}) %collective-permute-start.8) | collective-permute-done | bytes 32800 | tf_op jit(solution)/shard_map/ppermute | solution.py:579
  106.9 1.7 %inflow.1 = f32[8,128,128]{2,1,0:T(8,128)} custom-call(s32[4]{0:T(128)S(1)} %pad_add_fusion.1.team_ref.info_ref, f32[32,256]{1,0:T(8,128)S(1)} %bitcast.25, f32[32,256]{1,0:T(8,128)S(1)} %collective-permute-done.8.state_ref, bf16[2,512,256]{2,1,0:T(8,128)(2,1)S(1)} %get-tuple-element.121.high_ref, bf16[2,512,256]{2,1,0:T(8,128)(2,1)S(1)} %get-tuple-element.122.low_ref, ...), custom_call_target="tpu_custom_call" | custom-call | tf_op jit(solution)/shard_map/inflow/pallas_call | solution.py:569
  108.6 3.6 %reduce-scatter.3.cloned.1.call-done = f32[1,64,256]{2,1,0:T(8,128)} async-done(((f32[8,64,256]{2,1,0:T(8,128)}), f32[1,64,256]{2,1,0:T(8,128)}) %reduce-scatter.3.cloned.1.call-update) | async-done | bytes 65552 | tf_op jit(solution)/shard_map/reduce_scatter | solution.py:482
  112.3 6.9 %all-to-all-done.1.recv_ref = f32[8,512,128]{2,1,0:T(8,128)} async-done(((f32[8,512,128]{2,1,0:T(8,128)}), f32[8,512,128]{2,1,0:T(8,128)}, u32[]{:S(2)}, u32[]{:S(2)}) %all-to-all-start.1) | async-done | bytes 2097184 | tf_op jit(solution)/shard_map/all_to_all | solution.py:410
  119.2 3.5 %all-to-all-start.2 = ((f32[8,128,128]{2,1,0:T(8,128)}), f32[8,128,128]{2,1,0:T(8,128)S(1)}, u32[]{:S(2)}, u32[]{:S(2)}) async-start(f32[8,128,128]{2,1,0:T(8,128)} %inflow.1), calls=%async_computation.4 | async-start | bytes 1048576 | tf_op jit(solution)/shard_map/all_to_all | solution.py:410
  123.6 2.6 %arrange_rows.1 = (bf16[2,2,2,256,256]{4,3,2,1,0:T(8,128)(2,1)S(1)}, bf16[2,2,2,256,256]{4,3,2,1,0:T(8,128)(2,1)S(1)}, f32[2,2,2,64,256]{4,3,2,1,0:T(8,128)S(1)}) custom-call(s32[2]{0:T(128)S(1)} %pad_add_fusion.3.place_ref, s32[2,64]{1,0:T(2,128)S(1)} %get-tuple-element.266, f32[8,512,128]{2,1,0:T(8,128)} %all-to-all-done.1.recv_ref, ...), custom_call_target="tpu_custom_call" | custom-call | tf_op jit(solution)/shard_map/arrange_rows/pallas_call | solution.py:569
  126.2 12.4 %all-to-all-done.2.last_ref = f32[8,128,128]{2,1,0:T(8,128)S(1)} async-done(((f32[8,128,128]{2,1,0:T(8,128)}), f32[8,128,128]{2,1,0:T(8,128)S(1)}, u32[]{:S(2)}, u32[]{:S(2)}) %all-to-all-start.2) | async-done | bytes 524320 | tf_op jit(solution)/shard_map/all_to_all | solution.py:410
  (45 shorter events, 15.2 us)
Async XLA Ops:
  8.0 30.3 %copy-start = (f32[2,2,256,64]{2,3,1,0:T(8,128)S(1)}, f32[2,2,256,64]{2,3,1,0:T(8,128)}, u32[]{:S(2)}) copy-start(f32[2,2,256,64]{2,3,1,0:T(8,128)} %param.11) | copy-start | bytes 786436
  15.1 8.6 %copy-start.10 = (s32[2,64]{1,0:T(2,128)S(1)}, s32[2,64]{1,0:T(2,128)}, u32[]{:S(2)}) copy-start(s32[2,64]{1,0:T(2,128)} %inject_ref.4) | copy-start | bytes 1540
  15.1 10.2 %copy-start.8 = (f32[2,2,256,64]{2,3,1,0:T(8,128)S(1)}, f32[2,2,256,64]{2,3,1,0:T(8,128)}, u32[]{:S(2)}) copy-start(f32[2,2,256,64]{2,3,1,0:T(8,128)} %param.9) | copy-start | bytes 786436
  15.2 43.0 %all-to-all-start = ((f32[8,320,128]{2,1,0:T(8,128)}), f32[8,320,128]{2,1,0:T(8,128)S(1)}, u32[]{:S(2)}, u32[]{:S(2)}) async-start(f32[8,320,128]{2,1,0:T(8,128)} %interface_terms.1), calls=%async_computation.1 | async-start | bytes 2621440 | tf_op jit(solution)/shard_map/all_to_all | solution.py:410
  26.5 0.7 copy-start.5
  27.2 2.3 %copy-start.6 = (bf16[2,128,256]{2,1,0:T(8,128)(2,1)}, bf16[2,128,256]{2,1,0:T(8,128)(2,1)S(1)}, u32[]{:S(2)}) copy-start(bf16[2,128,256]{2,1,0:T(8,128)(2,1)S(1)} %get-tuple-element.93.low_ref) | copy-start | bytes 393220
  27.3 1.2 copy-start.4
  38.4 19.9 %copy-start.9 = (f32[256,256]{1,0:T(8,128)}, f32[256,256]{1,0:T(8,128)S(1)}, u32[]{:S(2)}) copy-start(f32[256,256]{1,0:T(8,128)S(1)} %get-tuple-element.127.extra_ref) | copy-start | bytes 786436
  58.3 60.9 %all-to-all-start.1 = ((f32[8,512,128]{2,1,0:T(8,128)}), f32[8,512,128]{2,1,0:T(8,128)}, u32[]{:S(2)}, u32[]{:S(2)}) async-start(f32[8,512,128]{2,1,0:T(8,128)} %get-tuple-element.96), calls=%async_computation.2 | async-start | bytes 4194304 | tf_op jit(solution)/shard_map/all_to_all | solution.py:410
  62.6 49.6 %reduce-scatter.3.cloned.1.call-start = ((), (), s32[]{:S(2)}) async-start(), calls=%async_computation.5 | async-start | bytes 589824 | tf_op jit(solution)/shard_map/reduce_scatter | solution.py:482
  66.0 9.6 %collective-permute-start.2 = (f32[544,128]{1,0:T(8,128)S(1)}, f32[544,128]{1,0:T(8,128)S(1)}, u32[]{:S(2)}, u32[]{:S(2)}) collective-permute-start(f32[544,128]{1,0:T(8,128)S(1)} %get-tuple-element.102.refs_0_), channel_id=1, source_target_pairs={{0,16},{16,32},{32,48},{48,0},{64,80},{80,96},{96,112},{112,64},{1... | collective-permute-start | bytes 835592 | tf_op jit(solution)/shard_map/ppermute | solution.py:537
  67.7 9.6 %collective-permute-start.1 = (f32[544,128]{1,0:T(8,128)S(1)}, f32[544,128]{1,0:T(8,128)S(1)}, u32[]{:S(2)}, u32[]{:S(2)}) collective-permute-start(f32[544,128]{1,0:T(8,128)S(1)} %get-tuple-element.103.refs_1_), channel_id=1, source_target_pairs={{0,48},{16,0},{32,16},{48,32},{64,112},{80,64},{96,80},{112,96},{1... | collective-permute-start | bytes 835592 | tf_op jit(solution)/shard_map/ppermute | solution.py:537
  68.1 15.1 %collective-permute-start = (f32[544,128]{1,0:T(8,128)S(1)}, f32[544,128]{1,0:T(8,128)S(1)}, u32[]{:S(2)}, u32[]{:S(2)}) collective-permute-start(f32[544,128]{1,0:T(8,128)S(1)} %get-tuple-element.102.refs_0_), channel_id=1, source_target_pairs={{0,48},{16,0},{32,16},{48,32},{64,112},{80,64},{96,80},{112,96},{1... | collective-permute-start | bytes 835592 | tf_op jit(solution)/shard_map/ppermute | solution.py:537
  69.8 13.4 %collective-permute-start.5 = (f32[544,128]{1,0:T(8,128)S(1)}, f32[544,128]{1,0:T(8,128)S(1)}, u32[]{:S(2)}, u32[]{:S(2)}) collective-permute-start(f32[544,128]{1,0:T(8,128)S(1)} %get-tuple-element.103.refs_1_), channel_id=1, source_target_pairs={{0,16},{16,32},{32,48},{48,0},{64,80},{80,96},{96,112},{112,64},{1... | collective-permute-start | bytes 835592 | tf_op jit(solution)/shard_map/ppermute | solution.py:537
  75.6 11.0 %collective-permute-start.3 = (f32[544,128]{1,0:T(8,128)S(1)}, f32[544,128]{1,0:T(8,128)S(1)}, u32[]{:S(2)}, u32[]{:S(2)}) collective-permute-start(f32[544,128]{1,0:T(8,128)S(1)} %collective-permute-done.2.refs_6_), channel_id=1, source_target_pairs={{0,16},{16,32},{32,48},{48,0},{64,80},{80,96},{96,112},{112,64},{1... | collective-permute-start | bytes 835592 | tf_op jit(solution)/shard_map/ppermute | solution.py:537
  77.2 10.7 %collective-permute-start.4 = (f32[544,128]{1,0:T(8,128)S(1)}, f32[544,128]{1,0:T(8,128)S(1)}, u32[]{:S(2)}, u32[]{:S(2)}) collective-permute-start(f32[544,128]{1,0:T(8,128)S(1)} %collective-permute-done.1.refs_3_), channel_id=1, source_target_pairs={{0,48},{16,0},{32,16},{48,32},{64,112},{80,64},{96,80},{112,96},{1... | collective-permute-start | bytes 835592 | tf_op jit(solution)/shard_map/ppermute | solution.py:537
  89.8 5.4 %collective-permute-start.6 = (f32[32,256]{1,0:T(8,128)S(1)}, f32[32,256]{1,0:T(8,128)S(1)}, u32[]{:S(2)}, u32[]{:S(2)}) collective-permute-start(f32[32,256]{1,0:T(8,128)S(1)} %get-tuple-element.104), channel_id=1, source_target_pairs={{0,64},{2,66},{4,68},{6,70},{8,200},{10,202},{12,204},{14,206},{16... | collective-permute-start | bytes 98312 | tf_op jit(solution)/shard_map/ppermute | solution.py:579
  95.9 5.2 %collective-permute-start.7 = (f32[32,256]{1,0:T(8,128)S(1)}, f32[32,256]{1,0:T(8,128)S(1)}, u32[]{:S(2)}, u32[]{:S(2)}) collective-permute-start(f32[32,256]{1,0:T(8,128)S(1)} %row_step.2), channel_id=1, source_target_pairs={{0,64},{2,66},{4,68},{6,70},{8,200},{10,202},{12,204},{14,206},{16... | collective-permute-start | bytes 98312 | tf_op jit(solution)/shard_map/ppermute | solution.py:579
  101.8 5.2 %collective-permute-start.8 = (f32[32,256]{1,0:T(8,128)S(1)}, f32[32,256]{1,0:T(8,128)S(1)}, u32[]{:S(2)}, u32[]{:S(2)}) collective-permute-start(f32[32,256]{1,0:T(8,128)S(1)} %row_step.3), channel_id=1, source_target_pairs={{0,64},{2,66},{4,68},{6,70},{8,200},{10,202},{12,204},{14,206},{16... | collective-permute-start | bytes 98312 | tf_op jit(solution)/shard_map/ppermute | solution.py:579
  119.2 19.4 %all-to-all-start.2 = ((f32[8,128,128]{2,1,0:T(8,128)}), f32[8,128,128]{2,1,0:T(8,128)S(1)}, u32[]{:S(2)}, u32[]{:S(2)}) async-start(f32[8,128,128]{2,1,0:T(8,128)} %inflow.1), calls=%async_computation.4 | async-start | bytes 1048576 | tf_op jit(solution)/shard_map/all_to_all | solution.py:410
  122.7 0.8 copy-start.7
Sparse Core Ops, SparseCore 1:
  65.6 46.6 reduce-scatter.2

commit v14 on v13

--- a/solution.py
+++ b/solution.py
@@ -51,21 +51,20 @@
 def interface_kernel(inject_ref, src_hbm, g_hbm, out_ref, g_ref, src_ref, sems, src_sem):
     first = lax.axis_index("slab") * 2
     modes, width = src_ref.shape[2], src_ref.shape[3]
-    lanes = width // 2
     lead = width // 8
     fetch_src = pltpu.make_async_copy(src_hbm, src_ref, src_sem)
     fetch_src.start()
     fetches = {}
     for slab in range(2):
         for plane in range(2):
-            for side in range(2):
+            for sweep in range(2):
                 fetch = pltpu.make_async_copy(
-                    g_hbm.at[slab, plane, :, side * lanes : (side + 1) * lanes],
-                    g_ref.at[slab, plane, side],
-                    sems.at[slab, plane, side],
+                    g_hbm.at[slab, plane, :, 1 - sweep, :],
+                    g_ref.at[slab, plane, sweep],
+                    sems.at[slab, plane, sweep],
                 )
                 fetch.start()
-                fetches[slab, plane, side] = fetch
+                fetches[slab, plane, sweep] = fetch
     rows = lax.broadcasted_iota(jnp.int32, (width, lead), 0)
     cols = lax.broadcasted_iota(jnp.int32, (width, lead), 1)
     fetch_src.wait()
@@ -73,7 +72,6 @@
         jnp.concatenate([src_ref[sweep, part] for part in range(2)], axis=0).T
         for sweep in range(2)
     ]
-    count = g_ref.shape[3] // 8
     sums = [[0.0, 0.0], [0.0, 0.0]]
     picks = [{}, {}]
     for slab in range(2):
@@ -85,17 +83,9 @@
             source = jnp.where(chosen, columns[sweep], 0.0)
             right.append(split(jnp.concatenate([source, unit], axis=1)))
         for plane in range(2):
-            for side in range(2):
-                fetches[slab, plane, side].wait()
             for sweep in range(2):
-                picked = jnp.concatenate(
-                    [
-                        g_ref[slab, plane, side, pl.ds(1 - sweep, count, stride=8), :]
-                        for side in range(2)
-                    ],
-                    axis=1,
-                )
-                term = mm3(split(picked), right[sweep])
+                fetches[slab, plane, sweep].wait()
+                term = mm3(split(g_ref[slab, plane, sweep]), right[sweep])
                 sums[sweep][plane] += term[:, : 2 * modes]
                 picks[sweep][slab, plane] = term[:, 2 * modes :]
     for sweep in range(2):
@@ -437,14 +427,14 @@
         out_specs=whole((8, 2 * block_rows, LANES)),
         out_shape=jax.ShapeDtypeStruct((8, 2 * block_rows, LANES), F32),
         scratch_shapes=[
-            pltpu.VMEM((2, 2, 2, orbitals, width // 2), F32),
+            pltpu.VMEM((2, 2, 2, size, width), F32),
             pltpu.VMEM(sources.shape, F32),
             pltpu.SemaphoreType.DMA((2, 2, 2)),
             pltpu.SemaphoreType.DMA,
         ],
         compiler_params=params(LARGE),
         name="interface_terms",
-    )(inject, sources, diag_inverse)
+    )(inject, sources, diag_inverse.reshape(2, 2, size, orbitals // size, width))
     sent, inject_after = lax.optimization_barrier((sent, inject))
     received = exchange(sent)
 

time: 148 us -> 148 us (level)
  no operation moved by 1% of the time
where the time goes in v14:
time: 148 us; the launch traced here: 146 us
  waiting for transfers between devices  65.4 us (44%)
  Pallas kernels  35.1 us (24%)
  starting transfers between devices  25.6 us (17%)
  between operations  16.3 us (11%)
  local copies, waits for them, and re-layouts  2.95 us (2%)
    all_to_all x3, waiting for transfers between devices, exchange(): return lax.all_to_all(value, 'col', split_axis=0, concat_axis=0, tiled=True)  39.5 us
    all_to_all x3, starting transfers between devices, exchange(): return lax.all_to_all(value, 'col', split_axis=0, concat_axis=0, tiled=True)  16.5 us
    ppermute x6, waiting for transfers between devices, turn(): lax.ppermute(value, 'slab', [(slab, slab // 4 * 4 + (slab + step) % 4) fo...  15.7 us
    pallas_call x7, Pallas kernels, local(): pl.pallas_call(kernel, in_specs=[SMEM] + [VMEM] * (len(args) - 1), out_sp...  12.3 us
    pallas_call x1, Pallas kernels, chunk_terms(): pl.pallas_call(spread_kernel, grid=(8,), in_specs=[whole(terms.shape), wh...  8.73 us
    ppermute x3, waiting for transfers between devices, hop(): return lax.ppermute(value, ('slab', 'col'), pairs)  6.31 us
    ppermute x6, starting transfers between devices, turn(): lax.ppermute(value, 'slab', [(slab, slab // 4 * 4 + (slab + step) % 4) fo...  6.15 us
    pallas_call x1, Pallas kernels, on_device(): pl.pallas_call(interface_kernel, grid=(1,), in_specs=[whole(inject.shape)...  6.09 us
  transfers between devices with their start and end apart: 13, of which 11 were waited for; matrix products, arithmetic and copies ran while one was open for 1% of the time, Pallas kernels for 19%

profile of v14, /device:TPU:8, one launch (start us, length us, event | category | flops | bytes accessed | tf_op | source)
XLA Modules:
  0.0 146.3 jit_solution(17249967971692257716)
XLA Ops:
  8.0 6.1 %interface_terms.1 = f32[8,320,128]{2,1,0:T(8,128)} custom-call(s32[2,64]{1,0:T(2,128)} %inject_ref.4, f32[2,2,64,256]{3,2,1,0:T(8,128)} %bitcast.29, f32[2,2,256,8,256]{4,3,2,1,0:T(8,128)} %bitcast.28), custom_call_target="tpu_custom_call" | custom-call | tf_op jit(solution)/shard_map/interface_terms/pallas_call | solution.py:423
  14.1 8.6 %all-to-all-start = ((f32[8,320,128]{2,1,0:T(8,128)}), f32[8,320,128]{2,1,0:T(8,128)S(1)}, u32[]{:S(2)}, u32[]{:S(2)}) async-start(f32[8,320,128]{2,1,0:T(8,128)} %interface_terms.1), calls=%async_computation.1 | async-start | bytes 2621440 | tf_op jit(solution)/shard_map/all_to_all | solution.py:400
  28.5 8.7 %spread_terms.2 = (f32[8,512,128]{2,1,0:T(8,128)}, f32[8,64,256]{2,1,0:T(8,128)}) custom-call(bf16[2,128,256]{2,1,0:T(8,128)(2,1)} %copy-done.5, bf16[2,128,256]{2,1,0:T(8,128)(2,1)} %copy-done.6, f32[2,2,2048,256]{3,2,1,0:T(8,128)} %g_ref.1), custom_call_target="tpu_custom_call" | custom-call | tf_op jit(solution)/shard_map/spread_terms/pallas_call | solution.py:451
  37.4 19.8 %all-to-all-done.recv_ref = f32[8,320,128]{2,1,0:T(8,128)S(1)} async-done(((f32[8,320,128]{2,1,0:T(8,128)}), f32[8,320,128]{2,1,0:T(8,128)S(1)}, u32[]{:S(2)}, u32[]{:S(2)}) %all-to-all-start) | async-done | bytes 1310752 | tf_op jit(solution)/shard_map/all_to_all | solution.py:400
  57.3 4.4 %all-to-all-start.1 = ((f32[8,512,128]{2,1,0:T(8,128)}), f32[8,512,128]{2,1,0:T(8,128)}, u32[]{:S(2)}, u32[]{:S(2)}) async-start(f32[8,512,128]{2,1,0:T(8,128)} %get-tuple-element.96), calls=%async_computation.2 | async-start | bytes 4194304 | tf_op jit(solution)/shard_map/all_to_all | solution.py:400
  62.2 2.8 %pair_map.1 = (f32[544,128]{1,0:T(8,128)S(1)}, f32[544,128]{1,0:T(8,128)S(1)}, f32[32,256]{1,0:T(8,128)S(1)}, f32[512,256]{1,0:T(8,128)S(1)}) custom-call(s32[4]{0:T(128)S(1)} %pad_add_fusion.1.team_ref.info_ref, f32[8,320,128]{2,1,0:T(8,128)S(1)} %all-to-all-done.recv_ref, f32[2,512,256]{2,1,0:T(8,128)S(1)} %coupling_rows.1.x_ref, ...), custom_call_target="tpu_custom_call" | custom-call | tf_op jit(solution)/shard_map/pair_map/pallas_call | solution.py:512
  65.0 1.7 %collective-permute-start.2 = (f32[544,128]{1,0:T(8,128)S(1)}, f32[544,128]{1,0:T(8,128)S(1)}, u32[]{:S(2)}, u32[]{:S(2)}) collective-permute-start(f32[544,128]{1,0:T(8,128)S(1)} %get-tuple-element.102.refs_0_), channel_id=1, source_target_pairs={{0,16},{16,32},{32,48},{48,0},{64,80},{80,96},{96,112},{112,64},{1... | collective-permute-start | bytes 835592 | tf_op jit(solution)/shard_map/ppermute | solution.py:527
  67.1 1.7 %collective-permute-start = (f32[544,128]{1,0:T(8,128)S(1)}, f32[544,128]{1,0:T(8,128)S(1)}, u32[]{:S(2)}, u32[]{:S(2)}) collective-permute-start(f32[544,128]{1,0:T(8,128)S(1)} %get-tuple-element.102.refs_0_), channel_id=1, source_target_pairs={{0,48},{16,0},{32,16},{48,32},{64,112},{80,64},{96,80},{112,96},{1... | collective-permute-start | bytes 835592 | tf_op jit(solution)/shard_map/ppermute | solution.py:527
  69.1 5.5 %collective-permute-done.2.refs_6_ = f32[544,128]{1,0:T(8,128)S(1)} collective-permute-done((f32[544,128]{1,0:T(8,128)S(1)}, f32[544,128]{1,0:T(8,128)S(1)}, u32[]{:S(2)}, u32[]{:S(2)}) %collective-permute-start.2) | collective-permute-done | bytes 278560 | tf_op jit(solution)/shard_map/ppermute | solution.py:527
  76.6 5.5 %collective-permute-done.refs_2_ = f32[544,128]{1,0:T(8,128)S(1)} collective-permute-done((f32[544,128]{1,0:T(8,128)S(1)}, f32[544,128]{1,0:T(8,128)S(1)}, u32[]{:S(2)}, u32[]{:S(2)}) %collective-permute-start) | collective-permute-done | bytes 278560 | tf_op jit(solution)/shard_map/ppermute | solution.py:527
  82.2 3.4 %collective-permute-done.3.refs_4_ = f32[544,128]{1,0:T(8,128)S(1)} collective-permute-done((f32[544,128]{1,0:T(8,128)S(1)}, f32[544,128]{1,0:T(8,128)S(1)}, u32[]{:S(2)}, u32[]{:S(2)}) %collective-permute-start.3) | collective-permute-done | bytes 278560 | tf_op jit(solution)/shard_map/ppermute | solution.py:527
  86.9 1.9 %gather_maps.1 = (bf16[4,512,256]{2,1,0:T(8,128)(2,1)S(1)}, bf16[4,512,256]{2,1,0:T(8,128)(2,1)S(1)}, f32[4,32,256]{2,1,0:T(8,128)S(1)}, f32[32,256]{1,0:T(8,128)S(1)}) custom-call(s32[4]{0:T(128)S(1)} %pad_add_fusion.1.team_ref.info_ref, f32[32,256]{1,0:T(8,128)S(1)} %bitcast.23, f32[544,128]{1,0:T(8,128)S(1)} %get-tuple-element.102.refs_0_, ...), custom_call_target="tpu_custom_call" | custom-call | tf_op jit(solution)/shard_map/gather_maps/pallas_call | solution.py:541
  88.7 1.8 %collective-permute-start.6 = (f32[32,256]{1,0:T(8,128)S(1)}, f32[32,256]{1,0:T(8,128)S(1)}, u32[]{:S(2)}, u32[]{:S(2)}) collective-permute-start(f32[32,256]{1,0:T(8,128)S(1)} %get-tuple-element.104), channel_id=1, source_target_pairs={{0,64},{2,66},{4,68},{6,70},{8,200},{10,202},{12,204},{14,206},{16... | collective-permute-start | bytes 98312 | tf_op jit(solution)/shard_map/ppermute | solution.py:569
  90.5 3.1 %row_map.1 = (bf16[512,256]{1,0:T(8,128)(2,1)S(1)}, bf16[512,256]{1,0:T(8,128)(2,1)S(1)}, f32[32,256]{1,0:T(8,128)S(1)}, f32[544,256]{1,0:T(8,128)S(1)}) custom-call(s32[4]{0:T(128)S(1)} %pad_add_fusion.1.team_ref.info_ref, bf16[4,512,256]{2,1,0:T(8,128)(2,1)S(1)} %get-tuple-element.105.high_ref, bf16[4,512,256]{2,1,0:T(8,128)(2,1)S(1)} %get-tuple-element.106.low_ref, ...), custom_call_target="tpu_custom_call" | custom-call | tf_op jit(solution)/shard_map/row_map/pallas_call | solution.py:559
  96.0 1.7 %prefix_map.1 = (f32[544,256]{1,0:T(8,128)S(1)}, f32[544,256]{1,0:T(8,128)S(1)}) custom-call(s32[4]{0:T(128)S(1)} %pad_add_fusion.1.team_ref.info_ref, bf16[4,512,256]{2,1,0:T(8,128)(2,1)S(1)} %get-tuple-element.105.high_ref, bf16[4,512,256]{2,1,0:T(8,128)(2,1)S(1)} %get-tuple-element.106.low_ref, f32[4,32,256]{2,1,0:T(8,128)S(1)} %get-tuple-element.107.flow_ref, ...), custom_call_target="tpu_custom_call" | custom-call | tf_op jit(solution)/shard_map/prefix_map/pallas_call | solution.py:559
  97.6 2.4 %collective-permute-done.7.state_ref = f32[32,256]{1,0:T(8,128)S(1)} collective-permute-done((f32[32,256]{1,0:T(8,128)S(1)}, f32[32,256]{1,0:T(8,128)S(1)}, u32[]{:S(2)}, u32[]{:S(2)}) %collective-permute-start.7) | collective-permute-done | bytes 32800 | tf_op jit(solution)/shard_map/ppermute | solution.py:569
  100.8 1.7 %entry_map.1 = (bf16[2,512,256]{2,1,0:T(8,128)(2,1)S(1)}, bf16[2,512,256]{2,1,0:T(8,128)(2,1)S(1)}, f32[2,32,256]{2,1,0:T(8,128)S(1)}) custom-call(s32[4]{0:T(128)S(1)} %pad_add_fusion.1.team_ref.info_ref, f32[544,256]{1,0:T(8,128)S(1)} %get-tuple-element.119.prefix_ref, f32[544,256]{1,0:T(8,128)S(1)} %get-tuple-element.120.inner_ref, ...), custom_call_target="tpu_custom_call" | custom-call | tf_op jit(solution)/shard_map/entry_map/pallas_call | solution.py:559
  102.5 3.4 %collective-permute-done.8.state_ref = f32[32,256]{1,0:T(8,128)S(1)} collective-permute-done((f32[32,256]{1,0:T(8,128)S(1)}, f32[32,256]{1,0:T(8,128)S(1)}, u32[]{:S(2)}, u32[]{:S(2)}) %collective-permute-start.8) | collective-permute-done | bytes 32800 | tf_op jit(solution)/shard_map/ppermute | solution.py:569
  105.9 1.7 %inflow.1 = f32[8,128,128]{2,1,0:T(8,128)} custom-call(s32[4]{0:T(128)S(1)} %pad_add_fusion.1.team_ref.info_ref, f32[32,256]{1,0:T(8,128)S(1)} %bitcast.26, f32[32,256]{1,0:T(8,128)S(1)} %collective-permute-done.8.state_ref, bf16[2,512,256]{2,1,0:T(8,128)(2,1)S(1)} %get-tuple-element.121.high_ref, bf16[2,512,256]{2,1,0:T(8,128)(2,1)S(1)} %get-tuple-element.122.low_ref, ...), custom_call_target="tpu_custom_call" | custom-call | tf_op jit(solution)/shard_map/inflow/pallas_call | solution.py:559
  107.6 3.3 %reduce-scatter.3.cloned.1.call-done = f32[1,64,256]{2,1,0:T(8,128)} async-done(((f32[8,64,256]{2,1,0:T(8,128)}), f32[1,64,256]{2,1,0:T(8,128)}) %reduce-scatter.3.cloned.1.call-update) | async-done | bytes 65552 | tf_op jit(solution)/shard_map/reduce_scatter | solution.py:472
  110.9 7.3 %all-to-all-done.1.recv_ref = f32[8,512,128]{2,1,0:T(8,128)} async-done(((f32[8,512,128]{2,1,0:T(8,128)}), f32[8,512,128]{2,1,0:T(8,128)}, u32[]{:S(2)}, u32[]{:S(2)}) %all-to-all-start.1) | async-done | bytes 2097184 | tf_op jit(solution)/shard_map/all_to_all | solution.py:400
  118.2 3.5 %all-to-all-start.2 = ((f32[8,128,128]{2,1,0:T(8,128)}), f32[8,128,128]{2,1,0:T(8,128)S(1)}, u32[]{:S(2)}, u32[]{:S(2)}) async-start(f32[8,128,128]{2,1,0:T(8,128)} %inflow.1), calls=%async_computation.4 | async-start | bytes 1048576 | tf_op jit(solution)/shard_map/all_to_all | solution.py:400
  122.5 2.6 %arrange_rows.1 = (bf16[2,2,2,256,256]{4,3,2,1,0:T(8,128)(2,1)S(1)}, bf16[2,2,2,256,256]{4,3,2,1,0:T(8,128)(2,1)S(1)}, f32[2,2,2,64,256]{4,3,2,1,0:T(8,128)S(1)}) custom-call(s32[2]{0:T(128)S(1)} %pad_add_fusion.3.place_ref, s32[2,64]{1,0:T(2,128)S(1)} %get-tuple-element.266, f32[8,512,128]{2,1,0:T(8,128)} %all-to-all-done.1.recv_ref, ...), custom_call_target="tpu_custom_call" | custom-call | tf_op jit(solution)/shard_map/arrange_rows/pallas_call | solution.py:559
  125.2 12.4 %all-to-all-done.2.last_ref = f32[8,128,128]{2,1,0:T(8,128)S(1)} async-done(((f32[8,128,128]{2,1,0:T(8,128)}), f32[8,128,128]{2,1,0:T(8,128)S(1)}, u32[]{:S(2)}, u32[]{:S(2)}) %all-to-all-start.2) | async-done | bytes 524320 | tf_op jit(solution)/shard_map/all_to_all | solution.py:400
  (45 shorter events, 15.1 us)
Async XLA Ops:
  8.0 29.3 %copy-start = (f32[2,2,256,64]{2,3,1,0:T(8,128)S(1)}, f32[2,2,256,64]{2,3,1,0:T(8,128)}, u32[]{:S(2)}) copy-start(f32[2,2,256,64]{2,3,1,0:T(8,128)} %param.11) | copy-start | bytes 786436
  14.1 8.6 %copy-start.10 = (s32[2,64]{1,0:T(2,128)S(1)}, s32[2,64]{1,0:T(2,128)}, u32[]{:S(2)}) copy-start(s32[2,64]{1,0:T(2,128)} %inject_ref.4) | copy-start | bytes 1540
  14.1 10.2 %copy-start.8 = (f32[2,2,256,64]{2,3,1,0:T(8,128)S(1)}, f32[2,2,256,64]{2,3,1,0:T(8,128)}, u32[]{:S(2)}) copy-start(f32[2,2,256,64]{2,3,1,0:T(8,128)} %param.9) | copy-start | bytes 786436
  14.1 43.0 %all-to-all-start = ((f32[8,320,128]{2,1,0:T(8,128)}), f32[8,320,128]{2,1,0:T(8,128)S(1)}, u32[]{:S(2)}, u32[]{:S(2)}) async-start(f32[8,320,128]{2,1,0:T(8,128)} %interface_terms.1), calls=%async_computation.1 | async-start | bytes 2621440 | tf_op jit(solution)/shard_map/all_to_all | solution.py:400
  25.5 0.7 copy-start.5
  26.2 2.3 %copy-start.6 = (bf16[2,128,256]{2,1,0:T(8,128)(2,1)}, bf16[2,128,256]{2,1,0:T(8,128)(2,1)S(1)}, u32[]{:S(2)}) copy-start(bf16[2,128,256]{2,1,0:T(8,128)(2,1)S(1)} %get-tuple-element.93.low_ref) | copy-start | bytes 393220
  26.3 1.2 copy-start.4
  37.4 19.9 %copy-start.9 = (f32[256,256]{1,0:T(8,128)}, f32[256,256]{1,0:T(8,128)S(1)}, u32[]{:S(2)}) copy-start(f32[256,256]{1,0:T(8,128)S(1)} %get-tuple-element.127.extra_ref) | copy-start | bytes 786436
  57.3 60.9 %all-to-all-start.1 = ((f32[8,512,128]{2,1,0:T(8,128)}), f32[8,512,128]{2,1,0:T(8,128)}, u32[]{:S(2)}, u32[]{:S(2)}) async-start(f32[8,512,128]{2,1,0:T(8,128)} %get-tuple-element.96), calls=%async_computation.2 | async-start | bytes 4194304 | tf_op jit(solution)/shard_map/all_to_all | solution.py:400
  61.6 49.3 %reduce-scatter.3.cloned.1.call-start = ((), (), s32[]{:S(2)}) async-start(), calls=%async_computation.5 | async-start | bytes 589824 | tf_op jit(solution)/shard_map/reduce_scatter | solution.py:472
  65.0 9.6 %collective-permute-start.2 = (f32[544,128]{1,0:T(8,128)S(1)}, f32[544,128]{1,0:T(8,128)S(1)}, u32[]{:S(2)}, u32[]{:S(2)}) collective-permute-start(f32[544,128]{1,0:T(8,128)S(1)} %get-tuple-element.102.refs_0_), channel_id=1, source_target_pairs={{0,16},{16,32},{32,48},{48,0},{64,80},{80,96},{96,112},{112,64},{1... | collective-permute-start | bytes 835592 | tf_op jit(solution)/shard_map/ppermute | solution.py:527
  66.6 9.6 %collective-permute-start.1 = (f32[544,128]{1,0:T(8,128)S(1)}, f32[544,128]{1,0:T(8,128)S(1)}, u32[]{:S(2)}, u32[]{:S(2)}) collective-permute-start(f32[544,128]{1,0:T(8,128)S(1)} %get-tuple-element.103.refs_1_), channel_id=1, source_target_pairs={{0,48},{16,0},{32,16},{48,32},{64,112},{80,64},{96,80},{112,96},{1... | collective-permute-start | bytes 835592 | tf_op jit(solution)/shard_map/ppermute | solution.py:527
  67.1 15.1 %collective-permute-start = (f32[544,128]{1,0:T(8,128)S(1)}, f32[544,128]{1,0:T(8,128)S(1)}, u32[]{:S(2)}, u32[]{:S(2)}) collective-permute-start(f32[544,128]{1,0:T(8,128)S(1)} %get-tuple-element.102.refs_0_), channel_id=1, source_target_pairs={{0,48},{16,0},{32,16},{48,32},{64,112},{80,64},{96,80},{112,96},{1... | collective-permute-start | bytes 835592 | tf_op jit(solution)/shard_map/ppermute | solution.py:527
  68.8 13.4 %collective-permute-start.5 = (f32[544,128]{1,0:T(8,128)S(1)}, f32[544,128]{1,0:T(8,128)S(1)}, u32[]{:S(2)}, u32[]{:S(2)}) collective-permute-start(f32[544,128]{1,0:T(8,128)S(1)} %get-tuple-element.103.refs_1_), channel_id=1, source_target_pairs={{0,16},{16,32},{32,48},{48,0},{64,80},{80,96},{96,112},{112,64},{1... | collective-permute-start | bytes 835592 | tf_op jit(solution)/shard_map/ppermute | solution.py:527
  74.6 11.0 %collective-permute-start.3 = (f32[544,128]{1,0:T(8,128)S(1)}, f32[544,128]{1,0:T(8,128)S(1)}, u32[]{:S(2)}, u32[]{:S(2)}) collective-permute-start(f32[544,128]{1,0:T(8,128)S(1)} %collective-permute-done.2.refs_6_), channel_id=1, source_target_pairs={{0,16},{16,32},{32,48},{48,0},{64,80},{80,96},{96,112},{112,64},{1... | collective-permute-start | bytes 835592 | tf_op jit(solution)/shard_map/ppermute | solution.py:527
  76.2 10.7 %collective-permute-start.4 = (f32[544,128]{1,0:T(8,128)S(1)}, f32[544,128]{1,0:T(8,128)S(1)}, u32[]{:S(2)}, u32[]{:S(2)}) collective-permute-start(f32[544,128]{1,0:T(8,128)S(1)} %collective-permute-done.1.refs_3_), channel_id=1, source_target_pairs={{0,48},{16,0},{32,16},{48,32},{64,112},{80,64},{96,80},{112,96},{1... | collective-permute-start | bytes 835592 | tf_op jit(solution)/shard_map/ppermute | solution.py:527
  88.7 5.4 %collective-permute-start.6 = (f32[32,256]{1,0:T(8,128)S(1)}, f32[32,256]{1,0:T(8,128)S(1)}, u32[]{:S(2)}, u32[]{:S(2)}) collective-permute-start(f32[32,256]{1,0:T(8,128)S(1)} %get-tuple-element.104), channel_id=1, source_target_pairs={{0,64},{2,66},{4,68},{6,70},{8,200},{10,202},{12,204},{14,206},{16... | collective-permute-start | bytes 98312 | tf_op jit(solution)/shard_map/ppermute | solution.py:569
  94.9 5.2 %collective-permute-start.7 = (f32[32,256]{1,0:T(8,128)S(1)}, f32[32,256]{1,0:T(8,128)S(1)}, u32[]{:S(2)}, u32[]{:S(2)}) collective-permute-start(f32[32,256]{1,0:T(8,128)S(1)} %row_step.2), channel_id=1, source_target_pairs={{0,64},{2,66},{4,68},{6,70},{8,200},{10,202},{12,204},{14,206},{16... | collective-permute-start | bytes 98312 | tf_op jit(solution)/shard_map/ppermute | solution.py:569
  100.8 5.2 %collective-permute-start.8 = (f32[32,256]{1,0:T(8,128)S(1)}, f32[32,256]{1,0:T(8,128)S(1)}, u32[]{:S(2)}, u32[]{:S(2)}) collective-permute-start(f32[32,256]{1,0:T(8,128)S(1)} %row_step.3), channel_id=1, source_target_pairs={{0,64},{2,66},{4,68},{6,70},{8,200},{10,202},{12,204},{14,206},{16... | collective-permute-start | bytes 98312 | tf_op jit(solution)/shard_map/ppermute | solution.py:569
  118.2 19.4 %all-to-all-start.2 = ((f32[8,128,128]{2,1,0:T(8,128)}), f32[8,128,128]{2,1,0:T(8,128)S(1)}, u32[]{:S(2)}, u32[]{:S(2)}) async-start(f32[8,128,128]{2,1,0:T(8,128)} %inflow.1), calls=%async_computation.4 | async-start | bytes 1048576 | tf_op jit(solution)/shard_map/all_to_all | solution.py:400
  121.7 0.8 copy-start.7
Sparse Core Ops, SparseCore 1:
  64.6 46.3 reduce-scatter.2

commit v15 on v12

--- a/solution.py
+++ b/solution.py
@@ -51,21 +51,20 @@
 def interface_kernel(inject_ref, src_hbm, g_hbm, out_ref, g_ref, src_ref, sems, src_sem):
     first = lax.axis_index("slab") * 2
     modes, width = src_ref.shape[2], src_ref.shape[3]
-    lanes = width // 2
     lead = width // 8
     fetch_src = pltpu.make_async_copy(src_hbm, src_ref, src_sem)
     fetch_src.start()
     fetches = {}
     for slab in range(2):
         for plane in range(2):
-            for side in range(2):
+            for sweep in range(2):
                 fetch = pltpu.make_async_copy(
-                    g_hbm.at[slab, plane, :, side * lanes : (side + 1) * lanes],
-                    g_ref.at[slab, plane, side],
-                    sems.at[slab, plane, side],
+                    g_hbm.at[slab, plane, :, 1 - sweep, :],
+                    g_ref.at[slab, plane, sweep],
+                    sems.at[slab, plane, sweep],
                 )
                 fetch.start()
-                fetches[slab, plane, side] = fetch
+                fetches[slab, plane, sweep] = fetch
     rows = lax.broadcasted_iota(jnp.int32, (lead, width), 0)
     cols = lax.broadcasted_iota(jnp.int32, (lead, width), 1)
     targets = [
@@ -73,7 +72,6 @@
         for sweep in range(2)
     ]
     fetch_src.wait()
-    count = g_ref.shape[3] // 8
     total = [0.0] * 4
     for slab in range(2):
         chosen = [target == (first + slab).astype(F32) for target in targets]
@@ -83,17 +81,9 @@
             source = [jnp.where(chosen[sweep], src_ref[sweep, part], 0.0) for part in range(2)]
             left.append(split(jnp.concatenate([unit] + source, axis=0)))
         for plane in range(2):
-            for side in range(2):
-                fetches[slab, plane, side].wait()
             for sweep in range(2):
-                picked = jnp.concatenate(
-                    [
-                        g_ref[slab, plane, side, pl.ds(1 - sweep, count, stride=8), :]
-                        for side in range(2)
-                    ],
-                    axis=1,
-                )
-                term = mm3(left[sweep], split(picked), True)
+                fetches[slab, plane, sweep].wait()
+                term = mm3(left[sweep], split(g_ref[slab, plane, sweep]), True)
                 order = slab if sweep == 0 else 1 - slab
                 for member in range(4):
                     put(out_ref, sweep * 4 + member, (order * 2 + plane) * lead, term[:lead])
@@ -436,14 +426,14 @@
         out_specs=whole((8, 2 * block_rows, LANES)),
         out_shape=jax.ShapeDtypeStruct((8, 2 * block_rows, LANES), F32),
         scratch_shapes=[
-            pltpu.VMEM((2, 2, 2, orbitals, width // 2), F32),
+            pltpu.VMEM((2, 2, 2, size, width), F32),
             pltpu.VMEM(sources.shape, F32),
             pltpu.SemaphoreType.DMA((2, 2, 2)),
             pltpu.SemaphoreType.DMA,
         ],
         compiler_params=params(LARGE),
         name="interface_terms",
-    )(inject, sources, diag_inverse)
+    )(inject, sources, diag_inverse.reshape(2, 2, size, orbitals // size, width))
     sent, inject_after = lax.optimization_barrier((sent, inject))
     received = exchange(sent)
 

time: 148 us -> 147 us (level)
  no operation moved by 1% of the time
where the time goes in v15:
time: 147 us; the launch traced here: 146 us
  waiting for transfers between devices  65.9 us (45%)
  Pallas kernels  34.5 us (23%)
  starting transfers between devices  25.5 us (17%)
  between operations  16.3 us (11%)
  local copies, waits for them, and re-layouts  2.95 us (2%)
    all_to_all x3, waiting for transfers between devices, exchange(): return lax.all_to_all(value, 'col', split_axis=0, concat_axis=0, tiled=True)  39.5 us
    all_to_all x3, starting transfers between devices, exchange(): return lax.all_to_all(value, 'col', split_axis=0, concat_axis=0, tiled=True)  16.5 us
    ppermute x6, waiting for transfers between devices, turn(): lax.ppermute(value, 'slab', [(slab, slab // 4 * 4 + (slab + step) % 4) fo...  15.7 us
    pallas_call x7, Pallas kernels, local(): pl.pallas_call(kernel, in_specs=[SMEM] + [VMEM] * (len(args) - 1), out_sp...  12.3 us
    pallas_call x1, Pallas kernels, chunk_terms(): pl.pallas_call(spread_kernel, grid=(8,), in_specs=[whole(terms.shape), wh...  8.73 us
    ppermute x3, waiting for transfers between devices, hop(): return lax.ppermute(value, ('slab', 'col'), pairs)  6.33 us
    ppermute x6, starting transfers between devices, turn(): lax.ppermute(value, 'slab', [(slab, slab // 4 * 4 + (slab + step) % 4) fo...  6.15 us
    pallas_call x1, Pallas kernels, on_device(): pl.pallas_call(interface_kernel, grid=(1,), in_specs=[whole(inject.shape)...  5.45 us
  transfers between devices with their start and end apart: 13, of which 11 were waited for; matrix products, arithmetic and copies ran while one was open for 1% of the time, Pallas kernels for 19%

profile of v15, /device:TPU:8, one launch (start us, length us, event | category | flops | bytes accessed | tf_op | source)
XLA Modules:
  0.0 146.2 jit_solution(14296043074044847683)
XLA Ops:
  8.0 5.5 %interface_terms.1 = f32[8,320,128]{2,1,0:T(8,128)} custom-call(s32[2,64]{1,0:T(2,128)} %inject_ref.4, f32[2,2,64,256]{3,2,1,0:T(8,128)} %bitcast.29, f32[2,2,256,8,256]{4,3,2,1,0:T(8,128)} %bitcast.28), custom_call_target="tpu_custom_call" | custom-call | tf_op jit(solution)/shard_map/interface_terms/pallas_call | solution.py:422
  13.5 8.6 %all-to-all-start = ((f32[8,320,128]{2,1,0:T(8,128)}), f32[8,320,128]{2,1,0:T(8,128)S(1)}, u32[]{:S(2)}, u32[]{:S(2)}) async-start(f32[8,320,128]{2,1,0:T(8,128)} %interface_terms.1), calls=%async_computation.1 | async-start | bytes 2621440 | tf_op jit(solution)/shard_map/all_to_all | solution.py:399
  27.8 8.7 %spread_terms.2 = (f32[8,512,128]{2,1,0:T(8,128)}, f32[8,64,256]{2,1,0:T(8,128)}) custom-call(bf16[2,128,256]{2,1,0:T(8,128)(2,1)} %copy-done.5, bf16[2,128,256]{2,1,0:T(8,128)(2,1)} %copy-done.6, f32[2,2,2048,256]{3,2,1,0:T(8,128)} %g_ref.1), custom_call_target="tpu_custom_call" | custom-call | tf_op jit(solution)/shard_map/spread_terms/pallas_call | solution.py:450
  36.7 19.8 %all-to-all-done.recv_ref = f32[8,320,128]{2,1,0:T(8,128)S(1)} async-done(((f32[8,320,128]{2,1,0:T(8,128)}), f32[8,320,128]{2,1,0:T(8,128)S(1)}, u32[]{:S(2)}, u32[]{:S(2)}) %all-to-all-start) | async-done | bytes 1310752 | tf_op jit(solution)/shard_map/all_to_all | solution.py:399
  56.6 4.4 %all-to-all-start.1 = ((f32[8,512,128]{2,1,0:T(8,128)}), f32[8,512,128]{2,1,0:T(8,128)}, u32[]{:S(2)}, u32[]{:S(2)}) async-start(f32[8,512,128]{2,1,0:T(8,128)} %get-tuple-element.96), calls=%async_computation.2 | async-start | bytes 4194304 | tf_op jit(solution)/shard_map/all_to_all | solution.py:399
  61.6 2.8 %pair_map.1 = (f32[544,128]{1,0:T(8,128)S(1)}, f32[544,128]{1,0:T(8,128)S(1)}, f32[32,256]{1,0:T(8,128)S(1)}, f32[512,256]{1,0:T(8,128)S(1)}) custom-call(s32[4]{0:T(128)S(1)} %pad_add_fusion.1.team_ref.info_ref, f32[8,320,128]{2,1,0:T(8,128)S(1)} %all-to-all-done.recv_ref, f32[2,512,256]{2,1,0:T(8,128)S(1)} %coupling_rows.1.x_ref, ...), custom_call_target="tpu_custom_call" | custom-call | tf_op jit(solution)/shard_map/pair_map/pallas_call | solution.py:511
  64.3 1.7 %collective-permute-start.2 = (f32[544,128]{1,0:T(8,128)S(1)}, f32[544,128]{1,0:T(8,128)S(1)}, u32[]{:S(2)}, u32[]{:S(2)}) collective-permute-start(f32[544,128]{1,0:T(8,128)S(1)} %get-tuple-element.102.refs_0_), channel_id=1, source_target_pairs={{0,16},{16,32},{32,48},{48,0},{64,80},{80,96},{96,112},{112,64},{1... | collective-permute-start | bytes 835592 | tf_op jit(solution)/shard_map/ppermute | solution.py:526
  66.4 1.7 %collective-permute-start = (f32[544,128]{1,0:T(8,128)S(1)}, f32[544,128]{1,0:T(8,128)S(1)}, u32[]{:S(2)}, u32[]{:S(2)}) collective-permute-start(f32[544,128]{1,0:T(8,128)S(1)} %get-tuple-element.102.refs_0_), channel_id=1, source_target_pairs={{0,48},{16,0},{32,16},{48,32},{64,112},{80,64},{96,80},{112,96},{1... | collective-permute-start | bytes 835592 | tf_op jit(solution)/shard_map/ppermute | solution.py:526
  68.5 5.5 %collective-permute-done.2.refs_6_ = f32[544,128]{1,0:T(8,128)S(1)} collective-permute-done((f32[544,128]{1,0:T(8,128)S(1)}, f32[544,128]{1,0:T(8,128)S(1)}, u32[]{:S(2)}, u32[]{:S(2)}) %collective-permute-start.2) | collective-permute-done | bytes 278560 | tf_op jit(solution)/shard_map/ppermute | solution.py:526
  76.0 5.5 %collective-permute-done.refs_2_ = f32[544,128]{1,0:T(8,128)S(1)} collective-permute-done((f32[544,128]{1,0:T(8,128)S(1)}, f32[544,128]{1,0:T(8,128)S(1)}, u32[]{:S(2)}, u32[]{:S(2)}) %collective-permute-start) | collective-permute-done | bytes 278560 | tf_op jit(solution)/shard_map/ppermute | solution.py:526
  81.5 3.4 %collective-permute-done.3.refs_4_ = f32[544,128]{1,0:T(8,128)S(1)} collective-permute-done((f32[544,128]{1,0:T(8,128)S(1)}, f32[544,128]{1,0:T(8,128)S(1)}, u32[]{:S(2)}, u32[]{:S(2)}) %collective-permute-start.3) | collective-permute-done | bytes 278560 | tf_op jit(solution)/shard_map/ppermute | solution.py:526
  86.2 1.9 %gather_maps.1 = (bf16[4,512,256]{2,1,0:T(8,128)(2,1)S(1)}, bf16[4,512,256]{2,1,0:T(8,128)(2,1)S(1)}, f32[4,32,256]{2,1,0:T(8,128)S(1)}, f32[32,256]{1,0:T(8,128)S(1)}) custom-call(s32[4]{0:T(128)S(1)} %pad_add_fusion.1.team_ref.info_ref, f32[32,256]{1,0:T(8,128)S(1)} %bitcast.23, f32[544,128]{1,0:T(8,128)S(1)} %get-tuple-element.102.refs_0_, ...), custom_call_target="tpu_custom_call" | custom-call | tf_op jit(solution)/shard_map/gather_maps/pallas_call | solution.py:540
  88.1 1.8 %collective-permute-start.6 = (f32[32,256]{1,0:T(8,128)S(1)}, f32[32,256]{1,0:T(8,128)S(1)}, u32[]{:S(2)}, u32[]{:S(2)}) collective-permute-start(f32[32,256]{1,0:T(8,128)S(1)} %get-tuple-element.104), channel_id=1, source_target_pairs={{0,64},{2,66},{4,68},{6,70},{8,200},{10,202},{12,204},{14,206},{16... | collective-permute-start | bytes 98312 | tf_op jit(solution)/shard_map/ppermute | solution.py:568
  89.9 3.1 %row_map.1 = (bf16[512,256]{1,0:T(8,128)(2,1)S(1)}, bf16[512,256]{1,0:T(8,128)(2,1)S(1)}, f32[32,256]{1,0:T(8,128)S(1)}, f32[544,256]{1,0:T(8,128)S(1)}) custom-call(s32[4]{0:T(128)S(1)} %pad_add_fusion.1.team_ref.info_ref, bf16[4,512,256]{2,1,0:T(8,128)(2,1)S(1)} %get-tuple-element.105.high_ref, bf16[4,512,256]{2,1,0:T(8,128)(2,1)S(1)} %get-tuple-element.106.low_ref, ...), custom_call_target="tpu_custom_call" | custom-call | tf_op jit(solution)/shard_map/row_map/pallas_call | solution.py:558
  95.3 1.7 %prefix_map.1 = (f32[544,256]{1,0:T(8,128)S(1)}, f32[544,256]{1,0:T(8,128)S(1)}) custom-call(s32[4]{0:T(128)S(1)} %pad_add_fusion.1.team_ref.info_ref, bf16[4,512,256]{2,1,0:T(8,128)(2,1)S(1)} %get-tuple-element.105.high_ref, bf16[4,512,256]{2,1,0:T(8,128)(2,1)S(1)} %get-tuple-element.106.low_ref, f32[4,32,256]{2,1,0:T(8,128)S(1)} %get-tuple-element.107.flow_ref, ...), custom_call_target="tpu_custom_call" | custom-call | tf_op jit(solution)/shard_map/prefix_map/pallas_call | solution.py:558
  97.0 2.4 %collective-permute-done.7.state_ref = f32[32,256]{1,0:T(8,128)S(1)} collective-permute-done((f32[32,256]{1,0:T(8,128)S(1)}, f32[32,256]{1,0:T(8,128)S(1)}, u32[]{:S(2)}, u32[]{:S(2)}) %collective-permute-start.7) | collective-permute-done | bytes 32800 | tf_op jit(solution)/shard_map/ppermute | solution.py:568
  100.2 1.7 %entry_map.1 = (bf16[2,512,256]{2,1,0:T(8,128)(2,1)S(1)}, bf16[2,512,256]{2,1,0:T(8,128)(2,1)S(1)}, f32[2,32,256]{2,1,0:T(8,128)S(1)}) custom-call(s32[4]{0:T(128)S(1)} %pad_add_fusion.1.team_ref.info_ref, f32[544,256]{1,0:T(8,128)S(1)} %get-tuple-element.119.prefix_ref, f32[544,256]{1,0:T(8,128)S(1)} %get-tuple-element.120.inner_ref, ...), custom_call_target="tpu_custom_call" | custom-call | tf_op jit(solution)/shard_map/entry_map/pallas_call | solution.py:558
  101.9 3.4 %collective-permute-done.8.state_ref = f32[32,256]{1,0:T(8,128)S(1)} collective-permute-done((f32[32,256]{1,0:T(8,128)S(1)}, f32[32,256]{1,0:T(8,128)S(1)}, u32[]{:S(2)}, u32[]{:S(2)}) %collective-permute-start.8) | collective-permute-done | bytes 32800 | tf_op jit(solution)/shard_map/ppermute | solution.py:568
  105.3 1.7 %inflow.1 = f32[8,128,128]{2,1,0:T(8,128)} custom-call(s32[4]{0:T(128)S(1)} %pad_add_fusion.1.team_ref.info_ref, f32[32,256]{1,0:T(8,128)S(1)} %bitcast.26, f32[32,256]{1,0:T(8,128)S(1)} %collective-permute-done.8.state_ref, bf16[2,512,256]{2,1,0:T(8,128)(2,1)S(1)} %get-tuple-element.121.high_ref, bf16[2,512,256]{2,1,0:T(8,128)(2,1)S(1)} %get-tuple-element.122.low_ref, ...), custom_call_target="tpu_custom_call" | custom-call | tf_op jit(solution)/shard_map/inflow/pallas_call | solution.py:558
  107.0 3.8 %reduce-scatter.3.cloned.1.call-done = f32[1,64,256]{2,1,0:T(8,128)} async-done(((f32[8,64,256]{2,1,0:T(8,128)}), f32[1,64,256]{2,1,0:T(8,128)}) %reduce-scatter.3.cloned.1.call-update) | async-done | bytes 65552 | tf_op jit(solution)/shard_map/reduce_scatter | solution.py:471
  110.8 6.7 %all-to-all-done.1.recv_ref = f32[8,512,128]{2,1,0:T(8,128)} async-done(((f32[8,512,128]{2,1,0:T(8,128)}), f32[8,512,128]{2,1,0:T(8,128)}, u32[]{:S(2)}, u32[]{:S(2)}) %all-to-all-start.1) | async-done | bytes 2097184 | tf_op jit(solution)/shard_map/all_to_all | solution.py:399
  117.6 3.5 %all-to-all-start.2 = ((f32[8,128,128]{2,1,0:T(8,128)}), f32[8,128,128]{2,1,0:T(8,128)S(1)}, u32[]{:S(2)}, u32[]{:S(2)}) async-start(f32[8,128,128]{2,1,0:T(8,128)} %inflow.1), calls=%async_computation.4 | async-start | bytes 1048576 | tf_op jit(solution)/shard_map/all_to_all | solution.py:399
  121.9 2.6 %arrange_rows.1 = (bf16[2,2,2,256,256]{4,3,2,1,0:T(8,128)(2,1)S(1)}, bf16[2,2,2,256,256]{4,3,2,1,0:T(8,128)(2,1)S(1)}, f32[2,2,2,64,256]{4,3,2,1,0:T(8,128)S(1)}) custom-call(s32[2]{0:T(128)S(1)} %pad_add_fusion.3.place_ref, s32[2,64]{1,0:T(2,128)S(1)} %get-tuple-element.266, f32[8,512,128]{2,1,0:T(8,128)} %all-to-all-done.1.recv_ref, ...), custom_call_target="tpu_custom_call" | custom-call | tf_op jit(solution)/shard_map/arrange_rows/pallas_call | solution.py:558
  124.5 12.9 %all-to-all-done.2.last_ref = f32[8,128,128]{2,1,0:T(8,128)S(1)} async-done(((f32[8,128,128]{2,1,0:T(8,128)}), f32[8,128,128]{2,1,0:T(8,128)S(1)}, u32[]{:S(2)}, u32[]{:S(2)}) %all-to-all-start.2) | async-done | bytes 524320 | tf_op jit(solution)/shard_map/all_to_all | solution.py:399
  (45 shorter events, 15.1 us)
Async XLA Ops:
  8.0 28.6 %copy-start = (f32[2,2,256,64]{2,3,1,0:T(8,128)S(1)}, f32[2,2,256,64]{2,3,1,0:T(8,128)}, u32[]{:S(2)}) copy-start(f32[2,2,256,64]{2,3,1,0:T(8,128)} %param.11) | copy-start | bytes 786436
  13.5 8.6 %copy-start.10 = (s32[2,64]{1,0:T(2,128)S(1)}, s32[2,64]{1,0:T(2,128)}, u32[]{:S(2)}) copy-start(s32[2,64]{1,0:T(2,128)} %inject_ref.4) | copy-start | bytes 1540
  13.5 10.2 %copy-start.8 = (f32[2,2,256,64]{2,3,1,0:T(8,128)S(1)}, f32[2,2,256,64]{2,3,1,0:T(8,128)}, u32[]{:S(2)}) copy-start(f32[2,2,256,64]{2,3,1,0:T(8,128)} %param.9) | copy-start | bytes 786436
  13.5 43.0 %all-to-all-start = ((f32[8,320,128]{2,1,0:T(8,128)}), f32[8,320,128]{2,1,0:T(8,128)S(1)}, u32[]{:S(2)}, u32[]{:S(2)}) async-start(f32[8,320,128]{2,1,0:T(8,128)} %interface_terms.1), calls=%async_computation.1 | async-start | bytes 2621440 | tf_op jit(solution)/shard_map/all_to_all | solution.py:399
  24.9 0.7 copy-start.5
  25.5 2.3 %copy-start.6 = (bf16[2,128,256]{2,1,0:T(8,128)(2,1)}, bf16[2,128,256]{2,1,0:T(8,128)(2,1)S(1)}, u32[]{:S(2)}) copy-start(bf16[2,128,256]{2,1,0:T(8,128)(2,1)S(1)} %get-tuple-element.93.low_ref) | copy-start | bytes 393220
  25.7 1.2 copy-start.4
  36.7 19.9 %copy-start.9 = (f32[256,256]{1,0:T(8,128)}, f32[256,256]{1,0:T(8,128)S(1)}, u32[]{:S(2)}) copy-start(f32[256,256]{1,0:T(8,128)S(1)} %get-tuple-element.127.extra_ref) | copy-start | bytes 786436
  56.6 60.9 %all-to-all-start.1 = ((f32[8,512,128]{2,1,0:T(8,128)}), f32[8,512,128]{2,1,0:T(8,128)}, u32[]{:S(2)}, u32[]{:S(2)}) async-start(f32[8,512,128]{2,1,0:T(8,128)} %get-tuple-element.96), calls=%async_computation.2 | async-start | bytes 4194304 | tf_op jit(solution)/shard_map/all_to_all | solution.py:399
  61.0 49.8 %reduce-scatter.3.cloned.1.call-start = ((), (), s32[]{:S(2)}) async-start(), calls=%async_computation.5 | async-start | bytes 589824 | tf_op jit(solution)/shard_map/reduce_scatter | solution.py:471
  64.3 9.6 %collective-permute-start.2 = (f32[544,128]{1,0:T(8,128)S(1)}, f32[544,128]{1,0:T(8,128)S(1)}, u32[]{:S(2)}, u32[]{:S(2)}) collective-permute-start(f32[544,128]{1,0:T(8,128)S(1)} %get-tuple-element.102.refs_0_), channel_id=1, source_target_pairs={{0,16},{16,32},{32,48},{48,0},{64,80},{80,96},{96,112},{112,64},{1... | collective-permute-start | bytes 835592 | tf_op jit(solution)/shard_map/ppermute | solution.py:526
  66.0 9.6 %collective-permute-start.1 = (f32[544,128]{1,0:T(8,128)S(1)}, f32[544,128]{1,0:T(8,128)S(1)}, u32[]{:S(2)}, u32[]{:S(2)}) collective-permute-start(f32[544,128]{1,0:T(8,128)S(1)} %get-tuple-element.103.refs_1_), channel_id=1, source_target_pairs={{0,48},{16,0},{32,16},{48,32},{64,112},{80,64},{96,80},{112,96},{1... | collective-permute-start | bytes 835592 | tf_op jit(solution)/shard_map/ppermute | solution.py:526
  66.4 15.1 %collective-permute-start = (f32[544,128]{1,0:T(8,128)S(1)}, f32[544,128]{1,0:T(8,128)S(1)}, u32[]{:S(2)}, u32[]{:S(2)}) collective-permute-start(f32[544,128]{1,0:T(8,128)S(1)} %get-tuple-element.102.refs_0_), channel_id=1, source_target_pairs={{0,48},{16,0},{32,16},{48,32},{64,112},{80,64},{96,80},{112,96},{1... | collective-permute-start | bytes 835592 | tf_op jit(solution)/shard_map/ppermute | solution.py:526
  68.1 13.4 %collective-permute-start.5 = (f32[544,128]{1,0:T(8,128)S(1)}, f32[544,128]{1,0:T(8,128)S(1)}, u32[]{:S(2)}, u32[]{:S(2)}) collective-permute-start(f32[544,128]{1,0:T(8,128)S(1)} %get-tuple-element.103.refs_1_), channel_id=1, source_target_pairs={{0,16},{16,32},{32,48},{48,0},{64,80},{80,96},{96,112},{112,64},{1... | collective-permute-start | bytes 835592 | tf_op jit(solution)/shard_map/ppermute | solution.py:526
  73.9 11.0 %collective-permute-start.3 = (f32[544,128]{1,0:T(8,128)S(1)}, f32[544,128]{1,0:T(8,128)S(1)}, u32[]{:S(2)}, u32[]{:S(2)}) collective-permute-start(f32[544,128]{1,0:T(8,128)S(1)} %collective-permute-done.2.refs_6_), channel_id=1, source_target_pairs={{0,16},{16,32},{32,48},{48,0},{64,80},{80,96},{96,112},{112,64},{1... | collective-permute-start | bytes 835592 | tf_op jit(solution)/shard_map/ppermute | solution.py:526
  75.5 10.7 %collective-permute-start.4 = (f32[544,128]{1,0:T(8,128)S(1)}, f32[544,128]{1,0:T(8,128)S(1)}, u32[]{:S(2)}, u32[]{:S(2)}) collective-permute-start(f32[544,128]{1,0:T(8,128)S(1)} %collective-permute-done.1.refs_3_), channel_id=1, source_target_pairs={{0,48},{16,0},{32,16},{48,32},{64,112},{80,64},{96,80},{112,96},{1... | collective-permute-start | bytes 835592 | tf_op jit(solution)/shard_map/ppermute | solution.py:526
  88.1 5.4 %collective-permute-start.6 = (f32[32,256]{1,0:T(8,128)S(1)}, f32[32,256]{1,0:T(8,128)S(1)}, u32[]{:S(2)}, u32[]{:S(2)}) collective-permute-start(f32[32,256]{1,0:T(8,128)S(1)} %get-tuple-element.104), channel_id=1, source_target_pairs={{0,64},{2,66},{4,68},{6,70},{8,200},{10,202},{12,204},{14,206},{16... | collective-permute-start | bytes 98312 | tf_op jit(solution)/shard_map/ppermute | solution.py:568
  94.2 5.2 %collective-permute-start.7 = (f32[32,256]{1,0:T(8,128)S(1)}, f32[32,256]{1,0:T(8,128)S(1)}, u32[]{:S(2)}, u32[]{:S(2)}) collective-permute-start(f32[32,256]{1,0:T(8,128)S(1)} %row_step.2), channel_id=1, source_target_pairs={{0,64},{2,66},{4,68},{6,70},{8,200},{10,202},{12,204},{14,206},{16... | collective-permute-start | bytes 98312 | tf_op jit(solution)/shard_map/ppermute | solution.py:568
  100.1 5.2 %collective-permute-start.8 = (f32[32,256]{1,0:T(8,128)S(1)}, f32[32,256]{1,0:T(8,128)S(1)}, u32[]{:S(2)}, u32[]{:S(2)}) collective-permute-start(f32[32,256]{1,0:T(8,128)S(1)} %row_step.3), channel_id=1, source_target_pairs={{0,64},{2,66},{4,68},{6,70},{8,200},{10,202},{12,204},{14,206},{16... | collective-permute-start | bytes 98312 | tf_op jit(solution)/shard_map/ppermute | solution.py:568
  117.6 19.9 %all-to-all-start.2 = ((f32[8,128,128]{2,1,0:T(8,128)}), f32[8,128,128]{2,1,0:T(8,128)S(1)}, u32[]{:S(2)}, u32[]{:S(2)}) async-start(f32[8,128,128]{2,1,0:T(8,128)} %inflow.1), calls=%async_computation.4 | async-start | bytes 1048576 | tf_op jit(solution)/shard_map/all_to_all | solution.py:399
  121.1 0.8 copy-start.7
Sparse Core Ops, SparseCore 1:
  64.0 46.8 reduce-scatter.2
